TPU v7x, 32 devices: a whole 2x2x4 slice. The times are simulated.
32 devices in a mesh: gx: 4 (over y, x), gy: 4 (over z), gz: 2 (over core).
Axes of the slice: x: 2, y: 2, z: 4, core: 2. Of those that a mesh axis runs over, the one named last changes fastest.
Arguments:
- phase: int32 [32, 256, 256], P('gx', 'gy', 'gz'), may hold values 0 or 1
- density: float32 [32, 256, 256], P('gx', 'gy', 'gz'), may hold values from 0.5 to 2
- rhs: float32 [1, 32, 256, 256], P(None, 'gx', 'gy', 'gz'), may hold values from -6 to 6
Outputs:
- scaled_solution: float32 [1, 32, 256, 256], P(None, 'gx', 'gy', 'gz')
- residual: float32 [1, 32, 256, 256], P(None, 'gx', 'gy', 'gz')
All inputs are finite; a program needn't handle non-finite values. No bound on the sum of `phase` on one device may be relied on, other than what follows from the above.
Results may differ from a plain program's by a relative error of at most 0.0003.
Values sent between devices are 32-bit elements; how exact they have to be, the bound alone decides.
No kernel may reach another device: no remote copies, remote signals or barrier semaphores. Data moves between devices by JAX's collectives and lax.ppermute only.
A program may use at most 128 MiB of HBM per device.

v0:
```python
import functools

import jax
import jax.numpy as jnp
from jax import lax
from jax.experimental import pallas as pl
from jax.experimental.pallas import tpu as pltpu
from jax.sharding import PartitionSpec as P


DAMPING = 2.0 / 3.0
LANES = 128
WIDE = 256
HALO = 7
FAR = 3
F32 = jnp.float32
VMEM_LIMIT = 24 * 1024 * 1024


class Plan:
    def __init__(self, sizes, shape):
        self.gx, self.gy, self.gz = sizes
        self.px, self.ny, self.nz = shape
        self.nx = self.px * self.gx
        self.by = self.ny // self.gx
        self.blocks = self.gx * self.gy
        self.rows = self.by + 2 * HALO
        self.paired = self.gz == 2
        order = [0, 1, 3, 2] if self.gx == 4 else list(range(self.gx))
        self.place = [order.index(i) for i in range(self.gx)]
        self.order = order

    def device(self, block):
        j, q = divmod(block, self.gx)
        i = self.order[q if j % 2 == 0 else self.gx - 1 - q]
        return i * self.gy + j

    def look_up(self, table, i):
        return sum(jnp.where(i == k, v, 0) for k, v in enumerate(table))

    def start_of(self, i):
        q = self.look_up(self.place, i)
        q = jnp.where(lax.rem(lax.axis_index("gy"), 2) == 0, q, self.gx - 1 - q)
        return pl.multiple_of(q * self.by, self.by)

    def block_here(self):
        q = self.look_up(self.place, lax.axis_index("gx"))
        j = lax.axis_index("gy")
        return j * self.gx + jnp.where(lax.rem(j, 2) == 0, q, self.gx - 1 - q)

    def gx_of(self, block):
        block = jnp.clip(block, 0, self.blocks - 1)
        j, q = lax.div(block, self.gx), lax.rem(block, self.gx)
        return self.look_up(self.order, jnp.where(lax.rem(j, 2) == 0, q, self.gx - 1 - q))

    def is_up(self, block, k, one):
        return lax.rem(lax.div(block, k), 2) == one


def x_up(a, s=1):
    return pltpu.roll(a, a.shape[0] - s, 0)


def x_down(a, s=1):
    return pltpu.roll(a, s, 0)


def z_up(a, g):
    return pltpu.roll(a, a.shape[1] - g, 1)


def z_down(a, g):
    return pltpu.roll(a, g, 1)


def inverse(a):
    r = pl.reciprocal(a, approx=True)
    return r * (2.0 - a * r)


def each(first, last, step, body):
    count = last + 1 - first
    if count <= 2 * step:
        for i in range(first, last + 1):
            body(i)
        return

    def go(c, _):
        for k in range(step):
            body(first + c * step + k)
        return 0

    lax.fori_loop(0, count // step, go, 0)
    for i in range(first + count // step * step, last + 1):
        body(i)


def wave(*stages):
    start = min(first + delay for _, first, _, delay in stages)
    end = max(last + delay for _, _, last, delay in stages)
    full = max(first + delay for _, first, _, delay in stages)
    full_end = min(last + delay for _, _, last, delay in stages)

    def step(t):
        for body, first, last, delay in stages:
            if first <= t - delay <= last:
                body(t - delay)

    def all_of_them(t, _):
        for body, _, _, delay in stages:
            body(t - delay)
        return 0

    if full_end - full < 3:
        full = full_end = end + 1
    for t in range(start, min(full, end + 1)):
        step(t)
    if full <= end:
        lax.fori_loop(full, full_end + 1, all_of_them, 0)
        for t in range(full_end + 1, end + 1):
            step(t)


class Wide:
    def __init__(self, ref):
        self.ref = ref

    def __getitem__(self, key):
        r, xs = key if isinstance(key, tuple) else (key, slice(None))
        return jnp.concatenate([self.ref[r, 0, xs, :], self.ref[r, 1, xs, :]], axis=1)

    def __setitem__(self, key, value):
        r, xs = key if isinstance(key, tuple) else (key, slice(None))
        self.ref[r, 0, xs, :] = value[:, :LANES]
        self.ref[r, 1, xs, :] = value[:, LANES:]


class Level:
    def __init__(self, s, g, kx, ky, kz, d, w, f, step=2):
        self.s, self.g, self.step = s, g, step
        self.kx, self.ky, self.kz, self.d, self.w, self.f = kx, ky, kz, d, w, f

    def beside(self, u, r):
        here = u[r]
        kx, kz = self.kx[r], self.kz[r]
        a = kx * x_up(here, self.s) + x_down(kx * here, self.s)
        b = kz * z_up(here, self.g) + z_down(kz * here, self.g)
        return a + b + (self.ky[r + 1] * u[r + 1] + self.ky[r] * u[r - 1])

    def weigh(self, first, last):
        def body(r):
            self.w[r] = DAMPING * inverse(self.d[r])

        each(first, last, self.step, body)

    def first(self, u, first, last):
        def body(r):
            u[r] = self.w[r] * self.f[r]

        each(first, last, self.step, body)

    def swept(self, u, r):
        return (1.0 / 3.0) * u[r] + self.w[r] * (self.f[r] + self.beside(u, r))

    def sweep(self, u, v, first, last):
        def body(r):
            v[r] = self.swept(u, r)

        each(first, last, self.step, body)

    def residual(self, u, r):
        return self.f[r] + self.beside(u, r) - self.d[r] * u[r]

    def residual_pairs(self, u, out, first, count):
        def body(j):
            out[j] = self.residual(u, first + 2 * j) + self.residual(u, first + 2 * j + 1)

        each(0, count - 1, self.step // 2, body)


def z_pairs(low, g):
    return lambda a: a + jnp.where(low, z_up(a, g), z_down(a, g))


def coarse_coefficients(level, r, x_count):
    even, odd = pl.ds(0, x_count, stride=2), pl.ds(1, x_count, stride=2)
    g = level.g
    low = (lax.broadcasted_iota(jnp.int32, (x_count, WIDE), 1) & g) == 0
    z_pair = z_pairs(low, g)

    def all_x(ref, row):
        return ref[row, even] + ref[row, odd]

    kx = level.kx[r, odd] + level.kx[r + 1, odd]
    inner = level.kx[r, even] + level.kx[r + 1, even] + all_x(level.ky, r + 1)
    kz = all_x(level.kz, r) + all_x(level.kz, r + 1)
    d = all_x(level.d, r) + all_x(level.d, r + 1)
    d = d - 2.0 * (inner + jnp.where(low, kz, 0.0))
    return z_pair(kx), coarse_sum(level.ky, r + 2, x_count, g), jnp.where(low, z_up(kz, g), kz), z_pair(d)


def coarse_sum(ref, r, x_count, g):
    even, odd = pl.ds(0, x_count, stride=2), pl.ds(1, x_count, stride=2)
    low = (lax.broadcasted_iota(jnp.int32, (x_count, WIDE), 1) & g) == 0
    return z_pairs(low, g)(ref[r, even] + ref[r, odd])


def correct(u, v, e, t, x_count, first, last, to):
    def body(j):
        part = e[j]
        t[j, pl.ds(0, x_count, stride=2)] = part
        t[j, pl.ds(1, x_count, stride=2)] = part
        wide = t[j]
        r = to + 2 * (j - first)
        v[r] = u[r] + wide
        v[r + 1] = u[r + 1] + wide

    each(first, last, 2, body)


def pick_lanes(a, lanes):
    return jnp.take_along_axis(a, lanes, axis=1, mode="promise_in_bounds")


def prepare_kernel(plan, phase_in, density_in, rhs_in, *refs):
    outs, (phase, density, rhs, sems) = refs[: plan.gx], refs[plan.gx :]
    pairs = ((phase_in, phase), (density_in, density), (rhs_in, rhs))
    copies = [pltpu.make_async_copy(a, b, sems.at[k]) for k, (a, b) in enumerate(pairs)]
    for copy in copies:
        copy.start()
    for copy in copies:
        copy.wait()
    here = lax.axis_index("gx")
    by, px = plan.by, plan.px
    for k, out in enumerate(outs):
        rows = pl.ds(plan.start_of(here ^ k), by)
        for p in range(px):
            half = jnp.where(phase[p, rows, :] == 1, 500.0, 0.5).astype(F32)
            out[pl.ds(p, by, stride=2 * px), :] = half * density[p, rows, :]
            out[pl.ds(px + p, by, stride=2 * px), :] = rhs[0, p, rows, :]


def gather_kernel(plan, *refs):
    parts, (c, *sets) = refs[: plan.gx], refs[plan.gx :]
    block = plan.block_here()
    for k, part in enumerate(parts):
        c[k] = part[...]
        for one, out in enumerate(sets):
            first = jnp.where(plan.is_up(block, 1, one), plan.by - HALO, 0)
            out[k] = part[pl.ds(first, HALO)]


def down_kernel(plan, c, zc, sides, zsides, *refs):
    near_count = 1 if plan.paired else 2
    pack, nears, refs = refs[0], refs[1 : 1 + near_count], refs[1 + near_count :]
    kx0, ky0, kz0, d0, w0, f0, ub, kx1, ky1, kz1, w1, f1, u1 = [Wide(r) for r in refs[:13]]
    h0, ua, face, r0, uc, r1, d1 = [Wide(r) for r in refs[13:20]]
    stage = refs[20]
    nx, by, rows, gx, px = plan.nx, plan.by, plan.rows, plan.gx, plan.px
    shape = (nx, WIDE)
    block, here = plan.block_here(), lax.axis_index("gx")
    base = block * by - HALO
    y_count, z_count = plan.by * plan.blocks, plan.nz * plan.gz

    x = lax.broadcasted_iota(jnp.int32, shape, 0)
    lane = lax.broadcasted_iota(jnp.int32, shape, 1)
    core = lax.axis_index("gz")
    if plan.paired:
        z = lax.rem(core * LANES + lane, WIDE)
    else:
        z = core * LANES + jnp.where(lane < LANES + LANES // 2, lane, lane - WIDE)
    x_top, x_bottom = x == nx - 1, x == 0
    z_top, z_bottom = z == z_count - 1, z == 0
    z_shut = (z < 0) | (z >= z_count - 1)
    z_out = (z < 0) | (z >= z_count)

    def take(a, b, at, other, r, to):
        y = base + to
        inside = (y >= 0) & (y < y_count)
        for k in range(gx):
            xs = pl.ds(pl.multiple_of((other ^ k) * px, px), px)
            for s, ref in enumerate((a, b)):
                h = jnp.where(inside, ref[at + k, r, 0], 0.5)
                if not plan.paired:
                    h = jnp.where(z_out[:px, s * LANES : (s + 1) * LANES], 0.5, h)
                h0.ref[to, s, xs, :] = h
                f0.ref[to, s, xs, :] = ref[at + k, r, 1]

    each(0, by - 1, 4, lambda r: take(c, zc, 0, here, r, r + HALO))
    up_first = plan.is_up(block, 1, 0)
    below, above = jnp.where(up_first, gx, 0), jnp.where(up_first, 0, gx)
    gx_below, gx_above = plan.gx_of(block - 1), plan.gx_of(block + 1)
    each(0, HALO - 1, 4, lambda r: take(sides, zsides, below, gx_below, r, r))
    each(0, HALO - 1, 4, lambda r: take(sides, zsides, above, gx_above, r, r + HALO + by))

    @pl.when(block == 0)
    def _():
        h0[HALO - 1] = h0[HALO]

    @pl.when(block == plan.blocks - 1)
    def _():
        h0[HALO + by] = h0[HALO + by - 1]

    def is_open(r):
        y = base + r
        return (y >= 0) & (y < y_count - 1)

    first_face = inverse(h0[0] + h0[1])
    face[1] = first_face
    ky0[1] = jnp.where(is_open(0), first_face, 0.0)

    def faces(j):
        yd = face[2 * j - 1]
        for r in (2 * j - 1, 2 * j):
            h = h0[r]
            alone = 0.5 * inverse(h)
            xu = inverse(h + jnp.where(x_top, h, x_up(h)))
            xd = jnp.where(x_bottom, alone, x_down(xu))
            yu = inverse(h + h0[r + 1])
            zu = inverse(h + jnp.where(z_top, h, z_up(h, 1)))
            zd = jnp.where(z_bottom, alone, z_down(zu, 1))
            d = xu + xd + yu + yd + zu + zd
            w = DAMPING * inverse(d)
            kx0[r] = jnp.where(x_top, 0.0, xu)
            ky0[r + 1] = jnp.where(is_open(r), yu, 0.0)
            kz0[r] = jnp.where(z_shut, 0.0, zu)
            d0[r], w0[r] = d, w
            ua[r] = w * f0[r]
            yd = yu
        face[2 * j + 1] = yd

    fine = Level(1, 1, kx0, ky0, kz0, d0, w0, f0)

    own = by // 2
    half_x = nx // 2
    middle = Level(1, 2, kx1, ky1, kz1, d1, w1, f1, 8)
    def coarsen(j):
        kx1[j], ky1[j + 1], kz1[j], d1[j] = coarse_coefficients(fine, 2 * j - 1, half_x)

    def restrict(j):
        f1[j] = coarse_sum(r0, j, half_x, 1)

    def sweep(j):
        ub[2 * j] = fine.swept(ua, 2 * j)
        ub[2 * j + 1] = fine.swept(ua, 2 * j + 1)

    def residual(j):
        r0[j] = fine.residual(ub, 2 * j - 1) + fine.residual(ub, 2 * j)

    wave(
        (restrict, 2, own + 5, 4),
        (residual, 2, own + 5, 3),
        (sweep, 1, own + 5, 2),
        (coarsen, 1, own + 6, 1),
        (faces, 1, own + 6, 0),
    )
    ky1[1] = coarse_sum(ky0, 1, half_x, 1)
    middle.weigh(1, own + 6)
    middle.first(uc, 2, own + 5)
    middle.sweep(uc, u1, 3, own + 4)
    middle.residual_pairs(u1, r1, 4, own // 2)

    quarter_x = nx // 4
    own2 = own // 2
    part = own2 // 2
    for j in range(own2):
        fields = (coarse_sum(r1, j, quarter_x, 2),) + coarse_coefficients(middle, 4 + 2 * j, quarter_x)
        for t, a in enumerate(fields):
            stage[j // part, pl.ds((t * part + j % part) * quarter_x, quarter_x), :] = a
    cell = lax.broadcasted_iota(jnp.int32, pack.shape, 1)
    lanes = lax.rem(4 * cell, LANES)
    quarter = lax.div(4 * cell, LANES)
    total = pick_lanes(stage[0, :, :LANES], lanes)
    for k in range(1, 4):
        half = slice((k % 2) * LANES, (k % 2 + 1) * LANES)
        total = jnp.where(quarter == k, pick_lanes(stage[k // 2, :, half], lanes), total)
    pack[...] = total

    size = pack.shape[0]

    def near(out, first):
        out[pl.ds(0, size), :] = total
        for k, (ref, r) in enumerate(((u1, first), (u1, first + 1), (u1, first + 2), (f1, first + 1))):
            for s in range(2):
                out[pl.ds(size + (2 * k + s) * half_x, half_x), :] = ref.ref[r, s]

    for one, out in enumerate(nears):
        near(out, jnp.where(plan.is_up(block, 1, core if plan.paired else one), own, 5))


def up_kernel(plan, pack, mine, theirs, *refs):
    refs, out, scratch = refs[:13], refs[13], refs[14:]
    kx0, ky0, kz0, d0, w0, f0, u0, kx1, ky1, kz1, w1, f1_in, u1_in = [Wide(r) for r in refs]
    stage = scratch[0]
    wide = [Wide(r) for r in scratch[1:]]
    f2, kx2, ky2, kz2, d2, w2, ua2, ub2, r2 = wide[:9]
    f3, kx3, ky3, kz3, d3, w3, ua3, ub3 = wide[9:17]
    t1, t0, f1, ua1, ub1, ua0, ub0, uc0 = wide[17:]
    nx, by = plan.nx, plan.by
    own, own2 = by // 2, by // 4
    part = own2 // 2
    half_x, quarter_x = nx // 2, nx // 4
    size = pack.shape[0]
    side = size + 8 * half_x
    core = lax.axis_index("gz")
    block = plan.block_here()
    here = lax.axis_index("gx")
    turn = 1 if plan.paired else 0

    for r in range(2, own + 6):
        f1[r] = f1_in[r]
    for r in range(3, own + 5):
        ua1[r] = u1_in[r]

    ups = {k: plan.is_up(block, k, core if plan.paired else 0) for k in range(1, FAR + 1)}
    stage[FAR] = pack[...]
    for k, up in ups.items():
        at = 0 if k == 1 else side + (k - 2) * size
        stage[jnp.where(up, FAR + k, FAR - k)] = mine[pl.ds(at, size), :]
        stage[jnp.where(up, FAR - k, FAR + k)] = theirs[pl.ds(at, size), :]
    for ref, up, half_turn in ((mine, ups[1], 0), (theirs, jnp.logical_not(ups[1]), turn)):
        row = jnp.where(up, own + 5, 0)
        for k, (to, r) in enumerate(((ua1, row), (ua1, row + 1), (ua1, row + 2), (f1, row + 1))):
            for s in range(2):
                to.ref[r, s ^ half_turn] = ref[pl.ds(size + (2 * k + s) * half_x, half_x), :]

    lane = lax.broadcasted_iota(jnp.int32, (size, LANES), 1)
    lanes = [lax.div(lane, 4) + k * (LANES // 4) for k in range(4)]

    def expand(k):
        there = block + k - FAR
        exists = (there >= 0) & (there < plan.blocks)
        swapped = 0
        if plan.paired and k != FAR:
            swapped = jnp.where(ups[abs(k - FAR)] == (k > FAR), 0, 1)
        rows = stage[k]
        for quarter in range(4):
            part_of, half = divmod(quarter, 2)
            a = pick_lanes(rows, lanes[quarter])
            for t, ref in enumerate((f2, kx2, ky2, kz2, d2)):
                for j in range(part):
                    at = (t * part + j) * quarter_x
                    b = a[at : at + quarter_x]
                    if t == 2:
                        b = jnp.where(exists, b, 0.0)
                    r = k * own2 + part_of * part + j + (1 if t == 2 else 0)
                    ref.ref[r, swapped if half == 0 else 1 - swapped] = b

    for k in range(2 * FAR + 1):
        expand(k)

    rows2 = (2 * FAR + 1) * own2
    two = Level(1, 4, kx2, ky2, kz2, d2, w2, f2, 14)
    two.weigh(0, rows2 - 1)
    two.first(ua2, 0, rows2 - 1)
    two.sweep(ua2, ub2, 1, rows2 - 2)
    two.residual_pairs(ub2, r2, 2, rows2 // 2 - 2)

    x = lax.broadcasted_iota(jnp.int32, (quarter_x, WIDE), 0)
    even_x = (x & 1) == 0
    low = (lax.broadcasted_iota(jnp.int32, (quarter_x, WIDE), 1) & 4) == 0
    z_pair = z_pairs(low, 4)

    def x_pair(a):
        return a + jnp.where(even_x, x_up(a), x_down(a))

    last3 = rows2 // 2 - 2

    def coarsen(j):
        r = 2 * j
        kx = kx2[r] + kx2[r + 1]
        kz = kz2[r] + kz2[r + 1]
        inner = ky2[r + 1] + jnp.where(even_x, kx, 0.0) + jnp.where(low, kz, 0.0)
        f3[j] = z_pair(x_pair(r2[j - 1]))
        kx3[j] = z_pair(jnp.where(even_x, x_up(kx), kx))
        ky3[j + 1] = z_pair(x_pair(ky2[r + 2]))
        kz = x_pair(kz)
        kz3[j] = jnp.where(low, z_up(kz, 4), kz)
        d3[j] = z_pair(x_pair(d2[r] + d2[r + 1] - 2.0 * inner))

    each(1, last3, 6, coarsen)
    three = Level(2, 8, kx3, ky3, kz3, d3, w3, f3, 16)
    three.weigh(1, last3)
    three.first(ua3, 1, last3)
    three.sweep(ua3, ub3, 2, last3 - 1)
    three.sweep(ub3, ua3, 3, last3 - 2)
    three.sweep(ua3, ub3, 4, last3 - 3)

    first2 = FAR * own2
    for j in range(4, last3 - 2):
        e = ub3[j]
        ua2[2 * j] = ub2[2 * j] + e
        ua2[2 * j + 1] = ub2[2 * j + 1] + e
    two.sweep(ua2, ub2, first2 - 3, first2 + own2 + 2)
    two.sweep(ub2, ua2, first2 - 2, first2 + own2 + 1)

    one = Level(1, 2, kx1, ky1, kz1, None, w1, f1, 8)
    correct(ua1, ub1, ua2, t1, quarter_x, first2 - 2, first2 + own2 + 1, 0)
    one.sweep(ub1, ua1, 1, own + 6)
    one.sweep(ua1, ub1, 2, own + 5)

    finest = Level(1, 1, kx0, ky0, kz0, d0, w0, f0)

    def corrected(j):
        part = ub1[j]
        t0[j, pl.ds(0, half_x, stride=2)] = part
        t0[j, pl.ds(1, half_x, stride=2)] = part
        both = t0[j]
        ua0[2 * j - 1] = u0[2 * j - 1] + both
        ua0[2 * j] = u0[2 * j] + both

    def sweep(j):
        ub0[2 * j - 1] = finest.swept(ua0, 2 * j - 1)
        ub0[2 * j] = finest.swept(ua0, 2 * j)

    def sweep_again(j):
        uc0[2 * j] = finest.swept(ub0, 2 * j)
        uc0[2 * j + 1] = finest.swept(ub0, 2 * j + 1)

    def finish(j):
        for r in (2 * j - 1, 2 * j):
            scaled = d0[r] * uc0[r]
            rest = f0[r] + finest.beside(uc0, r) - scaled
            for s in range(plan.gx):
                part = slice(s * plan.px, (s + 1) * plan.px)
                out[s ^ here, r - HALO, 0] = scaled[part, :LANES]
                out[s ^ here, r - HALO, 1] = rest[part, :LANES]

    wave(
        (finish, 4, own + 3, 5),
        (sweep_again, 3, own + 3, 4),
        (sweep, 3, own + 4, 2),
        (corrected, 2, own + 5, 0),
    )


def place_kernel(plan, *refs):
    parts, (scaled, residual) = refs[: plan.gx], refs[plan.gx :]
    here = lax.axis_index("gx")
    by, px = plan.by, plan.px
    for k, part in enumerate(parts):
        rows = pl.ds(plan.start_of(here ^ k), by)
        for p in range(px):
            scaled[0, p, rows, :] = part[pl.ds(p, by, stride=2 * px), :]
            residual[0, p, rows, :] = part[pl.ds(px + p, by, stride=2 * px), :]


def in_vmem(*shape):
    return pltpu.VMEM(shape, F32)


def call(kernel, out_shape, scratch=(), **more):
    return pl.pallas_call(
        kernel,
        out_shape=out_shape,
        scratch_shapes=list(scratch),
        compiler_params=pltpu.CompilerParams(vmem_limit_bytes=VMEM_LIMIT),
        **more,
    )


def pinned(*arrays, where=pltpu.VMEM):
    return [pltpu.with_memory_space_constraint(a, where) for a in arrays]


def beside_in_z(plan, a):
    count = plan.gz
    if plan.paired:
        return lax.ppermute(a, "gz", [(0, 1), (1, 0)])
    cut = LANES // 2
    right = lax.ppermute(a[..., :cut], "gz", [(i + 1, i) for i in range(count - 1)])
    left = lax.ppermute(a[..., cut:], "gz", [(i, i + 1) for i in range(count - 1)])
    return jnp.concatenate([right, left], axis=-1)


def exchange(plan, parts):
    got = [parts[0]] * plan.gx
    for k in range(plan.gx - 1, 0, -1):
        got[k] = lax.ppermute(parts[k], "gx", [(i, i ^ k) for i in range(plan.gx)])
    return got


def pairs_of(plan, k, one):
    partner = list(range(plan.blocks))
    for b in range(plan.blocks - k):
        if b // k % 2 == one:
            partner[b], partner[b + k] = b + k, b
    return [(plan.device(a), plan.device(b)) for a, b in enumerate(partner)]


def swap_blocks(plan, a, k, one):
    return lax.ppermute(a, ("gx", "gy"), pairs_of(plan, k, one))


def swap_blocks_apart(plan, a, k):
    pairs = [(2 * p + one, 2 * q + one) for one in range(2) for p, q in pairs_of(plan, k, one)]
    return lax.ppermute(a, ("gx", "gy", "gz"), pairs)


def far_blocks(plan, pack, nears):
    def line(move, near):
        parts = [move(pack, k) for k in range(FAR, 1, -1)] + [move(near, 1)]
        return jnp.concatenate(parts[::-1], axis=0)

    if plan.paired:
        mine = line(functools.partial(swap_blocks_apart, plan), nears[0])
        return mine, beside_in_z(plan, mine)
    return [line(functools.partial(swap_blocks, plan, one=one), nears[one]) for one in range(2)]


def on_device(plan, phase, density, rhs):
    nx, by, rows, px, gx = plan.nx, plan.by, plan.rows, plan.px, plan.gx
    flat = by * 2 * px
    block = (px, plan.ny, LANES)
    outside = pl.BlockSpec(memory_space=pltpu.HBM)
    parts = call(
        functools.partial(prepare_kernel, plan),
        [in_vmem(flat, LANES)] * gx,
        [pltpu.VMEM(block, jnp.int32), in_vmem(*block), in_vmem(1, *block), pltpu.SemaphoreType.DMA((3,))],
        in_specs=[outside] * 3,
    )(*pinned(phase, density, rhs, where=pltpu.HBM))
    parts = [a.reshape(by, 2, px, LANES) for a in exchange(plan, parts)]
    c, *sets = call(
        functools.partial(gather_kernel, plan),
        [in_vmem(gx, by, 2, px, LANES)] + [in_vmem(gx, HALO, 2, px, LANES)] * 2,
    )(*pinned(*parts))
    sides = jnp.concatenate([swap_blocks(plan, a, 1, one) for one, a in enumerate(sets)], axis=0)
    zc = beside_in_z(plan, c)
    zsides = beside_in_z(plan, sides)

    own, own2 = by // 2, by // 4
    size = 5 * (own2 // 2) * (nx // 4)
    side = size + 8 * (nx // 2)

    def level0(n):
        return in_vmem(n, 2, nx, LANES)

    def level1(n):
        return in_vmem(n, 2, nx // 2, LANES)

    outs = [in_vmem(size, LANES)] + [in_vmem(side, LANES)] * (1 if plan.paired else 2)
    fields = [level0(rows)] * 7 + [level1(own + 8)] * 6
    scratch = [level0(rows)] * 3 + [level0(own + 8), level1(own + 8), level1(own2), level1(own + 8)]
    scratch += [in_vmem(2, size, WIDE)]
    down = call(functools.partial(down_kernel, plan), outs + fields, scratch)(*pinned(c, zc, sides, zsides))
    pack, nears, fields = down[0], down[1 : len(outs)], down[len(outs) :]

    mine, theirs = far_blocks(plan, pack, nears)
    rows2 = (2 * FAR + 1) * own2
    scratch = [in_vmem(2 * FAR + 1, size, LANES)]
    scratch += [in_vmem(rows2 + 1, 2, nx // 4, LANES)] * 9 + [in_vmem(rows2 // 2 + 1, 2, nx // 4, LANES)] * 8
    scratch += [level1(rows2), level0(own + 8)] + [level1(own + 8)] * 3 + [level0(rows)] * 3
    (result,) = call(
        functools.partial(up_kernel, plan), [in_vmem(gx, by, 2, px, LANES)], scratch
    )(*pinned(pack, mine, theirs, *fields))

    parts = exchange(plan, [result[k].reshape(flat, LANES) for k in range(gx)])
    return call(
        functools.partial(place_kernel, plan),
        [jax.ShapeDtypeStruct((1, px, plan.ny, LANES), F32)] * 2,
    )(*pinned(*parts))


def solution(mesh):
    sizes = [mesh.shape[a] for a in ("gx", "gy", "gz")]

    def local(phase, density, rhs):
        return tuple(on_device(Plan(sizes, phase.shape), phase, density, rhs))

    in_specs = (P("gx", "gy", "gz"), P("gx", "gy", "gz"), P(None, "gx", "gy", "gz"))
    out_specs = (P(None, "gx", "gy", "gz"), P(None, "gx", "gy", "gz"))
    return jax.shard_map(local, mesh=mesh, in_specs=in_specs, out_specs=out_specs, check_vma=False)
```

profile of v0, /device:TPU:0, one launch (start us, length us, event | category | flops | bytes accessed | tf_op | source)
XLA Modules:
  0.0 56.9 jit_solution(14401786973061428702)
XLA Ops:
  0.6 1.3 %shard_map.50 = (f32[256,128]{1,0:T(8,128)S(1)}, f32[256,128]{1,0:T(8,128)S(1)}, f32[256,128]{1,0:T(8,128)S(1)}, f32[256,128]{1,0:T(8,128)S(1)}) custom-call(s32[8,64,128]{2,1,0:T(8,128)} %phase_in.1, f32[8,64,128]{2,1,0:T(8,128)} %density_in.1, f32[1,8,64,128]{3,2,1,0:T(8,128)} %rhs_in.1), custom_call_target="tpu_custom_call" | custom-call | tf_op jit(solution)/shard_map/pallas_call | solution.py:616
  2.0 3.0 %collective-permute-start = (f32[256,128]{1,0:T(8,128)S(1)}, f32[256,128]{1,0:T(8,128)S(1)}, u32[]{:S(2)}, u32[]{:S(2)}) collective-permute-start(f32[256,128]{1,0:T(8,128)S(1)} %get-tuple-element.25), channel_id=1, source_target_pairs={{0,8},{8,0},{16,24},{24,16},{1,9},{9,1},{17,25},{25,17},{2,10},{10... | collective-permute-start | bytes 393224 | tf_op jit(solution)/shard_map/ppermute | solution.py:579
  5.0 1.5 %collective-permute-start.1 = (f32[256,128]{1,0:T(8,128)S(1)}, f32[256,128]{1,0:T(8,128)S(1)}, u32[]{:S(2)}, u32[]{:S(2)}) collective-permute-start(f32[256,128]{1,0:T(8,128)S(1)} %get-tuple-element.26), channel_id=1, source_target_pairs={{0,16},{8,24},{16,0},{24,8},{1,17},{9,25},{17,1},{25,9},{2,18},{10... | collective-permute-start | bytes 393224 | tf_op jit(solution)/shard_map/ppermute | solution.py:579
  6.5 0.0 collective-permute-start.2
  6.5 2.4 %collective-permute-done = f32[256,128]{1,0:T(8,128)S(1)} collective-permute-done((f32[256,128]{1,0:T(8,128)S(1)}, f32[256,128]{1,0:T(8,128)S(1)}, u32[]{:S(2)}, u32[]{:S(2)}) %collective-permute-start) | collective-permute-done | bytes 131104 | tf_op jit(solution)/shard_map/ppermute | solution.py:579
  8.9 3.9 %collective-permute-done.1 = f32[256,128]{1,0:T(8,128)S(1)} collective-permute-done((f32[256,128]{1,0:T(8,128)S(1)}, f32[256,128]{1,0:T(8,128)S(1)}, u32[]{:S(2)}, u32[]{:S(2)}) %collective-permute-start.1) | collective-permute-done | bytes 131104 | tf_op jit(solution)/shard_map/ppermute | solution.py:579
  12.7 0.0 collective-permute-done.2
  12.7 0.1 shard_map.51
  12.8 1.3 %collective-permute-start.4 = (f32[4,7,2,8,128]{4,3,2,1,0:T(8,128)S(1)}, f32[4,7,2,8,128]{4,3,2,1,0:T(8,128)S(1)}, u32[]{:S(2)}, u32[]{:S(2)}) collective-permute-start(f32[4,7,2,8,128]{4,3,2,1,0:T(8,128)S(1)} %get-tuple-element.29), channel_id=1, source_target_pairs={{0,8},{8,0},{24,16},{16,24},{18,26},{26,18},{10,2},{2,10},{4,12},{... | collective-permute-start | bytes 688136 | tf_op jit(solution)/shard_map/ppermute | solution.py:592
  14.1 0.7 %collective-permute-start.5 = (f32[4,7,2,8,128]{4,3,2,1,0:T(8,128)S(1)}, f32[4,7,2,8,128]{4,3,2,1,0:T(8,128)S(1)}, u32[]{:S(2)}, u32[]{:S(2)}) collective-permute-start(f32[4,7,2,8,128]{4,3,2,1,0:T(8,128)S(1)} %get-tuple-element.30), channel_id=1, source_target_pairs={{0,0},{8,24},{24,8},{16,18},{18,16},{26,10},{10,26},{2,4},{4,2},{1... | collective-permute-start | bytes 688136 | tf_op jit(solution)/shard_map/ppermute | solution.py:592
  14.8 0.1 collective-permute-start.3
  14.8 4.1 %collective-permute-done.4 = f32[4,7,2,8,128]{4,3,2,1,0:T(8,128)S(1)} collective-permute-done((f32[4,7,2,8,128]{4,3,2,1,0:T(8,128)S(1)}, f32[4,7,2,8,128]{4,3,2,1,0:T(8,128)S(1)}, u32[]{:S(2)}, u32[]{:S(2)}) %collective-permute-start.4) | collective-permute-done | bytes 229408 | tf_op jit(solution)/shard_map/ppermute | solution.py:592
  18.9 0.0 collective-permute-done.5
  19.0 0.1 collective-permute-start.6
  19.1 0.0 collective-permute-done.3.zc
  19.1 1.8 %collective-permute-done.6.zsides = f32[8,7,2,8,128]{4,3,2,1,0:T(8,128)S(1)} collective-permute-done((f32[8,7,2,8,128]{4,3,2,1,0:T(8,128)S(1)}, f32[8,7,2,8,128]{4,3,2,1,0:T(8,128)S(1)}, u32[]{:S(2)}, u32[]{:S(2)}) %collective-permute-start.6) | collective-permute-done | bytes 458784 | tf_op jit(solution)/shard_map/ppermute | solution.py:569
  20.9 4.3 %shard_map.52 = (f32[80,128]{1,0:T(8,128)S(1)}, f32[208,128]{1,0:T(8,128)S(1)}, f32[30,2,32,128]{3,2,1,0:T(8,128)S(1)}, f32[30,2,32,128]{3,2,1,0:T(8,128)S(1)}, ...) custom-call(f32[4,16,2,8,128]{4,3,2,1,0:T(8,128)S(1)} %get-tuple-ele, ...), custom_call_target="tpu_custom_call" | custom-call | tf_op jit(solution)/shard_map/pallas_call | solution.py:645
  25.2 5.7 %collective-permute-start.7 = (f32[208,128]{1,0:T(8,128)S(1)}, f32[208,128]{1,0:T(8,128)S(1)}, u32[]{:S(2)}, u32[]{:S(2)}) collective-permute-start(f32[208,128]{1,0:T(8,128)S(1)} %get-tuple-element.32), channel_id=1, source_target_pairs={{0,8},{8,0},{24,16},{16,24},{18,26},{26,18},{10,2},{2,10},{4,12},{... | collective-permute-start | bytes 319496 | tf_op jit(solution)/shard_map/ppermute | solution.py:597
  30.9 3.4 %collective-permute-start.9 = (f32[80,128]{1,0:T(8,128)S(1)}, f32[80,128]{1,0:T(8,128)S(1)}, u32[]{:S(2)}, u32[]{:S(2)}) collective-permute-start(f32[80,128]{1,0:T(8,128)S(1)} %get-tuple-element.31.pack), channel_id=1, source_target_pairs={{0,16},{8,18},{24,26},{16,0},{18,8},{26,24},{10,12},{2,28},{4,20},... | collective-permute-start | bytes 122888 | tf_op jit(solution)/shard_map/ppermute | solution.py:597
  34.4 3.5 %collective-permute-start.8 = (f32[80,128]{1,0:T(8,128)S(1)}, f32[80,128]{1,0:T(8,128)S(1)}, u32[]{:S(2)}, u32[]{:S(2)}) collective-permute-start(f32[80,128]{1,0:T(8,128)S(1)} %get-tuple-element.31.pack), channel_id=1, source_target_pairs={{0,24},{8,16},{24,0},{16,8},{18,10},{26,2},{10,18},{2,26},{4,28},{... | collective-permute-start | bytes 122888 | tf_op jit(solution)/shard_map/ppermute | solution.py:597
  37.8 0.0 collective-permute-done.7
  37.9 3.3 %collective-permute-done.8 = f32[80,128]{1,0:T(8,128)S(1)} collective-permute-done((f32[80,128]{1,0:T(8,128)S(1)}, f32[80,128]{1,0:T(8,128)S(1)}, u32[]{:S(2)}, u32[]{:S(2)}) %collective-permute-start.8) | collective-permute-done | bytes 40992 | tf_op jit(solution)/shard_map/ppermute | solution.py:597
  41.2 0.0 collective-permute-done.9
  41.2 0.1 collective-permute-start.10
  41.3 1.4 %collective-permute-done.10.theirs = f32[368,128]{1,0:T(8,128)S(1)} collective-permute-done((f32[368,128]{1,0:T(8,128)S(1)}, f32[368,128]{1,0:T(8,128)S(1)}, u32[]{:S(2)}, u32[]{:S(2)}) %collective-permute-start.10) | collective-permute-done | bytes 188448 | tf_op jit(solution)/shard_map/ppermute | solution.py:569
  42.7 3.5 %shard_map.53 = f32[4,16,2,8,128]{4,3,2,1,0:T(8,128)S(1)} custom-call(f32[80,128]{1,0:T(8,128)S(1)} %get-tuple-element.31.pack, f32[368,128]{1,0:T(8,128)S(1)} %constant_dynamic-update-slice_fusion.2.mine, f32[368,128]{1,0:T(8,128)S(1)} %collective-permute-done.10.theirs, f32[30,2,32,128]{3,2,1,0:T(8,128)S(1)} %get-tuple-element.33.refs_0_, ...), custom_call_target="tpu_custom_call" | custom-call | tf_op jit(solution)/shard_map/pallas_call | solution.py:653
  46.3 1.1 %collective-permute-start.12 = (f32[256,128]{1,0:T(8,128)S(1)}, f32[256,128]{1,0:T(8,128)S(1)}, u32[]{:S(2)}, u32[]{:S(2)}) collective-permute-start(f32[256,128]{1,0:T(8,128)S(1)} %bitcast.15), channel_id=1, source_target_pairs={{0,16},{8,24},{16,0},{24,8},{1,17},{9,25},{17,1},{25,9},{2,18},{10... | collective-permute-start | bytes 393224 | tf_op jit(solution)/shard_map/ppermute | solution.py:579
  47.4 2.9 %collective-permute-start.13 = (f32[256,128]{1,0:T(8,128)S(1)}, f32[256,128]{1,0:T(8,128)S(1)}, u32[]{:S(2)}, u32[]{:S(2)}) collective-permute-start(f32[256,128]{1,0:T(8,128)S(1)} %bitcast.14), channel_id=1, source_target_pairs={{0,24},{8,16},{16,8},{24,0},{1,25},{9,17},{17,9},{25,1},{2,26},{10... | collective-permute-start | bytes 393224 | tf_op jit(solution)/shard_map/ppermute | solution.py:579
  50.3 0.0 collective-permute-start.11
  50.3 4.4 %collective-permute-done.12.refs_2_ = f32[256,128]{1,0:T(8,128)S(1)} collective-permute-done((f32[256,128]{1,0:T(8,128)S(1)}, f32[256,128]{1,0:T(8,128)S(1)}, u32[]{:S(2)}, u32[]{:S(2)}) %collective-permute-start.12) | collective-permute-done | bytes 131104 | tf_op jit(solution)/shard_map/ppermute | solution.py:579
  54.7 0.0 collective-permute-done.13.refs_3_
  54.7 1.2 %collective-permute-done.11.refs_1_ = f32[256,128]{1,0:T(8,128)S(1)} collective-permute-done((f32[256,128]{1,0:T(8,128)S(1)}, f32[256,128]{1,0:T(8,128)S(1)}, u32[]{:S(2)}, u32[]{:S(2)}) %collective-permute-start.11) | collective-permute-done | bytes 131104 | tf_op jit(solution)/shard_map/ppermute | solution.py:579
  55.9 1.0 %shard_map.54 = (f32[1,8,64,128]{3,2,1,0:T(8,128)}, f32[1,8,64,128]{3,2,1,0:T(8,128)}) custom-call(f32[256,128]{1,0:T(8,128)S(1)} %bitcast.8, f32[256,128]{1,0:T(8,128)S(1)} %collective-permute-done.11.refs_1_, f32[256,128]{1,0:T(8,128)S(1)} %collective-permute-done.12.refs_2_, f32[256,128]{1,0:T(8,128)S(1)} %collective-permute-done.13.refs_3_), custom_call_target="tpu_custom_call" | custom-call | tf_op jit(solution)/shard_map/pallas_call | solution.py:658
  (6 shorter events, 0.1 us)
Async XLA Ops:
  2.0 6.9 %collective-permute-start = (f32[256,128]{1,0:T(8,128)S(1)}, f32[256,128]{1,0:T(8,128)S(1)}, u32[]{:S(2)}, u32[]{:S(2)}) collective-permute-start(f32[256,128]{1,0:T(8,128)S(1)} %get-tuple-element.25), channel_id=1, source_target_pairs={{0,8},{8,0},{16,24},{24,16},{1,9},{9,1},{17,25},{25,17},{2,10},{10... | collective-permute-start | bytes 393224 | tf_op jit(solution)/shard_map/ppermute | solution.py:579
  5.0 7.8 %collective-permute-start.1 = (f32[256,128]{1,0:T(8,128)S(1)}, f32[256,128]{1,0:T(8,128)S(1)}, u32[]{:S(2)}, u32[]{:S(2)}) collective-permute-start(f32[256,128]{1,0:T(8,128)S(1)} %get-tuple-element.26), channel_id=1, source_target_pairs={{0,16},{8,24},{16,0},{24,8},{1,17},{9,25},{17,1},{25,9},{2,18},{10... | collective-permute-start | bytes 393224 | tf_op jit(solution)/shard_map/ppermute | solution.py:579
  6.5 6.3 %collective-permute-start.2 = (f32[256,128]{1,0:T(8,128)S(1)}, f32[256,128]{1,0:T(8,128)S(1)}, u32[]{:S(2)}, u32[]{:S(2)}) collective-permute-start(f32[256,128]{1,0:T(8,128)S(1)} %get-tuple-element.27), channel_id=1, source_target_pairs={{0,24},{8,16},{16,8},{24,0},{1,25},{9,17},{17,9},{25,1},{2,26},{10... | collective-permute-start | bytes 393224 | tf_op jit(solution)/shard_map/ppermute | solution.py:579
  12.8 6.1 %collective-permute-start.4 = (f32[4,7,2,8,128]{4,3,2,1,0:T(8,128)S(1)}, f32[4,7,2,8,128]{4,3,2,1,0:T(8,128)S(1)}, u32[]{:S(2)}, u32[]{:S(2)}) collective-permute-start(f32[4,7,2,8,128]{4,3,2,1,0:T(8,128)S(1)} %get-tuple-element.29), channel_id=1, source_target_pairs={{0,8},{8,0},{24,16},{16,24},{18,26},{26,18},{10,2},{2,10},{4,12},{... | collective-permute-start | bytes 688136 | tf_op jit(solution)/shard_map/ppermute | solution.py:592
  14.1 4.9 %collective-permute-start.5 = (f32[4,7,2,8,128]{4,3,2,1,0:T(8,128)S(1)}, f32[4,7,2,8,128]{4,3,2,1,0:T(8,128)S(1)}, u32[]{:S(2)}, u32[]{:S(2)}) collective-permute-start(f32[4,7,2,8,128]{4,3,2,1,0:T(8,128)S(1)} %get-tuple-element.30), channel_id=1, source_target_pairs={{0,0},{8,24},{24,8},{16,18},{18,16},{26,10},{10,26},{2,4},{4,2},{1... | collective-permute-start | bytes 688136 | tf_op jit(solution)/shard_map/ppermute | solution.py:592
  14.8 4.3 %collective-permute-start.3 = (f32[4,16,2,8,128]{4,3,2,1,0:T(8,128)S(1)}, f32[4,16,2,8,128]{4,3,2,1,0:T(8,128)S(1)}, u32[]{:S(2)}, u32[]{:S(2)}) collective-permute-start(f32[4,16,2,8,128]{4,3,2,1,0:T(8,128)S(1)} %get-tuple-element.28.c), channel_id=1, source_target_pairs={{0,1},{1,0},{2,3},{3,2},{4,5},{5,4},{6,7},{7,6},{8,9},{9,8},{10,11... | collective-permute-start | bytes 1572872 | tf_op jit(solution)/shard_map/ppermute | solution.py:569
  19.0 1.9 %collective-permute-start.6 = (f32[8,7,2,8,128]{4,3,2,1,0:T(8,128)S(1)}, f32[8,7,2,8,128]{4,3,2,1,0:T(8,128)S(1)}, u32[]{:S(2)}, u32[]{:S(2)}) collective-permute-start(f32[8,7,2,8,128]{4,3,2,1,0:T(8,128)S(1)} %constant_dynamic-update-slice_fusion.sides), channel_id=1, source_target_pairs={{0,1},{1,0},{2,3},{3,2},{4,5},{5,4},{6,7},{7,6},{8,9},{9,8},{10,11... | collective-permute-start | bytes 1376264 | tf_op jit(solution)/shard_map/ppermute | solution.py:569
  25.2 12.6 %collective-permute-start.7 = (f32[208,128]{1,0:T(8,128)S(1)}, f32[208,128]{1,0:T(8,128)S(1)}, u32[]{:S(2)}, u32[]{:S(2)}) collective-permute-start(f32[208,128]{1,0:T(8,128)S(1)} %get-tuple-element.32), channel_id=1, source_target_pairs={{0,8},{8,0},{24,16},{16,24},{18,26},{26,18},{10,2},{2,10},{4,12},{... | collective-permute-start | bytes 319496 | tf_op jit(solution)/shard_map/ppermute | solution.py:597
  30.9 10.2 %collective-permute-start.9 = (f32[80,128]{1,0:T(8,128)S(1)}, f32[80,128]{1,0:T(8,128)S(1)}, u32[]{:S(2)}, u32[]{:S(2)}) collective-permute-start(f32[80,128]{1,0:T(8,128)S(1)} %get-tuple-element.31.pack), channel_id=1, source_target_pairs={{0,16},{8,18},{24,26},{16,0},{18,8},{26,24},{10,12},{2,28},{4,20},... | collective-permute-start | bytes 122888 | tf_op jit(solution)/shard_map/ppermute | solution.py:597
  34.4 6.8 %collective-permute-start.8 = (f32[80,128]{1,0:T(8,128)S(1)}, f32[80,128]{1,0:T(8,128)S(1)}, u32[]{:S(2)}, u32[]{:S(2)}) collective-permute-start(f32[80,128]{1,0:T(8,128)S(1)} %get-tuple-element.31.pack), channel_id=1, source_target_pairs={{0,24},{8,16},{24,0},{16,8},{18,10},{26,2},{10,18},{2,26},{4,28},{... | collective-permute-start | bytes 122888 | tf_op jit(solution)/shard_map/ppermute | solution.py:597
  41.2 1.5 %collective-permute-start.10 = (f32[368,128]{1,0:T(8,128)S(1)}, f32[368,128]{1,0:T(8,128)S(1)}, u32[]{:S(2)}, u32[]{:S(2)}) collective-permute-start(f32[368,128]{1,0:T(8,128)S(1)} %constant_dynamic-update-slice_fusion.2.mine), channel_id=1, source_target_pairs={{0,1},{1,0},{2,3},{3,2},{4,5},{5,4},{6,7},{7,6},{8,9},{9,8},{10,11... | collective-permute-start | bytes 565256 | tf_op jit(solution)/shard_map/ppermute | solution.py:569
  46.3 8.4 %collective-permute-start.12 = (f32[256,128]{1,0:T(8,128)S(1)}, f32[256,128]{1,0:T(8,128)S(1)}, u32[]{:S(2)}, u32[]{:S(2)}) collective-permute-start(f32[256,128]{1,0:T(8,128)S(1)} %bitcast.15), channel_id=1, source_target_pairs={{0,16},{8,24},{16,0},{24,8},{1,17},{9,25},{17,1},{25,9},{2,18},{10... | collective-permute-start | bytes 393224 | tf_op jit(solution)/shard_map/ppermute | solution.py:579
  47.4 7.3 %collective-permute-start.13 = (f32[256,128]{1,0:T(8,128)S(1)}, f32[256,128]{1,0:T(8,128)S(1)}, u32[]{:S(2)}, u32[]{:S(2)}) collective-permute-start(f32[256,128]{1,0:T(8,128)S(1)} %bitcast.14), channel_id=1, source_target_pairs={{0,24},{8,16},{16,8},{24,0},{1,25},{9,17},{17,9},{25,1},{2,26},{10... | collective-permute-start | bytes 393224 | tf_op jit(solution)/shard_map/ppermute | solution.py:579
  50.3 5.6 %collective-permute-start.11 = (f32[256,128]{1,0:T(8,128)S(1)}, f32[256,128]{1,0:T(8,128)S(1)}, u32[]{:S(2)}, u32[]{:S(2)}) collective-permute-start(f32[256,128]{1,0:T(8,128)S(1)} %bitcast.13), channel_id=1, source_target_pairs={{0,8},{8,0},{16,24},{24,16},{1,9},{9,1},{17,25},{25,17},{2,10},{10... | collective-permute-start | bytes 393224 | tf_op jit(solution)/shard_map/ppermute | solution.py:579
where the time goes:
time: 57.1 us; the launch traced here: 56.9 us
  starting transfers between devices  23.3 us (41%)
  waiting for transfers between devices  22.5 us (39%)
  Pallas kernels  10.2 us (18%)
  between operations  0.78 us (1%)
    ppermute x3, starting transfers between devices, swap_blocks_apart(): return lax.ppermute(a, ('gx', 'gy', 'gz'), pairs)  12.6 us
    ppermute x6, waiting for transfers between devices, exchange(): got[k] = lax.ppermute(parts[k], 'gx', [(i, i ^ k) for i in range(plan.gx)])  11.9 us
    ppermute x6, starting transfers between devices, exchange(): got[k] = lax.ppermute(parts[k], 'gx', [(i, i ^ k) for i in range(plan.gx)])  8.55 us
    pallas_call x1, Pallas kernels, on_device(): call(functools.partial(down_kernel, plan), outs + fields, scratch)  4.32 us
    ppermute x2, waiting for transfers between devices, swap_blocks(): return lax.ppermute(a, ('gx', 'gy'), pairs_of(plan, k, one))  4.08 us
    pallas_call x1, Pallas kernels, on_device(): call(functools.partial(up_kernel, plan), [in_vmem(gx, by, 2, px, LANES)],...  3.55 us
    ppermute x3, waiting for transfers between devices, swap_blocks_apart(): return lax.ppermute(a, ('gx', 'gy', 'gz'), pairs)  3.31 us
    ppermute x3, waiting for transfers between devices, beside_in_z(): return lax.ppermute(a, 'gz', [(0, 1), (1, 0)])  3.21 us
  transfers between devices with their start and end apart: 14, of which 8 were waited for; matrix products, arithmetic and copies ran while one was open for 0% of the time, Pallas kernels for 0%

commit v1 on v0

--- a/solution.py
+++ b/solution.py
@@ -585,6 +585,9 @@
     for b in range(plan.blocks - k):
         if b // k % 2 == one:
             partner[b], partner[b + k] = b + k, b
+    alone = [b for b in range(plan.blocks) if partner[b] == b]
+    for a, b in zip(alone[::2], alone[1::2]):
+        partner[a], partner[b] = b, a
     return [(plan.device(a), plan.device(b)) for a, b in enumerate(partner)]
 
 

time: 57.1 us -> 52.9 us (0.926); the launches traced: 56.9 us -> 52.1 us
  starting transfers between devices: 23.3 us -> 17.5 us
  waiting for transfers between devices: 22.5 us -> 23.6 us
    ppermute x3, starting transfers between devices: 12.6 us -> 1.78 us  [swap_blocks_apart(): return lax.ppermute(a, ('gx', 'gy', 'gz'), pairs)]
    ppermute x2, starting transfers between devices: 1.95 us -> 4.89 us  [swap_blocks(): return lax.ppermute(a, ('gx', 'gy'), pairs_of(plan, k, one))]
    ppermute x3, starting transfers between devices: 0.21 us -> 1.75 us  [beside_in_z(): return lax.ppermute(a, 'gz', [(0, 1), (1, 0)])]
    ppermute x6, waiting for transfers between devices: 11.9 us -> 12.8 us  [exchange(): got[k] = lax.ppermute(parts[k], 'gx', [(i, i ^ k) for i in range(plan.gx)])]
  transfers between devices with their start and end apart: 14 -> 14, of which waited for: 8 -> 11; matrix products, arithmetic and copies ran while one was open for 0% -> 0% of each run, Pallas kernels for 0% -> 0%
where the time goes in v1:
time: 52.9 us; the launch traced here: 52.1 us
  waiting for transfers between devices  23.6 us (45%)
  starting transfers between devices  17.5 us (33%)
  Pallas kernels  10.2 us (19%)
  between operations  0.72 us (1%)
    ppermute x6, waiting for transfers between devices, exchange(): got[k] = lax.ppermute(parts[k], 'gx', [(i, i ^ k) for i in range(plan.gx)])  12.8 us
    ppermute x6, starting transfers between devices, exchange(): got[k] = lax.ppermute(parts[k], 'gx', [(i, i ^ k) for i in range(plan.gx)])  9.08 us
    ppermute x2, starting transfers between devices, swap_blocks(): return lax.ppermute(a, ('gx', 'gy'), pairs_of(plan, k, one))  4.89 us
    ppermute x2, waiting for transfers between devices, swap_blocks(): return lax.ppermute(a, ('gx', 'gy'), pairs_of(plan, k, one))  4.53 us
    pallas_call x1, Pallas kernels, on_device(): call(functools.partial(down_kernel, plan), outs + fields, scratch)  4.32 us
    pallas_call x1, Pallas kernels, on_device(): call(functools.partial(up_kernel, plan), [in_vmem(gx, by, 2, px, LANES)],...  3.55 us
    ppermute x3, waiting for transfers between devices, swap_blocks_apart(): return lax.ppermute(a, ('gx', 'gy', 'gz'), pairs)  3.34 us
    ppermute x3, waiting for transfers between devices, beside_in_z(): return lax.ppermute(a, 'gz', [(0, 1), (1, 0)])  2.86 us
  transfers between devices with their start and end apart: 14, of which 11 were waited for; matrix products, arithmetic and copies ran while one was open for 0% of the time, Pallas kernels for 0%

profile of v1, /device:TPU:0, one launch (start us, length us, event | category | flops | bytes accessed | tf_op | source)
XLA Modules:
  0.0 52.1 jit_solution(11547533625641579222)
XLA Ops:
  0.6 1.3 %shard_map.50 = (f32[256,128]{1,0:T(8,128)S(1)}, f32[256,128]{1,0:T(8,128)S(1)}, f32[256,128]{1,0:T(8,128)S(1)}, f32[256,128]{1,0:T(8,128)S(1)}) custom-call(s32[8,64,128]{2,1,0:T(8,128)} %phase_in.1, f32[8,64,128]{2,1,0:T(8,128)} %density_in.1, f32[1,8,64,128]{3,2,1,0:T(8,128)} %rhs_in.1), custom_call_target="tpu_custom_call" | custom-call | tf_op jit(solution)/shard_map/pallas_call | solution.py:619
  2.0 3.0 %collective-permute-start = (f32[256,128]{1,0:T(8,128)S(1)}, f32[256,128]{1,0:T(8,128)S(1)}, u32[]{:S(2)}, u32[]{:S(2)}) collective-permute-start(f32[256,128]{1,0:T(8,128)S(1)} %get-tuple-element.25), channel_id=1, source_target_pairs={{0,8},{8,0},{16,24},{24,16},{1,9},{9,1},{17,25},{25,17},{2,10},{10... | collective-permute-start | bytes 393224 | tf_op jit(solution)/shard_map/ppermute | solution.py:579
  5.0 1.5 %collective-permute-start.1 = (f32[256,128]{1,0:T(8,128)S(1)}, f32[256,128]{1,0:T(8,128)S(1)}, u32[]{:S(2)}, u32[]{:S(2)}) collective-permute-start(f32[256,128]{1,0:T(8,128)S(1)} %get-tuple-element.26), channel_id=1, source_target_pairs={{0,16},{8,24},{16,0},{24,8},{1,17},{9,25},{17,1},{25,9},{2,18},{10... | collective-permute-start | bytes 393224 | tf_op jit(solution)/shard_map/ppermute | solution.py:579
  6.5 0.0 collective-permute-start.2
  6.5 2.4 %collective-permute-done = f32[256,128]{1,0:T(8,128)S(1)} collective-permute-done((f32[256,128]{1,0:T(8,128)S(1)}, f32[256,128]{1,0:T(8,128)S(1)}, u32[]{:S(2)}, u32[]{:S(2)}) %collective-permute-start) | collective-permute-done | bytes 131104 | tf_op jit(solution)/shard_map/ppermute | solution.py:579
  8.9 3.9 %collective-permute-done.1 = f32[256,128]{1,0:T(8,128)S(1)} collective-permute-done((f32[256,128]{1,0:T(8,128)S(1)}, f32[256,128]{1,0:T(8,128)S(1)}, u32[]{:S(2)}, u32[]{:S(2)}) %collective-permute-start.1) | collective-permute-done | bytes 131104 | tf_op jit(solution)/shard_map/ppermute | solution.py:579
  12.7 0.0 collective-permute-done.2
  12.7 0.1 shard_map.51
  12.8 1.3 %collective-permute-start.4 = (f32[4,7,2,8,128]{4,3,2,1,0:T(8,128)S(1)}, f32[4,7,2,8,128]{4,3,2,1,0:T(8,128)S(1)}, u32[]{:S(2)}, u32[]{:S(2)}) collective-permute-start(f32[4,7,2,8,128]{4,3,2,1,0:T(8,128)S(1)} %get-tuple-element.29), channel_id=1, source_target_pairs={{0,8},{8,0},{24,16},{16,24},{18,26},{26,18},{10,2},{2,10},{4,12},{... | collective-permute-start | bytes 688136 | tf_op jit(solution)/shard_map/ppermute | solution.py:595
  14.1 3.6 %collective-permute-start.5 = (f32[4,7,2,8,128]{4,3,2,1,0:T(8,128)S(1)}, f32[4,7,2,8,128]{4,3,2,1,0:T(8,128)S(1)}, u32[]{:S(2)}, u32[]{:S(2)}) collective-permute-start(f32[4,7,2,8,128]{4,3,2,1,0:T(8,128)S(1)} %get-tuple-element.30), channel_id=1, source_target_pairs={{0,6},{8,24},{24,8},{16,18},{18,16},{26,10},{10,26},{2,4},{4,2},{1... | collective-permute-start | bytes 688136 | tf_op jit(solution)/shard_map/ppermute | solution.py:595
  17.7 0.0 collective-permute-start.3
  17.7 1.2 %collective-permute-done.4 = f32[4,7,2,8,128]{4,3,2,1,0:T(8,128)S(1)} collective-permute-done((f32[4,7,2,8,128]{4,3,2,1,0:T(8,128)S(1)}, f32[4,7,2,8,128]{4,3,2,1,0:T(8,128)S(1)}, u32[]{:S(2)}, u32[]{:S(2)}) %collective-permute-start.4) | collective-permute-done | bytes 229408 | tf_op jit(solution)/shard_map/ppermute | solution.py:595
  18.9 3.3 %collective-permute-done.5 = f32[4,7,2,8,128]{4,3,2,1,0:T(8,128)S(1)} collective-permute-done((f32[4,7,2,8,128]{4,3,2,1,0:T(8,128)S(1)}, f32[4,7,2,8,128]{4,3,2,1,0:T(8,128)S(1)}, u32[]{:S(2)}, u32[]{:S(2)}) %collective-permute-start.5) | collective-permute-done | bytes 229408 | tf_op jit(solution)/shard_map/ppermute | solution.py:595
  22.3 0.1 collective-permute-start.6
  22.4 0.0 collective-permute-done.3.zc
  22.4 1.8 %collective-permute-done.6.zsides = f32[8,7,2,8,128]{4,3,2,1,0:T(8,128)S(1)} collective-permute-done((f32[8,7,2,8,128]{4,3,2,1,0:T(8,128)S(1)}, f32[8,7,2,8,128]{4,3,2,1,0:T(8,128)S(1)}, u32[]{:S(2)}, u32[]{:S(2)}) %collective-permute-start.6) | collective-permute-done | bytes 458784 | tf_op jit(solution)/shard_map/ppermute | solution.py:569
  24.2 4.3 %shard_map.52 = (f32[80,128]{1,0:T(8,128)S(1)}, f32[208,128]{1,0:T(8,128)S(1)}, f32[30,2,32,128]{3,2,1,0:T(8,128)S(1)}, f32[30,2,32,128]{3,2,1,0:T(8,128)S(1)}, ...) custom-call(f32[4,16,2,8,128]{4,3,2,1,0:T(8,128)S(1)} %get-tuple-ele, ...), custom_call_target="tpu_custom_call" | custom-call | tf_op jit(solution)/shard_map/pallas_call | solution.py:648
  28.5 0.1 collective-permute-start.7
  28.6 0.2 collective-permute-start.9
  28.7 1.5 %collective-permute-start.8 = (f32[80,128]{1,0:T(8,128)S(1)}, f32[80,128]{1,0:T(8,128)S(1)}, u32[]{:S(2)}, u32[]{:S(2)}) collective-permute-start(f32[80,128]{1,0:T(8,128)S(1)} %get-tuple-element.31.pack), channel_id=1, source_target_pairs={{0,24},{8,16},{24,0},{16,8},{18,10},{26,2},{10,18},{2,26},{4,28},{... | collective-permute-start | bytes 122888 | tf_op jit(solution)/shard_map/ppermute | solution.py:600
  30.3 3.0 %collective-permute-done.7 = f32[208,128]{1,0:T(8,128)S(1)} collective-permute-done((f32[208,128]{1,0:T(8,128)S(1)}, f32[208,128]{1,0:T(8,128)S(1)}, u32[]{:S(2)}, u32[]{:S(2)}) %collective-permute-start.7) | collective-permute-done | bytes 106528 | tf_op jit(solution)/shard_map/ppermute | solution.py:600
  33.3 0.4 collective-permute-done.8
  33.6 0.0 collective-permute-done.9
  33.6 1.7 %collective-permute-start.10 = (f32[368,128]{1,0:T(8,128)S(1)}, f32[368,128]{1,0:T(8,128)S(1)}, u32[]{:S(2)}, u32[]{:S(2)}) collective-permute-start(f32[368,128]{1,0:T(8,128)S(1)} %constant_dynamic-update-slice_fusion.2.mine), channel_id=1, source_target_pairs={{0,1},{1,0},{2,3},{3,2},{4,5},{5,4},{6,7},{7,6},{8,9},{9,8},{10,11... | collective-permute-start | bytes 565256 | tf_op jit(solution)/shard_map/ppermute | solution.py:569
  35.3 1.1 %collective-permute-done.10.theirs = f32[368,128]{1,0:T(8,128)S(1)} collective-permute-done((f32[368,128]{1,0:T(8,128)S(1)}, f32[368,128]{1,0:T(8,128)S(1)}, u32[]{:S(2)}, u32[]{:S(2)}) %collective-permute-start.10) | collective-permute-done | bytes 188448 | tf_op jit(solution)/shard_map/ppermute | solution.py:569
  36.4 3.5 %shard_map.53 = f32[4,16,2,8,128]{4,3,2,1,0:T(8,128)S(1)} custom-call(f32[80,128]{1,0:T(8,128)S(1)} %get-tuple-element.31.pack, f32[368,128]{1,0:T(8,128)S(1)} %constant_dynamic-update-slice_fusion.2.mine, f32[368,128]{1,0:T(8,128)S(1)} %collective-permute-done.10.theirs, f32[30,2,32,128]{3,2,1,0:T(8,128)S(1)} %get-tuple-element.33.refs_0_, ...), custom_call_target="tpu_custom_call" | custom-call | tf_op jit(solution)/shard_map/pallas_call | solution.py:656
  40.0 3.0 %collective-permute-start.12 = (f32[256,128]{1,0:T(8,128)S(1)}, f32[256,128]{1,0:T(8,128)S(1)}, u32[]{:S(2)}, u32[]{:S(2)}) collective-permute-start(f32[256,128]{1,0:T(8,128)S(1)} %bitcast.15), channel_id=1, source_target_pairs={{0,16},{8,24},{16,0},{24,8},{1,17},{9,25},{17,1},{25,9},{2,18},{10... | collective-permute-start | bytes 393224 | tf_op jit(solution)/shard_map/ppermute | solution.py:579
  43.0 0.2 collective-permute-start.13
  43.2 1.3 %collective-permute-start.11 = (f32[256,128]{1,0:T(8,128)S(1)}, f32[256,128]{1,0:T(8,128)S(1)}, u32[]{:S(2)}, u32[]{:S(2)}) collective-permute-start(f32[256,128]{1,0:T(8,128)S(1)} %bitcast.13), channel_id=1, source_target_pairs={{0,8},{8,0},{16,24},{24,16},{1,9},{9,1},{17,25},{25,17},{2,10},{10... | collective-permute-start | bytes 393224 | tf_op jit(solution)/shard_map/ppermute | solution.py:579
  44.5 4.8 %collective-permute-done.12.refs_2_ = f32[256,128]{1,0:T(8,128)S(1)} collective-permute-done((f32[256,128]{1,0:T(8,128)S(1)}, f32[256,128]{1,0:T(8,128)S(1)}, u32[]{:S(2)}, u32[]{:S(2)}) %collective-permute-start.12) | collective-permute-done | bytes 131104 | tf_op jit(solution)/shard_map/ppermute | solution.py:579
  49.3 1.0 %collective-permute-done.13.refs_3_ = f32[256,128]{1,0:T(8,128)S(1)} collective-permute-done((f32[256,128]{1,0:T(8,128)S(1)}, f32[256,128]{1,0:T(8,128)S(1)}, u32[]{:S(2)}, u32[]{:S(2)}) %collective-permute-start.13) | collective-permute-done | bytes 131104 | tf_op jit(solution)/shard_map/ppermute | solution.py:579
  50.3 0.8 %collective-permute-done.11.refs_1_ = f32[256,128]{1,0:T(8,128)S(1)} collective-permute-done((f32[256,128]{1,0:T(8,128)S(1)}, f32[256,128]{1,0:T(8,128)S(1)}, u32[]{:S(2)}, u32[]{:S(2)}) %collective-permute-start.11) | collective-permute-done | bytes 131104 | tf_op jit(solution)/shard_map/ppermute | solution.py:579
  51.1 1.0 %shard_map.54 = (f32[1,8,64,128]{3,2,1,0:T(8,128)}, f32[1,8,64,128]{3,2,1,0:T(8,128)}) custom-call(f32[256,128]{1,0:T(8,128)S(1)} %bitcast.8, f32[256,128]{1,0:T(8,128)S(1)} %collective-permute-done.11.refs_1_, f32[256,128]{1,0:T(8,128)S(1)} %collective-permute-done.12.refs_2_, f32[256,128]{1,0:T(8,128)S(1)} %collective-permute-done.13.refs_3_), custom_call_target="tpu_custom_call" | custom-call | tf_op jit(solution)/shard_map/pallas_call | solution.py:661
  (6 shorter events, 0.1 us)
Async XLA Ops:
  2.0 6.9 %collective-permute-start = (f32[256,128]{1,0:T(8,128)S(1)}, f32[256,128]{1,0:T(8,128)S(1)}, u32[]{:S(2)}, u32[]{:S(2)}) collective-permute-start(f32[256,128]{1,0:T(8,128)S(1)} %get-tuple-element.25), channel_id=1, source_target_pairs={{0,8},{8,0},{16,24},{24,16},{1,9},{9,1},{17,25},{25,17},{2,10},{10... | collective-permute-start | bytes 393224 | tf_op jit(solution)/shard_map/ppermute | solution.py:579
  5.0 7.8 %collective-permute-start.1 = (f32[256,128]{1,0:T(8,128)S(1)}, f32[256,128]{1,0:T(8,128)S(1)}, u32[]{:S(2)}, u32[]{:S(2)}) collective-permute-start(f32[256,128]{1,0:T(8,128)S(1)} %get-tuple-element.26), channel_id=1, source_target_pairs={{0,16},{8,24},{16,0},{24,8},{1,17},{9,25},{17,1},{25,9},{2,18},{10... | collective-permute-start | bytes 393224 | tf_op jit(solution)/shard_map/ppermute | solution.py:579
  6.5 6.3 %collective-permute-start.2 = (f32[256,128]{1,0:T(8,128)S(1)}, f32[256,128]{1,0:T(8,128)S(1)}, u32[]{:S(2)}, u32[]{:S(2)}) collective-permute-start(f32[256,128]{1,0:T(8,128)S(1)} %get-tuple-element.27), channel_id=1, source_target_pairs={{0,24},{8,16},{16,8},{24,0},{1,25},{9,17},{17,9},{25,1},{2,26},{10... | collective-permute-start | bytes 393224 | tf_op jit(solution)/shard_map/ppermute | solution.py:579
  12.8 6.1 %collective-permute-start.4 = (f32[4,7,2,8,128]{4,3,2,1,0:T(8,128)S(1)}, f32[4,7,2,8,128]{4,3,2,1,0:T(8,128)S(1)}, u32[]{:S(2)}, u32[]{:S(2)}) collective-permute-start(f32[4,7,2,8,128]{4,3,2,1,0:T(8,128)S(1)} %get-tuple-element.29), channel_id=1, source_target_pairs={{0,8},{8,0},{24,16},{16,24},{18,26},{26,18},{10,2},{2,10},{4,12},{... | collective-permute-start | bytes 688136 | tf_op jit(solution)/shard_map/ppermute | solution.py:595
  14.1 8.2 %collective-permute-start.5 = (f32[4,7,2,8,128]{4,3,2,1,0:T(8,128)S(1)}, f32[4,7,2,8,128]{4,3,2,1,0:T(8,128)S(1)}, u32[]{:S(2)}, u32[]{:S(2)}) collective-permute-start(f32[4,7,2,8,128]{4,3,2,1,0:T(8,128)S(1)} %get-tuple-element.30), channel_id=1, source_target_pairs={{0,6},{8,24},{24,8},{16,18},{18,16},{26,10},{10,26},{2,4},{4,2},{1... | collective-permute-start | bytes 688136 | tf_op jit(solution)/shard_map/ppermute | solution.py:595
  17.7 4.7 %collective-permute-start.3 = (f32[4,16,2,8,128]{4,3,2,1,0:T(8,128)S(1)}, f32[4,16,2,8,128]{4,3,2,1,0:T(8,128)S(1)}, u32[]{:S(2)}, u32[]{:S(2)}) collective-permute-start(f32[4,16,2,8,128]{4,3,2,1,0:T(8,128)S(1)} %get-tuple-element.28.c), channel_id=1, source_target_pairs={{0,1},{1,0},{2,3},{3,2},{4,5},{5,4},{6,7},{7,6},{8,9},{9,8},{10,11... | collective-permute-start | bytes 1572872 | tf_op jit(solution)/shard_map/ppermute | solution.py:569
  22.3 1.9 %collective-permute-start.6 = (f32[8,7,2,8,128]{4,3,2,1,0:T(8,128)S(1)}, f32[8,7,2,8,128]{4,3,2,1,0:T(8,128)S(1)}, u32[]{:S(2)}, u32[]{:S(2)}) collective-permute-start(f32[8,7,2,8,128]{4,3,2,1,0:T(8,128)S(1)} %constant_dynamic-update-slice_fusion.sides), channel_id=1, source_target_pairs={{0,1},{1,0},{2,3},{3,2},{4,5},{5,4},{6,7},{7,6},{8,9},{9,8},{10,11... | collective-permute-start | bytes 1376264 | tf_op jit(solution)/shard_map/ppermute | solution.py:569
  28.5 4.8 %collective-permute-start.7 = (f32[208,128]{1,0:T(8,128)S(1)}, f32[208,128]{1,0:T(8,128)S(1)}, u32[]{:S(2)}, u32[]{:S(2)}) collective-permute-start(f32[208,128]{1,0:T(8,128)S(1)} %get-tuple-element.32), channel_id=1, source_target_pairs={{0,8},{8,0},{24,16},{16,24},{18,26},{26,18},{10,2},{2,10},{4,12},{... | collective-permute-start | bytes 319496 | tf_op jit(solution)/shard_map/ppermute | solution.py:600
  28.6 5.1 %collective-permute-start.9 = (f32[80,128]{1,0:T(8,128)S(1)}, f32[80,128]{1,0:T(8,128)S(1)}, u32[]{:S(2)}, u32[]{:S(2)}) collective-permute-start(f32[80,128]{1,0:T(8,128)S(1)} %get-tuple-element.31.pack), channel_id=1, source_target_pairs={{0,16},{8,18},{24,26},{16,0},{18,8},{26,24},{10,12},{2,28},{4,20},... | collective-permute-start | bytes 122888 | tf_op jit(solution)/shard_map/ppermute | solution.py:600
  28.7 4.9 %collective-permute-start.8 = (f32[80,128]{1,0:T(8,128)S(1)}, f32[80,128]{1,0:T(8,128)S(1)}, u32[]{:S(2)}, u32[]{:S(2)}) collective-permute-start(f32[80,128]{1,0:T(8,128)S(1)} %get-tuple-element.31.pack), channel_id=1, source_target_pairs={{0,24},{8,16},{24,0},{16,8},{18,10},{26,2},{10,18},{2,26},{4,28},{... | collective-permute-start | bytes 122888 | tf_op jit(solution)/shard_map/ppermute | solution.py:600
  33.6 2.7 %collective-permute-start.10 = (f32[368,128]{1,0:T(8,128)S(1)}, f32[368,128]{1,0:T(8,128)S(1)}, u32[]{:S(2)}, u32[]{:S(2)}) collective-permute-start(f32[368,128]{1,0:T(8,128)S(1)} %constant_dynamic-update-slice_fusion.2.mine), channel_id=1, source_target_pairs={{0,1},{1,0},{2,3},{3,2},{4,5},{5,4},{6,7},{7,6},{8,9},{9,8},{10,11... | collective-permute-start | bytes 565256 | tf_op jit(solution)/shard_map/ppermute | solution.py:569
  40.0 9.3 %collective-permute-start.12 = (f32[256,128]{1,0:T(8,128)S(1)}, f32[256,128]{1,0:T(8,128)S(1)}, u32[]{:S(2)}, u32[]{:S(2)}) collective-permute-start(f32[256,128]{1,0:T(8,128)S(1)} %bitcast.15), channel_id=1, source_target_pairs={{0,16},{8,24},{16,0},{24,8},{1,17},{9,25},{17,1},{25,9},{2,18},{10... | collective-permute-start | bytes 393224 | tf_op jit(solution)/shard_map/ppermute | solution.py:579
  43.0 7.3 %collective-permute-start.13 = (f32[256,128]{1,0:T(8,128)S(1)}, f32[256,128]{1,0:T(8,128)S(1)}, u32[]{:S(2)}, u32[]{:S(2)}) collective-permute-start(f32[256,128]{1,0:T(8,128)S(1)} %bitcast.14), channel_id=1, source_target_pairs={{0,24},{8,16},{16,8},{24,0},{1,25},{9,17},{17,9},{25,1},{2,26},{10... | collective-permute-start | bytes 393224 | tf_op jit(solution)/shard_map/ppermute | solution.py:579
  43.2 7.9 %collective-permute-start.11 = (f32[256,128]{1,0:T(8,128)S(1)}, f32[256,128]{1,0:T(8,128)S(1)}, u32[]{:S(2)}, u32[]{:S(2)}) collective-permute-start(f32[256,128]{1,0:T(8,128)S(1)} %bitcast.13), channel_id=1, source_target_pairs={{0,8},{8,0},{16,24},{24,16},{1,9},{9,1},{17,25},{25,17},{2,10},{10... | collective-permute-start | bytes 393224 | tf_op jit(solution)/shard_map/ppermute | solution.py:579

commit v2 on v1

--- a/solution.py
+++ b/solution.py
@@ -26,32 +26,28 @@
         self.blocks = self.gx * self.gy
         self.rows = self.by + 2 * HALO
         self.paired = self.gz == 2
-        order = [0, 1, 3, 2] if self.gx == 4 else list(range(self.gx))
-        self.place = [order.index(i) for i in range(self.gx)]
-        self.order = order
+        self.ring = [0, 1, 3, 2] if self.gx == 4 else list(range(self.gx))
+        self.place = [self.ring.index(i) for i in range(self.gx)]
 
     def device(self, block):
         j, q = divmod(block, self.gx)
-        i = self.order[q if j % 2 == 0 else self.gx - 1 - q]
-        return i * self.gy + j
+        return self.ring[(q - j) % self.gx] * self.gy + j
 
     def look_up(self, table, i):
         return sum(jnp.where(i == k, v, 0) for k, v in enumerate(table))
 
     def start_of(self, i):
-        q = self.look_up(self.place, i)
-        q = jnp.where(lax.rem(lax.axis_index("gy"), 2) == 0, q, self.gx - 1 - q)
+        q = lax.rem(self.look_up(self.place, i) + lax.axis_index("gy"), self.gx)
         return pl.multiple_of(q * self.by, self.by)
 
     def block_here(self):
-        q = self.look_up(self.place, lax.axis_index("gx"))
         j = lax.axis_index("gy")
-        return j * self.gx + jnp.where(lax.rem(j, 2) == 0, q, self.gx - 1 - q)
+        return j * self.gx + lax.rem(self.look_up(self.place, lax.axis_index("gx")) + j, self.gx)
 
     def gx_of(self, block):
         block = jnp.clip(block, 0, self.blocks - 1)
         j, q = lax.div(block, self.gx), lax.rem(block, self.gx)
-        return self.look_up(self.order, jnp.where(lax.rem(j, 2) == 0, q, self.gx - 1 - q))
+        return self.look_up(self.ring, lax.rem(q + self.gx * self.gy - j, self.gx))
 
     def is_up(self, block, k, one):
         return lax.rem(lax.div(block, k), 2) == one

time: 52.9 us -> 51.2 us (0.968); the launches traced: 52.1 us -> 51.1 us
  waiting for transfers between devices: 23.6 us -> 22.2 us
    ppermute x3, starting transfers between devices: 1.78 us -> 2.83 us  [swap_blocks_apart(): return lax.ppermute(a, ('gx', 'gy', 'gz'), pairs)]
    ppermute x6, starting transfers between devices: 9.08 us -> 8.11 us  [exchange(): got[k] = lax.ppermute(parts[k], 'gx', [(i, i ^ k) for i in range(plan.gx)])]
    ppermute x3, waiting for transfers between devices: 3.34 us -> 2.46 us  [swap_blocks_apart(): return lax.ppermute(a, ('gx', 'gy', 'gz'), pairs)]
  transfers between devices with their start and end apart: 14 -> 14, of which waited for: 11 -> 10; matrix products, arithmetic and copies ran while one was open for 0% -> 0% of each run, Pallas kernels for 0% -> 0%
where the time goes in v2:
time: 51.2 us; the launch traced here: 51.1 us
  waiting for transfers between devices  22.2 us (43%)
  starting transfers between devices  17.9 us (35%)
  Pallas kernels  10.2 us (20%)
  between operations  0.72 us (1%)
    ppermute x6, waiting for transfers between devices, exchange(): got[k] = lax.ppermute(parts[k], 'gx', [(i, i ^ k) for i in range(plan.gx)])  12.8 us
    ppermute x6, starting transfers between devices, exchange(): got[k] = lax.ppermute(parts[k], 'gx', [(i, i ^ k) for i in range(plan.gx)])  8.11 us
    ppermute x2, starting transfers between devices, swap_blocks(): return lax.ppermute(a, ('gx', 'gy'), pairs_of(plan, k, one))  5.18 us
    pallas_call x1, Pallas kernels, on_device(): call(functools.partial(down_kernel, plan), outs + fields, scratch)  4.32 us
    ppermute x2, waiting for transfers between devices, swap_blocks(): return lax.ppermute(a, ('gx', 'gy'), pairs_of(plan, k, one))  4.08 us
    pallas_call x1, Pallas kernels, on_device(): call(functools.partial(up_kernel, plan), [in_vmem(gx, by, 2, px, LANES)],...  3.55 us
    ppermute x3, waiting for transfers between devices, beside_in_z(): return lax.ppermute(a, 'gz', [(0, 1), (1, 0)])  2.86 us
    ppermute x3, starting transfers between devices, swap_blocks_apart(): return lax.ppermute(a, ('gx', 'gy', 'gz'), pairs)  2.83 us
  transfers between devices with their start and end apart: 14, of which 10 were waited for; matrix products, arithmetic and copies ran while one was open for 0% of the time, Pallas kernels for 0%

profile of v2, /device:TPU:0, one launch (start us, length us, event | category | flops | bytes accessed | tf_op | source)
XLA Modules:
  0.0 51.1 jit_solution(9714974242794932783)
XLA Ops:
  0.6 1.3 %shard_map.50 = (f32[256,128]{1,0:T(8,128)S(1)}, f32[256,128]{1,0:T(8,128)S(1)}, f32[256,128]{1,0:T(8,128)S(1)}, f32[256,128]{1,0:T(8,128)S(1)}) custom-call(s32[8,64,128]{2,1,0:T(8,128)} %phase_in.1, f32[8,64,128]{2,1,0:T(8,128)} %density_in.1, f32[1,8,64,128]{3,2,1,0:T(8,128)} %rhs_in.1), custom_call_target="tpu_custom_call" | custom-call | tf_op jit(solution)/shard_map/pallas_call | solution.py:615
  2.0 3.0 %collective-permute-start = (f32[256,128]{1,0:T(8,128)S(1)}, f32[256,128]{1,0:T(8,128)S(1)}, u32[]{:S(2)}, u32[]{:S(2)}) collective-permute-start(f32[256,128]{1,0:T(8,128)S(1)} %get-tuple-element.25), channel_id=1, source_target_pairs={{0,8},{8,0},{16,24},{24,16},{1,9},{9,1},{17,25},{25,17},{2,10},{10... | collective-permute-start | bytes 393224 | tf_op jit(solution)/shard_map/ppermute | solution.py:575
  5.0 1.5 %collective-permute-start.1 = (f32[256,128]{1,0:T(8,128)S(1)}, f32[256,128]{1,0:T(8,128)S(1)}, u32[]{:S(2)}, u32[]{:S(2)}) collective-permute-start(f32[256,128]{1,0:T(8,128)S(1)} %get-tuple-element.26), channel_id=1, source_target_pairs={{0,16},{8,24},{16,0},{24,8},{1,17},{9,25},{17,1},{25,9},{2,18},{10... | collective-permute-start | bytes 393224 | tf_op jit(solution)/shard_map/ppermute | solution.py:575
  6.5 0.0 collective-permute-start.2
  6.5 2.4 %collective-permute-done = f32[256,128]{1,0:T(8,128)S(1)} collective-permute-done((f32[256,128]{1,0:T(8,128)S(1)}, f32[256,128]{1,0:T(8,128)S(1)}, u32[]{:S(2)}, u32[]{:S(2)}) %collective-permute-start) | collective-permute-done | bytes 131104 | tf_op jit(solution)/shard_map/ppermute | solution.py:575
  8.9 3.9 %collective-permute-done.1 = f32[256,128]{1,0:T(8,128)S(1)} collective-permute-done((f32[256,128]{1,0:T(8,128)S(1)}, f32[256,128]{1,0:T(8,128)S(1)}, u32[]{:S(2)}, u32[]{:S(2)}) %collective-permute-start.1) | collective-permute-done | bytes 131104 | tf_op jit(solution)/shard_map/ppermute | solution.py:575
  12.7 0.0 collective-permute-done.2
  12.7 0.1 shard_map.51
  12.8 1.3 %collective-permute-start.4 = (f32[4,7,2,8,128]{4,3,2,1,0:T(8,128)S(1)}, f32[4,7,2,8,128]{4,3,2,1,0:T(8,128)S(1)}, u32[]{:S(2)}, u32[]{:S(2)}) collective-permute-start(f32[4,7,2,8,128]{4,3,2,1,0:T(8,128)S(1)} %get-tuple-element.29), channel_id=1, source_target_pairs={{0,8},{8,0},{24,16},{16,24},{18,2},{2,18},{10,26},{26,10},{28,20},... | collective-permute-start | bytes 688136 | tf_op jit(solution)/shard_map/ppermute | solution.py:591
  14.1 3.9 %collective-permute-start.5 = (f32[4,7,2,8,128]{4,3,2,1,0:T(8,128)S(1)}, f32[4,7,2,8,128]{4,3,2,1,0:T(8,128)S(1)}, u32[]{:S(2)}, u32[]{:S(2)}) collective-permute-start(f32[4,7,2,8,128]{4,3,2,1,0:T(8,128)S(1)} %get-tuple-element.30), channel_id=1, source_target_pairs={{0,6},{8,24},{24,8},{16,18},{18,16},{2,10},{10,2},{26,28},{28,26},... | collective-permute-start | bytes 688136 | tf_op jit(solution)/shard_map/ppermute | solution.py:591
  18.0 0.0 collective-permute-start.3
  18.0 0.9 %collective-permute-done.4 = f32[4,7,2,8,128]{4,3,2,1,0:T(8,128)S(1)} collective-permute-done((f32[4,7,2,8,128]{4,3,2,1,0:T(8,128)S(1)}, f32[4,7,2,8,128]{4,3,2,1,0:T(8,128)S(1)}, u32[]{:S(2)}, u32[]{:S(2)}) %collective-permute-start.4) | collective-permute-done | bytes 229408 | tf_op jit(solution)/shard_map/ppermute | solution.py:591
  18.9 3.1 %collective-permute-done.5 = f32[4,7,2,8,128]{4,3,2,1,0:T(8,128)S(1)} collective-permute-done((f32[4,7,2,8,128]{4,3,2,1,0:T(8,128)S(1)}, f32[4,7,2,8,128]{4,3,2,1,0:T(8,128)S(1)}, u32[]{:S(2)}, u32[]{:S(2)}) %collective-permute-start.5) | collective-permute-done | bytes 229408 | tf_op jit(solution)/shard_map/ppermute | solution.py:591
  22.1 0.1 collective-permute-start.6
  22.2 0.0 collective-permute-done.3.zc
  22.2 1.8 %collective-permute-done.6.zsides = f32[8,7,2,8,128]{4,3,2,1,0:T(8,128)S(1)} collective-permute-done((f32[8,7,2,8,128]{4,3,2,1,0:T(8,128)S(1)}, f32[8,7,2,8,128]{4,3,2,1,0:T(8,128)S(1)}, u32[]{:S(2)}, u32[]{:S(2)}) %collective-permute-start.6) | collective-permute-done | bytes 458784 | tf_op jit(solution)/shard_map/ppermute | solution.py:565
  24.0 4.3 %shard_map.52 = (f32[80,128]{1,0:T(8,128)S(1)}, f32[208,128]{1,0:T(8,128)S(1)}, f32[30,2,32,128]{3,2,1,0:T(8,128)S(1)}, f32[30,2,32,128]{3,2,1,0:T(8,128)S(1)}, ...) custom-call(f32[4,16,2,8,128]{4,3,2,1,0:T(8,128)S(1)} %get-tuple-ele, ...), custom_call_target="tpu_custom_call" | custom-call | tf_op jit(solution)/shard_map/pallas_call | solution.py:644
  28.3 0.1 collective-permute-start.7
  28.4 0.3 collective-permute-start.9
  28.7 2.4 %collective-permute-start.8 = (f32[80,128]{1,0:T(8,128)S(1)}, f32[80,128]{1,0:T(8,128)S(1)}, u32[]{:S(2)}, u32[]{:S(2)}) collective-permute-start(f32[80,128]{1,0:T(8,128)S(1)} %get-tuple-element.31.pack), channel_id=1, source_target_pairs={{0,24},{8,16},{24,0},{16,8},{18,10},{2,26},{10,18},{26,2},{28,4},{... | collective-permute-start | bytes 122888 | tf_op jit(solution)/shard_map/ppermute | solution.py:596
  31.2 2.0 %collective-permute-done.7 = f32[208,128]{1,0:T(8,128)S(1)} collective-permute-done((f32[208,128]{1,0:T(8,128)S(1)}, f32[208,128]{1,0:T(8,128)S(1)}, u32[]{:S(2)}, u32[]{:S(2)}) %collective-permute-start.7) | collective-permute-done | bytes 106528 | tf_op jit(solution)/shard_map/ppermute | solution.py:596
  33.2 0.5 collective-permute-done.8
  33.6 0.0 collective-permute-done.9
  33.6 1.7 %collective-permute-start.10 = (f32[368,128]{1,0:T(8,128)S(1)}, f32[368,128]{1,0:T(8,128)S(1)}, u32[]{:S(2)}, u32[]{:S(2)}) collective-permute-start(f32[368,128]{1,0:T(8,128)S(1)} %constant_dynamic-update-slice_fusion.2.mine), channel_id=1, source_target_pairs={{0,1},{1,0},{2,3},{3,2},{4,5},{5,4},{6,7},{7,6},{8,9},{9,8},{10,11... | collective-permute-start | bytes 565256 | tf_op jit(solution)/shard_map/ppermute | solution.py:565
  35.3 1.1 %collective-permute-done.10.theirs = f32[368,128]{1,0:T(8,128)S(1)} collective-permute-done((f32[368,128]{1,0:T(8,128)S(1)}, f32[368,128]{1,0:T(8,128)S(1)}, u32[]{:S(2)}, u32[]{:S(2)}) %collective-permute-start.10) | collective-permute-done | bytes 188448 | tf_op jit(solution)/shard_map/ppermute | solution.py:565
  36.4 3.5 %shard_map.53 = f32[4,16,2,8,128]{4,3,2,1,0:T(8,128)S(1)} custom-call(f32[80,128]{1,0:T(8,128)S(1)} %get-tuple-element.31.pack, f32[368,128]{1,0:T(8,128)S(1)} %constant_dynamic-update-slice_fusion.2.mine, f32[368,128]{1,0:T(8,128)S(1)} %collective-permute-done.10.theirs, f32[30,2,32,128]{3,2,1,0:T(8,128)S(1)} %get-tuple-element.33.refs_0_, ...), custom_call_target="tpu_custom_call" | custom-call | tf_op jit(solution)/shard_map/pallas_call | solution.py:652
  40.0 0.9 %collective-permute-start.12 = (f32[256,128]{1,0:T(8,128)S(1)}, f32[256,128]{1,0:T(8,128)S(1)}, u32[]{:S(2)}, u32[]{:S(2)}) collective-permute-start(f32[256,128]{1,0:T(8,128)S(1)} %bitcast.15), channel_id=1, source_target_pairs={{0,16},{8,24},{16,0},{24,8},{1,17},{9,25},{17,1},{25,9},{2,18},{10... | collective-permute-start | bytes 393224 | tf_op jit(solution)/shard_map/ppermute | solution.py:575
  40.9 2.2 %collective-permute-start.13 = (f32[256,128]{1,0:T(8,128)S(1)}, f32[256,128]{1,0:T(8,128)S(1)}, u32[]{:S(2)}, u32[]{:S(2)}) collective-permute-start(f32[256,128]{1,0:T(8,128)S(1)} %bitcast.14), channel_id=1, source_target_pairs={{0,24},{8,16},{16,8},{24,0},{1,25},{9,17},{17,9},{25,1},{2,26},{10... | collective-permute-start | bytes 393224 | tf_op jit(solution)/shard_map/ppermute | solution.py:575
  43.2 0.4 collective-permute-start.11
  43.6 5.1 %collective-permute-done.12.refs_2_ = f32[256,128]{1,0:T(8,128)S(1)} collective-permute-done((f32[256,128]{1,0:T(8,128)S(1)}, f32[256,128]{1,0:T(8,128)S(1)}, u32[]{:S(2)}, u32[]{:S(2)}) %collective-permute-start.12) | collective-permute-done | bytes 131104 | tf_op jit(solution)/shard_map/ppermute | solution.py:575
  48.6 0.0 collective-permute-done.13.refs_3_
  48.6 1.5 %collective-permute-done.11.refs_1_ = f32[256,128]{1,0:T(8,128)S(1)} collective-permute-done((f32[256,128]{1,0:T(8,128)S(1)}, f32[256,128]{1,0:T(8,128)S(1)}, u32[]{:S(2)}, u32[]{:S(2)}) %collective-permute-start.11) | collective-permute-done | bytes 131104 | tf_op jit(solution)/shard_map/ppermute | solution.py:575
  50.1 1.0 %shard_map.54 = (f32[1,8,64,128]{3,2,1,0:T(8,128)}, f32[1,8,64,128]{3,2,1,0:T(8,128)}) custom-call(f32[256,128]{1,0:T(8,128)S(1)} %bitcast.8, f32[256,128]{1,0:T(8,128)S(1)} %collective-permute-done.11.refs_1_, f32[256,128]{1,0:T(8,128)S(1)} %collective-permute-done.12.refs_2_, f32[256,128]{1,0:T(8,128)S(1)} %collective-permute-done.13.refs_3_), custom_call_target="tpu_custom_call" | custom-call | tf_op jit(solution)/shard_map/pallas_call | solution.py:657
  (6 shorter events, 0.1 us)
Async XLA Ops:
  2.0 6.9 %collective-permute-start = (f32[256,128]{1,0:T(8,128)S(1)}, f32[256,128]{1,0:T(8,128)S(1)}, u32[]{:S(2)}, u32[]{:S(2)}) collective-permute-start(f32[256,128]{1,0:T(8,128)S(1)} %get-tuple-element.25), channel_id=1, source_target_pairs={{0,8},{8,0},{16,24},{24,16},{1,9},{9,1},{17,25},{25,17},{2,10},{10... | collective-permute-start | bytes 393224 | tf_op jit(solution)/shard_map/ppermute | solution.py:575
  5.0 7.8 %collective-permute-start.1 = (f32[256,128]{1,0:T(8,128)S(1)}, f32[256,128]{1,0:T(8,128)S(1)}, u32[]{:S(2)}, u32[]{:S(2)}) collective-permute-start(f32[256,128]{1,0:T(8,128)S(1)} %get-tuple-element.26), channel_id=1, source_target_pairs={{0,16},{8,24},{16,0},{24,8},{1,17},{9,25},{17,1},{25,9},{2,18},{10... | collective-permute-start | bytes 393224 | tf_op jit(solution)/shard_map/ppermute | solution.py:575
  6.5 6.3 %collective-permute-start.2 = (f32[256,128]{1,0:T(8,128)S(1)}, f32[256,128]{1,0:T(8,128)S(1)}, u32[]{:S(2)}, u32[]{:S(2)}) collective-permute-start(f32[256,128]{1,0:T(8,128)S(1)} %get-tuple-element.27), channel_id=1, source_target_pairs={{0,24},{8,16},{16,8},{24,0},{1,25},{9,17},{17,9},{25,1},{2,26},{10... | collective-permute-start | bytes 393224 | tf_op jit(solution)/shard_map/ppermute | solution.py:575
  12.8 6.1 %collective-permute-start.4 = (f32[4,7,2,8,128]{4,3,2,1,0:T(8,128)S(1)}, f32[4,7,2,8,128]{4,3,2,1,0:T(8,128)S(1)}, u32[]{:S(2)}, u32[]{:S(2)}) collective-permute-start(f32[4,7,2,8,128]{4,3,2,1,0:T(8,128)S(1)} %get-tuple-element.29), channel_id=1, source_target_pairs={{0,8},{8,0},{24,16},{16,24},{18,2},{2,18},{10,26},{26,10},{28,20},... | collective-permute-start | bytes 688136 | tf_op jit(solution)/shard_map/ppermute | solution.py:591
  14.1 8.0 %collective-permute-start.5 = (f32[4,7,2,8,128]{4,3,2,1,0:T(8,128)S(1)}, f32[4,7,2,8,128]{4,3,2,1,0:T(8,128)S(1)}, u32[]{:S(2)}, u32[]{:S(2)}) collective-permute-start(f32[4,7,2,8,128]{4,3,2,1,0:T(8,128)S(1)} %get-tuple-element.30), channel_id=1, source_target_pairs={{0,6},{8,24},{24,8},{16,18},{18,16},{2,10},{10,2},{26,28},{28,26},... | collective-permute-start | bytes 688136 | tf_op jit(solution)/shard_map/ppermute | solution.py:591
  18.0 4.2 %collective-permute-start.3 = (f32[4,16,2,8,128]{4,3,2,1,0:T(8,128)S(1)}, f32[4,16,2,8,128]{4,3,2,1,0:T(8,128)S(1)}, u32[]{:S(2)}, u32[]{:S(2)}) collective-permute-start(f32[4,16,2,8,128]{4,3,2,1,0:T(8,128)S(1)} %get-tuple-element.28.c), channel_id=1, source_target_pairs={{0,1},{1,0},{2,3},{3,2},{4,5},{5,4},{6,7},{7,6},{8,9},{9,8},{10,11... | collective-permute-start | bytes 1572872 | tf_op jit(solution)/shard_map/ppermute | solution.py:565
  22.1 1.9 %collective-permute-start.6 = (f32[8,7,2,8,128]{4,3,2,1,0:T(8,128)S(1)}, f32[8,7,2,8,128]{4,3,2,1,0:T(8,128)S(1)}, u32[]{:S(2)}, u32[]{:S(2)}) collective-permute-start(f32[8,7,2,8,128]{4,3,2,1,0:T(8,128)S(1)} %constant_dynamic-update-slice_fusion.sides), channel_id=1, source_target_pairs={{0,1},{1,0},{2,3},{3,2},{4,5},{5,4},{6,7},{7,6},{8,9},{9,8},{10,11... | collective-permute-start | bytes 1376264 | tf_op jit(solution)/shard_map/ppermute | solution.py:565
  28.3 4.8 %collective-permute-start.7 = (f32[208,128]{1,0:T(8,128)S(1)}, f32[208,128]{1,0:T(8,128)S(1)}, u32[]{:S(2)}, u32[]{:S(2)}) collective-permute-start(f32[208,128]{1,0:T(8,128)S(1)} %get-tuple-element.32), channel_id=1, source_target_pairs={{0,8},{8,0},{24,16},{16,24},{18,2},{2,18},{10,26},{26,10},{28,20},... | collective-permute-start | bytes 319496 | tf_op jit(solution)/shard_map/ppermute | solution.py:596
  28.4 5.2 %collective-permute-start.9 = (f32[80,128]{1,0:T(8,128)S(1)}, f32[80,128]{1,0:T(8,128)S(1)}, u32[]{:S(2)}, u32[]{:S(2)}) collective-permute-start(f32[80,128]{1,0:T(8,128)S(1)} %get-tuple-element.31.pack), channel_id=1, source_target_pairs={{0,16},{8,18},{24,2},{16,0},{18,8},{2,24},{10,20},{26,4},{28,12},{... | collective-permute-start | bytes 122888 | tf_op jit(solution)/shard_map/ppermute | solution.py:596
  28.7 4.9 %collective-permute-start.8 = (f32[80,128]{1,0:T(8,128)S(1)}, f32[80,128]{1,0:T(8,128)S(1)}, u32[]{:S(2)}, u32[]{:S(2)}) collective-permute-start(f32[80,128]{1,0:T(8,128)S(1)} %get-tuple-element.31.pack), channel_id=1, source_target_pairs={{0,24},{8,16},{24,0},{16,8},{18,10},{2,26},{10,18},{26,2},{28,4},{... | collective-permute-start | bytes 122888 | tf_op jit(solution)/shard_map/ppermute | solution.py:596
  33.6 2.7 %collective-permute-start.10 = (f32[368,128]{1,0:T(8,128)S(1)}, f32[368,128]{1,0:T(8,128)S(1)}, u32[]{:S(2)}, u32[]{:S(2)}) collective-permute-start(f32[368,128]{1,0:T(8,128)S(1)} %constant_dynamic-update-slice_fusion.2.mine), channel_id=1, source_target_pairs={{0,1},{1,0},{2,3},{3,2},{4,5},{5,4},{6,7},{7,6},{8,9},{9,8},{10,11... | collective-permute-start | bytes 565256 | tf_op jit(solution)/shard_map/ppermute | solution.py:565
  40.0 8.6 %collective-permute-start.12 = (f32[256,128]{1,0:T(8,128)S(1)}, f32[256,128]{1,0:T(8,128)S(1)}, u32[]{:S(2)}, u32[]{:S(2)}) collective-permute-start(f32[256,128]{1,0:T(8,128)S(1)} %bitcast.15), channel_id=1, source_target_pairs={{0,16},{8,24},{16,0},{24,8},{1,17},{9,25},{17,1},{25,9},{2,18},{10... | collective-permute-start | bytes 393224 | tf_op jit(solution)/shard_map/ppermute | solution.py:575
  40.9 7.7 %collective-permute-start.13 = (f32[256,128]{1,0:T(8,128)S(1)}, f32[256,128]{1,0:T(8,128)S(1)}, u32[]{:S(2)}, u32[]{:S(2)}) collective-permute-start(f32[256,128]{1,0:T(8,128)S(1)} %bitcast.14), channel_id=1, source_target_pairs={{0,24},{8,16},{16,8},{24,0},{1,25},{9,17},{17,9},{25,1},{2,26},{10... | collective-permute-start | bytes 393224 | tf_op jit(solution)/shard_map/ppermute | solution.py:575
  43.2 6.9 %collective-permute-start.11 = (f32[256,128]{1,0:T(8,128)S(1)}, f32[256,128]{1,0:T(8,128)S(1)}, u32[]{:S(2)}, u32[]{:S(2)}) collective-permute-start(f32[256,128]{1,0:T(8,128)S(1)} %bitcast.13), channel_id=1, source_target_pairs={{0,8},{8,0},{16,24},{24,16},{1,9},{9,1},{17,25},{25,17},{2,10},{10... | collective-permute-start | bytes 393224 | tf_op jit(solution)/shard_map/ppermute | solution.py:575

commit v3 on v2

--- a/solution.py
+++ b/solution.py
@@ -12,6 +12,7 @@
 LANES = 128
 WIDE = 256
 HALO = 7
+HALO_RHS = 6
 FAR = 3
 F32 = jnp.float32
 VMEM_LIMIT = 24 * 1024 * 1024
@@ -40,6 +41,11 @@
         q = lax.rem(self.look_up(self.place, i) + lax.axis_index("gy"), self.gx)
         return pl.multiple_of(q * self.by, self.by)
 
+    def distance(self, slot):
+        if self.gx != 4 or slot not in (1, 2):
+            return slot
+        return jnp.where(lax.rem(lax.axis_index("gz"), 2) == 0, slot, 3 - slot)
+
     def block_here(self):
         j = lax.axis_index("gy")
         return j * self.gx + lax.rem(self.look_up(self.place, lax.axis_index("gx")) + j, self.gx)
@@ -228,8 +234,8 @@
         copy.wait()
     here = lax.axis_index("gx")
     by, px = plan.by, plan.px
-    for k, out in enumerate(outs):
-        rows = pl.ds(plan.start_of(here ^ k), by)
+    for slot, out in enumerate(outs):
+        rows = pl.ds(plan.start_of(here ^ plan.distance(slot)), by)
         for p in range(px):
             half = jnp.where(phase[p, rows, :] == 1, 500.0, 0.5).astype(F32)
             out[pl.ds(p, by, stride=2 * px), :] = half * density[p, rows, :]
@@ -239,11 +245,26 @@
 def gather_kernel(plan, *refs):
     parts, (c, *sets) = refs[: plan.gx], refs[plan.gx :]
     block = plan.block_here()
-    for k, part in enumerate(parts):
+    for slot, part in enumerate(parts):
+        k = plan.distance(slot)
         c[k] = part[...]
         for one, out in enumerate(sets):
-            first = jnp.where(plan.is_up(block, 1, one), plan.by - HALO, 0)
-            out[k] = part[pl.ds(first, HALO)]
+            up = plan.is_up(block, 1, one)
+            for field, count, at in ((0, HALO, 0), (1, HALO_RHS, HALO)):
+                first = jnp.where(up, plan.by - count, 0)
+                for r in range(count):
+                    out[k, at + r] = part[first + r, field]
+
+
+def compress(stage, g):
+    halves, _, rows, _ = stage.shape
+    width = LANES // g
+    cell = lax.broadcasted_iota(jnp.int32, (rows, LANES), 1)
+    lanes, place = lax.rem(g * cell, LANES), lax.div(cell, width)
+    total = pick_lanes(stage[0, 0], lanes)
+    for k in range(1, 2 * halves):
+        total = jnp.where(place == k, pick_lanes(stage[k // 2, k % 2], lanes), total)
+    return total
 
 
 def down_kernel(plan, c, zc, sides, zsides, *refs):
@@ -251,7 +272,7 @@
     pack, nears, refs = refs[0], refs[1 : 1 + near_count], refs[1 + near_count :]
     kx0, ky0, kz0, d0, w0, f0, ub, kx1, ky1, kz1, w1, f1, u1 = [Wide(r) for r in refs[:13]]
     h0, ua, face, r0, uc, r1, d1 = [Wide(r) for r in refs[13:20]]
-    stage = refs[20]
+    stage, near_stage = refs[20:22]
     nx, by, rows, gx, px = plan.nx, plan.by, plan.rows, plan.gx, plan.px
     shape = (nx, WIDE)
     block, here = plan.block_here(), lax.axis_index("gx")
@@ -270,24 +291,41 @@
     z_shut = (z < 0) | (z >= z_count - 1)
     z_out = (z < 0) | (z >= z_count)
 
-    def take(a, b, at, other, r, to):
+    def put_h(to, s, xs, tile):
         y = base + to
-        inside = (y >= 0) & (y < y_count)
-        for k in range(gx):
-            xs = pl.ds(pl.multiple_of((other ^ k) * px, px), px)
-            for s, ref in enumerate((a, b)):
-                h = jnp.where(inside, ref[at + k, r, 0], 0.5)
-                if not plan.paired:
-                    h = jnp.where(z_out[:px, s * LANES : (s + 1) * LANES], 0.5, h)
-                h0.ref[to, s, xs, :] = h
-                f0.ref[to, s, xs, :] = ref[at + k, r, 1]
-
-    each(0, by - 1, 4, lambda r: take(c, zc, 0, here, r, r + HALO))
+        tile = jnp.where((y >= 0) & (y < y_count), tile, 0.5)
+        if not plan.paired:
+            tile = jnp.where(z_out[:px, s * LANES : (s + 1) * LANES], 0.5, tile)
+        h0.ref[to, s, xs, :] = tile
+
+    def tiles(other):
+        return [(k, pl.ds(pl.multiple_of((other ^ k) * px, px), px)) for k in range(gx)]
+
+    def take(r):
+        for k, xs in tiles(here):
+            for s, ref in enumerate((c, zc)):
+                put_h(r + HALO, s, xs, ref[k, r, 0])
+                f0.ref[r + HALO, s, xs, :] = ref[k, r, 1]
+
+    def take_side(at, other, to, count, field):
+        def one(r):
+            for k, xs in tiles(other):
+                for s, ref in enumerate((sides, zsides)):
+                    if field == 0:
+                        put_h(r + to, s, xs, ref[at + k, r])
+                    else:
+                        f0.ref[r + to, s, xs, :] = ref[at + k, HALO + r]
+
+        each(0, count - 1, 4, one)
+
+    each(0, by - 1, 4, take)
     up_first = plan.is_up(block, 1, 0)
-    below, above = jnp.where(up_first, gx, 0), jnp.where(up_first, 0, gx)
+    below, above = jnp.where(up_first, 0, gx), jnp.where(up_first, gx, 0)
     gx_below, gx_above = plan.gx_of(block - 1), plan.gx_of(block + 1)
-    each(0, HALO - 1, 4, lambda r: take(sides, zsides, below, gx_below, r, r))
-    each(0, HALO - 1, 4, lambda r: take(sides, zsides, above, gx_above, r, r + HALO + by))
+    take_side(below, gx_below, 0, HALO, 0)
+    take_side(above, gx_above, HALO + by, HALO, 0)
+    take_side(below, gx_below, HALO - HALO_RHS, HALO_RHS, 1)
+    take_side(above, gx_above, HALO + by, HALO_RHS, 1)
 
     @pl.when(block == 0)
     def _():
@@ -362,26 +400,20 @@
     for j in range(own2):
         fields = (coarse_sum(r1, j, quarter_x, 2),) + coarse_coefficients(middle, 4 + 2 * j, quarter_x)
         for t, a in enumerate(fields):
-            stage[j // part, pl.ds((t * part + j % part) * quarter_x, quarter_x), :] = a
-    cell = lax.broadcasted_iota(jnp.int32, pack.shape, 1)
-    lanes = lax.rem(4 * cell, LANES)
-    quarter = lax.div(4 * cell, LANES)
-    total = pick_lanes(stage[0, :, :LANES], lanes)
-    for k in range(1, 4):
-        half = slice((k % 2) * LANES, (k % 2 + 1) * LANES)
-        total = jnp.where(quarter == k, pick_lanes(stage[k // 2, :, half], lanes), total)
+            xs = pl.ds((t * part + j % part) * quarter_x, quarter_x)
+            stage[j // part, 0, xs, :] = a[:, :LANES]
+            stage[j // part, 1, xs, :] = a[:, LANES:]
+    total = compress(stage, 4)
     pack[...] = total
 
     size = pack.shape[0]
-
-    def near(out, first):
+    for one, out in enumerate(nears):
+        row = jnp.where(plan.is_up(block, 1, core if plan.paired else one), own, 5)
+        for k, (ref, r) in enumerate(((u1, row), (u1, row + 1), (u1, row + 2), (f1, row + 1))):
+            for s in range(2):
+                near_stage[0, s, pl.ds(k * half_x, half_x), :] = ref.ref[r, s]
         out[pl.ds(0, size), :] = total
-        for k, (ref, r) in enumerate(((u1, first), (u1, first + 1), (u1, first + 2), (f1, first + 1))):
-            for s in range(2):
-                out[pl.ds(size + (2 * k + s) * half_x, half_x), :] = ref.ref[r, s]
-
-    for one, out in enumerate(nears):
-        near(out, jnp.where(plan.is_up(block, 1, core if plan.paired else one), own, 5))
+        out[pl.ds(size, 4 * half_x), :] = compress(near_stage, 2)
 
 
 def up_kernel(plan, pack, mine, theirs, *refs):
@@ -397,7 +429,7 @@
     part = own2 // 2
     half_x, quarter_x = nx // 2, nx // 4
     size = pack.shape[0]
-    side = size + 8 * half_x
+    side = size + 4 * half_x
     core = lax.axis_index("gz")
     block = plan.block_here()
     here = lax.axis_index("gx")
@@ -417,8 +449,10 @@
     for ref, up, half_turn in ((mine, ups[1], 0), (theirs, jnp.logical_not(ups[1]), turn)):
         row = jnp.where(up, own + 5, 0)
         for k, (to, r) in enumerate(((ua1, row), (ua1, row + 1), (ua1, row + 2), (f1, row + 1))):
+            row_in = ref[pl.ds(size + k * half_x, half_x), :]
+            lane = lax.broadcasted_iota(jnp.int32, row_in.shape, 1)
             for s in range(2):
-                to.ref[r, s ^ half_turn] = ref[pl.ds(size + (2 * k + s) * half_x, half_x), :]
+                to.ref[r, s ^ half_turn] = pick_lanes(row_in, lax.div(lane, 2) + s * (LANES // 2))
 
     lane = lax.broadcasted_iota(jnp.int32, (size, LANES), 1)
     lanes = [lax.div(lane, 4) + k * (LANES // 4) for k in range(4)]
@@ -513,14 +547,22 @@
         uc0[2 * j] = finest.swept(ub0, 2 * j)
         uc0[2 * j + 1] = finest.swept(ub0, 2 * j + 1)
 
+    slots = []
+    for s in range(plan.gx):
+        slot = s ^ here
+        if plan.gx == 4:
+            for k in (1, 2):
+                slot = jnp.where((s ^ here) == k, plan.distance(k), slot)
+        slots.append(slot)
+
     def finish(j):
         for r in (2 * j - 1, 2 * j):
             scaled = d0[r] * uc0[r]
             rest = f0[r] + finest.beside(uc0, r) - scaled
             for s in range(plan.gx):
                 part = slice(s * plan.px, (s + 1) * plan.px)
-                out[s ^ here, r - HALO, 0] = scaled[part, :LANES]
-                out[s ^ here, r - HALO, 1] = rest[part, :LANES]
+                out[slots[s], r - HALO, 0] = scaled[part, :LANES]
+                out[slots[s], r - HALO, 1] = rest[part, :LANES]
 
     wave(
         (finish, 4, own + 3, 5),
@@ -534,8 +576,8 @@
     parts, (scaled, residual) = refs[: plan.gx], refs[plan.gx :]
     here = lax.axis_index("gx")
     by, px = plan.by, plan.px
-    for k, part in enumerate(parts):
-        rows = pl.ds(plan.start_of(here ^ k), by)
+    for slot, part in enumerate(parts):
+        rows = pl.ds(plan.start_of(here ^ plan.distance(slot)), by)
         for p in range(px):
             scaled[0, p, rows, :] = part[pl.ds(p, by, stride=2 * px), :]
             residual[0, p, rows, :] = part[pl.ds(px + p, by, stride=2 * px), :]
@@ -571,8 +613,14 @@
 
 def exchange(plan, parts):
     got = [parts[0]] * plan.gx
-    for k in range(plan.gx - 1, 0, -1):
-        got[k] = lax.ppermute(parts[k], "gx", [(i, i ^ k) for i in range(plan.gx)])
+    for slot in range(plan.gx - 1, 0, -1):
+        mixed = plan.gx == 4 and slot in (1, 2)
+        pairs = []
+        for i in range(plan.gx):
+            for g in range(plan.gz):
+                k = 3 - slot if mixed and g % 2 else slot
+                pairs.append((i * plan.gz + g, (i ^ k) * plan.gz + g))
+        got[slot] = lax.ppermute(parts[slot], ("gx", "gz"), pairs)
     return got
 
 
@@ -621,15 +669,15 @@
     parts = [a.reshape(by, 2, px, LANES) for a in exchange(plan, parts)]
     c, *sets = call(
         functools.partial(gather_kernel, plan),
-        [in_vmem(gx, by, 2, px, LANES)] + [in_vmem(gx, HALO, 2, px, LANES)] * 2,
+        [in_vmem(gx, by, 2, px, LANES)] + [in_vmem(gx, HALO + HALO_RHS, px, LANES)] * 2,
     )(*pinned(*parts))
-    sides = jnp.concatenate([swap_blocks(plan, a, 1, one) for one, a in enumerate(sets)], axis=0)
+    sides = jnp.concatenate([swap_blocks(plan, sets[one], 1, one) for one in (1, 0)], axis=0)
     zc = beside_in_z(plan, c)
     zsides = beside_in_z(plan, sides)
 
     own, own2 = by // 2, by // 4
     size = 5 * (own2 // 2) * (nx // 4)
-    side = size + 8 * (nx // 2)
+    side = size + 4 * (nx // 2)
 
     def level0(n):
         return in_vmem(n, 2, nx, LANES)
@@ -640,7 +688,7 @@
     outs = [in_vmem(size, LANES)] + [in_vmem(side, LANES)] * (1 if plan.paired else 2)
     fields = [level0(rows)] * 7 + [level1(own + 8)] * 6
     scratch = [level0(rows)] * 3 + [level0(own + 8), level1(own + 8), level1(own2), level1(own + 8)]
-    scratch += [in_vmem(2, size, WIDE)]
+    scratch += [in_vmem(2, 2, size, LANES), in_vmem(1, 2, 4 * (nx // 2), LANES)]
     down = call(functools.partial(down_kernel, plan), outs + fields, scratch)(*pinned(c, zc, sides, zsides))
     pack, nears, fields = down[0], down[1 : len(outs)], down[len(outs) :]
 

time: 51.2 us -> 50.4 us (0.984)
  starting transfers between devices: 17.9 us -> 15.8 us
  waiting for transfers between devices: 22.2 us -> 23.5 us
    ppermute x2, waiting for transfers between devices: 4.08 us -> 5.97 us  [swap_blocks(): return lax.ppermute(a, ('gx', 'gy'), pairs_of(plan, k, one))]
    ppermute x2, starting transfers between devices: 5.18 us -> 3.67 us  [swap_blocks(): return lax.ppermute(a, ('gx', 'gy'), pairs_of(plan, k, one))]
    ppermute x3, starting transfers between devices: 1.76 us -> 0.25 us  [beside_in_z(): return lax.ppermute(a, 'gz', [(0, 1), (1, 0)])]
    ppermute x6, starting transfers between devices: 8.11 us -> 8.91 us  [exchange(): got[slot] = lax.ppermute(parts[slot], ('gx', 'gz'), pairs)]
    ppermute x6, waiting for transfers between devices: 12.8 us -> 12 us  [exchange(): got[slot] = lax.ppermute(parts[slot], ('gx', 'gz'), pairs)]
  transfers between devices with their start and end apart: 14 -> 14, of which waited for: 10 -> 11; matrix products, arithmetic and copies ran while one was open for 0% -> 0% of each run, Pallas kernels for 0% -> 0%
where the time goes in v3:
time: 50.4 us; the launch traced here: 50.3 us
  waiting for transfers between devices  23.5 us (47%)
  starting transfers between devices  15.8 us (31%)
  Pallas kernels  10.2 us (20%)
  between operations  0.71 us (1%)
    ppermute x6, waiting for transfers between devices, exchange(): got[slot] = lax.ppermute(parts[slot], ('gx', 'gz'), pairs)  12 us
    ppermute x6, starting transfers between devices, exchange(): got[slot] = lax.ppermute(parts[slot], ('gx', 'gz'), pairs)  8.91 us
    ppermute x2, waiting for transfers between devices, swap_blocks(): return lax.ppermute(a, ('gx', 'gy'), pairs_of(plan, k, one))  5.97 us
    pallas_call x1, Pallas kernels, on_device(): call(functools.partial(down_kernel, plan), outs + fields, scratch)  4.28 us
    ppermute x2, starting transfers between devices, swap_blocks(): return lax.ppermute(a, ('gx', 'gy'), pairs_of(plan, k, one))  3.67 us
    pallas_call x1, Pallas kernels, on_device(): call(functools.partial(up_kernel, plan), [in_vmem(gx, by, 2, px, LANES)],...  3.54 us
    ppermute x3, waiting for transfers between devices, beside_in_z(): return lax.ppermute(a, 'gz', [(0, 1), (1, 0)])  3.02 us
    ppermute x3, starting transfers between devices, swap_blocks_apart(): return lax.ppermute(a, ('gx', 'gy', 'gz'), pairs)  2.97 us
  transfers between devices with their start and end apart: 14, of which 11 were waited for; matrix products, arithmetic and copies ran while one was open for 0% of the time, Pallas kernels for 0%

profile of v3, /device:TPU:0, one launch (start us, length us, event | category | flops | bytes accessed | tf_op | source)
XLA Modules:
  0.0 50.3 jit_solution(4843425017012340871)
XLA Ops:
  0.6 1.3 %shard_map.50 = (f32[256,128]{1,0:T(8,128)S(1)}, f32[256,128]{1,0:T(8,128)S(1)}, f32[256,128]{1,0:T(8,128)S(1)}, f32[256,128]{1,0:T(8,128)S(1)}) custom-call(s32[8,64,128]{2,1,0:T(8,128)} %phase_in.1, f32[8,64,128]{2,1,0:T(8,128)} %density_in.1, f32[1,8,64,128]{3,2,1,0:T(8,128)} %rhs_in.1), custom_call_target="tpu_custom_call" | custom-call | tf_op jit(solution)/shard_map/pallas_call | solution.py:663
  2.0 3.0 %collective-permute-start = (f32[256,128]{1,0:T(8,128)S(1)}, f32[256,128]{1,0:T(8,128)S(1)}, u32[]{:S(2)}, u32[]{:S(2)}) collective-permute-start(f32[256,128]{1,0:T(8,128)S(1)} %get-tuple-element.25), channel_id=1, source_target_pairs={{0,8},{1,17},{8,0},{9,25},{16,24},{17,1},{24,16},{25,9},{2,10},{3,... | collective-permute-start | bytes 393224 | tf_op jit(solution)/shard_map/ppermute | solution.py:623
  5.0 1.5 %collective-permute-start.1 = (f32[256,128]{1,0:T(8,128)S(1)}, f32[256,128]{1,0:T(8,128)S(1)}, u32[]{:S(2)}, u32[]{:S(2)}) collective-permute-start(f32[256,128]{1,0:T(8,128)S(1)} %get-tuple-element.26), channel_id=1, source_target_pairs={{0,16},{1,9},{8,24},{9,1},{16,0},{17,25},{24,8},{25,17},{2,18},{3,... | collective-permute-start | bytes 393224 | tf_op jit(solution)/shard_map/ppermute | solution.py:623
  6.5 0.0 collective-permute-start.2
  6.5 2.2 %collective-permute-done = f32[256,128]{1,0:T(8,128)S(1)} collective-permute-done((f32[256,128]{1,0:T(8,128)S(1)}, f32[256,128]{1,0:T(8,128)S(1)}, u32[]{:S(2)}, u32[]{:S(2)}) %collective-permute-start) | collective-permute-done | bytes 131104 | tf_op jit(solution)/shard_map/ppermute | solution.py:623
  8.7 4.0 %collective-permute-done.1 = f32[256,128]{1,0:T(8,128)S(1)} collective-permute-done((f32[256,128]{1,0:T(8,128)S(1)}, f32[256,128]{1,0:T(8,128)S(1)}, u32[]{:S(2)}, u32[]{:S(2)}) %collective-permute-start.1) | collective-permute-done | bytes 131104 | tf_op jit(solution)/shard_map/ppermute | solution.py:623
  12.7 0.0 collective-permute-done.2
  12.7 0.1 shard_map.51
  12.8 3.7 %collective-permute-start.4 = (f32[4,13,8,128]{3,2,1,0:T(8,128)S(1)}, f32[4,13,8,128]{3,2,1,0:T(8,128)S(1)}, u32[]{:S(2)}, u32[]{:S(2)}) collective-permute-start(f32[4,13,8,128]{3,2,1,0:T(8,128)S(1)} %get-tuple-element.29), channel_id=1, source_target_pairs={{0,6},{8,24},{24,8},{16,18},{18,16},{2,10},{10,2},{26,28},{28,26},... | collective-permute-start | bytes 638984 | tf_op jit(solution)/shard_map/ppermute | solution.py:639
  16.5 0.0 collective-permute-start.5
  16.5 0.0 collective-permute-start.3
  16.5 4.5 %collective-permute-done.4 = f32[4,13,8,128]{3,2,1,0:T(8,128)S(1)} collective-permute-done((f32[4,13,8,128]{3,2,1,0:T(8,128)S(1)}, f32[4,13,8,128]{3,2,1,0:T(8,128)S(1)}, u32[]{:S(2)}, u32[]{:S(2)}) %collective-permute-start.4) | collective-permute-done | bytes 213024 | tf_op jit(solution)/shard_map/ppermute | solution.py:639
  21.0 1.4 %collective-permute-done.5 = f32[4,13,8,128]{3,2,1,0:T(8,128)S(1)} collective-permute-done((f32[4,13,8,128]{3,2,1,0:T(8,128)S(1)}, f32[4,13,8,128]{3,2,1,0:T(8,128)S(1)}, u32[]{:S(2)}, u32[]{:S(2)}) %collective-permute-start.5) | collective-permute-done | bytes 213024 | tf_op jit(solution)/shard_map/ppermute | solution.py:639
  22.5 0.1 collective-permute-start.6
  22.6 0.0 collective-permute-done.3.zc
  22.6 1.7 %collective-permute-done.6.zsides = f32[8,13,8,128]{3,2,1,0:T(8,128)S(1)} collective-permute-done((f32[8,13,8,128]{3,2,1,0:T(8,128)S(1)}, f32[8,13,8,128]{3,2,1,0:T(8,128)S(1)}, u32[]{:S(2)}, u32[]{:S(2)}) %collective-permute-start.6) | collective-permute-done | bytes 426016 | tf_op jit(solution)/shard_map/ppermute | solution.py:607
  24.3 4.3 %shard_map.52 = (f32[80,128]{1,0:T(8,128)S(1)}, f32[144,128]{1,0:T(8,128)S(1)}, f32[30,2,32,128]{3,2,1,0:T(8,128)S(1)}, f32[30,2,32,128]{3,2,1,0:T(8,128)S(1)}, ...) custom-call(f32[4,16,2,8,128]{4,3,2,1,0:T(8,128)S(1)} %get-tuple-ele, ...), custom_call_target="tpu_custom_call" | custom-call | tf_op jit(solution)/shard_map/pallas_call | solution.py:692
  28.6 0.3 collective-permute-start.7
  29.0 0.2 collective-permute-start.9
  29.2 2.4 %collective-permute-start.8 = (f32[80,128]{1,0:T(8,128)S(1)}, f32[80,128]{1,0:T(8,128)S(1)}, u32[]{:S(2)}, u32[]{:S(2)}) collective-permute-start(f32[80,128]{1,0:T(8,128)S(1)} %get-tuple-element.31.pack), channel_id=1, source_target_pairs={{0,24},{8,16},{24,0},{16,8},{18,10},{2,26},{10,18},{26,2},{28,4},{... | collective-permute-start | bytes 122888 | tf_op jit(solution)/shard_map/ppermute | solution.py:644
  31.6 1.7 %collective-permute-done.7 = f32[144,128]{1,0:T(8,128)S(1)} collective-permute-done((f32[144,128]{1,0:T(8,128)S(1)}, f32[144,128]{1,0:T(8,128)S(1)}, u32[]{:S(2)}, u32[]{:S(2)}) %collective-permute-start.7) | collective-permute-done | bytes 73760 | tf_op jit(solution)/shard_map/ppermute | solution.py:644
  33.2 0.9 %collective-permute-done.8 = f32[80,128]{1,0:T(8,128)S(1)} collective-permute-done((f32[80,128]{1,0:T(8,128)S(1)}, f32[80,128]{1,0:T(8,128)S(1)}, u32[]{:S(2)}, u32[]{:S(2)}) %collective-permute-start.8) | collective-permute-done | bytes 40992 | tf_op jit(solution)/shard_map/ppermute | solution.py:644
  34.1 0.0 collective-permute-done.9
  34.1 0.2 collective-permute-start.10
  34.3 1.3 %collective-permute-done.10.theirs = f32[304,128]{1,0:T(8,128)S(1)} collective-permute-done((f32[304,128]{1,0:T(8,128)S(1)}, f32[304,128]{1,0:T(8,128)S(1)}, u32[]{:S(2)}, u32[]{:S(2)}) %collective-permute-start.10) | collective-permute-done | bytes 155680 | tf_op jit(solution)/shard_map/ppermute | solution.py:607
  35.6 3.5 %shard_map.53 = f32[4,16,2,8,128]{4,3,2,1,0:T(8,128)S(1)} custom-call(f32[80,128]{1,0:T(8,128)S(1)} %get-tuple-element.31.pack, f32[304,128]{1,0:T(8,128)S(1)} %constant_dynamic-update-slice_fusion.2.mine, f32[304,128]{1,0:T(8,128)S(1)} %collective-permute-done.10.theirs, f32[30,2,32,128]{3,2,1,0:T(8,128)S(1)} %get-tuple-element.33.refs_0_, ...), custom_call_target="tpu_custom_call" | custom-call | tf_op jit(solution)/shard_map/pallas_call | solution.py:700
  39.2 2.2 %collective-permute-start.12 = (f32[256,128]{1,0:T(8,128)S(1)}, f32[256,128]{1,0:T(8,128)S(1)}, u32[]{:S(2)}, u32[]{:S(2)}) collective-permute-start(f32[256,128]{1,0:T(8,128)S(1)} %bitcast.15), channel_id=1, source_target_pairs={{0,16},{1,9},{8,24},{9,1},{16,0},{17,25},{24,8},{25,17},{2,18},{3,... | collective-permute-start | bytes 393224 | tf_op jit(solution)/shard_map/ppermute | solution.py:623
  41.4 1.7 %collective-permute-start.13 = (f32[256,128]{1,0:T(8,128)S(1)}, f32[256,128]{1,0:T(8,128)S(1)}, u32[]{:S(2)}, u32[]{:S(2)}) collective-permute-start(f32[256,128]{1,0:T(8,128)S(1)} %bitcast.14), channel_id=1, source_target_pairs={{0,24},{1,25},{8,16},{9,17},{16,8},{17,9},{24,0},{25,1},{2,26},{3,... | collective-permute-start | bytes 393224 | tf_op jit(solution)/shard_map/ppermute | solution.py:623
  43.0 0.5 collective-permute-start.11
  43.5 0.8 %collective-permute-done.12.refs_2_ = f32[256,128]{1,0:T(8,128)S(1)} collective-permute-done((f32[256,128]{1,0:T(8,128)S(1)}, f32[256,128]{1,0:T(8,128)S(1)}, u32[]{:S(2)}, u32[]{:S(2)}) %collective-permute-start.12) | collective-permute-done | bytes 131104 | tf_op jit(solution)/shard_map/ppermute | solution.py:623
  44.3 4.2 %collective-permute-done.13.refs_3_ = f32[256,128]{1,0:T(8,128)S(1)} collective-permute-done((f32[256,128]{1,0:T(8,128)S(1)}, f32[256,128]{1,0:T(8,128)S(1)}, u32[]{:S(2)}, u32[]{:S(2)}) %collective-permute-start.13) | collective-permute-done | bytes 131104 | tf_op jit(solution)/shard_map/ppermute | solution.py:623
  48.5 0.8 %collective-permute-done.11.refs_1_ = f32[256,128]{1,0:T(8,128)S(1)} collective-permute-done((f32[256,128]{1,0:T(8,128)S(1)}, f32[256,128]{1,0:T(8,128)S(1)}, u32[]{:S(2)}, u32[]{:S(2)}) %collective-permute-start.11) | collective-permute-done | bytes 131104 | tf_op jit(solution)/shard_map/ppermute | solution.py:623
  49.3 1.0 %shard_map.54 = (f32[1,8,64,128]{3,2,1,0:T(8,128)}, f32[1,8,64,128]{3,2,1,0:T(8,128)}) custom-call(f32[256,128]{1,0:T(8,128)S(1)} %bitcast.8, f32[256,128]{1,0:T(8,128)S(1)} %collective-permute-done.11.refs_1_, f32[256,128]{1,0:T(8,128)S(1)} %collective-permute-done.12.refs_2_, f32[256,128]{1,0:T(8,128)S(1)} %collective-permute-done.13.refs_3_), custom_call_target="tpu_custom_call" | custom-call | tf_op jit(solution)/shard_map/pallas_call | solution.py:705
  (6 shorter events, 0.1 us)
Async XLA Ops:
  2.0 6.8 %collective-permute-start = (f32[256,128]{1,0:T(8,128)S(1)}, f32[256,128]{1,0:T(8,128)S(1)}, u32[]{:S(2)}, u32[]{:S(2)}) collective-permute-start(f32[256,128]{1,0:T(8,128)S(1)} %get-tuple-element.25), channel_id=1, source_target_pairs={{0,8},{1,17},{8,0},{9,25},{16,24},{17,1},{24,16},{25,9},{2,10},{3,... | collective-permute-start | bytes 393224 | tf_op jit(solution)/shard_map/ppermute | solution.py:623
  5.0 7.8 %collective-permute-start.1 = (f32[256,128]{1,0:T(8,128)S(1)}, f32[256,128]{1,0:T(8,128)S(1)}, u32[]{:S(2)}, u32[]{:S(2)}) collective-permute-start(f32[256,128]{1,0:T(8,128)S(1)} %get-tuple-element.26), channel_id=1, source_target_pairs={{0,16},{1,9},{8,24},{9,1},{16,0},{17,25},{24,8},{25,17},{2,18},{3,... | collective-permute-start | bytes 393224 | tf_op jit(solution)/shard_map/ppermute | solution.py:623
  6.5 6.3 %collective-permute-start.2 = (f32[256,128]{1,0:T(8,128)S(1)}, f32[256,128]{1,0:T(8,128)S(1)}, u32[]{:S(2)}, u32[]{:S(2)}) collective-permute-start(f32[256,128]{1,0:T(8,128)S(1)} %get-tuple-element.27), channel_id=1, source_target_pairs={{0,24},{1,25},{8,16},{9,17},{16,8},{17,9},{24,0},{25,1},{2,26},{3,... | collective-permute-start | bytes 393224 | tf_op jit(solution)/shard_map/ppermute | solution.py:623
  12.8 8.2 %collective-permute-start.4 = (f32[4,13,8,128]{3,2,1,0:T(8,128)S(1)}, f32[4,13,8,128]{3,2,1,0:T(8,128)S(1)}, u32[]{:S(2)}, u32[]{:S(2)}) collective-permute-start(f32[4,13,8,128]{3,2,1,0:T(8,128)S(1)} %get-tuple-element.29), channel_id=1, source_target_pairs={{0,6},{8,24},{24,8},{16,18},{18,16},{2,10},{10,2},{26,28},{28,26},... | collective-permute-start | bytes 638984 | tf_op jit(solution)/shard_map/ppermute | solution.py:639
  16.5 6.0 %collective-permute-start.5 = (f32[4,13,8,128]{3,2,1,0:T(8,128)S(1)}, f32[4,13,8,128]{3,2,1,0:T(8,128)S(1)}, u32[]{:S(2)}, u32[]{:S(2)}) collective-permute-start(f32[4,13,8,128]{3,2,1,0:T(8,128)S(1)} %get-tuple-element.30), channel_id=1, source_target_pairs={{0,8},{8,0},{24,16},{16,24},{18,2},{2,18},{10,26},{26,10},{28,20},... | collective-permute-start | bytes 638984 | tf_op jit(solution)/shard_map/ppermute | solution.py:639
  16.5 6.1 %collective-permute-start.3 = (f32[4,16,2,8,128]{4,3,2,1,0:T(8,128)S(1)}, f32[4,16,2,8,128]{4,3,2,1,0:T(8,128)S(1)}, u32[]{:S(2)}, u32[]{:S(2)}) collective-permute-start(f32[4,16,2,8,128]{4,3,2,1,0:T(8,128)S(1)} %get-tuple-element.28.c), channel_id=1, source_target_pairs={{0,1},{1,0},{2,3},{3,2},{4,5},{5,4},{6,7},{7,6},{8,9},{9,8},{10,11... | collective-permute-start | bytes 1572872 | tf_op jit(solution)/shard_map/ppermute | solution.py:607
  22.5 1.8 %collective-permute-start.6 = (f32[8,13,8,128]{3,2,1,0:T(8,128)S(1)}, f32[8,13,8,128]{3,2,1,0:T(8,128)S(1)}, u32[]{:S(2)}, u32[]{:S(2)}) collective-permute-start(f32[8,13,8,128]{3,2,1,0:T(8,128)S(1)} %constant_dynamic-update-slice_fusion.sides), channel_id=1, source_target_pairs={{0,1},{1,0},{2,3},{3,2},{4,5},{5,4},{6,7},{7,6},{8,9},{9,8},{10,11... | collective-permute-start | bytes 1277960 | tf_op jit(solution)/shard_map/ppermute | solution.py:607
  28.6 4.6 %collective-permute-start.7 = (f32[144,128]{1,0:T(8,128)S(1)}, f32[144,128]{1,0:T(8,128)S(1)}, u32[]{:S(2)}, u32[]{:S(2)}) collective-permute-start(f32[144,128]{1,0:T(8,128)S(1)} %get-tuple-element.32), channel_id=1, source_target_pairs={{0,8},{8,0},{24,16},{16,24},{18,2},{2,18},{10,26},{26,10},{28,20},... | collective-permute-start | bytes 221192 | tf_op jit(solution)/shard_map/ppermute | solution.py:644
  29.0 5.1 %collective-permute-start.9 = (f32[80,128]{1,0:T(8,128)S(1)}, f32[80,128]{1,0:T(8,128)S(1)}, u32[]{:S(2)}, u32[]{:S(2)}) collective-permute-start(f32[80,128]{1,0:T(8,128)S(1)} %get-tuple-element.31.pack), channel_id=1, source_target_pairs={{0,16},{8,18},{24,2},{16,0},{18,8},{2,24},{10,20},{26,4},{28,12},{... | collective-permute-start | bytes 122888 | tf_op jit(solution)/shard_map/ppermute | solution.py:644
  29.2 4.9 %collective-permute-start.8 = (f32[80,128]{1,0:T(8,128)S(1)}, f32[80,128]{1,0:T(8,128)S(1)}, u32[]{:S(2)}, u32[]{:S(2)}) collective-permute-start(f32[80,128]{1,0:T(8,128)S(1)} %get-tuple-element.31.pack), channel_id=1, source_target_pairs={{0,24},{8,16},{24,0},{16,8},{18,10},{2,26},{10,18},{26,2},{28,4},{... | collective-permute-start | bytes 122888 | tf_op jit(solution)/shard_map/ppermute | solution.py:644
  34.1 1.4 %collective-permute-start.10 = (f32[304,128]{1,0:T(8,128)S(1)}, f32[304,128]{1,0:T(8,128)S(1)}, u32[]{:S(2)}, u32[]{:S(2)}) collective-permute-start(f32[304,128]{1,0:T(8,128)S(1)} %constant_dynamic-update-slice_fusion.2.mine), channel_id=1, source_target_pairs={{0,1},{1,0},{2,3},{3,2},{4,5},{5,4},{6,7},{7,6},{8,9},{9,8},{10,11... | collective-permute-start | bytes 466952 | tf_op jit(solution)/shard_map/ppermute | solution.py:607
  39.2 5.1 %collective-permute-start.12 = (f32[256,128]{1,0:T(8,128)S(1)}, f32[256,128]{1,0:T(8,128)S(1)}, u32[]{:S(2)}, u32[]{:S(2)}) collective-permute-start(f32[256,128]{1,0:T(8,128)S(1)} %bitcast.15), channel_id=1, source_target_pairs={{0,16},{1,9},{8,24},{9,1},{16,0},{17,25},{24,8},{25,17},{2,18},{3,... | collective-permute-start | bytes 393224 | tf_op jit(solution)/shard_map/ppermute | solution.py:623
  41.4 7.1 %collective-permute-start.13 = (f32[256,128]{1,0:T(8,128)S(1)}, f32[256,128]{1,0:T(8,128)S(1)}, u32[]{:S(2)}, u32[]{:S(2)}) collective-permute-start(f32[256,128]{1,0:T(8,128)S(1)} %bitcast.14), channel_id=1, source_target_pairs={{0,24},{1,25},{8,16},{9,17},{16,8},{17,9},{24,0},{25,1},{2,26},{3,... | collective-permute-start | bytes 393224 | tf_op jit(solution)/shard_map/ppermute | solution.py:623
  43.0 6.3 %collective-permute-start.11 = (f32[256,128]{1,0:T(8,128)S(1)}, f32[256,128]{1,0:T(8,128)S(1)}, u32[]{:S(2)}, u32[]{:S(2)}) collective-permute-start(f32[256,128]{1,0:T(8,128)S(1)} %bitcast.13), channel_id=1, source_target_pairs={{0,8},{1,17},{8,0},{9,25},{16,24},{17,1},{24,16},{25,9},{2,10},{3,... | collective-permute-start | bytes 393224 | tf_op jit(solution)/shard_map/ppermute | solution.py:623

commit v4 on v3

--- a/solution.py
+++ b/solution.py
@@ -624,23 +624,36 @@
     return got
 
 
-def pairs_of(plan, k, one):
-    partner = list(range(plan.blocks))
+def partners(plan, k, one):
+    partner = [None] * plan.blocks
     for b in range(plan.blocks - k):
         if b // k % 2 == one:
             partner[b], partner[b + k] = b + k, b
-    alone = [b for b in range(plan.blocks) if partner[b] == b]
-    for a, b in zip(alone[::2], alone[1::2]):
-        partner[a], partner[b] = b, a
-    return [(plan.device(a), plan.device(b)) for a, b in enumerate(partner)]
+    return partner
 
 
 def swap_blocks(plan, a, k, one):
-    return lax.ppermute(a, ("gx", "gy"), pairs_of(plan, k, one))
+    pairs = []
+    for b, partner in enumerate(partners(plan, k, one)):
+        for g in range(plan.gz):
+            to = (b, g ^ 1) if partner is None else (partner, g)
+            pairs.append((plan.device(b) * plan.gz + g, plan.device(to[0]) * plan.gz + to[1]))
+    return lax.ppermute(a, ("gx", "gy", "gz"), pairs)
 
 
 def swap_blocks_apart(plan, a, k):
-    pairs = [(2 * p + one, 2 * q + one) for one in range(2) for p, q in pairs_of(plan, k, one)]
+    pairs = []
+    for one in range(2):
+        partner = partners(plan, k, one)
+        alone = [b for b in range(plan.blocks) if partner[b] is None]
+        low = [b for b in alone if 2 * b < plan.blocks]
+        high = [b for b in alone if 2 * b >= plan.blocks]
+        couples = [(low.pop(0), high.pop())] if len(low) % 2 else []
+        for group in (low, high):
+            couples += zip(group[::2], group[1::2])
+        for x, y in couples:
+            partner[x], partner[y] = y, x
+        pairs += [(2 * plan.device(b) + one, 2 * plan.device(p) + one) for b, p in enumerate(partner)]
     return lax.ppermute(a, ("gx", "gy", "gz"), pairs)
 
 

time: 50.4 us -> 49.7 us (0.986)
  waiting for transfers between devices: 23.5 us -> 21.9 us
  starting transfers between devices: 15.8 us -> 16.6 us
    ppermute x3, starting transfers between devices: 2.97 us -> 4.55 us  [swap_blocks_apart(): return lax.ppermute(a, ('gx', 'gy', 'gz'), pairs)]
    ppermute x3, starting transfers between devices: 0.25 us -> 1.16 us  [beside_in_z(): return lax.ppermute(a, 'gz', [(0, 1), (1, 0)])]
    ppermute x2, starting transfers between devices: 3.67 us -> 2.81 us  [swap_blocks(): return lax.ppermute(a, ('gx', 'gy', 'gz'), pairs)]
    ppermute x6, starting transfers between devices: 8.91 us -> 8.13 us  [exchange(): got[slot] = lax.ppermute(parts[slot], ('gx', 'gz'), pairs)]
    ppermute x2, waiting for transfers between devices: 5.97 us -> 5.23 us  [swap_blocks(): return lax.ppermute(a, ('gx', 'gy', 'gz'), pairs)]
    ppermute x6, waiting for transfers between devices: 12 us -> 11.4 us  [exchange(): got[slot] = lax.ppermute(parts[slot], ('gx', 'gz'), pairs)]
  transfers between devices with their start and end apart: 14 -> 14, of which waited for: 11 -> 8; matrix products, arithmetic and copies ran while one was open for 0% -> 0% of each run, Pallas kernels for 0% -> 0%
where the time goes in v4:
time: 49.7 us; the launch traced here: 49.5 us
  waiting for transfers between devices  21.9 us (44%)
  starting transfers between devices  16.6 us (33%)
  Pallas kernels  10.2 us (21%)
  between operations  0.72 us (1%)
    ppermute x6, waiting for transfers between devices, exchange(): got[slot] = lax.ppermute(parts[slot], ('gx', 'gz'), pairs)  11.4 us
    ppermute x6, starting transfers between devices, exchange(): got[slot] = lax.ppermute(parts[slot], ('gx', 'gz'), pairs)  8.13 us
    ppermute x2, waiting for transfers between devices, swap_blocks(): return lax.ppermute(a, ('gx', 'gy', 'gz'), pairs)  5.23 us
    ppermute x3, starting transfers between devices, swap_blocks_apart(): return lax.ppermute(a, ('gx', 'gy', 'gz'), pairs)  4.55 us
    pallas_call x1, Pallas kernels, on_device(): call(functools.partial(down_kernel, plan), outs + fields, scratch)  4.28 us
    pallas_call x1, Pallas kernels, on_device(): call(functools.partial(up_kernel, plan), [in_vmem(gx, by, 2, px, LANES)],...  3.53 us
    ppermute x2, starting transfers between devices, swap_blocks(): return lax.ppermute(a, ('gx', 'gy', 'gz'), pairs)  2.81 us
    ppermute x3, waiting for transfers between devices, beside_in_z(): return lax.ppermute(a, 'gz', [(0, 1), (1, 0)])  2.77 us
  transfers between devices with their start and end apart: 14, of which 8 were waited for; matrix products, arithmetic and copies ran while one was open for 0% of the time, Pallas kernels for 0%

profile of v4, /device:TPU:0, one launch (start us, length us, event | category | flops | bytes accessed | tf_op | source)
XLA Modules:
  0.0 49.5 jit_solution(2809725572114509267)
XLA Ops:
  0.6 1.3 %shard_map.50 = (f32[256,128]{1,0:T(8,128)S(1)}, f32[256,128]{1,0:T(8,128)S(1)}, f32[256,128]{1,0:T(8,128)S(1)}, f32[256,128]{1,0:T(8,128)S(1)}) custom-call(s32[8,64,128]{2,1,0:T(8,128)} %phase_in.1, f32[8,64,128]{2,1,0:T(8,128)} %density_in.1, f32[1,8,64,128]{3,2,1,0:T(8,128)} %rhs_in.1), custom_call_target="tpu_custom_call" | custom-call | tf_op jit(solution)/shard_map/pallas_call | solution.py:676
  2.0 3.0 %collective-permute-start = (f32[256,128]{1,0:T(8,128)S(1)}, f32[256,128]{1,0:T(8,128)S(1)}, u32[]{:S(2)}, u32[]{:S(2)}) collective-permute-start(f32[256,128]{1,0:T(8,128)S(1)} %get-tuple-element.25), channel_id=1, source_target_pairs={{0,8},{1,17},{8,0},{9,25},{16,24},{17,1},{24,16},{25,9},{2,10},{3,... | collective-permute-start | bytes 393224 | tf_op jit(solution)/shard_map/ppermute | solution.py:623
  5.0 1.5 %collective-permute-start.1 = (f32[256,128]{1,0:T(8,128)S(1)}, f32[256,128]{1,0:T(8,128)S(1)}, u32[]{:S(2)}, u32[]{:S(2)}) collective-permute-start(f32[256,128]{1,0:T(8,128)S(1)} %get-tuple-element.26), channel_id=1, source_target_pairs={{0,16},{1,9},{8,24},{9,1},{16,0},{17,25},{24,8},{25,17},{2,18},{3,... | collective-permute-start | bytes 393224 | tf_op jit(solution)/shard_map/ppermute | solution.py:623
  6.5 0.0 collective-permute-start.2
  6.5 2.2 %collective-permute-done = f32[256,128]{1,0:T(8,128)S(1)} collective-permute-done((f32[256,128]{1,0:T(8,128)S(1)}, f32[256,128]{1,0:T(8,128)S(1)}, u32[]{:S(2)}, u32[]{:S(2)}) %collective-permute-start) | collective-permute-done | bytes 131104 | tf_op jit(solution)/shard_map/ppermute | solution.py:623
  8.7 4.0 %collective-permute-done.1 = f32[256,128]{1,0:T(8,128)S(1)} collective-permute-done((f32[256,128]{1,0:T(8,128)S(1)}, f32[256,128]{1,0:T(8,128)S(1)}, u32[]{:S(2)}, u32[]{:S(2)}) %collective-permute-start.1) | collective-permute-done | bytes 131104 | tf_op jit(solution)/shard_map/ppermute | solution.py:623
  12.7 0.0 collective-permute-done.2
  12.7 0.1 shard_map.51
  12.8 0.1 collective-permute-start.4
  12.9 2.7 %collective-permute-start.5 = (f32[4,13,8,128]{3,2,1,0:T(8,128)S(1)}, f32[4,13,8,128]{3,2,1,0:T(8,128)S(1)}, u32[]{:S(2)}, u32[]{:S(2)}) collective-permute-start(f32[4,13,8,128]{3,2,1,0:T(8,128)S(1)} %get-tuple-element.30), channel_id=1, source_target_pairs={{0,8},{1,9},{8,0},{9,1},{24,16},{25,17},{16,24},{17,25},{18,2},{19... | collective-permute-start | bytes 638984 | tf_op jit(solution)/shard_map/ppermute | solution.py:641
  15.6 0.0 collective-permute-start.3
  15.6 0.0 collective-permute-done.4
  15.7 5.2 %collective-permute-done.5 = f32[4,13,8,128]{3,2,1,0:T(8,128)S(1)} collective-permute-done((f32[4,13,8,128]{3,2,1,0:T(8,128)S(1)}, f32[4,13,8,128]{3,2,1,0:T(8,128)S(1)}, u32[]{:S(2)}, u32[]{:S(2)}) %collective-permute-start.5) | collective-permute-done | bytes 213024 | tf_op jit(solution)/shard_map/ppermute | solution.py:641
  20.9 0.1 collective-permute-start.6
  21.0 0.0 collective-permute-done.3.zc
  21.0 1.7 %collective-permute-done.6.zsides = f32[8,13,8,128]{3,2,1,0:T(8,128)S(1)} collective-permute-done((f32[8,13,8,128]{3,2,1,0:T(8,128)S(1)}, f32[8,13,8,128]{3,2,1,0:T(8,128)S(1)}, u32[]{:S(2)}, u32[]{:S(2)}) %collective-permute-start.6) | collective-permute-done | bytes 426016 | tf_op jit(solution)/shard_map/ppermute | solution.py:607
  22.7 4.3 %shard_map.52 = (f32[80,128]{1,0:T(8,128)S(1)}, f32[144,128]{1,0:T(8,128)S(1)}, f32[30,2,32,128]{3,2,1,0:T(8,128)S(1)}, f32[30,2,32,128]{3,2,1,0:T(8,128)S(1)}, ...) custom-call(f32[4,16,2,8,128]{4,3,2,1,0:T(8,128)S(1)} %get-tuple-ele, ...), custom_call_target="tpu_custom_call" | custom-call | tf_op jit(solution)/shard_map/pallas_call | solution.py:705
  27.0 1.8 %collective-permute-start.7 = (f32[144,128]{1,0:T(8,128)S(1)}, f32[144,128]{1,0:T(8,128)S(1)}, u32[]{:S(2)}, u32[]{:S(2)}) collective-permute-start(f32[144,128]{1,0:T(8,128)S(1)} %get-tuple-element.32), channel_id=1, source_target_pairs={{0,8},{8,0},{24,16},{16,24},{18,2},{2,18},{10,26},{26,10},{28,20},... | collective-permute-start | bytes 221192 | tf_op jit(solution)/shard_map/ppermute | solution.py:657
  28.8 0.4 collective-permute-start.9
  29.2 2.4 %collective-permute-start.8 = (f32[80,128]{1,0:T(8,128)S(1)}, f32[80,128]{1,0:T(8,128)S(1)}, u32[]{:S(2)}, u32[]{:S(2)}) collective-permute-start(f32[80,128]{1,0:T(8,128)S(1)} %get-tuple-element.31.pack), channel_id=1, source_target_pairs={{0,24},{8,16},{24,0},{16,8},{18,10},{2,26},{10,18},{26,2},{28,4},{... | collective-permute-start | bytes 122888 | tf_op jit(solution)/shard_map/ppermute | solution.py:657
  31.6 0.0 collective-permute-done.7
  31.6 2.5 %collective-permute-done.8 = f32[80,128]{1,0:T(8,128)S(1)} collective-permute-done((f32[80,128]{1,0:T(8,128)S(1)}, f32[80,128]{1,0:T(8,128)S(1)}, u32[]{:S(2)}, u32[]{:S(2)}) %collective-permute-start.8) | collective-permute-done | bytes 40992 | tf_op jit(solution)/shard_map/ppermute | solution.py:657
  34.1 0.0 collective-permute-done.9
  34.1 1.1 %collective-permute-start.10 = (f32[304,128]{1,0:T(8,128)S(1)}, f32[304,128]{1,0:T(8,128)S(1)}, u32[]{:S(2)}, u32[]{:S(2)}) collective-permute-start(f32[304,128]{1,0:T(8,128)S(1)} %constant_dynamic-update-slice_fusion.2.mine), channel_id=1, source_target_pairs={{0,1},{1,0},{2,3},{3,2},{4,5},{5,4},{6,7},{7,6},{8,9},{9,8},{10,11... | collective-permute-start | bytes 466952 | tf_op jit(solution)/shard_map/ppermute | solution.py:607
  35.2 1.0 %collective-permute-done.10.theirs = f32[304,128]{1,0:T(8,128)S(1)} collective-permute-done((f32[304,128]{1,0:T(8,128)S(1)}, f32[304,128]{1,0:T(8,128)S(1)}, u32[]{:S(2)}, u32[]{:S(2)}) %collective-permute-start.10) | collective-permute-done | bytes 155680 | tf_op jit(solution)/shard_map/ppermute | solution.py:607
  36.2 3.5 %shard_map.53 = f32[4,16,2,8,128]{4,3,2,1,0:T(8,128)S(1)} custom-call(f32[80,128]{1,0:T(8,128)S(1)} %get-tuple-element.31.pack, f32[304,128]{1,0:T(8,128)S(1)} %constant_dynamic-update-slice_fusion.2.mine, f32[304,128]{1,0:T(8,128)S(1)} %collective-permute-done.10.theirs, f32[30,2,32,128]{3,2,1,0:T(8,128)S(1)} %get-tuple-element.33.refs_0_, ...), custom_call_target="tpu_custom_call" | custom-call | tf_op jit(solution)/shard_map/pallas_call | solution.py:713
  39.8 1.2 %collective-permute-start.12 = (f32[256,128]{1,0:T(8,128)S(1)}, f32[256,128]{1,0:T(8,128)S(1)}, u32[]{:S(2)}, u32[]{:S(2)}) collective-permute-start(f32[256,128]{1,0:T(8,128)S(1)} %bitcast.15), channel_id=1, source_target_pairs={{0,16},{1,9},{8,24},{9,1},{16,0},{17,25},{24,8},{25,17},{2,18},{3,... | collective-permute-start | bytes 393224 | tf_op jit(solution)/shard_map/ppermute | solution.py:623
  41.0 1.6 %collective-permute-start.13 = (f32[256,128]{1,0:T(8,128)S(1)}, f32[256,128]{1,0:T(8,128)S(1)}, u32[]{:S(2)}, u32[]{:S(2)}) collective-permute-start(f32[256,128]{1,0:T(8,128)S(1)} %bitcast.14), channel_id=1, source_target_pairs={{0,24},{1,25},{8,16},{9,17},{16,8},{17,9},{24,0},{25,1},{2,26},{3,... | collective-permute-start | bytes 393224 | tf_op jit(solution)/shard_map/ppermute | solution.py:623
  42.6 0.8 %collective-permute-start.11 = (f32[256,128]{1,0:T(8,128)S(1)}, f32[256,128]{1,0:T(8,128)S(1)}, u32[]{:S(2)}, u32[]{:S(2)}) collective-permute-start(f32[256,128]{1,0:T(8,128)S(1)} %bitcast.13), channel_id=1, source_target_pairs={{0,8},{1,17},{8,0},{9,25},{16,24},{17,1},{24,16},{25,9},{2,10},{3,... | collective-permute-start | bytes 393224 | tf_op jit(solution)/shard_map/ppermute | solution.py:623
  43.4 4.4 %collective-permute-done.12.refs_2_ = f32[256,128]{1,0:T(8,128)S(1)} collective-permute-done((f32[256,128]{1,0:T(8,128)S(1)}, f32[256,128]{1,0:T(8,128)S(1)}, u32[]{:S(2)}, u32[]{:S(2)}) %collective-permute-start.12) | collective-permute-done | bytes 131104 | tf_op jit(solution)/shard_map/ppermute | solution.py:623
  47.8 0.0 collective-permute-done.13.refs_3_
  47.8 0.8 %collective-permute-done.11.refs_1_ = f32[256,128]{1,0:T(8,128)S(1)} collective-permute-done((f32[256,128]{1,0:T(8,128)S(1)}, f32[256,128]{1,0:T(8,128)S(1)}, u32[]{:S(2)}, u32[]{:S(2)}) %collective-permute-start.11) | collective-permute-done | bytes 131104 | tf_op jit(solution)/shard_map/ppermute | solution.py:623
  48.6 1.0 %shard_map.54 = (f32[1,8,64,128]{3,2,1,0:T(8,128)}, f32[1,8,64,128]{3,2,1,0:T(8,128)}) custom-call(f32[256,128]{1,0:T(8,128)S(1)} %bitcast.8, f32[256,128]{1,0:T(8,128)S(1)} %collective-permute-done.11.refs_1_, f32[256,128]{1,0:T(8,128)S(1)} %collective-permute-done.12.refs_2_, f32[256,128]{1,0:T(8,128)S(1)} %collective-permute-done.13.refs_3_), custom_call_target="tpu_custom_call" | custom-call | tf_op jit(solution)/shard_map/pallas_call | solution.py:718
  (6 shorter events, 0.1 us)
Async XLA Ops:
  2.0 6.8 %collective-permute-start = (f32[256,128]{1,0:T(8,128)S(1)}, f32[256,128]{1,0:T(8,128)S(1)}, u32[]{:S(2)}, u32[]{:S(2)}) collective-permute-start(f32[256,128]{1,0:T(8,128)S(1)} %get-tuple-element.25), channel_id=1, source_target_pairs={{0,8},{1,17},{8,0},{9,25},{16,24},{17,1},{24,16},{25,9},{2,10},{3,... | collective-permute-start | bytes 393224 | tf_op jit(solution)/shard_map/ppermute | solution.py:623
  5.0 7.8 %collective-permute-start.1 = (f32[256,128]{1,0:T(8,128)S(1)}, f32[256,128]{1,0:T(8,128)S(1)}, u32[]{:S(2)}, u32[]{:S(2)}) collective-permute-start(f32[256,128]{1,0:T(8,128)S(1)} %get-tuple-element.26), channel_id=1, source_target_pairs={{0,16},{1,9},{8,24},{9,1},{16,0},{17,25},{24,8},{25,17},{2,18},{3,... | collective-permute-start | bytes 393224 | tf_op jit(solution)/shard_map/ppermute | solution.py:623
  6.5 6.3 %collective-permute-start.2 = (f32[256,128]{1,0:T(8,128)S(1)}, f32[256,128]{1,0:T(8,128)S(1)}, u32[]{:S(2)}, u32[]{:S(2)}) collective-permute-start(f32[256,128]{1,0:T(8,128)S(1)} %get-tuple-element.27), channel_id=1, source_target_pairs={{0,24},{1,25},{8,16},{9,17},{16,8},{17,9},{24,0},{25,1},{2,26},{3,... | collective-permute-start | bytes 393224 | tf_op jit(solution)/shard_map/ppermute | solution.py:623
  12.8 2.8 %collective-permute-start.4 = (f32[4,13,8,128]{3,2,1,0:T(8,128)S(1)}, f32[4,13,8,128]{3,2,1,0:T(8,128)S(1)}, u32[]{:S(2)}, u32[]{:S(2)}) collective-permute-start(f32[4,13,8,128]{3,2,1,0:T(8,128)S(1)} %get-tuple-element.29), channel_id=1, source_target_pairs={{0,1},{1,0},{8,24},{9,25},{24,8},{25,9},{16,18},{17,19},{18,16},{1... | collective-permute-start | bytes 638984 | tf_op jit(solution)/shard_map/ppermute | solution.py:641
  12.9 8.0 %collective-permute-start.5 = (f32[4,13,8,128]{3,2,1,0:T(8,128)S(1)}, f32[4,13,8,128]{3,2,1,0:T(8,128)S(1)}, u32[]{:S(2)}, u32[]{:S(2)}) collective-permute-start(f32[4,13,8,128]{3,2,1,0:T(8,128)S(1)} %get-tuple-element.30), channel_id=1, source_target_pairs={{0,8},{1,9},{8,0},{9,1},{24,16},{25,17},{16,24},{17,25},{18,2},{19... | collective-permute-start | bytes 638984 | tf_op jit(solution)/shard_map/ppermute | solution.py:641
  15.6 5.4 %collective-permute-start.3 = (f32[4,16,2,8,128]{4,3,2,1,0:T(8,128)S(1)}, f32[4,16,2,8,128]{4,3,2,1,0:T(8,128)S(1)}, u32[]{:S(2)}, u32[]{:S(2)}) collective-permute-start(f32[4,16,2,8,128]{4,3,2,1,0:T(8,128)S(1)} %get-tuple-element.28.c), channel_id=1, source_target_pairs={{0,1},{1,0},{2,3},{3,2},{4,5},{5,4},{6,7},{7,6},{8,9},{9,8},{10,11... | collective-permute-start | bytes 1572872 | tf_op jit(solution)/shard_map/ppermute | solution.py:607
  20.9 1.8 %collective-permute-start.6 = (f32[8,13,8,128]{3,2,1,0:T(8,128)S(1)}, f32[8,13,8,128]{3,2,1,0:T(8,128)S(1)}, u32[]{:S(2)}, u32[]{:S(2)}) collective-permute-start(f32[8,13,8,128]{3,2,1,0:T(8,128)S(1)} %constant_dynamic-update-slice_fusion.sides), channel_id=1, source_target_pairs={{0,1},{1,0},{2,3},{3,2},{4,5},{5,4},{6,7},{7,6},{8,9},{9,8},{10,11... | collective-permute-start | bytes 1277960 | tf_op jit(solution)/shard_map/ppermute | solution.py:607
  27.0 4.6 %collective-permute-start.7 = (f32[144,128]{1,0:T(8,128)S(1)}, f32[144,128]{1,0:T(8,128)S(1)}, u32[]{:S(2)}, u32[]{:S(2)}) collective-permute-start(f32[144,128]{1,0:T(8,128)S(1)} %get-tuple-element.32), channel_id=1, source_target_pairs={{0,8},{8,0},{24,16},{16,24},{18,2},{2,18},{10,26},{26,10},{28,20},... | collective-permute-start | bytes 221192 | tf_op jit(solution)/shard_map/ppermute | solution.py:657
  28.8 5.3 %collective-permute-start.9 = (f32[80,128]{1,0:T(8,128)S(1)}, f32[80,128]{1,0:T(8,128)S(1)}, u32[]{:S(2)}, u32[]{:S(2)}) collective-permute-start(f32[80,128]{1,0:T(8,128)S(1)} %get-tuple-element.31.pack), channel_id=1, source_target_pairs={{0,16},{8,18},{24,2},{16,0},{18,8},{2,24},{10,20},{26,4},{28,12},{... | collective-permute-start | bytes 122888 | tf_op jit(solution)/shard_map/ppermute | solution.py:657
  29.2 4.9 %collective-permute-start.8 = (f32[80,128]{1,0:T(8,128)S(1)}, f32[80,128]{1,0:T(8,128)S(1)}, u32[]{:S(2)}, u32[]{:S(2)}) collective-permute-start(f32[80,128]{1,0:T(8,128)S(1)} %get-tuple-element.31.pack), channel_id=1, source_target_pairs={{0,24},{8,16},{24,0},{16,8},{18,10},{2,26},{10,18},{26,2},{28,4},{... | collective-permute-start | bytes 122888 | tf_op jit(solution)/shard_map/ppermute | solution.py:657
  34.1 2.1 %collective-permute-start.10 = (f32[304,128]{1,0:T(8,128)S(1)}, f32[304,128]{1,0:T(8,128)S(1)}, u32[]{:S(2)}, u32[]{:S(2)}) collective-permute-start(f32[304,128]{1,0:T(8,128)S(1)} %constant_dynamic-update-slice_fusion.2.mine), channel_id=1, source_target_pairs={{0,1},{1,0},{2,3},{3,2},{4,5},{5,4},{6,7},{7,6},{8,9},{9,8},{10,11... | collective-permute-start | bytes 466952 | tf_op jit(solution)/shard_map/ppermute | solution.py:607
  39.8 8.0 %collective-permute-start.12 = (f32[256,128]{1,0:T(8,128)S(1)}, f32[256,128]{1,0:T(8,128)S(1)}, u32[]{:S(2)}, u32[]{:S(2)}) collective-permute-start(f32[256,128]{1,0:T(8,128)S(1)} %bitcast.15), channel_id=1, source_target_pairs={{0,16},{1,9},{8,24},{9,1},{16,0},{17,25},{24,8},{25,17},{2,18},{3,... | collective-permute-start | bytes 393224 | tf_op jit(solution)/shard_map/ppermute | solution.py:623
  41.0 6.7 %collective-permute-start.13 = (f32[256,128]{1,0:T(8,128)S(1)}, f32[256,128]{1,0:T(8,128)S(1)}, u32[]{:S(2)}, u32[]{:S(2)}) collective-permute-start(f32[256,128]{1,0:T(8,128)S(1)} %bitcast.14), channel_id=1, source_target_pairs={{0,24},{1,25},{8,16},{9,17},{16,8},{17,9},{24,0},{25,1},{2,26},{3,... | collective-permute-start | bytes 393224 | tf_op jit(solution)/shard_map/ppermute | solution.py:623
  42.6 6.0 %collective-permute-start.11 = (f32[256,128]{1,0:T(8,128)S(1)}, f32[256,128]{1,0:T(8,128)S(1)}, u32[]{:S(2)}, u32[]{:S(2)}) collective-permute-start(f32[256,128]{1,0:T(8,128)S(1)} %bitcast.13), channel_id=1, source_target_pairs={{0,8},{1,17},{8,0},{9,25},{16,24},{17,1},{24,16},{25,9},{2,10},{3,... | collective-permute-start | bytes 393224 | tf_op jit(solution)/shard_map/ppermute | solution.py:623

commit v5 on v4

--- a/solution.py
+++ b/solution.py
@@ -267,58 +267,143 @@
     return total
 
 
-def down_kernel(plan, c, zc, sides, zsides, *refs):
+class Finest:
+    COUNT = 16
+
+    @staticmethod
+    def shapes(plan):
+        level0 = in_vmem(plan.rows, 2, plan.nx, LANES)
+        pairs = in_vmem(plan.by // 2 + 8, 2, plan.nx, LANES)
+        level1 = in_vmem(plan.by // 2 + 8, 2, plan.nx // 2, LANES)
+        return [level0] * 10 + [pairs] + [level1] * 5
+
+    def __init__(self, plan, refs):
+        self.plan = plan
+        fields = [Wide(r) for r in refs]
+        self.kx, self.ky, self.kz, self.d, self.w, self.f, self.ub = fields[:7]
+        self.h, self.ua, self.face, self.r = fields[7:11]
+        self.kx1, self.ky1, self.kz1, self.d1, self.f1 = fields[11:]
+        self.level = Level(1, 1, self.kx, self.ky, self.kz, self.d, self.w, self.f)
+        nx = plan.nx
+        shape = (nx, WIDE)
+        self.half_x = nx // 2
+        self.base = plan.block_here() * plan.by - HALO
+        self.y_count, z_count = plan.by * plan.blocks, plan.nz * plan.gz
+        x = lax.broadcasted_iota(jnp.int32, shape, 0)
+        lane = lax.broadcasted_iota(jnp.int32, shape, 1)
+        core = lax.axis_index("gz")
+        if plan.paired:
+            z = lax.rem(core * LANES + lane, WIDE)
+        else:
+            z = core * LANES + jnp.where(lane < LANES + LANES // 2, lane, lane - WIDE)
+        self.x_top, self.x_bottom = x == nx - 1, x == 0
+        self.z_top, self.z_bottom = z == z_count - 1, z == 0
+        self.z_shut = (z < 0) | (z >= z_count - 1)
+        self.z_out = (z < 0) | (z >= z_count)
+
+    def put_h(self, to, s, xs, tile):
+        y = self.base + to
+        tile = jnp.where((y >= 0) & (y < self.y_count), tile, 0.5)
+        if not self.plan.paired:
+            tile = jnp.where(self.z_out[: self.plan.px, s * LANES : (s + 1) * LANES], 0.5, tile)
+        self.h.ref[to, s, xs, :] = tile
+
+    def tiles(self, other):
+        px = self.plan.px
+        return [(k, pl.ds(pl.multiple_of((other ^ k) * px, px), px)) for k in range(self.plan.gx)]
+
+    def is_open(self, r):
+        y = self.base + r
+        return (y >= 0) & (y < self.y_count - 1)
+
+    def start(self, r):
+        first = inverse(self.h[r] + self.h[r + 1])
+        self.face[r + 1] = first
+        self.ky[r + 1] = jnp.where(self.is_open(r), first, 0.0)
+
+    def faces(self, j):
+        yd = self.face[2 * j - 1]
+        for r in (2 * j - 1, 2 * j):
+            h = self.h[r]
+            alone = 0.5 * inverse(h)
+            xu = inverse(h + jnp.where(self.x_top, h, x_up(h)))
+            xd = jnp.where(self.x_bottom, alone, x_down(xu))
+            yu = inverse(h + self.h[r + 1])
+            zu = inverse(h + jnp.where(self.z_top, h, z_up(h, 1)))
+            zd = jnp.where(self.z_bottom, alone, z_down(zu, 1))
+            d = xu + xd + yu + yd + zu + zd
+            w = DAMPING * inverse(d)
+            self.kx[r] = jnp.where(self.x_top, 0.0, xu)
+            self.ky[r + 1] = jnp.where(self.is_open(r), yu, 0.0)
+            self.kz[r] = jnp.where(self.z_shut, 0.0, zu)
+            self.d[r], self.w[r] = d, w
+            self.ua[r] = w * self.f[r]
+            yd = yu
+        self.face[2 * j + 1] = yd
+
+    def coarsen(self, j):
+        coarse = coarse_coefficients(self.level, 2 * j - 1, self.half_x)
+        self.kx1[j], self.ky1[j + 1], self.kz1[j], self.d1[j] = coarse
+
+    def sweep(self, j):
+        self.ub[2 * j] = self.level.swept(self.ua, 2 * j)
+        self.ub[2 * j + 1] = self.level.swept(self.ua, 2 * j + 1)
+
+    def residual(self, j):
+        self.r[j] = self.level.residual(self.ub, 2 * j - 1) + self.level.residual(self.ub, 2 * j)
+
+    def restrict(self, j):
+        self.f1[j] = coarse_sum(self.r, j, self.half_x, 1)
+
+
+def inner_pairs(plan):
+    return (HALO + 3) // 2, (HALO + plan.by - 2) // 2
+
+
+def inner_kernel(plan, c, zc, *refs):
+    fine = Finest(plan, refs)
+
+    def take(r):
+        for k, xs in fine.tiles(lax.axis_index("gx")):
+            for s, ref in enumerate((c, zc)):
+                fine.put_h(r + HALO, s, xs, ref[k, r, 0])
+                fine.f.ref[r + HALO, s, xs, :] = ref[k, r, 1]
+
+    each(0, plan.by - 1, 4, take)
+    first, last = inner_pairs(plan)
+    fine.start(2 * first - 2)
+    wave(
+        (fine.restrict, first + 1, last - 1, 4),
+        (fine.residual, first + 1, last - 1, 3),
+        (fine.sweep, first, last - 1, 2),
+        (fine.coarsen, first, last, 1),
+        (fine.faces, first, last, 0),
+    )
+
+
+def down_kernel(plan, sides, zsides, *refs):
+    count = Finest.COUNT
     near_count = 1 if plan.paired else 2
-    pack, nears, refs = refs[0], refs[1 : 1 + near_count], refs[1 + near_count :]
-    kx0, ky0, kz0, d0, w0, f0, ub, kx1, ky1, kz1, w1, f1, u1 = [Wide(r) for r in refs[:13]]
-    h0, ua, face, r0, uc, r1, d1 = [Wide(r) for r in refs[13:20]]
-    stage, near_stage = refs[20:22]
-    nx, by, rows, gx, px = plan.nx, plan.by, plan.rows, plan.gx, plan.px
-    shape = (nx, WIDE)
-    block, here = plan.block_here(), lax.axis_index("gx")
-    base = block * by - HALO
-    y_count, z_count = plan.by * plan.blocks, plan.nz * plan.gz
-
-    x = lax.broadcasted_iota(jnp.int32, shape, 0)
-    lane = lax.broadcasted_iota(jnp.int32, shape, 1)
-    core = lax.axis_index("gz")
-    if plan.paired:
-        z = lax.rem(core * LANES + lane, WIDE)
-    else:
-        z = core * LANES + jnp.where(lane < LANES + LANES // 2, lane, lane - WIDE)
-    x_top, x_bottom = x == nx - 1, x == 0
-    z_top, z_bottom = z == z_count - 1, z == 0
-    z_shut = (z < 0) | (z >= z_count - 1)
-    z_out = (z < 0) | (z >= z_count)
-
-    def put_h(to, s, xs, tile):
-        y = base + to
-        tile = jnp.where((y >= 0) & (y < y_count), tile, 0.5)
-        if not plan.paired:
-            tile = jnp.where(z_out[:px, s * LANES : (s + 1) * LANES], 0.5, tile)
-        h0.ref[to, s, xs, :] = tile
-
-    def tiles(other):
-        return [(k, pl.ds(pl.multiple_of((other ^ k) * px, px), px)) for k in range(gx)]
-
-    def take(r):
-        for k, xs in tiles(here):
-            for s, ref in enumerate((c, zc)):
-                put_h(r + HALO, s, xs, ref[k, r, 0])
-                f0.ref[r + HALO, s, xs, :] = ref[k, r, 1]
+    refs = refs[count:]
+    fine = Finest(plan, refs[:count])
+    kx1, ky1, kz1, d1, f1 = fine.kx1, fine.ky1, fine.kz1, fine.d1, fine.f1
+    pack, nears, refs = refs[count], refs[count + 1 : count + 1 + near_count], refs[count + 1 + near_count :]
+    w1, u1, uc, r1 = [Wide(r) for r in refs[:4]]
+    stage, near_stage = refs[4:6]
+    nx, by, gx = plan.nx, plan.by, plan.gx
+    block, core = plan.block_here(), lax.axis_index("gz")
 
     def take_side(at, other, to, count, field):
         def one(r):
-            for k, xs in tiles(other):
+            for k, xs in fine.tiles(other):
                 for s, ref in enumerate((sides, zsides)):
                     if field == 0:
-                        put_h(r + to, s, xs, ref[at + k, r])
+                        fine.put_h(r + to, s, xs, ref[at + k, r])
                     else:
-                        f0.ref[r + to, s, xs, :] = ref[at + k, HALO + r]
+                        fine.f.ref[r + to, s, xs, :] = ref[at + k, HALO + r]
 
         each(0, count - 1, 4, one)
 
-    each(0, by - 1, 4, take)
     up_first = plan.is_up(block, 1, 0)
     below, above = jnp.where(up_first, 0, gx), jnp.where(up_first, gx, 0)
     gx_below, gx_above = plan.gx_of(block - 1), plan.gx_of(block + 1)
@@ -329,66 +414,33 @@
 
     @pl.when(block == 0)
     def _():
-        h0[HALO - 1] = h0[HALO]
+        fine.h[HALO - 1] = fine.h[HALO]
 
     @pl.when(block == plan.blocks - 1)
     def _():
-        h0[HALO + by] = h0[HALO + by - 1]
-
-    def is_open(r):
-        y = base + r
-        return (y >= 0) & (y < y_count - 1)
-
-    first_face = inverse(h0[0] + h0[1])
-    face[1] = first_face
-    ky0[1] = jnp.where(is_open(0), first_face, 0.0)
-
-    def faces(j):
-        yd = face[2 * j - 1]
-        for r in (2 * j - 1, 2 * j):
-            h = h0[r]
-            alone = 0.5 * inverse(h)
-            xu = inverse(h + jnp.where(x_top, h, x_up(h)))
-            xd = jnp.where(x_bottom, alone, x_down(xu))
-            yu = inverse(h + h0[r + 1])
-            zu = inverse(h + jnp.where(z_top, h, z_up(h, 1)))
-            zd = jnp.where(z_bottom, alone, z_down(zu, 1))
-            d = xu + xd + yu + yd + zu + zd
-            w = DAMPING * inverse(d)
-            kx0[r] = jnp.where(x_top, 0.0, xu)
-            ky0[r + 1] = jnp.where(is_open(r), yu, 0.0)
-            kz0[r] = jnp.where(z_shut, 0.0, zu)
-            d0[r], w0[r] = d, w
-            ua[r] = w * f0[r]
-            yd = yu
-        face[2 * j + 1] = yd
-
-    fine = Level(1, 1, kx0, ky0, kz0, d0, w0, f0)
+        fine.h[HALO + by] = fine.h[HALO + by - 1]
+
+    fine.start(0)
+    first, last = inner_pairs(plan)
+    end = by // 2 + 6
+    late = -last
+    wave(
+        (fine.restrict, 2, first, 4),
+        (fine.restrict, last, end - 1, late + 4),
+        (fine.residual, 2, first, 3),
+        (fine.residual, last, end - 1, late + 3),
+        (fine.sweep, 1, first - 1, 2),
+        (fine.sweep, last, end - 1, late + 2),
+        (fine.coarsen, 1, first - 1, 1),
+        (fine.coarsen, last + 1, end, late + 1),
+        (fine.faces, 1, first - 1, 0),
+        (fine.faces, last + 1, end, late),
+    )
+    ky1[1] = coarse_sum(fine.ky, 1, nx // 2, 1)
 
     own = by // 2
     half_x = nx // 2
     middle = Level(1, 2, kx1, ky1, kz1, d1, w1, f1, 8)
-    def coarsen(j):
-        kx1[j], ky1[j + 1], kz1[j], d1[j] = coarse_coefficients(fine, 2 * j - 1, half_x)
-
-    def restrict(j):
-        f1[j] = coarse_sum(r0, j, half_x, 1)
-
-    def sweep(j):
-        ub[2 * j] = fine.swept(ua, 2 * j)
-        ub[2 * j + 1] = fine.swept(ua, 2 * j + 1)
-
-    def residual(j):
-        r0[j] = fine.residual(ub, 2 * j - 1) + fine.residual(ub, 2 * j)
-
-    wave(
-        (restrict, 2, own + 5, 4),
-        (residual, 2, own + 5, 3),
-        (sweep, 1, own + 5, 2),
-        (coarsen, 1, own + 6, 1),
-        (faces, 1, own + 6, 0),
-    )
-    ky1[1] = coarse_sum(ky0, 1, half_x, 1)
     middle.weigh(1, own + 6)
     middle.first(uc, 2, own + 5)
     middle.sweep(uc, u1, 3, own + 4)
@@ -587,7 +639,9 @@
     return pltpu.VMEM(shape, F32)
 
 
-def call(kernel, out_shape, scratch=(), **more):
+def call(kernel, out_shape, scratch=(), work=0, **more):
+    if work:
+        more["cost_estimate"] = pl.CostEstimate(flops=0, bytes_accessed=work, transcendentals=0)
     return pl.pallas_call(
         kernel,
         out_shape=out_shape,
@@ -698,13 +752,20 @@
     def level1(n):
         return in_vmem(n, 2, nx // 2, LANES)
 
-    outs = [in_vmem(size, LANES)] + [in_vmem(side, LANES)] * (1 if plan.paired else 2)
-    fields = [level0(rows)] * 7 + [level1(own + 8)] * 6
-    scratch = [level0(rows)] * 3 + [level0(own + 8), level1(own + 8), level1(own2), level1(own + 8)]
-    scratch += [in_vmem(2, 2, size, LANES), in_vmem(1, 2, 4 * (nx // 2), LANES)]
-    down = call(functools.partial(down_kernel, plan), outs + fields, scratch)(*pinned(c, zc, sides, zsides))
-    pack, nears, fields = down[0], down[1 : len(outs)], down[len(outs) :]
-
+    inner = call(functools.partial(inner_kernel, plan), Finest.shapes(plan), work=9_000_000)(*pinned(c, zc))
+    near_count = 1 if plan.paired else 2
+    outs = Finest.shapes(plan) + [in_vmem(size, LANES)] + [in_vmem(side, LANES)] * near_count + [level1(own + 8)] * 2
+    scratch = [level1(own + 8), level1(own2), in_vmem(2, 2, size, LANES), in_vmem(1, 2, 4 * (nx // 2), LANES)]
+    down = call(
+        functools.partial(down_kernel, plan),
+        outs,
+        scratch,
+        input_output_aliases={2 + k: k for k in range(Finest.COUNT)},
+    )(*pinned(sides, zsides, *inner))
+    fine, rest = down[: Finest.COUNT], down[Finest.COUNT :]
+    pack, nears, (w1, u1) = rest[0], rest[1 : 1 + near_count], rest[1 + near_count :]
+    kx1, ky1, kz1, _, f1 = fine[11:]
+    fields = list(fine[:7]) + [kx1, ky1, kz1, w1, f1, u1]
     mine, theirs = far_blocks(plan, pack, nears)
     rows2 = (2 * FAR + 1) * own2
     scratch = [in_vmem(2 * FAR + 1, size, LANES)]

time: 49.7 us -> 48.9 us (0.984)
  waiting for transfers between devices: 21.9 us -> 20.1 us
  Pallas kernels: 10.2 us -> 10.8 us
    ppermute x3, waiting for transfers between devices: 2.77 us -> 1.02 us  [beside_in_z(): return lax.ppermute(a, 'gz', [(0, 1), (1, 0)])]
    pallas_call x1 -> x2, Pallas kernels: 4.28 us -> 4.93 us  [the longest x1 3.14 us: on_device(): call(functools.partial(down_kernel, plan), outs, scratch, input_output_al...]
  transfers between devices with their start and end apart: 14 -> 14, of which waited for: 8 -> 7; matrix products, arithmetic and copies ran while one was open for 0% -> 0% of each run, Pallas kernels for 0% -> 4%
where the time goes in v5:
time: 48.9 us; the launch traced here: 48.7 us
  waiting for transfers between devices  20.1 us (41%)
  starting transfers between devices  17 us (35%)
  Pallas kernels  10.8 us (22%)
  between operations  0.74 us (2%)
    ppermute x6, waiting for transfers between devices, exchange(): got[slot] = lax.ppermute(parts[slot], ('gx', 'gz'), pairs)  11.4 us
    ppermute x6, starting transfers between devices, exchange(): got[slot] = lax.ppermute(parts[slot], ('gx', 'gz'), pairs)  8.1 us
    ppermute x2, waiting for transfers between devices, swap_blocks(): return lax.ppermute(a, ('gx', 'gy', 'gz'), pairs)  5.23 us
    ppermute x3, starting transfers between devices, swap_blocks_apart(): return lax.ppermute(a, ('gx', 'gy', 'gz'), pairs)  4.55 us
    pallas_call x1, Pallas kernels, on_device(): call(functools.partial(up_kernel, plan), [in_vmem(gx, by, 2, px, LANES)],...  3.54 us
    pallas_call x1, Pallas kernels, on_device(): call(functools.partial(down_kernel, plan), outs, scratch, input_output_al...  3.14 us
    ppermute x2, starting transfers between devices, swap_blocks(): return lax.ppermute(a, ('gx', 'gy', 'gz'), pairs)  2.81 us
    ppermute x3, waiting for transfers between devices, swap_blocks_apart(): return lax.ppermute(a, ('gx', 'gy', 'gz'), pairs)  2.51 us
  transfers between devices with their start and end apart: 14, of which 7 were waited for; matrix products, arithmetic and copies ran while one was open for 0% of the time, Pallas kernels for 4%

profile of v5, /device:TPU:0, one launch (start us, length us, event | category | flops | bytes accessed | tf_op | source)
XLA Modules:
  0.0 48.7 jit_solution(514553882504640561)
XLA Ops:
  0.6 1.3 %shard_map.50 = (f32[256,128]{1,0:T(8,128)S(1)}, f32[256,128]{1,0:T(8,128)S(1)}, f32[256,128]{1,0:T(8,128)S(1)}, f32[256,128]{1,0:T(8,128)S(1)}) custom-call(s32[8,64,128]{2,1,0:T(8,128)} %phase_in.1, f32[8,64,128]{2,1,0:T(8,128)} %density_in.1, f32[1,8,64,128]{3,2,1,0:T(8,128)} %rhs_in.1), custom_call_target="tpu_custom_call" | custom-call | tf_op jit(solution)/shard_map/pallas_call | solution.py:730
  2.0 3.0 %collective-permute-start = (f32[256,128]{1,0:T(8,128)S(1)}, f32[256,128]{1,0:T(8,128)S(1)}, u32[]{:S(2)}, u32[]{:S(2)}) collective-permute-start(f32[256,128]{1,0:T(8,128)S(1)} %get-tuple-element.41), channel_id=1, source_target_pairs={{0,8},{1,17},{8,0},{9,25},{16,24},{17,1},{24,16},{25,9},{2,10},{3,... | collective-permute-start | bytes 393224 | tf_op jit(solution)/shard_map/ppermute | solution.py:677
  5.0 1.5 %collective-permute-start.1 = (f32[256,128]{1,0:T(8,128)S(1)}, f32[256,128]{1,0:T(8,128)S(1)}, u32[]{:S(2)}, u32[]{:S(2)}) collective-permute-start(f32[256,128]{1,0:T(8,128)S(1)} %get-tuple-element.42), channel_id=1, source_target_pairs={{0,16},{1,9},{8,24},{9,1},{16,0},{17,25},{24,8},{25,17},{2,18},{3,... | collective-permute-start | bytes 393224 | tf_op jit(solution)/shard_map/ppermute | solution.py:677
  6.5 0.0 collective-permute-start.2
  6.5 2.2 %collective-permute-done = f32[256,128]{1,0:T(8,128)S(1)} collective-permute-done((f32[256,128]{1,0:T(8,128)S(1)}, f32[256,128]{1,0:T(8,128)S(1)}, u32[]{:S(2)}, u32[]{:S(2)}) %collective-permute-start) | collective-permute-done | bytes 131104 | tf_op jit(solution)/shard_map/ppermute | solution.py:677
  8.7 4.0 %collective-permute-done.1 = f32[256,128]{1,0:T(8,128)S(1)} collective-permute-done((f32[256,128]{1,0:T(8,128)S(1)}, f32[256,128]{1,0:T(8,128)S(1)}, u32[]{:S(2)}, u32[]{:S(2)}) %collective-permute-start.1) | collective-permute-done | bytes 131104 | tf_op jit(solution)/shard_map/ppermute | solution.py:677
  12.7 0.0 collective-permute-done.2
  12.7 0.1 shard_map.51
  12.8 0.1 collective-permute-start.3
  12.9 2.7 %collective-permute-start.4 = (f32[4,13,8,128]{3,2,1,0:T(8,128)S(1)}, f32[4,13,8,128]{3,2,1,0:T(8,128)S(1)}, u32[]{:S(2)}, u32[]{:S(2)}) collective-permute-start(f32[4,13,8,128]{3,2,1,0:T(8,128)S(1)} %get-tuple-element.45), channel_id=1, source_target_pairs={{0,8},{1,9},{8,0},{9,1},{24,16},{25,17},{16,24},{17,25},{18,2},{19... | collective-permute-start | bytes 638984 | tf_op jit(solution)/shard_map/ppermute | solution.py:695
  15.6 0.0 collective-permute-start.6
  15.6 0.0 collective-permute-done.3
  15.7 5.2 %collective-permute-done.4 = f32[4,13,8,128]{3,2,1,0:T(8,128)S(1)} collective-permute-done((f32[4,13,8,128]{3,2,1,0:T(8,128)S(1)}, f32[4,13,8,128]{3,2,1,0:T(8,128)S(1)}, u32[]{:S(2)}, u32[]{:S(2)}) %collective-permute-start.4) | collective-permute-done | bytes 213024 | tf_op jit(solution)/shard_map/ppermute | solution.py:695
  20.9 0.1 collective-permute-start.5
  21.0 0.0 collective-permute-done.6.zc
  21.0 1.8 %shard_map.52 = (f32[30,2,32,128]{3,2,1,0:T(8,128)S(1)}, f32[30,2,32,128]{3,2,1,0:T(8,128)S(1)}, f32[30,2,32,128]{3,2,1,0:T(8,128)S(1)}, f32[30,2,32,128]{3,2,1,...) custom-call(f32[4,16,2,8,128]{4,3,2,1,0:T(8,128)S(1)} %get-tuple-ele, ...), custom_call_target="tpu_custom_call" | custom-call | bytes 9000000 | tf_op jit(solution)/shard_map/pallas_call | solution.py:755
  22.8 0.0 collective-permute-done.5.zsides
  22.8 3.1 %shard_map.53 = (f32[30,2,32,128]{3,2,1,0:T(8,128)S(1)}, f32[30,2,32,128]{3,2,1,0:T(8,128)S(1)}, f32[30,2,32,128]{3,2,1,0:T(8,128)S(1)}, f32[30,2,32,128]{3,2,1,...) custom-call(f32[8,13,8,128]{3,2,1,0:T(8,128)S(1)} %constant_dynamic-, ...), custom_call_target="tpu_custom_call", output_to_operand_aliasing={{0}: (2, {}), {1}: (3, {}), {2}: (4, {}), {3}: (5, {}), {4}... | custom-call | tf_op jit(solution)/shard_map/pallas_call | solution.py:759
  26.0 1.8 %collective-permute-start.7 = (f32[144,128]{1,0:T(8,128)S(1)}, f32[144,128]{1,0:T(8,128)S(1)}, u32[]{:S(2)}, u32[]{:S(2)}) collective-permute-start(f32[144,128]{1,0:T(8,128)S(1)} %get-tuple-element.64), channel_id=1, source_target_pairs={{0,8},{8,0},{24,16},{16,24},{18,2},{2,18},{10,26},{26,10},{28,20},... | collective-permute-start | bytes 221192 | tf_op jit(solution)/shard_map/ppermute | solution.py:711
  27.8 0.4 collective-permute-start.9
  28.1 2.4 %collective-permute-start.8 = (f32[80,128]{1,0:T(8,128)S(1)}, f32[80,128]{1,0:T(8,128)S(1)}, u32[]{:S(2)}, u32[]{:S(2)}) collective-permute-start(f32[80,128]{1,0:T(8,128)S(1)} %get-tuple-element.63.pack), channel_id=1, source_target_pairs={{0,24},{8,16},{24,0},{16,8},{18,10},{2,26},{10,18},{26,2},{28,4},{... | collective-permute-start | bytes 122888 | tf_op jit(solution)/shard_map/ppermute | solution.py:711
  30.5 0.0 collective-permute-done.7
  30.5 2.5 %collective-permute-done.8 = f32[80,128]{1,0:T(8,128)S(1)} collective-permute-done((f32[80,128]{1,0:T(8,128)S(1)}, f32[80,128]{1,0:T(8,128)S(1)}, u32[]{:S(2)}, u32[]{:S(2)}) %collective-permute-start.8) | collective-permute-done | bytes 40992 | tf_op jit(solution)/shard_map/ppermute | solution.py:711
  33.0 0.0 collective-permute-done.9
  33.0 1.4 %collective-permute-start.10 = (f32[304,128]{1,0:T(8,128)S(1)}, f32[304,128]{1,0:T(8,128)S(1)}, u32[]{:S(2)}, u32[]{:S(2)}) collective-permute-start(f32[304,128]{1,0:T(8,128)S(1)} %constant_dynamic-update-slice_fusion.2.mine), channel_id=1, source_target_pairs={{0,1},{1,0},{2,3},{3,2},{4,5},{5,4},{6,7},{7,6},{8,9},{9,8},{10,11... | collective-permute-start | bytes 466952 | tf_op jit(solution)/shard_map/ppermute | solution.py:661
  34.5 1.0 %collective-permute-done.10.theirs = f32[304,128]{1,0:T(8,128)S(1)} collective-permute-done((f32[304,128]{1,0:T(8,128)S(1)}, f32[304,128]{1,0:T(8,128)S(1)}, u32[]{:S(2)}, u32[]{:S(2)}) %collective-permute-start.10) | collective-permute-done | bytes 155680 | tf_op jit(solution)/shard_map/ppermute | solution.py:661
  35.5 3.5 %shard_map.54 = f32[4,16,2,8,128]{4,3,2,1,0:T(8,128)S(1)} custom-call(f32[80,128]{1,0:T(8,128)S(1)} %get-tuple-element.63.pack, f32[304,128]{1,0:T(8,128)S(1)} %constant_dynamic-update-slice_fusion.2.mine, f32[304,128]{1,0:T(8,128)S(1)} %collective-permute-done.10.theirs, f32[30,2,32,128]{3,2,1,0:T(8,128)S(1)} %get-tuple-element.65.refs_0_, ...), custom_call_target="tpu_custom_call" | custom-call | tf_op jit(solution)/shard_map/pallas_call | solution.py:774
  39.1 1.1 %collective-permute-start.12 = (f32[256,128]{1,0:T(8,128)S(1)}, f32[256,128]{1,0:T(8,128)S(1)}, u32[]{:S(2)}, u32[]{:S(2)}) collective-permute-start(f32[256,128]{1,0:T(8,128)S(1)} %bitcast.15), channel_id=1, source_target_pairs={{0,16},{1,9},{8,24},{9,1},{16,0},{17,25},{24,8},{25,17},{2,18},{3,... | collective-permute-start | bytes 393224 | tf_op jit(solution)/shard_map/ppermute | solution.py:677
  40.1 1.4 %collective-permute-start.13 = (f32[256,128]{1,0:T(8,128)S(1)}, f32[256,128]{1,0:T(8,128)S(1)}, u32[]{:S(2)}, u32[]{:S(2)}) collective-permute-start(f32[256,128]{1,0:T(8,128)S(1)} %bitcast.14), channel_id=1, source_target_pairs={{0,24},{1,25},{8,16},{9,17},{16,8},{17,9},{24,0},{25,1},{2,26},{3,... | collective-permute-start | bytes 393224 | tf_op jit(solution)/shard_map/ppermute | solution.py:677
  41.6 1.1 %collective-permute-start.11 = (f32[256,128]{1,0:T(8,128)S(1)}, f32[256,128]{1,0:T(8,128)S(1)}, u32[]{:S(2)}, u32[]{:S(2)}) collective-permute-start(f32[256,128]{1,0:T(8,128)S(1)} %bitcast.13), channel_id=1, source_target_pairs={{0,8},{1,17},{8,0},{9,25},{16,24},{17,1},{24,16},{25,9},{2,10},{3,... | collective-permute-start | bytes 393224 | tf_op jit(solution)/shard_map/ppermute | solution.py:677
  42.6 4.6 %collective-permute-done.12.refs_2_ = f32[256,128]{1,0:T(8,128)S(1)} collective-permute-done((f32[256,128]{1,0:T(8,128)S(1)}, f32[256,128]{1,0:T(8,128)S(1)}, u32[]{:S(2)}, u32[]{:S(2)}) %collective-permute-start.12) | collective-permute-done | bytes 131104 | tf_op jit(solution)/shard_map/ppermute | solution.py:677
  47.2 0.0 collective-permute-done.13.refs_3_
  47.2 0.5 %collective-permute-done.11.refs_1_ = f32[256,128]{1,0:T(8,128)S(1)} collective-permute-done((f32[256,128]{1,0:T(8,128)S(1)}, f32[256,128]{1,0:T(8,128)S(1)}, u32[]{:S(2)}, u32[]{:S(2)}) %collective-permute-start.11) | collective-permute-done | bytes 131104 | tf_op jit(solution)/shard_map/ppermute | solution.py:677
  47.8 1.0 %shard_map.55 = (f32[1,8,64,128]{3,2,1,0:T(8,128)}, f32[1,8,64,128]{3,2,1,0:T(8,128)}) custom-call(f32[256,128]{1,0:T(8,128)S(1)} %bitcast.8, f32[256,128]{1,0:T(8,128)S(1)} %collective-permute-done.11.refs_1_, f32[256,128]{1,0:T(8,128)S(1)} %collective-permute-done.12.refs_2_, f32[256,128]{1,0:T(8,128)S(1)} %collective-permute-done.13.refs_3_), custom_call_target="tpu_custom_call" | custom-call | tf_op jit(solution)/shard_map/pallas_call | solution.py:779
  (6 shorter events, 0.1 us)
Async XLA Ops:
  2.0 6.8 %collective-permute-start = (f32[256,128]{1,0:T(8,128)S(1)}, f32[256,128]{1,0:T(8,128)S(1)}, u32[]{:S(2)}, u32[]{:S(2)}) collective-permute-start(f32[256,128]{1,0:T(8,128)S(1)} %get-tuple-element.41), channel_id=1, source_target_pairs={{0,8},{1,17},{8,0},{9,25},{16,24},{17,1},{24,16},{25,9},{2,10},{3,... | collective-permute-start | bytes 393224 | tf_op jit(solution)/shard_map/ppermute | solution.py:677
  5.0 7.8 %collective-permute-start.1 = (f32[256,128]{1,0:T(8,128)S(1)}, f32[256,128]{1,0:T(8,128)S(1)}, u32[]{:S(2)}, u32[]{:S(2)}) collective-permute-start(f32[256,128]{1,0:T(8,128)S(1)} %get-tuple-element.42), channel_id=1, source_target_pairs={{0,16},{1,9},{8,24},{9,1},{16,0},{17,25},{24,8},{25,17},{2,18},{3,... | collective-permute-start | bytes 393224 | tf_op jit(solution)/shard_map/ppermute | solution.py:677
  6.5 6.3 %collective-permute-start.2 = (f32[256,128]{1,0:T(8,128)S(1)}, f32[256,128]{1,0:T(8,128)S(1)}, u32[]{:S(2)}, u32[]{:S(2)}) collective-permute-start(f32[256,128]{1,0:T(8,128)S(1)} %get-tuple-element.43), channel_id=1, source_target_pairs={{0,24},{1,25},{8,16},{9,17},{16,8},{17,9},{24,0},{25,1},{2,26},{3,... | collective-permute-start | bytes 393224 | tf_op jit(solution)/shard_map/ppermute | solution.py:677
  12.8 2.8 %collective-permute-start.3 = (f32[4,13,8,128]{3,2,1,0:T(8,128)S(1)}, f32[4,13,8,128]{3,2,1,0:T(8,128)S(1)}, u32[]{:S(2)}, u32[]{:S(2)}) collective-permute-start(f32[4,13,8,128]{3,2,1,0:T(8,128)S(1)} %get-tuple-element.44), channel_id=1, source_target_pairs={{0,1},{1,0},{8,24},{9,25},{24,8},{25,9},{16,18},{17,19},{18,16},{1... | collective-permute-start | bytes 638984 | tf_op jit(solution)/shard_map/ppermute | solution.py:695
  12.9 8.0 %collective-permute-start.4 = (f32[4,13,8,128]{3,2,1,0:T(8,128)S(1)}, f32[4,13,8,128]{3,2,1,0:T(8,128)S(1)}, u32[]{:S(2)}, u32[]{:S(2)}) collective-permute-start(f32[4,13,8,128]{3,2,1,0:T(8,128)S(1)} %get-tuple-element.45), channel_id=1, source_target_pairs={{0,8},{1,9},{8,0},{9,1},{24,16},{25,17},{16,24},{17,25},{18,2},{19... | collective-permute-start | bytes 638984 | tf_op jit(solution)/shard_map/ppermute | solution.py:695
  15.6 5.4 %collective-permute-start.6 = (f32[4,16,2,8,128]{4,3,2,1,0:T(8,128)S(1)}, f32[4,16,2,8,128]{4,3,2,1,0:T(8,128)S(1)}, u32[]{:S(2)}, u32[]{:S(2)}) collective-permute-start(f32[4,16,2,8,128]{4,3,2,1,0:T(8,128)S(1)} %get-tuple-element.46.c), channel_id=1, source_target_pairs={{0,1},{1,0},{2,3},{3,2},{4,5},{5,4},{6,7},{7,6},{8,9},{9,8},{10,11... | collective-permute-start | bytes 1572872 | tf_op jit(solution)/shard_map/ppermute | solution.py:661
  20.9 1.9 %collective-permute-start.5 = (f32[8,13,8,128]{3,2,1,0:T(8,128)S(1)}, f32[8,13,8,128]{3,2,1,0:T(8,128)S(1)}, u32[]{:S(2)}, u32[]{:S(2)}) collective-permute-start(f32[8,13,8,128]{3,2,1,0:T(8,128)S(1)} %constant_dynamic-update-slice_fusion.sides), channel_id=1, source_target_pairs={{0,1},{1,0},{2,3},{3,2},{4,5},{5,4},{6,7},{7,6},{8,9},{9,8},{10,11... | collective-permute-start | bytes 1277960 | tf_op jit(solution)/shard_map/ppermute | solution.py:661
  26.0 4.6 %collective-permute-start.7 = (f32[144,128]{1,0:T(8,128)S(1)}, f32[144,128]{1,0:T(8,128)S(1)}, u32[]{:S(2)}, u32[]{:S(2)}) collective-permute-start(f32[144,128]{1,0:T(8,128)S(1)} %get-tuple-element.64), channel_id=1, source_target_pairs={{0,8},{8,0},{24,16},{16,24},{18,2},{2,18},{10,26},{26,10},{28,20},... | collective-permute-start | bytes 221192 | tf_op jit(solution)/shard_map/ppermute | solution.py:711
  27.8 5.3 %collective-permute-start.9 = (f32[80,128]{1,0:T(8,128)S(1)}, f32[80,128]{1,0:T(8,128)S(1)}, u32[]{:S(2)}, u32[]{:S(2)}) collective-permute-start(f32[80,128]{1,0:T(8,128)S(1)} %get-tuple-element.63.pack), channel_id=1, source_target_pairs={{0,16},{8,18},{24,2},{16,0},{18,8},{2,24},{10,20},{26,4},{28,12},{... | collective-permute-start | bytes 122888 | tf_op jit(solution)/shard_map/ppermute | solution.py:711
  28.1 4.9 %collective-permute-start.8 = (f32[80,128]{1,0:T(8,128)S(1)}, f32[80,128]{1,0:T(8,128)S(1)}, u32[]{:S(2)}, u32[]{:S(2)}) collective-permute-start(f32[80,128]{1,0:T(8,128)S(1)} %get-tuple-element.63.pack), channel_id=1, source_target_pairs={{0,24},{8,16},{24,0},{16,8},{18,10},{2,26},{10,18},{26,2},{28,4},{... | collective-permute-start | bytes 122888 | tf_op jit(solution)/shard_map/ppermute | solution.py:711
  33.0 2.4 %collective-permute-start.10 = (f32[304,128]{1,0:T(8,128)S(1)}, f32[304,128]{1,0:T(8,128)S(1)}, u32[]{:S(2)}, u32[]{:S(2)}) collective-permute-start(f32[304,128]{1,0:T(8,128)S(1)} %constant_dynamic-update-slice_fusion.2.mine), channel_id=1, source_target_pairs={{0,1},{1,0},{2,3},{3,2},{4,5},{5,4},{6,7},{7,6},{8,9},{9,8},{10,11... | collective-permute-start | bytes 466952 | tf_op jit(solution)/shard_map/ppermute | solution.py:661
  39.1 8.1 %collective-permute-start.12 = (f32[256,128]{1,0:T(8,128)S(1)}, f32[256,128]{1,0:T(8,128)S(1)}, u32[]{:S(2)}, u32[]{:S(2)}) collective-permute-start(f32[256,128]{1,0:T(8,128)S(1)} %bitcast.15), channel_id=1, source_target_pairs={{0,16},{1,9},{8,24},{9,1},{16,0},{17,25},{24,8},{25,17},{2,18},{3,... | collective-permute-start | bytes 393224 | tf_op jit(solution)/shard_map/ppermute | solution.py:677
  40.1 7.1 %collective-permute-start.13 = (f32[256,128]{1,0:T(8,128)S(1)}, f32[256,128]{1,0:T(8,128)S(1)}, u32[]{:S(2)}, u32[]{:S(2)}) collective-permute-start(f32[256,128]{1,0:T(8,128)S(1)} %bitcast.14), channel_id=1, source_target_pairs={{0,24},{1,25},{8,16},{9,17},{16,8},{17,9},{24,0},{25,1},{2,26},{3,... | collective-permute-start | bytes 393224 | tf_op jit(solution)/shard_map/ppermute | solution.py:677
  41.6 6.2 %collective-permute-start.11 = (f32[256,128]{1,0:T(8,128)S(1)}, f32[256,128]{1,0:T(8,128)S(1)}, u32[]{:S(2)}, u32[]{:S(2)}) collective-permute-start(f32[256,128]{1,0:T(8,128)S(1)} %bitcast.13), channel_id=1, source_target_pairs={{0,8},{1,17},{8,0},{9,25},{16,24},{17,1},{24,16},{25,9},{2,10},{3,... | collective-permute-start | bytes 393224 | tf_op jit(solution)/shard_map/ppermute | solution.py:677

commit v6 on v5

--- a/solution.py
+++ b/solution.py
@@ -41,10 +41,20 @@
         q = lax.rem(self.look_up(self.place, i) + lax.axis_index("gy"), self.gx)
         return pl.multiple_of(q * self.by, self.by)
 
+    def distances(self, core):
+        if self.gx != 4:
+            return list(range(self.gx))
+        return [0, 3, 2, 1] if core else [0, 3, 1, 2]
+
+    def by_core(self, even, odd):
+        return even if even == odd else jnp.where(lax.rem(lax.axis_index("gz"), 2) == 0, even, odd)
+
     def distance(self, slot):
-        if self.gx != 4 or slot not in (1, 2):
-            return slot
-        return jnp.where(lax.rem(lax.axis_index("gz"), 2) == 0, slot, 3 - slot)
+        return self.by_core(self.distances(0)[slot], self.distances(1)[slot])
+
+    def slot(self, distance):
+        found = [self.by_core(self.distances(0).index(k), self.distances(1).index(k)) for k in range(self.gx)]
+        return self.look_up(found, distance)
 
     def block_here(self):
         j = lax.axis_index("gy")
@@ -495,13 +505,13 @@
     ups = {k: plan.is_up(block, k, core if plan.paired else 0) for k in range(1, FAR + 1)}
     stage[FAR] = pack[...]
     for k, up in ups.items():
-        at = 0 if k == 1 else side + (k - 2) * size
+        at = (FAR - k) * size
         stage[jnp.where(up, FAR + k, FAR - k)] = mine[pl.ds(at, size), :]
         stage[jnp.where(up, FAR - k, FAR + k)] = theirs[pl.ds(at, size), :]
     for ref, up, half_turn in ((mine, ups[1], 0), (theirs, jnp.logical_not(ups[1]), turn)):
         row = jnp.where(up, own + 5, 0)
         for k, (to, r) in enumerate(((ua1, row), (ua1, row + 1), (ua1, row + 2), (f1, row + 1))):
-            row_in = ref[pl.ds(size + k * half_x, half_x), :]
+            row_in = ref[pl.ds(FAR * size + k * half_x, half_x), :]
             lane = lax.broadcasted_iota(jnp.int32, row_in.shape, 1)
             for s in range(2):
                 to.ref[r, s ^ half_turn] = pick_lanes(row_in, lax.div(lane, 2) + s * (LANES // 2))
@@ -599,13 +609,7 @@
         uc0[2 * j] = finest.swept(ub0, 2 * j)
         uc0[2 * j + 1] = finest.swept(ub0, 2 * j + 1)
 
-    slots = []
-    for s in range(plan.gx):
-        slot = s ^ here
-        if plan.gx == 4:
-            for k in (1, 2):
-                slot = jnp.where((s ^ here) == k, plan.distance(k), slot)
-        slots.append(slot)
+    slots = [plan.slot(s ^ here) for s in range(plan.gx)]
 
     def finish(j):
         for r in (2 * j - 1, 2 * j):
@@ -666,15 +670,14 @@
 
 
 def exchange(plan, parts):
-    got = [parts[0]] * plan.gx
-    for slot in range(plan.gx - 1, 0, -1):
-        mixed = plan.gx == 4 and slot in (1, 2)
+    got = [parts[0]]
+    for slot in range(1, plan.gx):
         pairs = []
         for i in range(plan.gx):
             for g in range(plan.gz):
-                k = 3 - slot if mixed and g % 2 else slot
-                pairs.append((i * plan.gz + g, (i ^ k) * plan.gz + g))
-        got[slot] = lax.ppermute(parts[slot], ("gx", "gz"), pairs)
+                to = i ^ plan.distances(g % 2)[slot]
+                pairs.append((i * plan.gz + g, to * plan.gz + g))
+        got.append(lax.ppermute(parts[slot], ("gx", "gz"), pairs))
     return got
 
 
@@ -714,7 +717,7 @@
 def far_blocks(plan, pack, nears):
     def line(move, near):
         parts = [move(pack, k) for k in range(FAR, 1, -1)] + [move(near, 1)]
-        return jnp.concatenate(parts[::-1], axis=0)
+        return jnp.concatenate(parts, axis=0)
 
     if plan.paired:
         mine = line(functools.partial(swap_blocks_apart, plan), nears[0])

time: 48.9 us -> 49.5 us (1.012)
  waiting for transfers between devices: 20.1 us -> 22.7 us
  starting transfers between devices: 17 us -> 14.9 us
    ppermute x3, waiting for transfers between devices: 2.51 us -> 4.34 us  [swap_blocks_apart(): return lax.ppermute(a, ('gx', 'gy', 'gz'), pairs)]
    ppermute x3, starting transfers between devices: 1.49 us -> 0.68 us  [beside_in_z(): return lax.ppermute(a, 'gz', [(0, 1), (1, 0)])]
    ppermute x3, starting transfers between devices: 4.55 us -> 3.9 us  [swap_blocks_apart(): return lax.ppermute(a, ('gx', 'gy', 'gz'), pairs)]
    ppermute x2, starting transfers between devices: 2.81 us -> 2.19 us  [swap_blocks(): return lax.ppermute(a, ('gx', 'gy', 'gz'), pairs)]
  transfers between devices with their start and end apart: 14 -> 14, of which waited for: 7 -> 9; matrix products, arithmetic and copies ran while one was open for 0% -> 0% of each run, Pallas kernels for 4% -> 4%
where the time goes in v6:
time: 49.5 us; the launch traced here: 49.3 us
  waiting for transfers between devices  22.7 us (46%)
  starting transfers between devices  14.9 us (30%)
  Pallas kernels  10.8 us (22%)
  between operations  0.72 us (1%)
    ppermute x6, waiting for transfers between devices, exchange(): got.append(lax.ppermute(parts[slot], ('gx', 'gz'), pairs))  11.9 us
    ppermute x6, starting transfers between devices, exchange(): got.append(lax.ppermute(parts[slot], ('gx', 'gz'), pairs))  8.15 us
    ppermute x2, waiting for transfers between devices, swap_blocks(): return lax.ppermute(a, ('gx', 'gy', 'gz'), pairs)  5.53 us
    ppermute x3, waiting for transfers between devices, swap_blocks_apart(): return lax.ppermute(a, ('gx', 'gy', 'gz'), pairs)  4.34 us
    ppermute x3, starting transfers between devices, swap_blocks_apart(): return lax.ppermute(a, ('gx', 'gy', 'gz'), pairs)  3.9 us
    pallas_call x1, Pallas kernels, on_device(): call(functools.partial(up_kernel, plan), [in_vmem(gx, by, 2, px, LANES)],...  3.56 us
    pallas_call x1, Pallas kernels, on_device(): call(functools.partial(down_kernel, plan), outs, scratch, input_output_al...  3.14 us
    ppermute x2, starting transfers between devices, swap_blocks(): return lax.ppermute(a, ('gx', 'gy', 'gz'), pairs)  2.19 us
  transfers between devices with their start and end apart: 14, of which 9 were waited for; matrix products, arithmetic and copies ran while one was open for 0% of the time, Pallas kernels for 4%

profile of v6, /device:TPU:0, one launch (start us, length us, event | category | flops | bytes accessed | tf_op | source)
XLA Modules:
  0.0 49.3 jit_solution(9809028660188517024)
XLA Ops:
  0.6 1.3 %shard_map.50 = (f32[256,128]{1,0:T(8,128)S(1)}, f32[256,128]{1,0:T(8,128)S(1)}, f32[256,128]{1,0:T(8,128)S(1)}, f32[256,128]{1,0:T(8,128)S(1)}) custom-call(s32[8,64,128]{2,1,0:T(8,128)} %phase_in.1, f32[8,64,128]{2,1,0:T(8,128)} %density_in.1, f32[1,8,64,128]{3,2,1,0:T(8,128)} %rhs_in.1), custom_call_target="tpu_custom_call" | custom-call | tf_op jit(solution)/shard_map/pallas_call | solution.py:733
  2.0 4.0 %collective-permute-start = (f32[256,128]{1,0:T(8,128)S(1)}, f32[256,128]{1,0:T(8,128)S(1)}, u32[]{:S(2)}, u32[]{:S(2)}) collective-permute-start(f32[256,128]{1,0:T(8,128)S(1)} %get-tuple-element.41), channel_id=1, source_target_pairs={{0,24},{1,25},{8,16},{9,17},{16,8},{17,9},{24,0},{25,1},{2,26},{3,... | collective-permute-start | bytes 393224 | tf_op jit(solution)/shard_map/ppermute | solution.py:680
  5.9 0.5 %collective-permute-start.1 = (f32[256,128]{1,0:T(8,128)S(1)}, f32[256,128]{1,0:T(8,128)S(1)}, u32[]{:S(2)}, u32[]{:S(2)}) collective-permute-start(f32[256,128]{1,0:T(8,128)S(1)} %get-tuple-element.42), channel_id=1, source_target_pairs={{0,8},{1,17},{8,0},{9,25},{16,24},{17,1},{24,16},{25,9},{2,10},{3,... | collective-permute-start | bytes 393224 | tf_op jit(solution)/shard_map/ppermute | solution.py:680
  6.5 0.1 collective-permute-start.2
  6.6 3.3 %collective-permute-done = f32[256,128]{1,0:T(8,128)S(1)} collective-permute-done((f32[256,128]{1,0:T(8,128)S(1)}, f32[256,128]{1,0:T(8,128)S(1)}, u32[]{:S(2)}, u32[]{:S(2)}) %collective-permute-start) | collective-permute-done | bytes 131104 | tf_op jit(solution)/shard_map/ppermute | solution.py:680
  9.8 2.6 %collective-permute-done.1 = f32[256,128]{1,0:T(8,128)S(1)} collective-permute-done((f32[256,128]{1,0:T(8,128)S(1)}, f32[256,128]{1,0:T(8,128)S(1)}, u32[]{:S(2)}, u32[]{:S(2)}) %collective-permute-start.1) | collective-permute-done | bytes 131104 | tf_op jit(solution)/shard_map/ppermute | solution.py:680
  12.5 0.0 collective-permute-done.2
  12.5 0.1 shard_map.51
  12.6 0.1 collective-permute-start.3
  12.6 2.1 %collective-permute-start.4 = (f32[4,13,8,128]{3,2,1,0:T(8,128)S(1)}, f32[4,13,8,128]{3,2,1,0:T(8,128)S(1)}, u32[]{:S(2)}, u32[]{:S(2)}) collective-permute-start(f32[4,13,8,128]{3,2,1,0:T(8,128)S(1)} %get-tuple-element.45), channel_id=1, source_target_pairs={{0,8},{1,9},{8,0},{9,1},{24,16},{25,17},{16,24},{17,25},{18,2},{19... | collective-permute-start | bytes 638984 | tf_op jit(solution)/shard_map/ppermute | solution.py:698
  14.7 0.0 collective-permute-start.6
  14.7 0.0 collective-permute-done.3
  14.8 5.5 %collective-permute-done.4 = f32[4,13,8,128]{3,2,1,0:T(8,128)S(1)} collective-permute-done((f32[4,13,8,128]{3,2,1,0:T(8,128)S(1)}, f32[4,13,8,128]{3,2,1,0:T(8,128)S(1)}, u32[]{:S(2)}, u32[]{:S(2)}) %collective-permute-start.4) | collective-permute-done | bytes 213024 | tf_op jit(solution)/shard_map/ppermute | solution.py:698
  20.3 0.1 collective-permute-start.5
  20.4 0.0 collective-permute-done.6.zc
  20.4 1.8 %shard_map.52 = (f32[30,2,32,128]{3,2,1,0:T(8,128)S(1)}, f32[30,2,32,128]{3,2,1,0:T(8,128)S(1)}, f32[30,2,32,128]{3,2,1,0:T(8,128)S(1)}, f32[30,2,32,128]{3,2,1,...) custom-call(f32[4,16,2,8,128]{4,3,2,1,0:T(8,128)S(1)} %get-tuple-ele, ...), custom_call_target="tpu_custom_call" | custom-call | bytes 9000000 | tf_op jit(solution)/shard_map/pallas_call | solution.py:758
  22.2 0.0 collective-permute-done.5.zsides
  22.2 3.1 %shard_map.53 = (f32[30,2,32,128]{3,2,1,0:T(8,128)S(1)}, f32[30,2,32,128]{3,2,1,0:T(8,128)S(1)}, f32[30,2,32,128]{3,2,1,0:T(8,128)S(1)}, f32[30,2,32,128]{3,2,1,...) custom-call(f32[8,13,8,128]{3,2,1,0:T(8,128)S(1)} %constant_dynamic-, ...), custom_call_target="tpu_custom_call", output_to_operand_aliasing={{0}: (2, {}), {1}: (3, {}), {2}: (4, {}), {3}: (5, {}), {4}... | custom-call | tf_op jit(solution)/shard_map/pallas_call | solution.py:762
  25.4 2.1 %collective-permute-start.7 = (f32[80,128]{1,0:T(8,128)S(1)}, f32[80,128]{1,0:T(8,128)S(1)}, u32[]{:S(2)}, u32[]{:S(2)}) collective-permute-start(f32[80,128]{1,0:T(8,128)S(1)} %get-tuple-element.63.pack), channel_id=1, source_target_pairs={{0,16},{8,18},{24,2},{16,0},{18,8},{2,24},{10,20},{26,4},{28,12},{... | collective-permute-start | bytes 122888 | tf_op jit(solution)/shard_map/ppermute | solution.py:714
  27.5 1.8 %collective-permute-start.8 = (f32[80,128]{1,0:T(8,128)S(1)}, f32[80,128]{1,0:T(8,128)S(1)}, u32[]{:S(2)}, u32[]{:S(2)}) collective-permute-start(f32[80,128]{1,0:T(8,128)S(1)} %get-tuple-element.63.pack), channel_id=1, source_target_pairs={{0,24},{8,16},{24,0},{16,8},{18,10},{2,26},{10,18},{26,2},{28,4},{... | collective-permute-start | bytes 122888 | tf_op jit(solution)/shard_map/ppermute | solution.py:714
  29.3 0.0 collective-permute-start.9
  29.3 0.2 collective-permute-done.7
  29.5 2.9 %collective-permute-done.8 = f32[80,128]{1,0:T(8,128)S(1)} collective-permute-done((f32[80,128]{1,0:T(8,128)S(1)}, f32[80,128]{1,0:T(8,128)S(1)}, u32[]{:S(2)}, u32[]{:S(2)}) %collective-permute-start.8) | collective-permute-done | bytes 40992 | tf_op jit(solution)/shard_map/ppermute | solution.py:714
  32.4 1.2 %collective-permute-done.9 = f32[144,128]{1,0:T(8,128)S(1)} collective-permute-done((f32[144,128]{1,0:T(8,128)S(1)}, f32[144,128]{1,0:T(8,128)S(1)}, u32[]{:S(2)}, u32[]{:S(2)}) %collective-permute-start.9) | collective-permute-done | bytes 73760 | tf_op jit(solution)/shard_map/ppermute | solution.py:714
  33.6 0.6 %collective-permute-start.10 = (f32[304,128]{1,0:T(8,128)S(1)}, f32[304,128]{1,0:T(8,128)S(1)}, u32[]{:S(2)}, u32[]{:S(2)}) collective-permute-start(f32[304,128]{1,0:T(8,128)S(1)} %constant_dynamic-update-slice_fusion.2.mine), channel_id=1, source_target_pairs={{0,1},{1,0},{2,3},{3,2},{4,5},{5,4},{6,7},{7,6},{8,9},{9,8},{10,11... | collective-permute-start | bytes 466952 | tf_op jit(solution)/shard_map/ppermute | solution.py:665
  34.2 1.0 %collective-permute-done.10.theirs = f32[304,128]{1,0:T(8,128)S(1)} collective-permute-done((f32[304,128]{1,0:T(8,128)S(1)}, f32[304,128]{1,0:T(8,128)S(1)}, u32[]{:S(2)}, u32[]{:S(2)}) %collective-permute-start.10) | collective-permute-done | bytes 155680 | tf_op jit(solution)/shard_map/ppermute | solution.py:665
  35.2 3.6 %shard_map.54 = f32[4,16,2,8,128]{4,3,2,1,0:T(8,128)S(1)} custom-call(f32[80,128]{1,0:T(8,128)S(1)} %get-tuple-element.63.pack, f32[304,128]{1,0:T(8,128)S(1)} %constant_dynamic-update-slice_fusion.2.mine, f32[304,128]{1,0:T(8,128)S(1)} %collective-permute-done.10.theirs, f32[30,2,32,128]{3,2,1,0:T(8,128)S(1)} %get-tuple-element.65.refs_0_, ...), custom_call_target="tpu_custom_call" | custom-call | tf_op jit(solution)/shard_map/pallas_call | solution.py:777
  38.9 0.4 collective-permute-start.12
  39.2 1.2 %collective-permute-start.13 = (f32[256,128]{1,0:T(8,128)S(1)}, f32[256,128]{1,0:T(8,128)S(1)}, u32[]{:S(2)}, u32[]{:S(2)}) collective-permute-start(f32[256,128]{1,0:T(8,128)S(1)} %bitcast.14), channel_id=1, source_target_pairs={{0,16},{1,9},{8,24},{9,1},{16,0},{17,25},{24,8},{25,17},{2,18},{3,... | collective-permute-start | bytes 393224 | tf_op jit(solution)/shard_map/ppermute | solution.py:680
  40.4 2.0 %collective-permute-start.11 = (f32[256,128]{1,0:T(8,128)S(1)}, f32[256,128]{1,0:T(8,128)S(1)}, u32[]{:S(2)}, u32[]{:S(2)}) collective-permute-start(f32[256,128]{1,0:T(8,128)S(1)} %bitcast.13), channel_id=1, source_target_pairs={{0,24},{1,25},{8,16},{9,17},{16,8},{17,9},{24,0},{25,1},{2,26},{3,... | collective-permute-start | bytes 393224 | tf_op jit(solution)/shard_map/ppermute | solution.py:680
  42.4 2.9 %collective-permute-done.12.refs_2_ = f32[256,128]{1,0:T(8,128)S(1)} collective-permute-done((f32[256,128]{1,0:T(8,128)S(1)}, f32[256,128]{1,0:T(8,128)S(1)}, u32[]{:S(2)}, u32[]{:S(2)}) %collective-permute-start.12) | collective-permute-done | bytes 131104 | tf_op jit(solution)/shard_map/ppermute | solution.py:680
  45.3 0.0 collective-permute-done.13.refs_3_
  45.3 3.1 %collective-permute-done.11.refs_1_ = f32[256,128]{1,0:T(8,128)S(1)} collective-permute-done((f32[256,128]{1,0:T(8,128)S(1)}, f32[256,128]{1,0:T(8,128)S(1)}, u32[]{:S(2)}, u32[]{:S(2)}) %collective-permute-start.11) | collective-permute-done | bytes 131104 | tf_op jit(solution)/shard_map/ppermute | solution.py:680
  48.4 1.0 %shard_map.55 = (f32[1,8,64,128]{3,2,1,0:T(8,128)}, f32[1,8,64,128]{3,2,1,0:T(8,128)}) custom-call(f32[256,128]{1,0:T(8,128)S(1)} %bitcast.8, f32[256,128]{1,0:T(8,128)S(1)} %collective-permute-done.11.refs_1_, f32[256,128]{1,0:T(8,128)S(1)} %collective-permute-done.12.refs_2_, f32[256,128]{1,0:T(8,128)S(1)} %collective-permute-done.13.refs_3_), custom_call_target="tpu_custom_call" | custom-call | tf_op jit(solution)/shard_map/pallas_call | solution.py:782
  (6 shorter events, 0.1 us)
Async XLA Ops:
  2.0 7.9 %collective-permute-start = (f32[256,128]{1,0:T(8,128)S(1)}, f32[256,128]{1,0:T(8,128)S(1)}, u32[]{:S(2)}, u32[]{:S(2)}) collective-permute-start(f32[256,128]{1,0:T(8,128)S(1)} %get-tuple-element.41), channel_id=1, source_target_pairs={{0,24},{1,25},{8,16},{9,17},{16,8},{17,9},{24,0},{25,1},{2,26},{3,... | collective-permute-start | bytes 393224 | tf_op jit(solution)/shard_map/ppermute | solution.py:680
  5.9 6.6 %collective-permute-start.1 = (f32[256,128]{1,0:T(8,128)S(1)}, f32[256,128]{1,0:T(8,128)S(1)}, u32[]{:S(2)}, u32[]{:S(2)}) collective-permute-start(f32[256,128]{1,0:T(8,128)S(1)} %get-tuple-element.42), channel_id=1, source_target_pairs={{0,8},{1,17},{8,0},{9,25},{16,24},{17,1},{24,16},{25,9},{2,10},{3,... | collective-permute-start | bytes 393224 | tf_op jit(solution)/shard_map/ppermute | solution.py:680
  6.5 6.0 %collective-permute-start.2 = (f32[256,128]{1,0:T(8,128)S(1)}, f32[256,128]{1,0:T(8,128)S(1)}, u32[]{:S(2)}, u32[]{:S(2)}) collective-permute-start(f32[256,128]{1,0:T(8,128)S(1)} %get-tuple-element.43), channel_id=1, source_target_pairs={{0,16},{1,9},{8,24},{9,1},{16,0},{17,25},{24,8},{25,17},{2,18},{3,... | collective-permute-start | bytes 393224 | tf_op jit(solution)/shard_map/ppermute | solution.py:680
  12.6 2.2 %collective-permute-start.3 = (f32[4,13,8,128]{3,2,1,0:T(8,128)S(1)}, f32[4,13,8,128]{3,2,1,0:T(8,128)S(1)}, u32[]{:S(2)}, u32[]{:S(2)}) collective-permute-start(f32[4,13,8,128]{3,2,1,0:T(8,128)S(1)} %get-tuple-element.44), channel_id=1, source_target_pairs={{0,1},{1,0},{8,24},{9,25},{24,8},{25,9},{16,18},{17,19},{18,16},{1... | collective-permute-start | bytes 638984 | tf_op jit(solution)/shard_map/ppermute | solution.py:698
  12.6 7.7 %collective-permute-start.4 = (f32[4,13,8,128]{3,2,1,0:T(8,128)S(1)}, f32[4,13,8,128]{3,2,1,0:T(8,128)S(1)}, u32[]{:S(2)}, u32[]{:S(2)}) collective-permute-start(f32[4,13,8,128]{3,2,1,0:T(8,128)S(1)} %get-tuple-element.45), channel_id=1, source_target_pairs={{0,8},{1,9},{8,0},{9,1},{24,16},{25,17},{16,24},{17,25},{18,2},{19... | collective-permute-start | bytes 638984 | tf_op jit(solution)/shard_map/ppermute | solution.py:698
  14.7 5.7 %collective-permute-start.6 = (f32[4,16,2,8,128]{4,3,2,1,0:T(8,128)S(1)}, f32[4,16,2,8,128]{4,3,2,1,0:T(8,128)S(1)}, u32[]{:S(2)}, u32[]{:S(2)}) collective-permute-start(f32[4,16,2,8,128]{4,3,2,1,0:T(8,128)S(1)} %get-tuple-element.46.c), channel_id=1, source_target_pairs={{0,1},{1,0},{2,3},{3,2},{4,5},{5,4},{6,7},{7,6},{8,9},{9,8},{10,11... | collective-permute-start | bytes 1572872 | tf_op jit(solution)/shard_map/ppermute | solution.py:665
  20.3 1.9 %collective-permute-start.5 = (f32[8,13,8,128]{3,2,1,0:T(8,128)S(1)}, f32[8,13,8,128]{3,2,1,0:T(8,128)S(1)}, u32[]{:S(2)}, u32[]{:S(2)}) collective-permute-start(f32[8,13,8,128]{3,2,1,0:T(8,128)S(1)} %constant_dynamic-update-slice_fusion.sides), channel_id=1, source_target_pairs={{0,1},{1,0},{2,3},{3,2},{4,5},{5,4},{6,7},{7,6},{8,9},{9,8},{10,11... | collective-permute-start | bytes 1277960 | tf_op jit(solution)/shard_map/ppermute | solution.py:665
  25.4 4.1 %collective-permute-start.7 = (f32[80,128]{1,0:T(8,128)S(1)}, f32[80,128]{1,0:T(8,128)S(1)}, u32[]{:S(2)}, u32[]{:S(2)}) collective-permute-start(f32[80,128]{1,0:T(8,128)S(1)} %get-tuple-element.63.pack), channel_id=1, source_target_pairs={{0,16},{8,18},{24,2},{16,0},{18,8},{2,24},{10,20},{26,4},{28,12},{... | collective-permute-start | bytes 122888 | tf_op jit(solution)/shard_map/ppermute | solution.py:714
  27.5 4.9 %collective-permute-start.8 = (f32[80,128]{1,0:T(8,128)S(1)}, f32[80,128]{1,0:T(8,128)S(1)}, u32[]{:S(2)}, u32[]{:S(2)}) collective-permute-start(f32[80,128]{1,0:T(8,128)S(1)} %get-tuple-element.63.pack), channel_id=1, source_target_pairs={{0,24},{8,16},{24,0},{16,8},{18,10},{2,26},{10,18},{26,2},{28,4},{... | collective-permute-start | bytes 122888 | tf_op jit(solution)/shard_map/ppermute | solution.py:714
  29.3 4.4 %collective-permute-start.9 = (f32[144,128]{1,0:T(8,128)S(1)}, f32[144,128]{1,0:T(8,128)S(1)}, u32[]{:S(2)}, u32[]{:S(2)}) collective-permute-start(f32[144,128]{1,0:T(8,128)S(1)} %get-tuple-element.64), channel_id=1, source_target_pairs={{0,8},{8,0},{24,16},{16,24},{18,2},{2,18},{10,26},{26,10},{28,20},... | collective-permute-start | bytes 221192 | tf_op jit(solution)/shard_map/ppermute | solution.py:714
  33.6 1.6 %collective-permute-start.10 = (f32[304,128]{1,0:T(8,128)S(1)}, f32[304,128]{1,0:T(8,128)S(1)}, u32[]{:S(2)}, u32[]{:S(2)}) collective-permute-start(f32[304,128]{1,0:T(8,128)S(1)} %constant_dynamic-update-slice_fusion.2.mine), channel_id=1, source_target_pairs={{0,1},{1,0},{2,3},{3,2},{4,5},{5,4},{6,7},{7,6},{8,9},{9,8},{10,11... | collective-permute-start | bytes 466952 | tf_op jit(solution)/shard_map/ppermute | solution.py:665
  38.9 6.4 %collective-permute-start.12 = (f32[256,128]{1,0:T(8,128)S(1)}, f32[256,128]{1,0:T(8,128)S(1)}, u32[]{:S(2)}, u32[]{:S(2)}) collective-permute-start(f32[256,128]{1,0:T(8,128)S(1)} %bitcast.15), channel_id=1, source_target_pairs={{0,8},{1,17},{8,0},{9,25},{16,24},{17,1},{24,16},{25,9},{2,10},{3,... | collective-permute-start | bytes 393224 | tf_op jit(solution)/shard_map/ppermute | solution.py:680
  39.2 6.1 %collective-permute-start.13 = (f32[256,128]{1,0:T(8,128)S(1)}, f32[256,128]{1,0:T(8,128)S(1)}, u32[]{:S(2)}, u32[]{:S(2)}) collective-permute-start(f32[256,128]{1,0:T(8,128)S(1)} %bitcast.14), channel_id=1, source_target_pairs={{0,16},{1,9},{8,24},{9,1},{16,0},{17,25},{24,8},{25,17},{2,18},{3,... | collective-permute-start | bytes 393224 | tf_op jit(solution)/shard_map/ppermute | solution.py:680
  40.4 7.9 %collective-permute-start.11 = (f32[256,128]{1,0:T(8,128)S(1)}, f32[256,128]{1,0:T(8,128)S(1)}, u32[]{:S(2)}, u32[]{:S(2)}) collective-permute-start(f32[256,128]{1,0:T(8,128)S(1)} %bitcast.13), channel_id=1, source_target_pairs={{0,24},{1,25},{8,16},{9,17},{16,8},{17,9},{24,0},{25,1},{2,26},{3,... | collective-permute-start | bytes 393224 | tf_op jit(solution)/shard_map/ppermute | solution.py:680

commit v7 on v6

--- a/solution.py
+++ b/solution.py
@@ -29,6 +29,7 @@
         self.paired = self.gz == 2
         self.ring = [0, 1, 3, 2] if self.gx == 4 else list(range(self.gx))
         self.place = [self.ring.index(i) for i in range(self.gx)]
+        self.back = [0, 2, 1, 3] if self.gx == 4 else list(range(self.gx))
 
     def device(self, block):
         j, q = divmod(block, self.gx)
@@ -478,73 +479,96 @@
         out[pl.ds(size, 4 * half_x), :] = compress(near_stage, 2)
 
 
-def up_kernel(plan, pack, mine, theirs, *refs):
-    refs, out, scratch = refs[:13], refs[13], refs[14:]
-    kx0, ky0, kz0, d0, w0, f0, u0, kx1, ky1, kz1, w1, f1_in, u1_in = [Wide(r) for r in refs]
-    stage = scratch[0]
-    wide = [Wide(r) for r in scratch[1:]]
-    f2, kx2, ky2, kz2, d2, w2, ua2, ub2, r2 = wide[:9]
-    f3, kx3, ky3, kz3, d3, w3, ua3, ub3 = wide[9:17]
-    t1, t0, f1, ua1, ub1, ua0, ub0, uc0 = wide[17:]
+class Coarse:
+    COUNT = 9
+
+    @staticmethod
+    def shapes(plan):
+        rows = (2 * FAR + 1) * (plan.by // 4) + 1
+        level2 = in_vmem(rows, 2, plan.nx // 4, LANES)
+        level1 = in_vmem(plan.by // 2 + 8, 2, plan.nx // 2, LANES)
+        return [level2] * 7 + [level1] * 2
+
+    def __init__(self, plan, refs):
+        self.plan = plan
+        self.fields = [Wide(r) for r in refs[:5]]
+        self.f, self.kx, self.ky, self.kz, self.d = self.fields
+        self.w, self.u, self.f1, self.u1 = [Wide(r) for r in refs[5:]]
+        self.block = plan.block_here()
+
+    def spread(self, packed, at, turned):
+        plan = self.plan
+        own2, quarter_x = plan.by // 4, plan.nx // 4
+        part = own2 // 2
+        there = self.block + at - FAR
+        exists = (there >= 0) & (there < plan.blocks)
+        lane = lax.broadcasted_iota(jnp.int32, packed.shape, 1)
+        for quarter in range(4):
+            part_of, half = divmod(quarter, 2)
+            s = half ^ turned
+            a = pick_lanes(packed, lax.div(lane, 4) + quarter * (LANES // 4))
+            for j in range(part):
+                r = at * own2 + part_of * part + j
+                tiles = [a[(t * part + j) * quarter_x : (t * part + j + 1) * quarter_x] for t in range(5)]
+                for t, ref in enumerate(self.fields):
+                    if t == 2:
+                        ref.ref[r + 1, s] = jnp.where(exists, tiles[t], 0.0)
+                    else:
+                        ref.ref[r, s] = tiles[t]
+                w = DAMPING * inverse(tiles[4])
+                self.w.ref[r, s] = w
+                self.u.ref[r, s] = w * tiles[0]
+
+    def side(self, ref, ups, turned):
+        plan = self.plan
+        own, half_x = plan.by // 2, plan.nx // 2
+        size = 5 * (plan.by // 8) * (plan.nx // 4)
+        nearest = size + 4 * half_x
+        for k, up in ups.items():
+            first = 0 if k == 1 else nearest + (k - 2) * size
+            self.spread(ref[pl.ds(first, size), :], jnp.where(up, FAR + k, FAR - k), turned)
+        row = jnp.where(ups[1], own + 5, 0)
+        for k, (to, r) in enumerate(((self.u1, row), (self.u1, row + 1), (self.u1, row + 2), (self.f1, row + 1))):
+            row_in = ref[pl.ds(size + k * half_x, half_x), :]
+            lane = lax.broadcasted_iota(jnp.int32, row_in.shape, 1)
+            for s in range(2):
+                to.ref[r, s ^ turned] = pick_lanes(row_in, lax.div(lane, 2) + s * (LANES // 2))
+
+    def ups(self, opposite):
+        one = lax.axis_index("gz") if self.plan.paired else 0
+        one = 1 - one if opposite else one
+        return {k: self.plan.is_up(self.block, k, one) for k in range(1, FAR + 1)}
+
+
+def spread_kernel(plan, pack, mine, f1, u1, *refs):
+    coarse = Coarse(plan, refs)
+    own = plan.by // 2
+    for r in range(2, own + 6):
+        coarse.f1.ref[r] = f1[r]
+    for r in range(3, own + 5):
+        coarse.u1.ref[r] = u1[r]
+    coarse.spread(pack[...], FAR, 0)
+    coarse.side(mine, coarse.ups(False), 0)
+
+
+def up_kernel(plan, theirs, *refs):
+    count = Coarse.COUNT
+    refs = refs[count:]
+    kx0, ky0, kz0, d0, w0, f0, u0, kx1, ky1, kz1, w1 = [Wide(r) for r in refs[:11]]
+    out, coarse, scratch = refs[11], Coarse(plan, refs[12 : 12 + count]), refs[12 + count :]
+    f2, kx2, ky2, kz2, d2, w2, ua2 = *coarse.fields, coarse.w, coarse.u
+    f1, ua1 = coarse.f1, coarse.u1
+    wide = [Wide(r) for r in scratch]
+    ub2, r2, f3, kx3, ky3, kz3, d3, w3, ua3, ub3 = wide[:10]
+    t1, t0, ub1, ua0, ub0, uc0 = wide[10:]
     nx, by = plan.nx, plan.by
     own, own2 = by // 2, by // 4
-    part = own2 // 2
     half_x, quarter_x = nx // 2, nx // 4
-    size = pack.shape[0]
-    side = size + 4 * half_x
-    core = lax.axis_index("gz")
-    block = plan.block_here()
     here = lax.axis_index("gx")
-    turn = 1 if plan.paired else 0
-
-    for r in range(2, own + 6):
-        f1[r] = f1_in[r]
-    for r in range(3, own + 5):
-        ua1[r] = u1_in[r]
-
-    ups = {k: plan.is_up(block, k, core if plan.paired else 0) for k in range(1, FAR + 1)}
-    stage[FAR] = pack[...]
-    for k, up in ups.items():
-        at = (FAR - k) * size
-        stage[jnp.where(up, FAR + k, FAR - k)] = mine[pl.ds(at, size), :]
-        stage[jnp.where(up, FAR - k, FAR + k)] = theirs[pl.ds(at, size), :]
-    for ref, up, half_turn in ((mine, ups[1], 0), (theirs, jnp.logical_not(ups[1]), turn)):
-        row = jnp.where(up, own + 5, 0)
-        for k, (to, r) in enumerate(((ua1, row), (ua1, row + 1), (ua1, row + 2), (f1, row + 1))):
-            row_in = ref[pl.ds(FAR * size + k * half_x, half_x), :]
-            lane = lax.broadcasted_iota(jnp.int32, row_in.shape, 1)
-            for s in range(2):
-                to.ref[r, s ^ half_turn] = pick_lanes(row_in, lax.div(lane, 2) + s * (LANES // 2))
-
-    lane = lax.broadcasted_iota(jnp.int32, (size, LANES), 1)
-    lanes = [lax.div(lane, 4) + k * (LANES // 4) for k in range(4)]
-
-    def expand(k):
-        there = block + k - FAR
-        exists = (there >= 0) & (there < plan.blocks)
-        swapped = 0
-        if plan.paired and k != FAR:
-            swapped = jnp.where(ups[abs(k - FAR)] == (k > FAR), 0, 1)
-        rows = stage[k]
-        for quarter in range(4):
-            part_of, half = divmod(quarter, 2)
-            a = pick_lanes(rows, lanes[quarter])
-            for t, ref in enumerate((f2, kx2, ky2, kz2, d2)):
-                for j in range(part):
-                    at = (t * part + j) * quarter_x
-                    b = a[at : at + quarter_x]
-                    if t == 2:
-                        b = jnp.where(exists, b, 0.0)
-                    r = k * own2 + part_of * part + j + (1 if t == 2 else 0)
-                    ref.ref[r, swapped if half == 0 else 1 - swapped] = b
-
-    for k in range(2 * FAR + 1):
-        expand(k)
+    coarse.side(theirs, coarse.ups(True), 1 if plan.paired else 0)
 
     rows2 = (2 * FAR + 1) * own2
     two = Level(1, 4, kx2, ky2, kz2, d2, w2, f2, 14)
-    two.weigh(0, rows2 - 1)
-    two.first(ua2, 0, rows2 - 1)
     two.sweep(ua2, ub2, 1, rows2 - 2)
     two.residual_pairs(ub2, r2, 2, rows2 // 2 - 2)
 
@@ -632,7 +656,7 @@
     parts, (scaled, residual) = refs[: plan.gx], refs[plan.gx :]
     here = lax.axis_index("gx")
     by, px = plan.by, plan.px
-    for slot, part in enumerate(parts):
+    for slot, part in zip(plan.back, parts):
         rows = pl.ds(plan.start_of(here ^ plan.distance(slot)), by)
         for p in range(px):
             scaled[0, p, rows, :] = part[pl.ds(p, by, stride=2 * px), :]
@@ -717,7 +741,7 @@
 def far_blocks(plan, pack, nears):
     def line(move, near):
         parts = [move(pack, k) for k in range(FAR, 1, -1)] + [move(near, 1)]
-        return jnp.concatenate(parts, axis=0)
+        return jnp.concatenate(parts[::-1], axis=0)
 
     if plan.paired:
         mine = line(functools.partial(swap_blocks_apart, plan), nears[0])
@@ -768,21 +792,25 @@
     fine, rest = down[: Finest.COUNT], down[Finest.COUNT :]
     pack, nears, (w1, u1) = rest[0], rest[1 : 1 + near_count], rest[1 + near_count :]
     kx1, ky1, kz1, _, f1 = fine[11:]
-    fields = list(fine[:7]) + [kx1, ky1, kz1, w1, f1, u1]
     mine, theirs = far_blocks(plan, pack, nears)
+    coarse = call(functools.partial(spread_kernel, plan), Coarse.shapes(plan), work=3_000_000)(
+        *pinned(pack, mine, f1, u1)
+    )
     rows2 = (2 * FAR + 1) * own2
-    scratch = [in_vmem(2 * FAR + 1, size, LANES)]
-    scratch += [in_vmem(rows2 + 1, 2, nx // 4, LANES)] * 9 + [in_vmem(rows2 // 2 + 1, 2, nx // 4, LANES)] * 8
-    scratch += [level1(rows2), level0(own + 8)] + [level1(own + 8)] * 3 + [level0(rows)] * 3
-    (result,) = call(
-        functools.partial(up_kernel, plan), [in_vmem(gx, by, 2, px, LANES)], scratch
-    )(*pinned(pack, mine, theirs, *fields))
+    level2, level3 = in_vmem(rows2 + 1, 2, nx // 4, LANES), in_vmem(rows2 // 2 + 1, 2, nx // 4, LANES)
+    scratch = [level2] * 2 + [level3] * 8 + [level1(rows2), level0(own + 8), level1(own + 8)] + [level0(rows)] * 3
+    result = call(
+        functools.partial(up_kernel, plan),
+        [in_vmem(gx, by, 2, px, LANES)] + Coarse.shapes(plan),
+        scratch,
+        input_output_aliases={1 + k: 1 + k for k in range(Coarse.COUNT)},
+    )(*pinned(theirs, *coarse, *fine[:7], kx1, ky1, kz1, w1))[0]
 
     parts = exchange(plan, [result[k].reshape(flat, LANES) for k in range(gx)])
     return call(
         functools.partial(place_kernel, plan),
         [jax.ShapeDtypeStruct((1, px, plan.ny, LANES), F32)] * 2,
-    )(*pinned(*parts))
+    )(*pinned(*[parts[slot] for slot in plan.back]))
 
 
 def solution(mesh):

time: 49.5 us -> 49.4 us (level)
  waiting for transfers between devices: 22.7 us -> 20.3 us
  starting transfers between devices: 14.9 us -> 16.7 us
  Pallas kernels: 10.8 us -> 11.4 us
    ppermute x3, waiting for transfers between devices: 4.34 us -> 2.2 us  [swap_blocks_apart(): return lax.ppermute(a, ('gx', 'gy', 'gz'), pairs)]
    ppermute x3, starting transfers between devices: 3.9 us -> 5.12 us  [swap_blocks_apart(): return lax.ppermute(a, ('gx', 'gy', 'gz'), pairs)]
    ppermute x3, starting transfers between devices: 0.68 us -> 1.23 us  [beside_in_z(): return lax.ppermute(a, 'gz', [(0, 1), (1, 0)])]
    pallas_call x1 -> x2, Pallas kernels: 3.56 us -> 3.75 us  [the longest x1 3.43 us: on_device(): call(functools.partial(up_kernel, plan), [in_vmem(gx, by, 2, px, LANES)]...]
  transfers between devices with their start and end apart: 14 -> 14, of which waited for: 9 -> 7; matrix products, arithmetic and copies ran while one was open for 0% -> 0% of each run, Pallas kernels for 4% -> 5%
where the time goes in v7:
time: 49.4 us; the launch traced here: 49.2 us
  waiting for transfers between devices  20.3 us (41%)
  starting transfers between devices  16.7 us (34%)
  Pallas kernels  11.4 us (23%)
  between operations  0.74 us (1%)
    ppermute x6, waiting for transfers between devices, exchange(): got.append(lax.ppermute(parts[slot], ('gx', 'gz'), pairs))  11.9 us
    ppermute x6, starting transfers between devices, exchange(): got.append(lax.ppermute(parts[slot], ('gx', 'gz'), pairs))  8.17 us
    ppermute x2, waiting for transfers between devices, swap_blocks(): return lax.ppermute(a, ('gx', 'gy', 'gz'), pairs)  5.53 us
    ppermute x3, starting transfers between devices, swap_blocks_apart(): return lax.ppermute(a, ('gx', 'gy', 'gz'), pairs)  5.12 us
    pallas_call x1, Pallas kernels, on_device(): call(functools.partial(up_kernel, plan), [in_vmem(gx, by, 2, px, LANES)]...  3.43 us
    pallas_call x1, Pallas kernels, on_device(): call(functools.partial(down_kernel, plan), outs, scratch, input_output_al...  3.38 us
    ppermute x3, waiting for transfers between devices, swap_blocks_apart(): return lax.ppermute(a, ('gx', 'gy', 'gz'), pairs)  2.2 us
    ppermute x2, starting transfers between devices, swap_blocks(): return lax.ppermute(a, ('gx', 'gy', 'gz'), pairs)  2.19 us
  transfers between devices with their start and end apart: 14, of which 7 were waited for; matrix products, arithmetic and copies ran while one was open for 0% of the time, Pallas kernels for 5%

profile of v7, /device:TPU:0, one launch (start us, length us, event | category | flops | bytes accessed | tf_op | source)
XLA Modules:
  0.0 49.2 jit_solution(12421457479045476789)
XLA Ops:
  0.6 1.3 %shard_map.50 = (f32[256,128]{1,0:T(8,128)S(1)}, f32[256,128]{1,0:T(8,128)S(1)}, f32[256,128]{1,0:T(8,128)S(1)}, f32[256,128]{1,0:T(8,128)S(1)}) custom-call(s32[8,64,128]{2,1,0:T(8,128)} %phase_in.1, f32[8,64,128]{2,1,0:T(8,128)} %density_in.1, f32[1,8,64,128]{3,2,1,0:T(8,128)} %rhs_in.1), custom_call_target="tpu_custom_call" | custom-call | tf_op jit(solution)/shard_map/pallas_call | solution.py:757
  2.0 4.0 %collective-permute-start = (f32[256,128]{1,0:T(8,128)S(1)}, f32[256,128]{1,0:T(8,128)S(1)}, u32[]{:S(2)}, u32[]{:S(2)}) collective-permute-start(f32[256,128]{1,0:T(8,128)S(1)} %get-tuple-element.51), channel_id=1, source_target_pairs={{0,24},{1,25},{8,16},{9,17},{16,8},{17,9},{24,0},{25,1},{2,26},{3,... | collective-permute-start | bytes 393224 | tf_op jit(solution)/shard_map/ppermute | solution.py:704
  5.9 0.5 %collective-permute-start.1 = (f32[256,128]{1,0:T(8,128)S(1)}, f32[256,128]{1,0:T(8,128)S(1)}, u32[]{:S(2)}, u32[]{:S(2)}) collective-permute-start(f32[256,128]{1,0:T(8,128)S(1)} %get-tuple-element.52), channel_id=1, source_target_pairs={{0,8},{1,17},{8,0},{9,25},{16,24},{17,1},{24,16},{25,9},{2,10},{3,... | collective-permute-start | bytes 393224 | tf_op jit(solution)/shard_map/ppermute | solution.py:704
  6.5 0.1 collective-permute-start.2
  6.6 3.3 %collective-permute-done = f32[256,128]{1,0:T(8,128)S(1)} collective-permute-done((f32[256,128]{1,0:T(8,128)S(1)}, f32[256,128]{1,0:T(8,128)S(1)}, u32[]{:S(2)}, u32[]{:S(2)}) %collective-permute-start) | collective-permute-done | bytes 131104 | tf_op jit(solution)/shard_map/ppermute | solution.py:704
  9.8 2.6 %collective-permute-done.1 = f32[256,128]{1,0:T(8,128)S(1)} collective-permute-done((f32[256,128]{1,0:T(8,128)S(1)}, f32[256,128]{1,0:T(8,128)S(1)}, u32[]{:S(2)}, u32[]{:S(2)}) %collective-permute-start.1) | collective-permute-done | bytes 131104 | tf_op jit(solution)/shard_map/ppermute | solution.py:704
  12.5 0.0 collective-permute-done.2
  12.5 0.1 shard_map.51
  12.6 0.1 collective-permute-start.3
  12.6 2.1 %collective-permute-start.4 = (f32[4,13,8,128]{3,2,1,0:T(8,128)S(1)}, f32[4,13,8,128]{3,2,1,0:T(8,128)S(1)}, u32[]{:S(2)}, u32[]{:S(2)}) collective-permute-start(f32[4,13,8,128]{3,2,1,0:T(8,128)S(1)} %get-tuple-element.55), channel_id=1, source_target_pairs={{0,8},{1,9},{8,0},{9,1},{24,16},{25,17},{16,24},{17,25},{18,2},{19... | collective-permute-start | bytes 638984 | tf_op jit(solution)/shard_map/ppermute | solution.py:722
  14.7 0.0 collective-permute-start.6
  14.7 0.0 collective-permute-done.3
  14.8 5.5 %collective-permute-done.4 = f32[4,13,8,128]{3,2,1,0:T(8,128)S(1)} collective-permute-done((f32[4,13,8,128]{3,2,1,0:T(8,128)S(1)}, f32[4,13,8,128]{3,2,1,0:T(8,128)S(1)}, u32[]{:S(2)}, u32[]{:S(2)}) %collective-permute-start.4) | collective-permute-done | bytes 213024 | tf_op jit(solution)/shard_map/ppermute | solution.py:722
  20.3 0.1 collective-permute-start.5
  20.4 0.0 collective-permute-done.6.zc
  20.4 1.9 %shard_map.52 = (f32[30,2,32,128]{3,2,1,0:T(8,128)S(1)}, f32[30,2,32,128]{3,2,1,0:T(8,128)S(1)}, f32[30,2,32,128]{3,2,1,0:T(8,128)S(1)}, f32[30,2,32,128]{3,2,1,...) custom-call(f32[4,16,2,8,128]{4,3,2,1,0:T(8,128)S(1)} %get-tuple-ele, ...), custom_call_target="tpu_custom_call" | custom-call | bytes 9000000 | tf_op jit(solution)/shard_map/pallas_call | solution.py:782
  22.3 0.0 collective-permute-done.5.zsides
  22.3 3.4 %shard_map.53 = (f32[30,2,32,128]{3,2,1,0:T(8,128)S(1)}, f32[30,2,32,128]{3,2,1,0:T(8,128)S(1)}, f32[30,2,32,128]{3,2,1,0:T(8,128)S(1)}, f32[30,2,32,128]{3,2,1,...) custom-call(f32[8,13,8,128]{3,2,1,0:T(8,128)S(1)} %constant_dynamic-, ...), custom_call_target="tpu_custom_call", output_to_operand_aliasing={{0}: (2, {}), {1}: (3, {}), {2}: (4, {}), {3}: (5, {}), {4}... | custom-call | tf_op jit(solution)/shard_map/pallas_call | solution.py:786
  25.7 0.4 collective-permute-start.7
  26.1 2.1 %collective-permute-start.9 = (f32[80,128]{1,0:T(8,128)S(1)}, f32[80,128]{1,0:T(8,128)S(1)}, u32[]{:S(2)}, u32[]{:S(2)}) collective-permute-start(f32[80,128]{1,0:T(8,128)S(1)} %get-tuple-element.74.pack), channel_id=1, source_target_pairs={{0,16},{8,18},{24,2},{16,0},{18,8},{2,24},{10,20},{26,4},{28,12},{... | collective-permute-start | bytes 122888 | tf_op jit(solution)/shard_map/ppermute | solution.py:738
  28.1 2.7 %collective-permute-start.8 = (f32[80,128]{1,0:T(8,128)S(1)}, f32[80,128]{1,0:T(8,128)S(1)}, u32[]{:S(2)}, u32[]{:S(2)}) collective-permute-start(f32[80,128]{1,0:T(8,128)S(1)} %get-tuple-element.74.pack), channel_id=1, source_target_pairs={{0,24},{8,16},{24,0},{16,8},{18,10},{2,26},{10,18},{26,2},{28,4},{... | collective-permute-start | bytes 122888 | tf_op jit(solution)/shard_map/ppermute | solution.py:738
  30.8 0.0 collective-permute-done.7
  30.9 2.2 %collective-permute-done.8 = f32[80,128]{1,0:T(8,128)S(1)} collective-permute-done((f32[80,128]{1,0:T(8,128)S(1)}, f32[80,128]{1,0:T(8,128)S(1)}, u32[]{:S(2)}, u32[]{:S(2)}) %collective-permute-start.8) | collective-permute-done | bytes 40992 | tf_op jit(solution)/shard_map/ppermute | solution.py:738
  33.0 0.0 collective-permute-done.9
  33.1 1.2 %collective-permute-start.10 = (f32[304,128]{1,0:T(8,128)S(1)}, f32[304,128]{1,0:T(8,128)S(1)}, u32[]{:S(2)}, u32[]{:S(2)}) collective-permute-start(f32[304,128]{1,0:T(8,128)S(1)} %constant_dynamic-update-slice_fusion.2.mine), channel_id=1, source_target_pairs={{0,1},{1,0},{2,3},{3,2},{4,5},{5,4},{6,7},{7,6},{8,9},{9,8},{10,11... | collective-permute-start | bytes 466952 | tf_op jit(solution)/shard_map/ppermute | solution.py:689
  34.2 0.3 shard_map.54
  34.5 0.7 %collective-permute-done.10.theirs = f32[304,128]{1,0:T(8,128)S(1)} collective-permute-done((f32[304,128]{1,0:T(8,128)S(1)}, f32[304,128]{1,0:T(8,128)S(1)}, u32[]{:S(2)}, u32[]{:S(2)}) %collective-permute-start.10) | collective-permute-done | bytes 155680 | tf_op jit(solution)/shard_map/ppermute | solution.py:689
  35.2 3.4 %shard_map.55 = (f32[4,16,2,8,128]{4,3,2,1,0:T(8,128)S(1)}, f32[29,2,8,128]{3,2,1,0:T(8,128)S(1)}, f32[29,2,8,128]{3,2,1,0:T(8,128)S(1)}, f32[29,2,8,128]{3,2,1,...) custom-call(f32[304,128]{1,0:T(8,128)S(1)} %collective-permute-done., ...), custom_call_target="tpu_custom_call", output_to_operand_aliasing={{1}: (1, {}), {2}: (2, {}), {3}: (3, {}), {4}: (4, {}), {5}... | custom-call | tf_op jit(solution)/shard_map/pallas_call | solution.py:802
  38.7 2.1 %collective-permute-start.12 = (f32[256,128]{1,0:T(8,128)S(1)}, f32[256,128]{1,0:T(8,128)S(1)}, u32[]{:S(2)}, u32[]{:S(2)}) collective-permute-start(f32[256,128]{1,0:T(8,128)S(1)} %bitcast.15), channel_id=1, source_target_pairs={{0,24},{1,25},{8,16},{9,17},{16,8},{17,9},{24,0},{25,1},{2,26},{3,... | collective-permute-start | bytes 393224 | tf_op jit(solution)/shard_map/ppermute | solution.py:704
  40.8 0.8 %collective-permute-start.13 = (f32[256,128]{1,0:T(8,128)S(1)}, f32[256,128]{1,0:T(8,128)S(1)}, u32[]{:S(2)}, u32[]{:S(2)}) collective-permute-start(f32[256,128]{1,0:T(8,128)S(1)} %bitcast.14), channel_id=1, source_target_pairs={{0,16},{1,9},{8,24},{9,1},{16,0},{17,25},{24,8},{25,17},{2,18},{3,... | collective-permute-start | bytes 393224 | tf_op jit(solution)/shard_map/ppermute | solution.py:704
  41.6 0.7 %collective-permute-start.11 = (f32[256,128]{1,0:T(8,128)S(1)}, f32[256,128]{1,0:T(8,128)S(1)}, u32[]{:S(2)}, u32[]{:S(2)}) collective-permute-start(f32[256,128]{1,0:T(8,128)S(1)} %bitcast.13), channel_id=1, source_target_pairs={{0,8},{1,17},{8,0},{9,25},{16,24},{17,1},{24,16},{25,9},{2,10},{3,... | collective-permute-start | bytes 393224 | tf_op jit(solution)/shard_map/ppermute | solution.py:704
  42.3 3.7 %collective-permute-done.12.refs_2_ = f32[256,128]{1,0:T(8,128)S(1)} collective-permute-done((f32[256,128]{1,0:T(8,128)S(1)}, f32[256,128]{1,0:T(8,128)S(1)}, u32[]{:S(2)}, u32[]{:S(2)}) %collective-permute-start.12) | collective-permute-done | bytes 131104 | tf_op jit(solution)/shard_map/ppermute | solution.py:704
  46.0 2.2 %collective-permute-done.13.refs_3_ = f32[256,128]{1,0:T(8,128)S(1)} collective-permute-done((f32[256,128]{1,0:T(8,128)S(1)}, f32[256,128]{1,0:T(8,128)S(1)}, u32[]{:S(2)}, u32[]{:S(2)}) %collective-permute-start.13) | collective-permute-done | bytes 131104 | tf_op jit(solution)/shard_map/ppermute | solution.py:704
  48.3 0.0 collective-permute-done.11.refs_1_
  48.3 1.0 %shard_map.56 = (f32[1,8,64,128]{3,2,1,0:T(8,128)}, f32[1,8,64,128]{3,2,1,0:T(8,128)}) custom-call(f32[256,128]{1,0:T(8,128)S(1)} %bitcast.8, f32[256,128]{1,0:T(8,128)S(1)} %collective-permute-done.11.refs_1_, f32[256,128]{1,0:T(8,128)S(1)} %collective-permute-done.12.refs_2_, f32[256,128]{1,0:T(8,128)S(1)} %collective-permute-done.13.refs_3_), custom_call_target="tpu_custom_call" | custom-call | tf_op jit(solution)/shard_map/pallas_call | solution.py:810
  (6 shorter events, 0.1 us)
Async XLA Ops:
  2.0 7.9 %collective-permute-start = (f32[256,128]{1,0:T(8,128)S(1)}, f32[256,128]{1,0:T(8,128)S(1)}, u32[]{:S(2)}, u32[]{:S(2)}) collective-permute-start(f32[256,128]{1,0:T(8,128)S(1)} %get-tuple-element.51), channel_id=1, source_target_pairs={{0,24},{1,25},{8,16},{9,17},{16,8},{17,9},{24,0},{25,1},{2,26},{3,... | collective-permute-start | bytes 393224 | tf_op jit(solution)/shard_map/ppermute | solution.py:704
  5.9 6.6 %collective-permute-start.1 = (f32[256,128]{1,0:T(8,128)S(1)}, f32[256,128]{1,0:T(8,128)S(1)}, u32[]{:S(2)}, u32[]{:S(2)}) collective-permute-start(f32[256,128]{1,0:T(8,128)S(1)} %get-tuple-element.52), channel_id=1, source_target_pairs={{0,8},{1,17},{8,0},{9,25},{16,24},{17,1},{24,16},{25,9},{2,10},{3,... | collective-permute-start | bytes 393224 | tf_op jit(solution)/shard_map/ppermute | solution.py:704
  6.5 6.0 %collective-permute-start.2 = (f32[256,128]{1,0:T(8,128)S(1)}, f32[256,128]{1,0:T(8,128)S(1)}, u32[]{:S(2)}, u32[]{:S(2)}) collective-permute-start(f32[256,128]{1,0:T(8,128)S(1)} %get-tuple-element.53), channel_id=1, source_target_pairs={{0,16},{1,9},{8,24},{9,1},{16,0},{17,25},{24,8},{25,17},{2,18},{3,... | collective-permute-start | bytes 393224 | tf_op jit(solution)/shard_map/ppermute | solution.py:704
  12.6 2.2 %collective-permute-start.3 = (f32[4,13,8,128]{3,2,1,0:T(8,128)S(1)}, f32[4,13,8,128]{3,2,1,0:T(8,128)S(1)}, u32[]{:S(2)}, u32[]{:S(2)}) collective-permute-start(f32[4,13,8,128]{3,2,1,0:T(8,128)S(1)} %get-tuple-element.54), channel_id=1, source_target_pairs={{0,1},{1,0},{8,24},{9,25},{24,8},{25,9},{16,18},{17,19},{18,16},{1... | collective-permute-start | bytes 638984 | tf_op jit(solution)/shard_map/ppermute | solution.py:722
  12.6 7.7 %collective-permute-start.4 = (f32[4,13,8,128]{3,2,1,0:T(8,128)S(1)}, f32[4,13,8,128]{3,2,1,0:T(8,128)S(1)}, u32[]{:S(2)}, u32[]{:S(2)}) collective-permute-start(f32[4,13,8,128]{3,2,1,0:T(8,128)S(1)} %get-tuple-element.55), channel_id=1, source_target_pairs={{0,8},{1,9},{8,0},{9,1},{24,16},{25,17},{16,24},{17,25},{18,2},{19... | collective-permute-start | bytes 638984 | tf_op jit(solution)/shard_map/ppermute | solution.py:722
  14.7 5.7 %collective-permute-start.6 = (f32[4,16,2,8,128]{4,3,2,1,0:T(8,128)S(1)}, f32[4,16,2,8,128]{4,3,2,1,0:T(8,128)S(1)}, u32[]{:S(2)}, u32[]{:S(2)}) collective-permute-start(f32[4,16,2,8,128]{4,3,2,1,0:T(8,128)S(1)} %get-tuple-element.56.c), channel_id=1, source_target_pairs={{0,1},{1,0},{2,3},{3,2},{4,5},{5,4},{6,7},{7,6},{8,9},{9,8},{10,11... | collective-permute-start | bytes 1572872 | tf_op jit(solution)/shard_map/ppermute | solution.py:689
  20.3 2.0 %collective-permute-start.5 = (f32[8,13,8,128]{3,2,1,0:T(8,128)S(1)}, f32[8,13,8,128]{3,2,1,0:T(8,128)S(1)}, u32[]{:S(2)}, u32[]{:S(2)}) collective-permute-start(f32[8,13,8,128]{3,2,1,0:T(8,128)S(1)} %constant_dynamic-update-slice_fusion.sides), channel_id=1, source_target_pairs={{0,1},{1,0},{2,3},{3,2},{4,5},{5,4},{6,7},{7,6},{8,9},{9,8},{10,11... | collective-permute-start | bytes 1277960 | tf_op jit(solution)/shard_map/ppermute | solution.py:689
  25.7 5.1 %collective-permute-start.7 = (f32[144,128]{1,0:T(8,128)S(1)}, f32[144,128]{1,0:T(8,128)S(1)}, u32[]{:S(2)}, u32[]{:S(2)}) collective-permute-start(f32[144,128]{1,0:T(8,128)S(1)} %get-tuple-element.73), channel_id=1, source_target_pairs={{0,8},{8,0},{24,16},{16,24},{18,2},{2,18},{10,26},{26,10},{28,20},... | collective-permute-start | bytes 221192 | tf_op jit(solution)/shard_map/ppermute | solution.py:738
  26.1 7.0 %collective-permute-start.9 = (f32[80,128]{1,0:T(8,128)S(1)}, f32[80,128]{1,0:T(8,128)S(1)}, u32[]{:S(2)}, u32[]{:S(2)}) collective-permute-start(f32[80,128]{1,0:T(8,128)S(1)} %get-tuple-element.74.pack), channel_id=1, source_target_pairs={{0,16},{8,18},{24,2},{16,0},{18,8},{2,24},{10,20},{26,4},{28,12},{... | collective-permute-start | bytes 122888 | tf_op jit(solution)/shard_map/ppermute | solution.py:738
  28.1 4.9 %collective-permute-start.8 = (f32[80,128]{1,0:T(8,128)S(1)}, f32[80,128]{1,0:T(8,128)S(1)}, u32[]{:S(2)}, u32[]{:S(2)}) collective-permute-start(f32[80,128]{1,0:T(8,128)S(1)} %get-tuple-element.74.pack), channel_id=1, source_target_pairs={{0,24},{8,16},{24,0},{16,8},{18,10},{2,26},{10,18},{26,2},{28,4},{... | collective-permute-start | bytes 122888 | tf_op jit(solution)/shard_map/ppermute | solution.py:738
  33.1 2.2 %collective-permute-start.10 = (f32[304,128]{1,0:T(8,128)S(1)}, f32[304,128]{1,0:T(8,128)S(1)}, u32[]{:S(2)}, u32[]{:S(2)}) collective-permute-start(f32[304,128]{1,0:T(8,128)S(1)} %constant_dynamic-update-slice_fusion.2.mine), channel_id=1, source_target_pairs={{0,1},{1,0},{2,3},{3,2},{4,5},{5,4},{6,7},{7,6},{8,9},{9,8},{10,11... | collective-permute-start | bytes 466952 | tf_op jit(solution)/shard_map/ppermute | solution.py:689
  38.7 7.3 %collective-permute-start.12 = (f32[256,128]{1,0:T(8,128)S(1)}, f32[256,128]{1,0:T(8,128)S(1)}, u32[]{:S(2)}, u32[]{:S(2)}) collective-permute-start(f32[256,128]{1,0:T(8,128)S(1)} %bitcast.15), channel_id=1, source_target_pairs={{0,24},{1,25},{8,16},{9,17},{16,8},{17,9},{24,0},{25,1},{2,26},{3,... | collective-permute-start | bytes 393224 | tf_op jit(solution)/shard_map/ppermute | solution.py:704
  40.8 7.4 %collective-permute-start.13 = (f32[256,128]{1,0:T(8,128)S(1)}, f32[256,128]{1,0:T(8,128)S(1)}, u32[]{:S(2)}, u32[]{:S(2)}) collective-permute-start(f32[256,128]{1,0:T(8,128)S(1)} %bitcast.14), channel_id=1, source_target_pairs={{0,16},{1,9},{8,24},{9,1},{16,0},{17,25},{24,8},{25,17},{2,18},{3,... | collective-permute-start | bytes 393224 | tf_op jit(solution)/shard_map/ppermute | solution.py:704
  41.6 6.7 %collective-permute-start.11 = (f32[256,128]{1,0:T(8,128)S(1)}, f32[256,128]{1,0:T(8,128)S(1)}, u32[]{:S(2)}, u32[]{:S(2)}) collective-permute-start(f32[256,128]{1,0:T(8,128)S(1)} %bitcast.13), channel_id=1, source_target_pairs={{0,8},{1,17},{8,0},{9,25},{16,24},{17,1},{24,16},{25,9},{2,10},{3,... | collective-permute-start | bytes 393224 | tf_op jit(solution)/shard_map/ppermute | solution.py:704

commit v8 on v7

--- a/solution.py
+++ b/solution.py
@@ -29,7 +29,7 @@
         self.paired = self.gz == 2
         self.ring = [0, 1, 3, 2] if self.gx == 4 else list(range(self.gx))
         self.place = [self.ring.index(i) for i in range(self.gx)]
-        self.back = [0, 2, 1, 3] if self.gx == 4 else list(range(self.gx))
+        self.back = [0, 2, 3, 1] if self.gx == 4 else list(range(self.gx))
 
     def device(self, block):
         j, q = divmod(block, self.gx)

time: 49.4 us -> 48.7 us (0.986)
  waiting for transfers between devices: 20.3 us -> 19.6 us
    ppermute x6, waiting for transfers between devices: 11.9 us -> 11.2 us  [exchange(): got.append(lax.ppermute(parts[slot], ('gx', 'gz'), pairs))]
where the time goes in v8:
time: 48.7 us; the launch traced here: 48.5 us
  waiting for transfers between devices  19.6 us (40%)
  starting transfers between devices  16.7 us (34%)
  Pallas kernels  11.4 us (23%)
  between operations  0.74 us (2%)
    ppermute x6, waiting for transfers between devices, exchange(): got.append(lax.ppermute(parts[slot], ('gx', 'gz'), pairs))  11.2 us
    ppermute x6, starting transfers between devices, exchange(): got.append(lax.ppermute(parts[slot], ('gx', 'gz'), pairs))  8.16 us
    ppermute x2, waiting for transfers between devices, swap_blocks(): return lax.ppermute(a, ('gx', 'gy', 'gz'), pairs)  5.53 us
    ppermute x3, starting transfers between devices, swap_blocks_apart(): return lax.ppermute(a, ('gx', 'gy', 'gz'), pairs)  5.12 us
    pallas_call x1, Pallas kernels, on_device(): call(functools.partial(up_kernel, plan), [in_vmem(gx, by, 2, px, LANES)]...  3.43 us
    pallas_call x1, Pallas kernels, on_device(): call(functools.partial(down_kernel, plan), outs, scratch, input_output_al...  3.38 us
    ppermute x3, waiting for transfers between devices, swap_blocks_apart(): return lax.ppermute(a, ('gx', 'gy', 'gz'), pairs)  2.2 us
    ppermute x2, starting transfers between devices, swap_blocks(): return lax.ppermute(a, ('gx', 'gy', 'gz'), pairs)  2.19 us
  transfers between devices with their start and end apart: 14, of which 7 were waited for; matrix products, arithmetic and copies ran while one was open for 0% of the time, Pallas kernels for 5%

profile of v8, /device:TPU:0, one launch (start us, length us, event | category | flops | bytes accessed | tf_op | source)
XLA Modules:
  0.0 48.5 jit_solution(2350041301559829045)
XLA Ops:
  0.6 1.3 %shard_map.50 = (f32[256,128]{1,0:T(8,128)S(1)}, f32[256,128]{1,0:T(8,128)S(1)}, f32[256,128]{1,0:T(8,128)S(1)}, f32[256,128]{1,0:T(8,128)S(1)}) custom-call(s32[8,64,128]{2,1,0:T(8,128)} %phase_in.1, f32[8,64,128]{2,1,0:T(8,128)} %density_in.1, f32[1,8,64,128]{3,2,1,0:T(8,128)} %rhs_in.1), custom_call_target="tpu_custom_call" | custom-call | tf_op jit(solution)/shard_map/pallas_call | solution.py:757
  2.0 4.0 %collective-permute-start = (f32[256,128]{1,0:T(8,128)S(1)}, f32[256,128]{1,0:T(8,128)S(1)}, u32[]{:S(2)}, u32[]{:S(2)}) collective-permute-start(f32[256,128]{1,0:T(8,128)S(1)} %get-tuple-element.51), channel_id=1, source_target_pairs={{0,24},{1,25},{8,16},{9,17},{16,8},{17,9},{24,0},{25,1},{2,26},{3,... | collective-permute-start | bytes 393224 | tf_op jit(solution)/shard_map/ppermute | solution.py:704
  5.9 0.5 %collective-permute-start.1 = (f32[256,128]{1,0:T(8,128)S(1)}, f32[256,128]{1,0:T(8,128)S(1)}, u32[]{:S(2)}, u32[]{:S(2)}) collective-permute-start(f32[256,128]{1,0:T(8,128)S(1)} %get-tuple-element.52), channel_id=1, source_target_pairs={{0,8},{1,17},{8,0},{9,25},{16,24},{17,1},{24,16},{25,9},{2,10},{3,... | collective-permute-start | bytes 393224 | tf_op jit(solution)/shard_map/ppermute | solution.py:704
  6.5 0.1 collective-permute-start.2
  6.6 3.3 %collective-permute-done = f32[256,128]{1,0:T(8,128)S(1)} collective-permute-done((f32[256,128]{1,0:T(8,128)S(1)}, f32[256,128]{1,0:T(8,128)S(1)}, u32[]{:S(2)}, u32[]{:S(2)}) %collective-permute-start) | collective-permute-done | bytes 131104 | tf_op jit(solution)/shard_map/ppermute | solution.py:704
  9.8 2.6 %collective-permute-done.1 = f32[256,128]{1,0:T(8,128)S(1)} collective-permute-done((f32[256,128]{1,0:T(8,128)S(1)}, f32[256,128]{1,0:T(8,128)S(1)}, u32[]{:S(2)}, u32[]{:S(2)}) %collective-permute-start.1) | collective-permute-done | bytes 131104 | tf_op jit(solution)/shard_map/ppermute | solution.py:704
  12.5 0.0 collective-permute-done.2
  12.5 0.1 shard_map.51
  12.6 0.1 collective-permute-start.3
  12.6 2.1 %collective-permute-start.4 = (f32[4,13,8,128]{3,2,1,0:T(8,128)S(1)}, f32[4,13,8,128]{3,2,1,0:T(8,128)S(1)}, u32[]{:S(2)}, u32[]{:S(2)}) collective-permute-start(f32[4,13,8,128]{3,2,1,0:T(8,128)S(1)} %get-tuple-element.55), channel_id=1, source_target_pairs={{0,8},{1,9},{8,0},{9,1},{24,16},{25,17},{16,24},{17,25},{18,2},{19... | collective-permute-start | bytes 638984 | tf_op jit(solution)/shard_map/ppermute | solution.py:722
  14.7 0.0 collective-permute-start.6
  14.7 0.0 collective-permute-done.3
  14.8 5.5 %collective-permute-done.4 = f32[4,13,8,128]{3,2,1,0:T(8,128)S(1)} collective-permute-done((f32[4,13,8,128]{3,2,1,0:T(8,128)S(1)}, f32[4,13,8,128]{3,2,1,0:T(8,128)S(1)}, u32[]{:S(2)}, u32[]{:S(2)}) %collective-permute-start.4) | collective-permute-done | bytes 213024 | tf_op jit(solution)/shard_map/ppermute | solution.py:722
  20.3 0.1 collective-permute-start.5
  20.4 0.0 collective-permute-done.6.zc
  20.4 1.9 %shard_map.52 = (f32[30,2,32,128]{3,2,1,0:T(8,128)S(1)}, f32[30,2,32,128]{3,2,1,0:T(8,128)S(1)}, f32[30,2,32,128]{3,2,1,0:T(8,128)S(1)}, f32[30,2,32,128]{3,2,1,...) custom-call(f32[4,16,2,8,128]{4,3,2,1,0:T(8,128)S(1)} %get-tuple-ele, ...), custom_call_target="tpu_custom_call" | custom-call | bytes 9000000 | tf_op jit(solution)/shard_map/pallas_call | solution.py:782
  22.3 0.0 collective-permute-done.5.zsides
  22.3 3.4 %shard_map.53 = (f32[30,2,32,128]{3,2,1,0:T(8,128)S(1)}, f32[30,2,32,128]{3,2,1,0:T(8,128)S(1)}, f32[30,2,32,128]{3,2,1,0:T(8,128)S(1)}, f32[30,2,32,128]{3,2,1,...) custom-call(f32[8,13,8,128]{3,2,1,0:T(8,128)S(1)} %constant_dynamic-, ...), custom_call_target="tpu_custom_call", output_to_operand_aliasing={{0}: (2, {}), {1}: (3, {}), {2}: (4, {}), {3}: (5, {}), {4}... | custom-call | tf_op jit(solution)/shard_map/pallas_call | solution.py:786
  25.7 0.4 collective-permute-start.7
  26.1 2.1 %collective-permute-start.9 = (f32[80,128]{1,0:T(8,128)S(1)}, f32[80,128]{1,0:T(8,128)S(1)}, u32[]{:S(2)}, u32[]{:S(2)}) collective-permute-start(f32[80,128]{1,0:T(8,128)S(1)} %get-tuple-element.74.pack), channel_id=1, source_target_pairs={{0,16},{8,18},{24,2},{16,0},{18,8},{2,24},{10,20},{26,4},{28,12},{... | collective-permute-start | bytes 122888 | tf_op jit(solution)/shard_map/ppermute | solution.py:738
  28.1 2.7 %collective-permute-start.8 = (f32[80,128]{1,0:T(8,128)S(1)}, f32[80,128]{1,0:T(8,128)S(1)}, u32[]{:S(2)}, u32[]{:S(2)}) collective-permute-start(f32[80,128]{1,0:T(8,128)S(1)} %get-tuple-element.74.pack), channel_id=1, source_target_pairs={{0,24},{8,16},{24,0},{16,8},{18,10},{2,26},{10,18},{26,2},{28,4},{... | collective-permute-start | bytes 122888 | tf_op jit(solution)/shard_map/ppermute | solution.py:738
  30.8 0.0 collective-permute-done.7
  30.9 2.2 %collective-permute-done.8 = f32[80,128]{1,0:T(8,128)S(1)} collective-permute-done((f32[80,128]{1,0:T(8,128)S(1)}, f32[80,128]{1,0:T(8,128)S(1)}, u32[]{:S(2)}, u32[]{:S(2)}) %collective-permute-start.8) | collective-permute-done | bytes 40992 | tf_op jit(solution)/shard_map/ppermute | solution.py:738
  33.0 0.0 collective-permute-done.9
  33.1 1.2 %collective-permute-start.10 = (f32[304,128]{1,0:T(8,128)S(1)}, f32[304,128]{1,0:T(8,128)S(1)}, u32[]{:S(2)}, u32[]{:S(2)}) collective-permute-start(f32[304,128]{1,0:T(8,128)S(1)} %constant_dynamic-update-slice_fusion.2.mine), channel_id=1, source_target_pairs={{0,1},{1,0},{2,3},{3,2},{4,5},{5,4},{6,7},{7,6},{8,9},{9,8},{10,11... | collective-permute-start | bytes 466952 | tf_op jit(solution)/shard_map/ppermute | solution.py:689
  34.2 0.3 shard_map.54
  34.5 0.7 %collective-permute-done.10.theirs = f32[304,128]{1,0:T(8,128)S(1)} collective-permute-done((f32[304,128]{1,0:T(8,128)S(1)}, f32[304,128]{1,0:T(8,128)S(1)}, u32[]{:S(2)}, u32[]{:S(2)}) %collective-permute-start.10) | collective-permute-done | bytes 155680 | tf_op jit(solution)/shard_map/ppermute | solution.py:689
  35.2 3.4 %shard_map.55 = (f32[4,16,2,8,128]{4,3,2,1,0:T(8,128)S(1)}, f32[29,2,8,128]{3,2,1,0:T(8,128)S(1)}, f32[29,2,8,128]{3,2,1,0:T(8,128)S(1)}, f32[29,2,8,128]{3,2,1,...) custom-call(f32[304,128]{1,0:T(8,128)S(1)} %collective-permute-done., ...), custom_call_target="tpu_custom_call", output_to_operand_aliasing={{1}: (1, {}), {2}: (2, {}), {3}: (3, {}), {4}: (4, {}), {5}... | custom-call | tf_op jit(solution)/shard_map/pallas_call | solution.py:802
  38.7 0.6 %collective-permute-start.12 = (f32[256,128]{1,0:T(8,128)S(1)}, f32[256,128]{1,0:T(8,128)S(1)}, u32[]{:S(2)}, u32[]{:S(2)}) collective-permute-start(f32[256,128]{1,0:T(8,128)S(1)} %bitcast.15), channel_id=1, source_target_pairs={{0,16},{1,9},{8,24},{9,1},{16,0},{17,25},{24,8},{25,17},{2,18},{3,... | collective-permute-start | bytes 393224 | tf_op jit(solution)/shard_map/ppermute | solution.py:704
  39.3 2.2 %collective-permute-start.13 = (f32[256,128]{1,0:T(8,128)S(1)}, f32[256,128]{1,0:T(8,128)S(1)}, u32[]{:S(2)}, u32[]{:S(2)}) collective-permute-start(f32[256,128]{1,0:T(8,128)S(1)} %bitcast.14), channel_id=1, source_target_pairs={{0,24},{1,25},{8,16},{9,17},{16,8},{17,9},{24,0},{25,1},{2,26},{3,... | collective-permute-start | bytes 393224 | tf_op jit(solution)/shard_map/ppermute | solution.py:704
  41.6 0.7 %collective-permute-start.11 = (f32[256,128]{1,0:T(8,128)S(1)}, f32[256,128]{1,0:T(8,128)S(1)}, u32[]{:S(2)}, u32[]{:S(2)}) collective-permute-start(f32[256,128]{1,0:T(8,128)S(1)} %bitcast.13), channel_id=1, source_target_pairs={{0,8},{1,17},{8,0},{9,25},{16,24},{17,1},{24,16},{25,9},{2,10},{3,... | collective-permute-start | bytes 393224 | tf_op jit(solution)/shard_map/ppermute | solution.py:704
  42.3 4.7 %collective-permute-done.12.refs_2_ = f32[256,128]{1,0:T(8,128)S(1)} collective-permute-done((f32[256,128]{1,0:T(8,128)S(1)}, f32[256,128]{1,0:T(8,128)S(1)}, u32[]{:S(2)}, u32[]{:S(2)}) %collective-permute-start.12) | collective-permute-done | bytes 131104 | tf_op jit(solution)/shard_map/ppermute | solution.py:704
  47.0 0.0 collective-permute-done.13.refs_3_
  47.0 0.6 %collective-permute-done.11.refs_1_ = f32[256,128]{1,0:T(8,128)S(1)} collective-permute-done((f32[256,128]{1,0:T(8,128)S(1)}, f32[256,128]{1,0:T(8,128)S(1)}, u32[]{:S(2)}, u32[]{:S(2)}) %collective-permute-start.11) | collective-permute-done | bytes 131104 | tf_op jit(solution)/shard_map/ppermute | solution.py:704
  47.6 1.0 %shard_map.56 = (f32[1,8,64,128]{3,2,1,0:T(8,128)}, f32[1,8,64,128]{3,2,1,0:T(8,128)}) custom-call(f32[256,128]{1,0:T(8,128)S(1)} %bitcast.8, f32[256,128]{1,0:T(8,128)S(1)} %collective-permute-done.11.refs_1_, f32[256,128]{1,0:T(8,128)S(1)} %collective-permute-done.12.refs_2_, f32[256,128]{1,0:T(8,128)S(1)} %collective-permute-done.13.refs_3_), custom_call_target="tpu_custom_call" | custom-call | tf_op jit(solution)/shard_map/pallas_call | solution.py:810
  (6 shorter events, 0.1 us)
Async XLA Ops:
  2.0 7.9 %collective-permute-start = (f32[256,128]{1,0:T(8,128)S(1)}, f32[256,128]{1,0:T(8,128)S(1)}, u32[]{:S(2)}, u32[]{:S(2)}) collective-permute-start(f32[256,128]{1,0:T(8,128)S(1)} %get-tuple-element.51), channel_id=1, source_target_pairs={{0,24},{1,25},{8,16},{9,17},{16,8},{17,9},{24,0},{25,1},{2,26},{3,... | collective-permute-start | bytes 393224 | tf_op jit(solution)/shard_map/ppermute | solution.py:704
  5.9 6.6 %collective-permute-start.1 = (f32[256,128]{1,0:T(8,128)S(1)}, f32[256,128]{1,0:T(8,128)S(1)}, u32[]{:S(2)}, u32[]{:S(2)}) collective-permute-start(f32[256,128]{1,0:T(8,128)S(1)} %get-tuple-element.52), channel_id=1, source_target_pairs={{0,8},{1,17},{8,0},{9,25},{16,24},{17,1},{24,16},{25,9},{2,10},{3,... | collective-permute-start | bytes 393224 | tf_op jit(solution)/shard_map/ppermute | solution.py:704
  6.5 6.0 %collective-permute-start.2 = (f32[256,128]{1,0:T(8,128)S(1)}, f32[256,128]{1,0:T(8,128)S(1)}, u32[]{:S(2)}, u32[]{:S(2)}) collective-permute-start(f32[256,128]{1,0:T(8,128)S(1)} %get-tuple-element.53), channel_id=1, source_target_pairs={{0,16},{1,9},{8,24},{9,1},{16,0},{17,25},{24,8},{25,17},{2,18},{3,... | collective-permute-start | bytes 393224 | tf_op jit(solution)/shard_map/ppermute | solution.py:704
  12.6 2.2 %collective-permute-start.3 = (f32[4,13,8,128]{3,2,1,0:T(8,128)S(1)}, f32[4,13,8,128]{3,2,1,0:T(8,128)S(1)}, u32[]{:S(2)}, u32[]{:S(2)}) collective-permute-start(f32[4,13,8,128]{3,2,1,0:T(8,128)S(1)} %get-tuple-element.54), channel_id=1, source_target_pairs={{0,1},{1,0},{8,24},{9,25},{24,8},{25,9},{16,18},{17,19},{18,16},{1... | collective-permute-start | bytes 638984 | tf_op jit(solution)/shard_map/ppermute | solution.py:722
  12.6 7.7 %collective-permute-start.4 = (f32[4,13,8,128]{3,2,1,0:T(8,128)S(1)}, f32[4,13,8,128]{3,2,1,0:T(8,128)S(1)}, u32[]{:S(2)}, u32[]{:S(2)}) collective-permute-start(f32[4,13,8,128]{3,2,1,0:T(8,128)S(1)} %get-tuple-element.55), channel_id=1, source_target_pairs={{0,8},{1,9},{8,0},{9,1},{24,16},{25,17},{16,24},{17,25},{18,2},{19... | collective-permute-start | bytes 638984 | tf_op jit(solution)/shard_map/ppermute | solution.py:722
  14.7 5.7 %collective-permute-start.6 = (f32[4,16,2,8,128]{4,3,2,1,0:T(8,128)S(1)}, f32[4,16,2,8,128]{4,3,2,1,0:T(8,128)S(1)}, u32[]{:S(2)}, u32[]{:S(2)}) collective-permute-start(f32[4,16,2,8,128]{4,3,2,1,0:T(8,128)S(1)} %get-tuple-element.56.c), channel_id=1, source_target_pairs={{0,1},{1,0},{2,3},{3,2},{4,5},{5,4},{6,7},{7,6},{8,9},{9,8},{10,11... | collective-permute-start | bytes 1572872 | tf_op jit(solution)/shard_map/ppermute | solution.py:689
  20.3 2.0 %collective-permute-start.5 = (f32[8,13,8,128]{3,2,1,0:T(8,128)S(1)}, f32[8,13,8,128]{3,2,1,0:T(8,128)S(1)}, u32[]{:S(2)}, u32[]{:S(2)}) collective-permute-start(f32[8,13,8,128]{3,2,1,0:T(8,128)S(1)} %constant_dynamic-update-slice_fusion.sides), channel_id=1, source_target_pairs={{0,1},{1,0},{2,3},{3,2},{4,5},{5,4},{6,7},{7,6},{8,9},{9,8},{10,11... | collective-permute-start | bytes 1277960 | tf_op jit(solution)/shard_map/ppermute | solution.py:689
  25.7 5.1 %collective-permute-start.7 = (f32[144,128]{1,0:T(8,128)S(1)}, f32[144,128]{1,0:T(8,128)S(1)}, u32[]{:S(2)}, u32[]{:S(2)}) collective-permute-start(f32[144,128]{1,0:T(8,128)S(1)} %get-tuple-element.73), channel_id=1, source_target_pairs={{0,8},{8,0},{24,16},{16,24},{18,2},{2,18},{10,26},{26,10},{28,20},... | collective-permute-start | bytes 221192 | tf_op jit(solution)/shard_map/ppermute | solution.py:738
  26.1 7.0 %collective-permute-start.9 = (f32[80,128]{1,0:T(8,128)S(1)}, f32[80,128]{1,0:T(8,128)S(1)}, u32[]{:S(2)}, u32[]{:S(2)}) collective-permute-start(f32[80,128]{1,0:T(8,128)S(1)} %get-tuple-element.74.pack), channel_id=1, source_target_pairs={{0,16},{8,18},{24,2},{16,0},{18,8},{2,24},{10,20},{26,4},{28,12},{... | collective-permute-start | bytes 122888 | tf_op jit(solution)/shard_map/ppermute | solution.py:738
  28.1 4.9 %collective-permute-start.8 = (f32[80,128]{1,0:T(8,128)S(1)}, f32[80,128]{1,0:T(8,128)S(1)}, u32[]{:S(2)}, u32[]{:S(2)}) collective-permute-start(f32[80,128]{1,0:T(8,128)S(1)} %get-tuple-element.74.pack), channel_id=1, source_target_pairs={{0,24},{8,16},{24,0},{16,8},{18,10},{2,26},{10,18},{26,2},{28,4},{... | collective-permute-start | bytes 122888 | tf_op jit(solution)/shard_map/ppermute | solution.py:738
  33.1 2.2 %collective-permute-start.10 = (f32[304,128]{1,0:T(8,128)S(1)}, f32[304,128]{1,0:T(8,128)S(1)}, u32[]{:S(2)}, u32[]{:S(2)}) collective-permute-start(f32[304,128]{1,0:T(8,128)S(1)} %constant_dynamic-update-slice_fusion.2.mine), channel_id=1, source_target_pairs={{0,1},{1,0},{2,3},{3,2},{4,5},{5,4},{6,7},{7,6},{8,9},{9,8},{10,11... | collective-permute-start | bytes 466952 | tf_op jit(solution)/shard_map/ppermute | solution.py:689
  38.7 8.2 %collective-permute-start.12 = (f32[256,128]{1,0:T(8,128)S(1)}, f32[256,128]{1,0:T(8,128)S(1)}, u32[]{:S(2)}, u32[]{:S(2)}) collective-permute-start(f32[256,128]{1,0:T(8,128)S(1)} %bitcast.15), channel_id=1, source_target_pairs={{0,16},{1,9},{8,24},{9,1},{16,0},{17,25},{24,8},{25,17},{2,18},{3,... | collective-permute-start | bytes 393224 | tf_op jit(solution)/shard_map/ppermute | solution.py:704
  39.3 7.6 %collective-permute-start.13 = (f32[256,128]{1,0:T(8,128)S(1)}, f32[256,128]{1,0:T(8,128)S(1)}, u32[]{:S(2)}, u32[]{:S(2)}) collective-permute-start(f32[256,128]{1,0:T(8,128)S(1)} %bitcast.14), channel_id=1, source_target_pairs={{0,24},{1,25},{8,16},{9,17},{16,8},{17,9},{24,0},{25,1},{2,26},{3,... | collective-permute-start | bytes 393224 | tf_op jit(solution)/shard_map/ppermute | solution.py:704
  41.6 6.0 %collective-permute-start.11 = (f32[256,128]{1,0:T(8,128)S(1)}, f32[256,128]{1,0:T(8,128)S(1)}, u32[]{:S(2)}, u32[]{:S(2)}) collective-permute-start(f32[256,128]{1,0:T(8,128)S(1)} %bitcast.13), channel_id=1, source_target_pairs={{0,8},{1,17},{8,0},{9,25},{16,24},{17,1},{24,16},{25,9},{2,10},{3,... | collective-permute-start | bytes 393224 | tf_op jit(solution)/shard_map/ppermute | solution.py:704

commit v9 on v8

--- a/solution.py
+++ b/solution.py
@@ -705,6 +705,12 @@
     return got
 
 
+def after(arrays, other):
+    shapes = [in_vmem(*a.shape) for a in arrays]
+    pairs = {k: k for k in range(len(arrays))}
+    return call(lambda *refs: None, shapes, input_output_aliases=pairs)(*pinned(*arrays, other))
+
+
 def partners(plan, k, one):
     partner = [None] * plan.blocks
     for b in range(plan.blocks - k):
@@ -765,8 +771,10 @@
         functools.partial(gather_kernel, plan),
         [in_vmem(gx, by, 2, px, LANES)] + [in_vmem(gx, HALO + HALO_RHS, px, LANES)] * 2,
     )(*pinned(*parts))
-    sides = jnp.concatenate([swap_blocks(plan, sets[one], 1, one) for one in (1, 0)], axis=0)
+    sides = [swap_blocks(plan, sets[one], 1, one) for one in (1, 0)]
     zc = beside_in_z(plan, c)
+    inner = call(functools.partial(inner_kernel, plan), Finest.shapes(plan), work=9_000_000)(*pinned(c, zc))
+    sides = jnp.concatenate(after(sides, inner[-1]), axis=0)
     zsides = beside_in_z(plan, sides)
 
     own, own2 = by // 2, by // 4
@@ -779,7 +787,6 @@
     def level1(n):
         return in_vmem(n, 2, nx // 2, LANES)
 
-    inner = call(functools.partial(inner_kernel, plan), Finest.shapes(plan), work=9_000_000)(*pinned(c, zc))
     near_count = 1 if plan.paired else 2
     outs = Finest.shapes(plan) + [in_vmem(size, LANES)] + [in_vmem(side, LANES)] * near_count + [level1(own + 8)] * 2
     scratch = [level1(own + 8), level1(own2), in_vmem(2, 2, size, LANES), in_vmem(1, 2, 4 * (nx // 2), LANES)]

time: 48.7 us -> 49 us (level)
  waiting for transfers between devices: 19.6 us -> 20.1 us
    ppermute x3, waiting for transfers between devices: 0.71 us -> 2.74 us  [beside_in_z(): return lax.ppermute(a, 'gz', [(0, 1), (1, 0)])]
    ppermute x2, waiting for transfers between devices: 5.53 us -> 3.68 us  [swap_blocks(): return lax.ppermute(a, ('gx', 'gy', 'gz'), pairs)]
    ppermute x3, starting transfers between devices: 1.23 us -> 0.29 us  [beside_in_z(): return lax.ppermute(a, 'gz', [(0, 1), (1, 0)])]
  transfers between devices with their start and end apart: 14 -> 14, of which waited for: 7 -> 9; matrix products, arithmetic and copies ran while one was open for 0% -> 0% of each run, Pallas kernels for 5% -> 4%
where the time goes in v9:
time: 49 us; the launch traced here: 48.9 us
  waiting for transfers between devices  20.1 us (41%)
  starting transfers between devices  16.6 us (34%)
  Pallas kernels  11.3 us (23%)
  between operations  0.73 us (1%)
    ppermute x6, waiting for transfers between devices, exchange(): got.append(lax.ppermute(parts[slot], ('gx', 'gz'), pairs))  11.1 us
    ppermute x6, starting transfers between devices, exchange(): got.append(lax.ppermute(parts[slot], ('gx', 'gz'), pairs))  8.61 us
    ppermute x3, starting transfers between devices, swap_blocks_apart(): return lax.ppermute(a, ('gx', 'gy', 'gz'), pairs)  5.52 us
    ppermute x2, waiting for transfers between devices, swap_blocks(): return lax.ppermute(a, ('gx', 'gy', 'gz'), pairs)  3.68 us
    pallas_call x1, Pallas kernels, on_device(): call(functools.partial(up_kernel, plan), [in_vmem(gx, by, 2, px, LANES)]...  3.44 us
    pallas_call x1, Pallas kernels, on_device(): call(functools.partial(down_kernel, plan), outs, scratch, input_output_al...  3.34 us
    ppermute x3, waiting for transfers between devices, beside_in_z(): return lax.ppermute(a, 'gz', [(0, 1), (1, 0)])  2.74 us
    ppermute x3, waiting for transfers between devices, swap_blocks_apart(): return lax.ppermute(a, ('gx', 'gy', 'gz'), pairs)  2.61 us
  transfers between devices with their start and end apart: 14, of which 9 were waited for; matrix products, arithmetic and copies ran while one was open for 0% of the time, Pallas kernels for 4%

profile of v9, /device:TPU:0, one launch (start us, length us, event | category | flops | bytes accessed | tf_op | source)
XLA Modules:
  0.0 48.9 jit_solution(11947850337302539975)
XLA Ops:
  0.6 1.3 %shard_map.50 = (f32[256,128]{1,0:T(8,128)S(1)}, f32[256,128]{1,0:T(8,128)S(1)}, f32[256,128]{1,0:T(8,128)S(1)}, f32[256,128]{1,0:T(8,128)S(1)}) custom-call(s32[8,64,128]{2,1,0:T(8,128)} %phase_in.1, f32[8,64,128]{2,1,0:T(8,128)} %density_in.1, f32[1,8,64,128]{3,2,1,0:T(8,128)} %rhs_in.1), custom_call_target="tpu_custom_call" | custom-call | tf_op jit(solution)/shard_map/pallas_call | solution.py:763
  2.0 4.0 %collective-permute-start = (f32[256,128]{1,0:T(8,128)S(1)}, f32[256,128]{1,0:T(8,128)S(1)}, u32[]{:S(2)}, u32[]{:S(2)}) collective-permute-start(f32[256,128]{1,0:T(8,128)S(1)} %get-tuple-element.53), channel_id=1, source_target_pairs={{0,24},{1,25},{8,16},{9,17},{16,8},{17,9},{24,0},{25,1},{2,26},{3,... | collective-permute-start | bytes 393224 | tf_op jit(solution)/shard_map/ppermute | solution.py:704
  5.9 0.5 %collective-permute-start.1 = (f32[256,128]{1,0:T(8,128)S(1)}, f32[256,128]{1,0:T(8,128)S(1)}, u32[]{:S(2)}, u32[]{:S(2)}) collective-permute-start(f32[256,128]{1,0:T(8,128)S(1)} %get-tuple-element.54), channel_id=1, source_target_pairs={{0,8},{1,17},{8,0},{9,25},{16,24},{17,1},{24,16},{25,9},{2,10},{3,... | collective-permute-start | bytes 393224 | tf_op jit(solution)/shard_map/ppermute | solution.py:704
  6.5 0.1 collective-permute-start.2
  6.6 3.3 %collective-permute-done = f32[256,128]{1,0:T(8,128)S(1)} collective-permute-done((f32[256,128]{1,0:T(8,128)S(1)}, f32[256,128]{1,0:T(8,128)S(1)}, u32[]{:S(2)}, u32[]{:S(2)}) %collective-permute-start) | collective-permute-done | bytes 131104 | tf_op jit(solution)/shard_map/ppermute | solution.py:704
  9.8 2.6 %collective-permute-done.1 = f32[256,128]{1,0:T(8,128)S(1)} collective-permute-done((f32[256,128]{1,0:T(8,128)S(1)}, f32[256,128]{1,0:T(8,128)S(1)}, u32[]{:S(2)}, u32[]{:S(2)}) %collective-permute-start.1) | collective-permute-done | bytes 131104 | tf_op jit(solution)/shard_map/ppermute | solution.py:704
  12.5 0.0 collective-permute-done.2
  12.5 0.1 shard_map.51
  12.6 0.1 collective-permute-start.5
  12.6 0.5 %collective-permute-start.3 = (f32[4,13,8,128]{3,2,1,0:T(8,128)S(1)}, f32[4,13,8,128]{3,2,1,0:T(8,128)S(1)}, u32[]{:S(2)}, u32[]{:S(2)}) collective-permute-start(f32[4,13,8,128]{3,2,1,0:T(8,128)S(1)} %get-tuple-element.56), channel_id=1, source_target_pairs={{0,1},{1,0},{8,24},{9,25},{24,8},{25,9},{16,18},{17,19},{18,16},{1... | collective-permute-start | bytes 638984 | tf_op jit(solution)/shard_map/ppermute | solution.py:728
  13.1 1.7 %collective-permute-start.4 = (f32[4,13,8,128]{3,2,1,0:T(8,128)S(1)}, f32[4,13,8,128]{3,2,1,0:T(8,128)S(1)}, u32[]{:S(2)}, u32[]{:S(2)}) collective-permute-start(f32[4,13,8,128]{3,2,1,0:T(8,128)S(1)} %get-tuple-element.57), channel_id=1, source_target_pairs={{0,8},{1,9},{8,0},{9,1},{24,16},{25,17},{16,24},{17,25},{18,2},{19... | collective-permute-start | bytes 638984 | tf_op jit(solution)/shard_map/ppermute | solution.py:728
  14.8 0.0 collective-permute-done.5.zc
  14.8 1.9 %shard_map.52 = (f32[30,2,32,128]{3,2,1,0:T(8,128)S(1)}, f32[30,2,32,128]{3,2,1,0:T(8,128)S(1)}, f32[30,2,32,128]{3,2,1,0:T(8,128)S(1)}, f32[30,2,32,128]{3,2,1,...) custom-call(f32[4,16,2,8,128]{4,3,2,1,0:T(8,128)S(1)} %get-tuple-ele, ...), custom_call_target="tpu_custom_call" | custom-call | bytes 9000000 | tf_op jit(solution)/shard_map/pallas_call | solution.py:776
  16.7 0.0 collective-permute-done.3.refs_0_
  16.7 3.7 %collective-permute-done.4.refs_1_ = f32[4,13,8,128]{3,2,1,0:T(8,128)S(1)} collective-permute-done((f32[4,13,8,128]{3,2,1,0:T(8,128)S(1)}, f32[4,13,8,128]{3,2,1,0:T(8,128)S(1)}, u32[]{:S(2)}, u32[]{:S(2)}) %collective-permute-start.4) | collective-permute-done | bytes 213024 | tf_op jit(solution)/shard_map/ppermute | solution.py:728
  20.4 0.1 collective-permute-start.6
  20.5 1.8 %collective-permute-done.6.zsides = f32[8,13,8,128]{3,2,1,0:T(8,128)S(1)} collective-permute-done((f32[8,13,8,128]{3,2,1,0:T(8,128)S(1)}, f32[8,13,8,128]{3,2,1,0:T(8,128)S(1)}, u32[]{:S(2)}, u32[]{:S(2)}) %collective-permute-start.6) | collective-permute-done | bytes 426016 | tf_op jit(solution)/shard_map/ppermute | solution.py:689
  22.3 3.3 %shard_map.54 = (f32[30,2,32,128]{3,2,1,0:T(8,128)S(1)}, f32[30,2,32,128]{3,2,1,0:T(8,128)S(1)}, f32[30,2,32,128]{3,2,1,0:T(8,128)S(1)}, f32[30,2,32,128]{3,2,1,...) custom-call(f32[8,13,8,128]{3,2,1,0:T(8,128)S(1)} %constant_dynamic-, ...), custom_call_target="tpu_custom_call", output_to_operand_aliasing={{0}: (2, {}), {1}: (3, {}), {2}: (4, {}), {3}: (5, {}), {4}... | custom-call | tf_op jit(solution)/shard_map/pallas_call | solution.py:793
  25.6 1.8 %collective-permute-start.7 = (f32[144,128]{1,0:T(8,128)S(1)}, f32[144,128]{1,0:T(8,128)S(1)}, u32[]{:S(2)}, u32[]{:S(2)}) collective-permute-start(f32[144,128]{1,0:T(8,128)S(1)} %get-tuple-element.77), channel_id=1, source_target_pairs={{0,8},{8,0},{24,16},{16,24},{18,2},{2,18},{10,26},{26,10},{28,20},... | collective-permute-start | bytes 221192 | tf_op jit(solution)/shard_map/ppermute | solution.py:744
  27.4 1.4 %collective-permute-start.9 = (f32[80,128]{1,0:T(8,128)S(1)}, f32[80,128]{1,0:T(8,128)S(1)}, u32[]{:S(2)}, u32[]{:S(2)}) collective-permute-start(f32[80,128]{1,0:T(8,128)S(1)} %get-tuple-element.78.pack), channel_id=1, source_target_pairs={{0,16},{8,18},{24,2},{16,0},{18,8},{2,24},{10,20},{26,4},{28,12},{... | collective-permute-start | bytes 122888 | tf_op jit(solution)/shard_map/ppermute | solution.py:744
  28.9 2.3 %collective-permute-start.8 = (f32[80,128]{1,0:T(8,128)S(1)}, f32[80,128]{1,0:T(8,128)S(1)}, u32[]{:S(2)}, u32[]{:S(2)}) collective-permute-start(f32[80,128]{1,0:T(8,128)S(1)} %get-tuple-element.78.pack), channel_id=1, source_target_pairs={{0,24},{8,16},{24,0},{16,8},{18,10},{2,26},{10,18},{26,2},{28,4},{... | collective-permute-start | bytes 122888 | tf_op jit(solution)/shard_map/ppermute | solution.py:744
  31.2 0.0 collective-permute-done.7
  31.2 2.6 %collective-permute-done.8 = f32[80,128]{1,0:T(8,128)S(1)} collective-permute-done((f32[80,128]{1,0:T(8,128)S(1)}, f32[80,128]{1,0:T(8,128)S(1)}, u32[]{:S(2)}, u32[]{:S(2)}) %collective-permute-start.8) | collective-permute-done | bytes 40992 | tf_op jit(solution)/shard_map/ppermute | solution.py:744
  33.8 0.0 collective-permute-done.9
  33.8 0.1 collective-permute-start.10
  33.9 0.3 shard_map.55
  34.3 1.0 %collective-permute-done.10.theirs = f32[304,128]{1,0:T(8,128)S(1)} collective-permute-done((f32[304,128]{1,0:T(8,128)S(1)}, f32[304,128]{1,0:T(8,128)S(1)}, u32[]{:S(2)}, u32[]{:S(2)}) %collective-permute-start.10) | collective-permute-done | bytes 155680 | tf_op jit(solution)/shard_map/ppermute | solution.py:689
  35.2 3.4 %shard_map.56 = (f32[4,16,2,8,128]{4,3,2,1,0:T(8,128)S(1)}, f32[29,2,8,128]{3,2,1,0:T(8,128)S(1)}, f32[29,2,8,128]{3,2,1,0:T(8,128)S(1)}, f32[29,2,8,128]{3,2,1,...) custom-call(f32[304,128]{1,0:T(8,128)S(1)} %collective-permute-done., ...), custom_call_target="tpu_custom_call", output_to_operand_aliasing={{1}: (1, {}), {2}: (2, {}), {3}: (3, {}), {4}: (4, {}), {5}... | custom-call | tf_op jit(solution)/shard_map/pallas_call | solution.py:809
  38.7 1.3 %collective-permute-start.12 = (f32[256,128]{1,0:T(8,128)S(1)}, f32[256,128]{1,0:T(8,128)S(1)}, u32[]{:S(2)}, u32[]{:S(2)}) collective-permute-start(f32[256,128]{1,0:T(8,128)S(1)} %bitcast.15), channel_id=1, source_target_pairs={{0,16},{1,9},{8,24},{9,1},{16,0},{17,25},{24,8},{25,17},{2,18},{3,... | collective-permute-start | bytes 393224 | tf_op jit(solution)/shard_map/ppermute | solution.py:704
  40.0 2.7 %collective-permute-start.13 = (f32[256,128]{1,0:T(8,128)S(1)}, f32[256,128]{1,0:T(8,128)S(1)}, u32[]{:S(2)}, u32[]{:S(2)}) collective-permute-start(f32[256,128]{1,0:T(8,128)S(1)} %bitcast.14), channel_id=1, source_target_pairs={{0,24},{1,25},{8,16},{9,17},{16,8},{17,9},{24,0},{25,1},{2,26},{3,... | collective-permute-start | bytes 393224 | tf_op jit(solution)/shard_map/ppermute | solution.py:704
  42.7 0.0 collective-permute-start.11
  42.7 1.0 %collective-permute-done.12.refs_2_ = f32[256,128]{1,0:T(8,128)S(1)} collective-permute-done((f32[256,128]{1,0:T(8,128)S(1)}, f32[256,128]{1,0:T(8,128)S(1)}, u32[]{:S(2)}, u32[]{:S(2)}) %collective-permute-start.12) | collective-permute-done | bytes 131104 | tf_op jit(solution)/shard_map/ppermute | solution.py:704
  43.8 3.4 %collective-permute-done.13.refs_3_ = f32[256,128]{1,0:T(8,128)S(1)} collective-permute-done((f32[256,128]{1,0:T(8,128)S(1)}, f32[256,128]{1,0:T(8,128)S(1)}, u32[]{:S(2)}, u32[]{:S(2)}) %collective-permute-start.13) | collective-permute-done | bytes 131104 | tf_op jit(solution)/shard_map/ppermute | solution.py:704
  47.2 0.7 %collective-permute-done.11.refs_1_ = f32[256,128]{1,0:T(8,128)S(1)} collective-permute-done((f32[256,128]{1,0:T(8,128)S(1)}, f32[256,128]{1,0:T(8,128)S(1)}, u32[]{:S(2)}, u32[]{:S(2)}) %collective-permute-start.11) | collective-permute-done | bytes 131104 | tf_op jit(solution)/shard_map/ppermute | solution.py:704
  47.9 1.0 %shard_map.57 = (f32[1,8,64,128]{3,2,1,0:T(8,128)}, f32[1,8,64,128]{3,2,1,0:T(8,128)}) custom-call(f32[256,128]{1,0:T(8,128)S(1)} %bitcast.8, f32[256,128]{1,0:T(8,128)S(1)} %collective-permute-done.11.refs_1_, f32[256,128]{1,0:T(8,128)S(1)} %collective-permute-done.12.refs_2_, f32[256,128]{1,0:T(8,128)S(1)} %collective-permute-done.13.refs_3_), custom_call_target="tpu_custom_call" | custom-call | tf_op jit(solution)/shard_map/pallas_call | solution.py:817
  (7 shorter events, 0.1 us)
Async XLA Ops:
  2.0 7.9 %collective-permute-start = (f32[256,128]{1,0:T(8,128)S(1)}, f32[256,128]{1,0:T(8,128)S(1)}, u32[]{:S(2)}, u32[]{:S(2)}) collective-permute-start(f32[256,128]{1,0:T(8,128)S(1)} %get-tuple-element.53), channel_id=1, source_target_pairs={{0,24},{1,25},{8,16},{9,17},{16,8},{17,9},{24,0},{25,1},{2,26},{3,... | collective-permute-start | bytes 393224 | tf_op jit(solution)/shard_map/ppermute | solution.py:704
  5.9 6.6 %collective-permute-start.1 = (f32[256,128]{1,0:T(8,128)S(1)}, f32[256,128]{1,0:T(8,128)S(1)}, u32[]{:S(2)}, u32[]{:S(2)}) collective-permute-start(f32[256,128]{1,0:T(8,128)S(1)} %get-tuple-element.54), channel_id=1, source_target_pairs={{0,8},{1,17},{8,0},{9,25},{16,24},{17,1},{24,16},{25,9},{2,10},{3,... | collective-permute-start | bytes 393224 | tf_op jit(solution)/shard_map/ppermute | solution.py:704
  6.5 6.0 %collective-permute-start.2 = (f32[256,128]{1,0:T(8,128)S(1)}, f32[256,128]{1,0:T(8,128)S(1)}, u32[]{:S(2)}, u32[]{:S(2)}) collective-permute-start(f32[256,128]{1,0:T(8,128)S(1)} %get-tuple-element.55), channel_id=1, source_target_pairs={{0,16},{1,9},{8,24},{9,1},{16,0},{17,25},{24,8},{25,17},{2,18},{3,... | collective-permute-start | bytes 393224 | tf_op jit(solution)/shard_map/ppermute | solution.py:704
  12.6 2.3 %collective-permute-start.5 = (f32[4,16,2,8,128]{4,3,2,1,0:T(8,128)S(1)}, f32[4,16,2,8,128]{4,3,2,1,0:T(8,128)S(1)}, u32[]{:S(2)}, u32[]{:S(2)}) collective-permute-start(f32[4,16,2,8,128]{4,3,2,1,0:T(8,128)S(1)} %get-tuple-element.58.c), channel_id=1, source_target_pairs={{0,1},{1,0},{2,3},{3,2},{4,5},{5,4},{6,7},{7,6},{8,9},{9,8},{10,11... | collective-permute-start | bytes 1572872 | tf_op jit(solution)/shard_map/ppermute | solution.py:689
  12.6 4.1 %collective-permute-start.3 = (f32[4,13,8,128]{3,2,1,0:T(8,128)S(1)}, f32[4,13,8,128]{3,2,1,0:T(8,128)S(1)}, u32[]{:S(2)}, u32[]{:S(2)}) collective-permute-start(f32[4,13,8,128]{3,2,1,0:T(8,128)S(1)} %get-tuple-element.56), channel_id=1, source_target_pairs={{0,1},{1,0},{8,24},{9,25},{24,8},{25,9},{16,18},{17,19},{18,16},{1... | collective-permute-start | bytes 638984 | tf_op jit(solution)/shard_map/ppermute | solution.py:728
  13.1 7.3 %collective-permute-start.4 = (f32[4,13,8,128]{3,2,1,0:T(8,128)S(1)}, f32[4,13,8,128]{3,2,1,0:T(8,128)S(1)}, u32[]{:S(2)}, u32[]{:S(2)}) collective-permute-start(f32[4,13,8,128]{3,2,1,0:T(8,128)S(1)} %get-tuple-element.57), channel_id=1, source_target_pairs={{0,8},{1,9},{8,0},{9,1},{24,16},{25,17},{16,24},{17,25},{18,2},{19... | collective-permute-start | bytes 638984 | tf_op jit(solution)/shard_map/ppermute | solution.py:728
  20.4 1.8 %collective-permute-start.6 = (f32[8,13,8,128]{3,2,1,0:T(8,128)S(1)}, f32[8,13,8,128]{3,2,1,0:T(8,128)S(1)}, u32[]{:S(2)}, u32[]{:S(2)}) collective-permute-start(f32[8,13,8,128]{3,2,1,0:T(8,128)S(1)} %constant_dynamic-update-slice_fusion.sides), channel_id=1, source_target_pairs={{0,1},{1,0},{2,3},{3,2},{4,5},{5,4},{6,7},{7,6},{8,9},{9,8},{10,11... | collective-permute-start | bytes 1277960 | tf_op jit(solution)/shard_map/ppermute | solution.py:689
  25.6 5.5 %collective-permute-start.7 = (f32[144,128]{1,0:T(8,128)S(1)}, f32[144,128]{1,0:T(8,128)S(1)}, u32[]{:S(2)}, u32[]{:S(2)}) collective-permute-start(f32[144,128]{1,0:T(8,128)S(1)} %get-tuple-element.77), channel_id=1, source_target_pairs={{0,8},{8,0},{24,16},{16,24},{18,2},{2,18},{10,26},{26,10},{28,20},... | collective-permute-start | bytes 221192 | tf_op jit(solution)/shard_map/ppermute | solution.py:744
  27.4 6.3 %collective-permute-start.9 = (f32[80,128]{1,0:T(8,128)S(1)}, f32[80,128]{1,0:T(8,128)S(1)}, u32[]{:S(2)}, u32[]{:S(2)}) collective-permute-start(f32[80,128]{1,0:T(8,128)S(1)} %get-tuple-element.78.pack), channel_id=1, source_target_pairs={{0,16},{8,18},{24,2},{16,0},{18,8},{2,24},{10,20},{26,4},{28,12},{... | collective-permute-start | bytes 122888 | tf_op jit(solution)/shard_map/ppermute | solution.py:744
  28.9 4.9 %collective-permute-start.8 = (f32[80,128]{1,0:T(8,128)S(1)}, f32[80,128]{1,0:T(8,128)S(1)}, u32[]{:S(2)}, u32[]{:S(2)}) collective-permute-start(f32[80,128]{1,0:T(8,128)S(1)} %get-tuple-element.78.pack), channel_id=1, source_target_pairs={{0,24},{8,16},{24,0},{16,8},{18,10},{2,26},{10,18},{26,2},{28,4},{... | collective-permute-start | bytes 122888 | tf_op jit(solution)/shard_map/ppermute | solution.py:744
  33.8 1.4 %collective-permute-start.10 = (f32[304,128]{1,0:T(8,128)S(1)}, f32[304,128]{1,0:T(8,128)S(1)}, u32[]{:S(2)}, u32[]{:S(2)}) collective-permute-start(f32[304,128]{1,0:T(8,128)S(1)} %constant_dynamic-update-slice_fusion.2.mine), channel_id=1, source_target_pairs={{0,1},{1,0},{2,3},{3,2},{4,5},{5,4},{6,7},{7,6},{8,9},{9,8},{10,11... | collective-permute-start | bytes 466952 | tf_op jit(solution)/shard_map/ppermute | solution.py:689
  38.7 5.0 %collective-permute-start.12 = (f32[256,128]{1,0:T(8,128)S(1)}, f32[256,128]{1,0:T(8,128)S(1)}, u32[]{:S(2)}, u32[]{:S(2)}) collective-permute-start(f32[256,128]{1,0:T(8,128)S(1)} %bitcast.15), channel_id=1, source_target_pairs={{0,16},{1,9},{8,24},{9,1},{16,0},{17,25},{24,8},{25,17},{2,18},{3,... | collective-permute-start | bytes 393224 | tf_op jit(solution)/shard_map/ppermute | solution.py:704
  40.0 7.2 %collective-permute-start.13 = (f32[256,128]{1,0:T(8,128)S(1)}, f32[256,128]{1,0:T(8,128)S(1)}, u32[]{:S(2)}, u32[]{:S(2)}) collective-permute-start(f32[256,128]{1,0:T(8,128)S(1)} %bitcast.14), channel_id=1, source_target_pairs={{0,24},{1,25},{8,16},{9,17},{16,8},{17,9},{24,0},{25,1},{2,26},{3,... | collective-permute-start | bytes 393224 | tf_op jit(solution)/shard_map/ppermute | solution.py:704
  42.7 5.2 %collective-permute-start.11 = (f32[256,128]{1,0:T(8,128)S(1)}, f32[256,128]{1,0:T(8,128)S(1)}, u32[]{:S(2)}, u32[]{:S(2)}) collective-permute-start(f32[256,128]{1,0:T(8,128)S(1)} %bitcast.13), channel_id=1, source_target_pairs={{0,8},{1,17},{8,0},{9,25},{16,24},{17,1},{24,16},{25,9},{2,10},{3,... | collective-permute-start | bytes 393224 | tf_op jit(solution)/shard_map/ppermute | solution.py:704

commit v10 on v8

--- a/solution.py
+++ b/solution.py
@@ -241,15 +241,18 @@
     copies = [pltpu.make_async_copy(a, b, sems.at[k]) for k, (a, b) in enumerate(pairs)]
     for copy in copies:
         copy.start()
-    for copy in copies:
-        copy.wait()
     here = lax.axis_index("gx")
     by, px = plan.by, plan.px
-    for slot, out in enumerate(outs):
-        rows = pl.ds(plan.start_of(here ^ plan.distance(slot)), by)
+    places = [pl.ds(plan.start_of(here ^ plan.distance(slot)), by) for slot in range(plan.gx)]
+    copies[0].wait()
+    copies[1].wait()
+    for out, rows in zip(outs, places):
         for p in range(px):
             half = jnp.where(phase[p, rows, :] == 1, 500.0, 0.5).astype(F32)
             out[pl.ds(p, by, stride=2 * px), :] = half * density[p, rows, :]
+    copies[2].wait()
+    for out, rows in zip(outs, places):
+        for p in range(px):
             out[pl.ds(px + p, by, stride=2 * px), :] = rhs[0, p, rows, :]
 
 
@@ -653,14 +656,20 @@
 
 
 def place_kernel(plan, *refs):
-    parts, (scaled, residual) = refs[: plan.gx], refs[plan.gx :]
+    parts, outs, (fields, sems) = refs[: plan.gx], refs[plan.gx : plan.gx + 2], refs[plan.gx + 2 :]
     here = lax.axis_index("gx")
     by, px = plan.by, plan.px
+    copies = []
     for slot, part in zip(plan.back, parts):
         rows = pl.ds(plan.start_of(here ^ plan.distance(slot)), by)
-        for p in range(px):
-            scaled[0, p, rows, :] = part[pl.ds(p, by, stride=2 * px), :]
-            residual[0, p, rows, :] = part[pl.ds(px + p, by, stride=2 * px), :]
+        for t, out in enumerate(outs):
+            for p in range(px):
+                fields[t, p, rows, :] = part[pl.ds(t * px + p, by, stride=2 * px), :]
+            copy = pltpu.make_async_copy(fields.at[t, :, rows, :], out.at[0, :, rows, :], sems.at[t, slot])
+            copy.start()
+            copies.append(copy)
+    for copy in copies:
+        copy.wait()
 
 
 def in_vmem(*shape):
@@ -810,6 +819,8 @@
     return call(
         functools.partial(place_kernel, plan),
         [jax.ShapeDtypeStruct((1, px, plan.ny, LANES), F32)] * 2,
+        [in_vmem(2, px, plan.ny, LANES), pltpu.SemaphoreType.DMA((2, gx))],
+        out_specs=[outside] * 2,
     )(*pinned(*[parts[slot] for slot in plan.back]))
 
 

time: 48.7 us -> 48.5 us (level)
  no operation moved by 1% of the time
where the time goes in v10:
time: 48.5 us; the launch traced here: 48.4 us
  waiting for transfers between devices  19.6 us (40%)
  starting transfers between devices  16.7 us (34%)
  Pallas kernels  11.2 us (23%)
  between operations  0.74 us (2%)
    ppermute x6, waiting for transfers between devices, exchange(): got.append(lax.ppermute(parts[slot], ('gx', 'gz'), pairs))  11.2 us
    ppermute x6, starting transfers between devices, exchange(): got.append(lax.ppermute(parts[slot], ('gx', 'gz'), pairs))  8.16 us
    ppermute x2, waiting for transfers between devices, swap_blocks(): return lax.ppermute(a, ('gx', 'gy', 'gz'), pairs)  5.53 us
    ppermute x3, starting transfers between devices, swap_blocks_apart(): return lax.ppermute(a, ('gx', 'gy', 'gz'), pairs)  5.12 us
    pallas_call x1, Pallas kernels, on_device(): call(functools.partial(up_kernel, plan), [in_vmem(gx, by, 2, px, LANES)]...  3.43 us
    pallas_call x1, Pallas kernels, on_device(): call(functools.partial(down_kernel, plan), outs, scratch, input_output_al...  3.38 us
    ppermute x3, waiting for transfers between devices, swap_blocks_apart(): return lax.ppermute(a, ('gx', 'gy', 'gz'), pairs)  2.2 us
    ppermute x2, starting transfers between devices, swap_blocks(): return lax.ppermute(a, ('gx', 'gy', 'gz'), pairs)  2.19 us
  transfers between devices with their start and end apart: 14, of which 7 were waited for; matrix products, arithmetic and copies ran while one was open for 0% of the time, Pallas kernels for 5%

profile of v10, /device:TPU:0, one launch (start us, length us, event | category | flops | bytes accessed | tf_op | source)
XLA Modules:
  0.0 48.4 jit_solution(17242152698191554414)
XLA Ops:
  0.6 1.2 %shard_map.50 = (f32[256,128]{1,0:T(8,128)S(1)}, f32[256,128]{1,0:T(8,128)S(1)}, f32[256,128]{1,0:T(8,128)S(1)}, f32[256,128]{1,0:T(8,128)S(1)}) custom-call(s32[8,64,128]{2,1,0:T(8,128)} %phase_in.1, f32[8,64,128]{2,1,0:T(8,128)} %density_in.1, f32[1,8,64,128]{3,2,1,0:T(8,128)} %rhs_in.1), custom_call_target="tpu_custom_call" | custom-call | tf_op jit(solution)/shard_map/pallas_call | solution.py:766
  1.9 4.0 %collective-permute-start = (f32[256,128]{1,0:T(8,128)S(1)}, f32[256,128]{1,0:T(8,128)S(1)}, u32[]{:S(2)}, u32[]{:S(2)}) collective-permute-start(f32[256,128]{1,0:T(8,128)S(1)} %get-tuple-element.51), channel_id=1, source_target_pairs={{0,24},{1,25},{8,16},{9,17},{16,8},{17,9},{24,0},{25,1},{2,26},{3,... | collective-permute-start | bytes 393224 | tf_op jit(solution)/shard_map/ppermute | solution.py:713
  5.8 0.5 %collective-permute-start.1 = (f32[256,128]{1,0:T(8,128)S(1)}, f32[256,128]{1,0:T(8,128)S(1)}, u32[]{:S(2)}, u32[]{:S(2)}) collective-permute-start(f32[256,128]{1,0:T(8,128)S(1)} %get-tuple-element.52), channel_id=1, source_target_pairs={{0,8},{1,17},{8,0},{9,25},{16,24},{17,1},{24,16},{25,9},{2,10},{3,... | collective-permute-start | bytes 393224 | tf_op jit(solution)/shard_map/ppermute | solution.py:713
  6.4 0.1 collective-permute-start.2
  6.5 3.3 %collective-permute-done = f32[256,128]{1,0:T(8,128)S(1)} collective-permute-done((f32[256,128]{1,0:T(8,128)S(1)}, f32[256,128]{1,0:T(8,128)S(1)}, u32[]{:S(2)}, u32[]{:S(2)}) %collective-permute-start) | collective-permute-done | bytes 131104 | tf_op jit(solution)/shard_map/ppermute | solution.py:713
  9.7 2.6 %collective-permute-done.1 = f32[256,128]{1,0:T(8,128)S(1)} collective-permute-done((f32[256,128]{1,0:T(8,128)S(1)}, f32[256,128]{1,0:T(8,128)S(1)}, u32[]{:S(2)}, u32[]{:S(2)}) %collective-permute-start.1) | collective-permute-done | bytes 131104 | tf_op jit(solution)/shard_map/ppermute | solution.py:713
  12.4 0.0 collective-permute-done.2
  12.4 0.1 shard_map.51
  12.5 0.1 collective-permute-start.3
  12.5 2.1 %collective-permute-start.4 = (f32[4,13,8,128]{3,2,1,0:T(8,128)S(1)}, f32[4,13,8,128]{3,2,1,0:T(8,128)S(1)}, u32[]{:S(2)}, u32[]{:S(2)}) collective-permute-start(f32[4,13,8,128]{3,2,1,0:T(8,128)S(1)} %get-tuple-element.55), channel_id=1, source_target_pairs={{0,8},{1,9},{8,0},{9,1},{24,16},{25,17},{16,24},{17,25},{18,2},{19... | collective-permute-start | bytes 638984 | tf_op jit(solution)/shard_map/ppermute | solution.py:731
  14.7 0.0 collective-permute-start.6
  14.7 0.0 collective-permute-done.3
  14.7 5.5 %collective-permute-done.4 = f32[4,13,8,128]{3,2,1,0:T(8,128)S(1)} collective-permute-done((f32[4,13,8,128]{3,2,1,0:T(8,128)S(1)}, f32[4,13,8,128]{3,2,1,0:T(8,128)S(1)}, u32[]{:S(2)}, u32[]{:S(2)}) %collective-permute-start.4) | collective-permute-done | bytes 213024 | tf_op jit(solution)/shard_map/ppermute | solution.py:731
  20.2 0.1 collective-permute-start.5
  20.3 0.0 collective-permute-done.6.zc
  20.3 1.9 %shard_map.52 = (f32[30,2,32,128]{3,2,1,0:T(8,128)S(1)}, f32[30,2,32,128]{3,2,1,0:T(8,128)S(1)}, f32[30,2,32,128]{3,2,1,0:T(8,128)S(1)}, f32[30,2,32,128]{3,2,1,...) custom-call(f32[4,16,2,8,128]{4,3,2,1,0:T(8,128)S(1)} %get-tuple-ele, ...), custom_call_target="tpu_custom_call" | custom-call | bytes 9000000 | tf_op jit(solution)/shard_map/pallas_call | solution.py:791
  22.2 0.0 collective-permute-done.5.zsides
  22.3 3.4 %shard_map.53 = (f32[30,2,32,128]{3,2,1,0:T(8,128)S(1)}, f32[30,2,32,128]{3,2,1,0:T(8,128)S(1)}, f32[30,2,32,128]{3,2,1,0:T(8,128)S(1)}, f32[30,2,32,128]{3,2,1,...) custom-call(f32[8,13,8,128]{3,2,1,0:T(8,128)S(1)} %constant_dynamic-, ...), custom_call_target="tpu_custom_call", output_to_operand_aliasing={{0}: (2, {}), {1}: (3, {}), {2}: (4, {}), {3}: (5, {}), {4}... | custom-call | tf_op jit(solution)/shard_map/pallas_call | solution.py:795
  25.6 0.4 collective-permute-start.7
  26.0 2.1 %collective-permute-start.9 = (f32[80,128]{1,0:T(8,128)S(1)}, f32[80,128]{1,0:T(8,128)S(1)}, u32[]{:S(2)}, u32[]{:S(2)}) collective-permute-start(f32[80,128]{1,0:T(8,128)S(1)} %get-tuple-element.74.pack), channel_id=1, source_target_pairs={{0,16},{8,18},{24,2},{16,0},{18,8},{2,24},{10,20},{26,4},{28,12},{... | collective-permute-start | bytes 122888 | tf_op jit(solution)/shard_map/ppermute | solution.py:747
  28.1 2.7 %collective-permute-start.8 = (f32[80,128]{1,0:T(8,128)S(1)}, f32[80,128]{1,0:T(8,128)S(1)}, u32[]{:S(2)}, u32[]{:S(2)}) collective-permute-start(f32[80,128]{1,0:T(8,128)S(1)} %get-tuple-element.74.pack), channel_id=1, source_target_pairs={{0,24},{8,16},{24,0},{16,8},{18,10},{2,26},{10,18},{26,2},{28,4},{... | collective-permute-start | bytes 122888 | tf_op jit(solution)/shard_map/ppermute | solution.py:747
  30.8 0.0 collective-permute-done.7
  30.8 2.2 %collective-permute-done.8 = f32[80,128]{1,0:T(8,128)S(1)} collective-permute-done((f32[80,128]{1,0:T(8,128)S(1)}, f32[80,128]{1,0:T(8,128)S(1)}, u32[]{:S(2)}, u32[]{:S(2)}) %collective-permute-start.8) | collective-permute-done | bytes 40992 | tf_op jit(solution)/shard_map/ppermute | solution.py:747
  33.0 0.0 collective-permute-done.9
  33.0 1.2 %collective-permute-start.10 = (f32[304,128]{1,0:T(8,128)S(1)}, f32[304,128]{1,0:T(8,128)S(1)}, u32[]{:S(2)}, u32[]{:S(2)}) collective-permute-start(f32[304,128]{1,0:T(8,128)S(1)} %constant_dynamic-update-slice_fusion.2.mine), channel_id=1, source_target_pairs={{0,1},{1,0},{2,3},{3,2},{4,5},{5,4},{6,7},{7,6},{8,9},{9,8},{10,11... | collective-permute-start | bytes 466952 | tf_op jit(solution)/shard_map/ppermute | solution.py:698
  34.1 0.3 shard_map.54
  34.5 0.7 %collective-permute-done.10.theirs = f32[304,128]{1,0:T(8,128)S(1)} collective-permute-done((f32[304,128]{1,0:T(8,128)S(1)}, f32[304,128]{1,0:T(8,128)S(1)}, u32[]{:S(2)}, u32[]{:S(2)}) %collective-permute-start.10) | collective-permute-done | bytes 155680 | tf_op jit(solution)/shard_map/ppermute | solution.py:698
  35.2 3.4 %shard_map.55 = (f32[4,16,2,8,128]{4,3,2,1,0:T(8,128)S(1)}, f32[29,2,8,128]{3,2,1,0:T(8,128)S(1)}, f32[29,2,8,128]{3,2,1,0:T(8,128)S(1)}, f32[29,2,8,128]{3,2,1,...) custom-call(f32[304,128]{1,0:T(8,128)S(1)} %collective-permute-done., ...), custom_call_target="tpu_custom_call", output_to_operand_aliasing={{1}: (1, {}), {2}: (2, {}), {3}: (3, {}), {4}: (4, {}), {5}... | custom-call | tf_op jit(solution)/shard_map/pallas_call | solution.py:811
  38.6 0.6 %collective-permute-start.12 = (f32[256,128]{1,0:T(8,128)S(1)}, f32[256,128]{1,0:T(8,128)S(1)}, u32[]{:S(2)}, u32[]{:S(2)}) collective-permute-start(f32[256,128]{1,0:T(8,128)S(1)} %bitcast.15), channel_id=1, source_target_pairs={{0,16},{1,9},{8,24},{9,1},{16,0},{17,25},{24,8},{25,17},{2,18},{3,... | collective-permute-start | bytes 393224 | tf_op jit(solution)/shard_map/ppermute | solution.py:713
  39.3 2.2 %collective-permute-start.13 = (f32[256,128]{1,0:T(8,128)S(1)}, f32[256,128]{1,0:T(8,128)S(1)}, u32[]{:S(2)}, u32[]{:S(2)}) collective-permute-start(f32[256,128]{1,0:T(8,128)S(1)} %bitcast.14), channel_id=1, source_target_pairs={{0,24},{1,25},{8,16},{9,17},{16,8},{17,9},{24,0},{25,1},{2,26},{3,... | collective-permute-start | bytes 393224 | tf_op jit(solution)/shard_map/ppermute | solution.py:713
  41.5 0.7 %collective-permute-start.11 = (f32[256,128]{1,0:T(8,128)S(1)}, f32[256,128]{1,0:T(8,128)S(1)}, u32[]{:S(2)}, u32[]{:S(2)}) collective-permute-start(f32[256,128]{1,0:T(8,128)S(1)} %bitcast.13), channel_id=1, source_target_pairs={{0,8},{1,17},{8,0},{9,25},{16,24},{17,1},{24,16},{25,9},{2,10},{3,... | collective-permute-start | bytes 393224 | tf_op jit(solution)/shard_map/ppermute | solution.py:713
  42.2 4.7 %collective-permute-done.12.refs_2_ = f32[256,128]{1,0:T(8,128)S(1)} collective-permute-done((f32[256,128]{1,0:T(8,128)S(1)}, f32[256,128]{1,0:T(8,128)S(1)}, u32[]{:S(2)}, u32[]{:S(2)}) %collective-permute-start.12) | collective-permute-done | bytes 131104 | tf_op jit(solution)/shard_map/ppermute | solution.py:713
  46.9 0.0 collective-permute-done.13.refs_3_
  46.9 0.6 %collective-permute-done.11.refs_1_ = f32[256,128]{1,0:T(8,128)S(1)} collective-permute-done((f32[256,128]{1,0:T(8,128)S(1)}, f32[256,128]{1,0:T(8,128)S(1)}, u32[]{:S(2)}, u32[]{:S(2)}) %collective-permute-start.11) | collective-permute-done | bytes 131104 | tf_op jit(solution)/shard_map/ppermute | solution.py:713
  47.5 0.9 %shard_map.56 = (f32[1,8,64,128]{3,2,1,0:T(8,128)}, f32[1,8,64,128]{3,2,1,0:T(8,128)}) custom-call(f32[256,128]{1,0:T(8,128)S(1)} %bitcast.8, f32[256,128]{1,0:T(8,128)S(1)} %collective-permute-done.11.refs_1_, f32[256,128]{1,0:T(8,128)S(1)} %collective-permute-done.12.refs_2_, f32[256,128]{1,0:T(8,128)S(1)} %collective-permute-done.13.refs_3_), custom_call_target="tpu_custom_call" | custom-call | tf_op jit(solution)/shard_map/pallas_call | solution.py:819
  (6 shorter events, 0.1 us)
Async XLA Ops:
  1.9 7.9 %collective-permute-start = (f32[256,128]{1,0:T(8,128)S(1)}, f32[256,128]{1,0:T(8,128)S(1)}, u32[]{:S(2)}, u32[]{:S(2)}) collective-permute-start(f32[256,128]{1,0:T(8,128)S(1)} %get-tuple-element.51), channel_id=1, source_target_pairs={{0,24},{1,25},{8,16},{9,17},{16,8},{17,9},{24,0},{25,1},{2,26},{3,... | collective-permute-start | bytes 393224 | tf_op jit(solution)/shard_map/ppermute | solution.py:713
  5.8 6.6 %collective-permute-start.1 = (f32[256,128]{1,0:T(8,128)S(1)}, f32[256,128]{1,0:T(8,128)S(1)}, u32[]{:S(2)}, u32[]{:S(2)}) collective-permute-start(f32[256,128]{1,0:T(8,128)S(1)} %get-tuple-element.52), channel_id=1, source_target_pairs={{0,8},{1,17},{8,0},{9,25},{16,24},{17,1},{24,16},{25,9},{2,10},{3,... | collective-permute-start | bytes 393224 | tf_op jit(solution)/shard_map/ppermute | solution.py:713
  6.4 6.0 %collective-permute-start.2 = (f32[256,128]{1,0:T(8,128)S(1)}, f32[256,128]{1,0:T(8,128)S(1)}, u32[]{:S(2)}, u32[]{:S(2)}) collective-permute-start(f32[256,128]{1,0:T(8,128)S(1)} %get-tuple-element.53), channel_id=1, source_target_pairs={{0,16},{1,9},{8,24},{9,1},{16,0},{17,25},{24,8},{25,17},{2,18},{3,... | collective-permute-start | bytes 393224 | tf_op jit(solution)/shard_map/ppermute | solution.py:713
  12.5 2.2 %collective-permute-start.3 = (f32[4,13,8,128]{3,2,1,0:T(8,128)S(1)}, f32[4,13,8,128]{3,2,1,0:T(8,128)S(1)}, u32[]{:S(2)}, u32[]{:S(2)}) collective-permute-start(f32[4,13,8,128]{3,2,1,0:T(8,128)S(1)} %get-tuple-element.54), channel_id=1, source_target_pairs={{0,1},{1,0},{8,24},{9,25},{24,8},{25,9},{16,18},{17,19},{18,16},{1... | collective-permute-start | bytes 638984 | tf_op jit(solution)/shard_map/ppermute | solution.py:731
  12.5 7.7 %collective-permute-start.4 = (f32[4,13,8,128]{3,2,1,0:T(8,128)S(1)}, f32[4,13,8,128]{3,2,1,0:T(8,128)S(1)}, u32[]{:S(2)}, u32[]{:S(2)}) collective-permute-start(f32[4,13,8,128]{3,2,1,0:T(8,128)S(1)} %get-tuple-element.55), channel_id=1, source_target_pairs={{0,8},{1,9},{8,0},{9,1},{24,16},{25,17},{16,24},{17,25},{18,2},{19... | collective-permute-start | bytes 638984 | tf_op jit(solution)/shard_map/ppermute | solution.py:731
  14.7 5.7 %collective-permute-start.6 = (f32[4,16,2,8,128]{4,3,2,1,0:T(8,128)S(1)}, f32[4,16,2,8,128]{4,3,2,1,0:T(8,128)S(1)}, u32[]{:S(2)}, u32[]{:S(2)}) collective-permute-start(f32[4,16,2,8,128]{4,3,2,1,0:T(8,128)S(1)} %get-tuple-element.56.c), channel_id=1, source_target_pairs={{0,1},{1,0},{2,3},{3,2},{4,5},{5,4},{6,7},{7,6},{8,9},{9,8},{10,11... | collective-permute-start | bytes 1572872 | tf_op jit(solution)/shard_map/ppermute | solution.py:698
  20.2 2.0 %collective-permute-start.5 = (f32[8,13,8,128]{3,2,1,0:T(8,128)S(1)}, f32[8,13,8,128]{3,2,1,0:T(8,128)S(1)}, u32[]{:S(2)}, u32[]{:S(2)}) collective-permute-start(f32[8,13,8,128]{3,2,1,0:T(8,128)S(1)} %constant_dynamic-update-slice_fusion.sides), channel_id=1, source_target_pairs={{0,1},{1,0},{2,3},{3,2},{4,5},{5,4},{6,7},{7,6},{8,9},{9,8},{10,11... | collective-permute-start | bytes 1277960 | tf_op jit(solution)/shard_map/ppermute | solution.py:698
  25.6 5.1 %collective-permute-start.7 = (f32[144,128]{1,0:T(8,128)S(1)}, f32[144,128]{1,0:T(8,128)S(1)}, u32[]{:S(2)}, u32[]{:S(2)}) collective-permute-start(f32[144,128]{1,0:T(8,128)S(1)} %get-tuple-element.73), channel_id=1, source_target_pairs={{0,8},{8,0},{24,16},{16,24},{18,2},{2,18},{10,26},{26,10},{28,20},... | collective-permute-start | bytes 221192 | tf_op jit(solution)/shard_map/ppermute | solution.py:747
  26.0 7.0 %collective-permute-start.9 = (f32[80,128]{1,0:T(8,128)S(1)}, f32[80,128]{1,0:T(8,128)S(1)}, u32[]{:S(2)}, u32[]{:S(2)}) collective-permute-start(f32[80,128]{1,0:T(8,128)S(1)} %get-tuple-element.74.pack), channel_id=1, source_target_pairs={{0,16},{8,18},{24,2},{16,0},{18,8},{2,24},{10,20},{26,4},{28,12},{... | collective-permute-start | bytes 122888 | tf_op jit(solution)/shard_map/ppermute | solution.py:747
  28.1 4.9 %collective-permute-start.8 = (f32[80,128]{1,0:T(8,128)S(1)}, f32[80,128]{1,0:T(8,128)S(1)}, u32[]{:S(2)}, u32[]{:S(2)}) collective-permute-start(f32[80,128]{1,0:T(8,128)S(1)} %get-tuple-element.74.pack), channel_id=1, source_target_pairs={{0,24},{8,16},{24,0},{16,8},{18,10},{2,26},{10,18},{26,2},{28,4},{... | collective-permute-start | bytes 122888 | tf_op jit(solution)/shard_map/ppermute | solution.py:747
  33.0 2.2 %collective-permute-start.10 = (f32[304,128]{1,0:T(8,128)S(1)}, f32[304,128]{1,0:T(8,128)S(1)}, u32[]{:S(2)}, u32[]{:S(2)}) collective-permute-start(f32[304,128]{1,0:T(8,128)S(1)} %constant_dynamic-update-slice_fusion.2.mine), channel_id=1, source_target_pairs={{0,1},{1,0},{2,3},{3,2},{4,5},{5,4},{6,7},{7,6},{8,9},{9,8},{10,11... | collective-permute-start | bytes 466952 | tf_op jit(solution)/shard_map/ppermute | solution.py:698
  38.6 8.2 %collective-permute-start.12 = (f32[256,128]{1,0:T(8,128)S(1)}, f32[256,128]{1,0:T(8,128)S(1)}, u32[]{:S(2)}, u32[]{:S(2)}) collective-permute-start(f32[256,128]{1,0:T(8,128)S(1)} %bitcast.15), channel_id=1, source_target_pairs={{0,16},{1,9},{8,24},{9,1},{16,0},{17,25},{24,8},{25,17},{2,18},{3,... | collective-permute-start | bytes 393224 | tf_op jit(solution)/shard_map/ppermute | solution.py:713
  39.3 7.6 %collective-permute-start.13 = (f32[256,128]{1,0:T(8,128)S(1)}, f32[256,128]{1,0:T(8,128)S(1)}, u32[]{:S(2)}, u32[]{:S(2)}) collective-permute-start(f32[256,128]{1,0:T(8,128)S(1)} %bitcast.14), channel_id=1, source_target_pairs={{0,24},{1,25},{8,16},{9,17},{16,8},{17,9},{24,0},{25,1},{2,26},{3,... | collective-permute-start | bytes 393224 | tf_op jit(solution)/shard_map/ppermute | solution.py:713
  41.5 6.0 %collective-permute-start.11 = (f32[256,128]{1,0:T(8,128)S(1)}, f32[256,128]{1,0:T(8,128)S(1)}, u32[]{:S(2)}, u32[]{:S(2)}) collective-permute-start(f32[256,128]{1,0:T(8,128)S(1)} %bitcast.13), channel_id=1, source_target_pairs={{0,8},{1,17},{8,0},{9,25},{16,24},{17,1},{24,16},{25,9},{2,10},{3,... | collective-permute-start | bytes 393224 | tf_op jit(solution)/shard_map/ppermute | solution.py:713

commit v11 on v10

--- a/solution.py
+++ b/solution.py
@@ -419,7 +419,7 @@
         each(0, count - 1, 4, one)
 
     up_first = plan.is_up(block, 1, 0)
-    below, above = jnp.where(up_first, 0, gx), jnp.where(up_first, gx, 0)
+    below, above = jnp.where(up_first, gx, 0), jnp.where(up_first, 0, gx)
     gx_below, gx_above = plan.gx_of(block - 1), plan.gx_of(block + 1)
     take_side(below, gx_below, 0, HALO, 0)
     take_side(above, gx_above, HALO + by, HALO, 0)
@@ -774,7 +774,7 @@
         functools.partial(gather_kernel, plan),
         [in_vmem(gx, by, 2, px, LANES)] + [in_vmem(gx, HALO + HALO_RHS, px, LANES)] * 2,
     )(*pinned(*parts))
-    sides = jnp.concatenate([swap_blocks(plan, sets[one], 1, one) for one in (1, 0)], axis=0)
+    sides = jnp.concatenate([swap_blocks(plan, sets[one], 1, one) for one in (0, 1)], axis=0)
     zc = beside_in_z(plan, c)
     zsides = beside_in_z(plan, sides)
 

time: 48.5 us -> 48.3 us (level)
    ppermute x2, waiting for transfers between devices: 5.53 us -> 4.31 us  [swap_blocks(): return lax.ppermute(a, ('gx', 'gy', 'gz'), pairs)]
    ppermute x3, starting transfers between devices: 5.12 us -> 6.15 us  [swap_blocks_apart(): return lax.ppermute(a, ('gx', 'gy', 'gz'), pairs)]
    ppermute x3, waiting for transfers between devices: 2.2 us -> 2.79 us  [swap_blocks_apart(): return lax.ppermute(a, ('gx', 'gy', 'gz'), pairs)]
    ppermute x3, starting transfers between devices: 1.23 us -> 0.65 us  [beside_in_z(): return lax.ppermute(a, 'gz', [(0, 1), (1, 0)])]
    ppermute x2, starting transfers between devices: 2.19 us -> 1.6 us  [swap_blocks(): return lax.ppermute(a, ('gx', 'gy', 'gz'), pairs)]
  transfers between devices with their start and end apart: 14 -> 14, of which waited for: 7 -> 8; matrix products, arithmetic and copies ran while one was open for 0% -> 0% of each run, Pallas kernels for 5% -> 5%
where the time goes in v11:
time: 48.3 us; the launch traced here: 48.2 us
  waiting for transfers between devices  19.3 us (40%)
  starting transfers between devices  16.8 us (35%)
  Pallas kernels  11.2 us (23%)
  between operations  0.75 us (2%)
    ppermute x6, waiting for transfers between devices, exchange(): got.append(lax.ppermute(parts[slot], ('gx', 'gz'), pairs))  11.1 us
    ppermute x6, starting transfers between devices, exchange(): got.append(lax.ppermute(parts[slot], ('gx', 'gz'), pairs))  8.44 us
    ppermute x3, starting transfers between devices, swap_blocks_apart(): return lax.ppermute(a, ('gx', 'gy', 'gz'), pairs)  6.15 us
    ppermute x2, waiting for transfers between devices, swap_blocks(): return lax.ppermute(a, ('gx', 'gy', 'gz'), pairs)  4.31 us
    pallas_call x1, Pallas kernels, on_device(): call(functools.partial(up_kernel, plan), [in_vmem(gx, by, 2, px, LANES)]...  3.43 us
    pallas_call x1, Pallas kernels, on_device(): call(functools.partial(down_kernel, plan), outs, scratch, input_output_al...  3.38 us
    ppermute x3, waiting for transfers between devices, swap_blocks_apart(): return lax.ppermute(a, ('gx', 'gy', 'gz'), pairs)  2.79 us
    pallas_call x1, Pallas kernels, on_device(): call(functools.partial(inner_kernel, plan), Finest.shapes(plan), work=900...  1.91 us
  transfers between devices with their start and end apart: 14, of which 8 were waited for; matrix products, arithmetic and copies ran while one was open for 0% of the time, Pallas kernels for 5%

profile of v11, /device:TPU:0, one launch (start us, length us, event | category | flops | bytes accessed | tf_op | source)
XLA Modules:
  0.0 48.2 jit_solution(13764583393642642662)
XLA Ops:
  0.6 1.2 %shard_map.50 = (f32[256,128]{1,0:T(8,128)S(1)}, f32[256,128]{1,0:T(8,128)S(1)}, f32[256,128]{1,0:T(8,128)S(1)}, f32[256,128]{1,0:T(8,128)S(1)}) custom-call(s32[8,64,128]{2,1,0:T(8,128)} %phase_in.1, f32[8,64,128]{2,1,0:T(8,128)} %density_in.1, f32[1,8,64,128]{3,2,1,0:T(8,128)} %rhs_in.1), custom_call_target="tpu_custom_call" | custom-call | tf_op jit(solution)/shard_map/pallas_call | solution.py:766
  1.9 4.0 %collective-permute-start = (f32[256,128]{1,0:T(8,128)S(1)}, f32[256,128]{1,0:T(8,128)S(1)}, u32[]{:S(2)}, u32[]{:S(2)}) collective-permute-start(f32[256,128]{1,0:T(8,128)S(1)} %get-tuple-element.51), channel_id=1, source_target_pairs={{0,24},{1,25},{8,16},{9,17},{16,8},{17,9},{24,0},{25,1},{2,26},{3,... | collective-permute-start | bytes 393224 | tf_op jit(solution)/shard_map/ppermute | solution.py:713
  5.8 0.5 %collective-permute-start.1 = (f32[256,128]{1,0:T(8,128)S(1)}, f32[256,128]{1,0:T(8,128)S(1)}, u32[]{:S(2)}, u32[]{:S(2)}) collective-permute-start(f32[256,128]{1,0:T(8,128)S(1)} %get-tuple-element.52), channel_id=1, source_target_pairs={{0,8},{1,17},{8,0},{9,25},{16,24},{17,1},{24,16},{25,9},{2,10},{3,... | collective-permute-start | bytes 393224 | tf_op jit(solution)/shard_map/ppermute | solution.py:713
  6.4 0.1 collective-permute-start.2
  6.5 3.3 %collective-permute-done = f32[256,128]{1,0:T(8,128)S(1)} collective-permute-done((f32[256,128]{1,0:T(8,128)S(1)}, f32[256,128]{1,0:T(8,128)S(1)}, u32[]{:S(2)}, u32[]{:S(2)}) %collective-permute-start) | collective-permute-done | bytes 131104 | tf_op jit(solution)/shard_map/ppermute | solution.py:713
  9.7 2.6 %collective-permute-done.1 = f32[256,128]{1,0:T(8,128)S(1)} collective-permute-done((f32[256,128]{1,0:T(8,128)S(1)}, f32[256,128]{1,0:T(8,128)S(1)}, u32[]{:S(2)}, u32[]{:S(2)}) %collective-permute-start.1) | collective-permute-done | bytes 131104 | tf_op jit(solution)/shard_map/ppermute | solution.py:713
  12.4 0.0 collective-permute-done.2
  12.4 0.1 shard_map.51
  12.5 1.6 %collective-permute-start.3 = (f32[4,13,8,128]{3,2,1,0:T(8,128)S(1)}, f32[4,13,8,128]{3,2,1,0:T(8,128)S(1)}, u32[]{:S(2)}, u32[]{:S(2)}) collective-permute-start(f32[4,13,8,128]{3,2,1,0:T(8,128)S(1)} %get-tuple-element.54), channel_id=1, source_target_pairs={{0,8},{1,9},{8,0},{9,1},{24,16},{25,17},{16,24},{17,25},{18,2},{19... | collective-permute-start | bytes 638984 | tf_op jit(solution)/shard_map/ppermute | solution.py:731
  14.1 0.0 collective-permute-start.4
  14.1 0.5 %collective-permute-start.6 = (f32[4,16,2,8,128]{4,3,2,1,0:T(8,128)S(1)}, f32[4,16,2,8,128]{4,3,2,1,0:T(8,128)S(1)}, u32[]{:S(2)}, u32[]{:S(2)}) collective-permute-start(f32[4,16,2,8,128]{4,3,2,1,0:T(8,128)S(1)} %get-tuple-element.56.c), channel_id=1, source_target_pairs={{0,1},{1,0},{2,3},{3,2},{4,5},{5,4},{6,7},{7,6},{8,9},{9,8},{10,11... | collective-permute-start | bytes 1572872 | tf_op jit(solution)/shard_map/ppermute | solution.py:698
  14.6 4.3 %collective-permute-done.3 = f32[4,13,8,128]{3,2,1,0:T(8,128)S(1)} collective-permute-done((f32[4,13,8,128]{3,2,1,0:T(8,128)S(1)}, f32[4,13,8,128]{3,2,1,0:T(8,128)S(1)}, u32[]{:S(2)}, u32[]{:S(2)}) %collective-permute-start.3) | collective-permute-done | bytes 213024 | tf_op jit(solution)/shard_map/ppermute | solution.py:731
  18.9 0.0 collective-permute-done.4
  18.9 0.1 collective-permute-start.5
  19.0 0.0 collective-permute-done.6.zc
  19.0 1.9 %shard_map.52 = (f32[30,2,32,128]{3,2,1,0:T(8,128)S(1)}, f32[30,2,32,128]{3,2,1,0:T(8,128)S(1)}, f32[30,2,32,128]{3,2,1,0:T(8,128)S(1)}, f32[30,2,32,128]{3,2,1,...) custom-call(f32[4,16,2,8,128]{4,3,2,1,0:T(8,128)S(1)} %get-tuple-ele, ...), custom_call_target="tpu_custom_call" | custom-call | bytes 9000000 | tf_op jit(solution)/shard_map/pallas_call | solution.py:791
  20.9 0.0 collective-permute-done.5.zsides
  21.0 3.4 %shard_map.53 = (f32[30,2,32,128]{3,2,1,0:T(8,128)S(1)}, f32[30,2,32,128]{3,2,1,0:T(8,128)S(1)}, f32[30,2,32,128]{3,2,1,0:T(8,128)S(1)}, f32[30,2,32,128]{3,2,1,...) custom-call(f32[8,13,8,128]{3,2,1,0:T(8,128)S(1)} %constant_dynamic-, ...), custom_call_target="tpu_custom_call", output_to_operand_aliasing={{0}: (2, {}), {1}: (3, {}), {2}: (4, {}), {3}: (5, {}), {4}... | custom-call | tf_op jit(solution)/shard_map/pallas_call | solution.py:795
  24.3 2.3 %collective-permute-start.7 = (f32[144,128]{1,0:T(8,128)S(1)}, f32[144,128]{1,0:T(8,128)S(1)}, u32[]{:S(2)}, u32[]{:S(2)}) collective-permute-start(f32[144,128]{1,0:T(8,128)S(1)} %get-tuple-element.73), channel_id=1, source_target_pairs={{0,8},{8,0},{24,16},{16,24},{18,2},{2,18},{10,26},{26,10},{28,20},... | collective-permute-start | bytes 221192 | tf_op jit(solution)/shard_map/ppermute | solution.py:747
  26.7 1.7 %collective-permute-start.9 = (f32[80,128]{1,0:T(8,128)S(1)}, f32[80,128]{1,0:T(8,128)S(1)}, u32[]{:S(2)}, u32[]{:S(2)}) collective-permute-start(f32[80,128]{1,0:T(8,128)S(1)} %get-tuple-element.74.pack), channel_id=1, source_target_pairs={{0,16},{8,18},{24,2},{16,0},{18,8},{2,24},{10,20},{26,4},{28,12},{... | collective-permute-start | bytes 122888 | tf_op jit(solution)/shard_map/ppermute | solution.py:747
  28.4 2.1 %collective-permute-start.8 = (f32[80,128]{1,0:T(8,128)S(1)}, f32[80,128]{1,0:T(8,128)S(1)}, u32[]{:S(2)}, u32[]{:S(2)}) collective-permute-start(f32[80,128]{1,0:T(8,128)S(1)} %get-tuple-element.74.pack), channel_id=1, source_target_pairs={{0,24},{8,16},{24,0},{16,8},{18,10},{2,26},{10,18},{26,2},{28,4},{... | collective-permute-start | bytes 122888 | tf_op jit(solution)/shard_map/ppermute | solution.py:747
  30.5 0.0 collective-permute-done.7
  30.5 2.8 %collective-permute-done.8 = f32[80,128]{1,0:T(8,128)S(1)} collective-permute-done((f32[80,128]{1,0:T(8,128)S(1)}, f32[80,128]{1,0:T(8,128)S(1)}, u32[]{:S(2)}, u32[]{:S(2)}) %collective-permute-start.8) | collective-permute-done | bytes 40992 | tf_op jit(solution)/shard_map/ppermute | solution.py:747
  33.3 0.0 collective-permute-done.9
  33.3 0.1 collective-permute-start.10
  33.4 0.3 shard_map.54
  33.7 1.0 %collective-permute-done.10.theirs = f32[304,128]{1,0:T(8,128)S(1)} collective-permute-done((f32[304,128]{1,0:T(8,128)S(1)}, f32[304,128]{1,0:T(8,128)S(1)}, u32[]{:S(2)}, u32[]{:S(2)}) %collective-permute-start.10) | collective-permute-done | bytes 155680 | tf_op jit(solution)/shard_map/ppermute | solution.py:698
  34.8 3.4 %shard_map.55 = (f32[4,16,2,8,128]{4,3,2,1,0:T(8,128)S(1)}, f32[29,2,8,128]{3,2,1,0:T(8,128)S(1)}, f32[29,2,8,128]{3,2,1,0:T(8,128)S(1)}, f32[29,2,8,128]{3,2,1,...) custom-call(f32[304,128]{1,0:T(8,128)S(1)} %collective-permute-done., ...), custom_call_target="tpu_custom_call", output_to_operand_aliasing={{1}: (1, {}), {2}: (2, {}), {3}: (3, {}), {4}: (4, {}), {5}... | custom-call | tf_op jit(solution)/shard_map/pallas_call | solution.py:811
  38.3 0.9 %collective-permute-start.12 = (f32[256,128]{1,0:T(8,128)S(1)}, f32[256,128]{1,0:T(8,128)S(1)}, u32[]{:S(2)}, u32[]{:S(2)}) collective-permute-start(f32[256,128]{1,0:T(8,128)S(1)} %bitcast.15), channel_id=1, source_target_pairs={{0,16},{1,9},{8,24},{9,1},{16,0},{17,25},{24,8},{25,17},{2,18},{3,... | collective-permute-start | bytes 393224 | tf_op jit(solution)/shard_map/ppermute | solution.py:713
  39.2 2.9 %collective-permute-start.13 = (f32[256,128]{1,0:T(8,128)S(1)}, f32[256,128]{1,0:T(8,128)S(1)}, u32[]{:S(2)}, u32[]{:S(2)}) collective-permute-start(f32[256,128]{1,0:T(8,128)S(1)} %bitcast.14), channel_id=1, source_target_pairs={{0,24},{1,25},{8,16},{9,17},{16,8},{17,9},{24,0},{25,1},{2,26},{3,... | collective-permute-start | bytes 393224 | tf_op jit(solution)/shard_map/ppermute | solution.py:713
  42.1 0.0 collective-permute-start.11
  42.1 1.4 %collective-permute-done.12.refs_2_ = f32[256,128]{1,0:T(8,128)S(1)} collective-permute-done((f32[256,128]{1,0:T(8,128)S(1)}, f32[256,128]{1,0:T(8,128)S(1)}, u32[]{:S(2)}, u32[]{:S(2)}) %collective-permute-start.12) | collective-permute-done | bytes 131104 | tf_op jit(solution)/shard_map/ppermute | solution.py:713
  43.5 2.8 %collective-permute-done.13.refs_3_ = f32[256,128]{1,0:T(8,128)S(1)} collective-permute-done((f32[256,128]{1,0:T(8,128)S(1)}, f32[256,128]{1,0:T(8,128)S(1)}, u32[]{:S(2)}, u32[]{:S(2)}) %collective-permute-start.13) | collective-permute-done | bytes 131104 | tf_op jit(solution)/shard_map/ppermute | solution.py:713
  46.3 1.0 %collective-permute-done.11.refs_1_ = f32[256,128]{1,0:T(8,128)S(1)} collective-permute-done((f32[256,128]{1,0:T(8,128)S(1)}, f32[256,128]{1,0:T(8,128)S(1)}, u32[]{:S(2)}, u32[]{:S(2)}) %collective-permute-start.11) | collective-permute-done | bytes 131104 | tf_op jit(solution)/shard_map/ppermute | solution.py:713
  47.3 0.9 %shard_map.56 = (f32[1,8,64,128]{3,2,1,0:T(8,128)}, f32[1,8,64,128]{3,2,1,0:T(8,128)}) custom-call(f32[256,128]{1,0:T(8,128)S(1)} %bitcast.8, f32[256,128]{1,0:T(8,128)S(1)} %collective-permute-done.11.refs_1_, f32[256,128]{1,0:T(8,128)S(1)} %collective-permute-done.12.refs_2_, f32[256,128]{1,0:T(8,128)S(1)} %collective-permute-done.13.refs_3_), custom_call_target="tpu_custom_call" | custom-call | tf_op jit(solution)/shard_map/pallas_call | solution.py:819
  (6 shorter events, 0.1 us)
Async XLA Ops:
  1.9 7.9 %collective-permute-start = (f32[256,128]{1,0:T(8,128)S(1)}, f32[256,128]{1,0:T(8,128)S(1)}, u32[]{:S(2)}, u32[]{:S(2)}) collective-permute-start(f32[256,128]{1,0:T(8,128)S(1)} %get-tuple-element.51), channel_id=1, source_target_pairs={{0,24},{1,25},{8,16},{9,17},{16,8},{17,9},{24,0},{25,1},{2,26},{3,... | collective-permute-start | bytes 393224 | tf_op jit(solution)/shard_map/ppermute | solution.py:713
  5.8 6.6 %collective-permute-start.1 = (f32[256,128]{1,0:T(8,128)S(1)}, f32[256,128]{1,0:T(8,128)S(1)}, u32[]{:S(2)}, u32[]{:S(2)}) collective-permute-start(f32[256,128]{1,0:T(8,128)S(1)} %get-tuple-element.52), channel_id=1, source_target_pairs={{0,8},{1,17},{8,0},{9,25},{16,24},{17,1},{24,16},{25,9},{2,10},{3,... | collective-permute-start | bytes 393224 | tf_op jit(solution)/shard_map/ppermute | solution.py:713
  6.4 6.0 %collective-permute-start.2 = (f32[256,128]{1,0:T(8,128)S(1)}, f32[256,128]{1,0:T(8,128)S(1)}, u32[]{:S(2)}, u32[]{:S(2)}) collective-permute-start(f32[256,128]{1,0:T(8,128)S(1)} %get-tuple-element.53), channel_id=1, source_target_pairs={{0,16},{1,9},{8,24},{9,1},{16,0},{17,25},{24,8},{25,17},{2,18},{3,... | collective-permute-start | bytes 393224 | tf_op jit(solution)/shard_map/ppermute | solution.py:713
  12.5 6.4 %collective-permute-start.3 = (f32[4,13,8,128]{3,2,1,0:T(8,128)S(1)}, f32[4,13,8,128]{3,2,1,0:T(8,128)S(1)}, u32[]{:S(2)}, u32[]{:S(2)}) collective-permute-start(f32[4,13,8,128]{3,2,1,0:T(8,128)S(1)} %get-tuple-element.54), channel_id=1, source_target_pairs={{0,8},{1,9},{8,0},{9,1},{24,16},{25,17},{16,24},{17,25},{18,2},{19... | collective-permute-start | bytes 638984 | tf_op jit(solution)/shard_map/ppermute | solution.py:731
  14.1 4.8 %collective-permute-start.4 = (f32[4,13,8,128]{3,2,1,0:T(8,128)S(1)}, f32[4,13,8,128]{3,2,1,0:T(8,128)S(1)}, u32[]{:S(2)}, u32[]{:S(2)}) collective-permute-start(f32[4,13,8,128]{3,2,1,0:T(8,128)S(1)} %get-tuple-element.55), channel_id=1, source_target_pairs={{0,1},{1,0},{8,24},{9,25},{24,8},{25,9},{16,18},{17,19},{18,16},{1... | collective-permute-start | bytes 638984 | tf_op jit(solution)/shard_map/ppermute | solution.py:731
  14.1 4.9 %collective-permute-start.6 = (f32[4,16,2,8,128]{4,3,2,1,0:T(8,128)S(1)}, f32[4,16,2,8,128]{4,3,2,1,0:T(8,128)S(1)}, u32[]{:S(2)}, u32[]{:S(2)}) collective-permute-start(f32[4,16,2,8,128]{4,3,2,1,0:T(8,128)S(1)} %get-tuple-element.56.c), channel_id=1, source_target_pairs={{0,1},{1,0},{2,3},{3,2},{4,5},{5,4},{6,7},{7,6},{8,9},{9,8},{10,11... | collective-permute-start | bytes 1572872 | tf_op jit(solution)/shard_map/ppermute | solution.py:698
  18.9 2.0 %collective-permute-start.5 = (f32[8,13,8,128]{3,2,1,0:T(8,128)S(1)}, f32[8,13,8,128]{3,2,1,0:T(8,128)S(1)}, u32[]{:S(2)}, u32[]{:S(2)}) collective-permute-start(f32[8,13,8,128]{3,2,1,0:T(8,128)S(1)} %constant_dynamic-update-slice_fusion.sides), channel_id=1, source_target_pairs={{0,1},{1,0},{2,3},{3,2},{4,5},{5,4},{6,7},{7,6},{8,9},{9,8},{10,11... | collective-permute-start | bytes 1277960 | tf_op jit(solution)/shard_map/ppermute | solution.py:698
  24.3 6.2 %collective-permute-start.7 = (f32[144,128]{1,0:T(8,128)S(1)}, f32[144,128]{1,0:T(8,128)S(1)}, u32[]{:S(2)}, u32[]{:S(2)}) collective-permute-start(f32[144,128]{1,0:T(8,128)S(1)} %get-tuple-element.73), channel_id=1, source_target_pairs={{0,8},{8,0},{24,16},{16,24},{18,2},{2,18},{10,26},{26,10},{28,20},... | collective-permute-start | bytes 221192 | tf_op jit(solution)/shard_map/ppermute | solution.py:747
  26.7 6.7 %collective-permute-start.9 = (f32[80,128]{1,0:T(8,128)S(1)}, f32[80,128]{1,0:T(8,128)S(1)}, u32[]{:S(2)}, u32[]{:S(2)}) collective-permute-start(f32[80,128]{1,0:T(8,128)S(1)} %get-tuple-element.74.pack), channel_id=1, source_target_pairs={{0,16},{8,18},{24,2},{16,0},{18,8},{2,24},{10,20},{26,4},{28,12},{... | collective-permute-start | bytes 122888 | tf_op jit(solution)/shard_map/ppermute | solution.py:747
  28.4 4.9 %collective-permute-start.8 = (f32[80,128]{1,0:T(8,128)S(1)}, f32[80,128]{1,0:T(8,128)S(1)}, u32[]{:S(2)}, u32[]{:S(2)}) collective-permute-start(f32[80,128]{1,0:T(8,128)S(1)} %get-tuple-element.74.pack), channel_id=1, source_target_pairs={{0,24},{8,16},{24,0},{16,8},{18,10},{2,26},{10,18},{26,2},{28,4},{... | collective-permute-start | bytes 122888 | tf_op jit(solution)/shard_map/ppermute | solution.py:747
  33.3 1.4 %collective-permute-start.10 = (f32[304,128]{1,0:T(8,128)S(1)}, f32[304,128]{1,0:T(8,128)S(1)}, u32[]{:S(2)}, u32[]{:S(2)}) collective-permute-start(f32[304,128]{1,0:T(8,128)S(1)} %constant_dynamic-update-slice_fusion.2.mine), channel_id=1, source_target_pairs={{0,1},{1,0},{2,3},{3,2},{4,5},{5,4},{6,7},{7,6},{8,9},{9,8},{10,11... | collective-permute-start | bytes 466952 | tf_op jit(solution)/shard_map/ppermute | solution.py:698
  38.3 5.2 %collective-permute-start.12 = (f32[256,128]{1,0:T(8,128)S(1)}, f32[256,128]{1,0:T(8,128)S(1)}, u32[]{:S(2)}, u32[]{:S(2)}) collective-permute-start(f32[256,128]{1,0:T(8,128)S(1)} %bitcast.15), channel_id=1, source_target_pairs={{0,16},{1,9},{8,24},{9,1},{16,0},{17,25},{24,8},{25,17},{2,18},{3,... | collective-permute-start | bytes 393224 | tf_op jit(solution)/shard_map/ppermute | solution.py:713
  39.2 7.1 %collective-permute-start.13 = (f32[256,128]{1,0:T(8,128)S(1)}, f32[256,128]{1,0:T(8,128)S(1)}, u32[]{:S(2)}, u32[]{:S(2)}) collective-permute-start(f32[256,128]{1,0:T(8,128)S(1)} %bitcast.14), channel_id=1, source_target_pairs={{0,24},{1,25},{8,16},{9,17},{16,8},{17,9},{24,0},{25,1},{2,26},{3,... | collective-permute-start | bytes 393224 | tf_op jit(solution)/shard_map/ppermute | solution.py:713
  42.1 5.2 %collective-permute-start.11 = (f32[256,128]{1,0:T(8,128)S(1)}, f32[256,128]{1,0:T(8,128)S(1)}, u32[]{:S(2)}, u32[]{:S(2)}) collective-permute-start(f32[256,128]{1,0:T(8,128)S(1)} %bitcast.13), channel_id=1, source_target_pairs={{0,8},{1,17},{8,0},{9,25},{16,24},{17,1},{24,16},{25,9},{2,10},{3,... | collective-permute-start | bytes 393224 | tf_op jit(solution)/shard_map/ppermute | solution.py:713

commit v12 on v11

--- a/solution.py
+++ b/solution.py
@@ -528,7 +528,7 @@
         size = 5 * (plan.by // 8) * (plan.nx // 4)
         nearest = size + 4 * half_x
         for k, up in ups.items():
-            first = 0 if k == 1 else nearest + (k - 2) * size
+            first = 0 if k == 1 else nearest + (FAR - k) * size
             self.spread(ref[pl.ds(first, size), :], jnp.where(up, FAR + k, FAR - k), turned)
         row = jnp.where(ups[1], own + 5, 0)
         for k, (to, r) in enumerate(((self.u1, row), (self.u1, row + 1), (self.u1, row + 2), (self.f1, row + 1))):
@@ -749,8 +749,8 @@
 
 def far_blocks(plan, pack, nears):
     def line(move, near):
-        parts = [move(pack, k) for k in range(FAR, 1, -1)] + [move(near, 1)]
-        return jnp.concatenate(parts[::-1], axis=0)
+        parts = [move(near, 1)] + [move(pack, k) for k in range(FAR, 1, -1)]
+        return jnp.concatenate(parts, axis=0)
 
     if plan.paired:
         mine = line(functools.partial(swap_blocks_apart, plan), nears[0])

time: 48.3 us -> 48.4 us (level)
  waiting for transfers between devices: 19.3 us -> 19.9 us
  starting transfers between devices: 16.8 us -> 16.3 us
    ppermute x3, starting transfers between devices: 6.15 us -> 4.06 us  [swap_blocks_apart(): return lax.ppermute(a, ('gx', 'gy', 'gz'), pairs)]
    ppermute x3, starting transfers between devices: 0.65 us -> 1.73 us  [beside_in_z(): return lax.ppermute(a, 'gz', [(0, 1), (1, 0)])]
    ppermute x3, waiting for transfers between devices: 2.79 us -> 3.79 us  [swap_blocks_apart(): return lax.ppermute(a, ('gx', 'gy', 'gz'), pairs)]
  transfers between devices with their start and end apart: 14 -> 14, of which waited for: 8 -> 9; matrix products, arithmetic and copies ran while one was open for 0% -> 0% of each run, Pallas kernels for 5% -> 5%
where the time goes in v12:
time: 48.4 us; the launch traced here: 48.2 us
  waiting for transfers between devices  19.9 us (41%)
  starting transfers between devices  16.3 us (34%)
  Pallas kernels  11.2 us (23%)
  between operations  0.74 us (2%)
    ppermute x6, waiting for transfers between devices, exchange(): got.append(lax.ppermute(parts[slot], ('gx', 'gz'), pairs))  11.1 us
    ppermute x6, starting transfers between devices, exchange(): got.append(lax.ppermute(parts[slot], ('gx', 'gz'), pairs))  8.88 us
    ppermute x2, waiting for transfers between devices, swap_blocks(): return lax.ppermute(a, ('gx', 'gy', 'gz'), pairs)  4.31 us
    ppermute x3, starting transfers between devices, swap_blocks_apart(): return lax.ppermute(a, ('gx', 'gy', 'gz'), pairs)  4.06 us
    ppermute x3, waiting for transfers between devices, swap_blocks_apart(): return lax.ppermute(a, ('gx', 'gy', 'gz'), pairs)  3.79 us
    pallas_call x1, Pallas kernels, on_device(): call(functools.partial(up_kernel, plan), [in_vmem(gx, by, 2, px, LANES)]...  3.43 us
    pallas_call x1, Pallas kernels, on_device(): call(functools.partial(down_kernel, plan), outs, scratch, input_output_al...  3.38 us
    pallas_call x1, Pallas kernels, on_device(): call(functools.partial(inner_kernel, plan), Finest.shapes(plan), work=900...  1.91 us
  transfers between devices with their start and end apart: 14, of which 9 were waited for; matrix products, arithmetic and copies ran while one was open for 0% of the time, Pallas kernels for 5%

profile of v12, /device:TPU:0, one launch (start us, length us, event | category | flops | bytes accessed | tf_op | source)
XLA Modules:
  0.0 48.2 jit_solution(9418915018758779026)
XLA Ops:
  0.6 1.2 %shard_map.50 = (f32[256,128]{1,0:T(8,128)S(1)}, f32[256,128]{1,0:T(8,128)S(1)}, f32[256,128]{1,0:T(8,128)S(1)}, f32[256,128]{1,0:T(8,128)S(1)}) custom-call(s32[8,64,128]{2,1,0:T(8,128)} %phase_in.1, f32[8,64,128]{2,1,0:T(8,128)} %density_in.1, f32[1,8,64,128]{3,2,1,0:T(8,128)} %rhs_in.1), custom_call_target="tpu_custom_call" | custom-call | tf_op jit(solution)/shard_map/pallas_call | solution.py:766
  1.9 4.0 %collective-permute-start = (f32[256,128]{1,0:T(8,128)S(1)}, f32[256,128]{1,0:T(8,128)S(1)}, u32[]{:S(2)}, u32[]{:S(2)}) collective-permute-start(f32[256,128]{1,0:T(8,128)S(1)} %get-tuple-element.51), channel_id=1, source_target_pairs={{0,24},{1,25},{8,16},{9,17},{16,8},{17,9},{24,0},{25,1},{2,26},{3,... | collective-permute-start | bytes 393224 | tf_op jit(solution)/shard_map/ppermute | solution.py:713
  5.8 0.5 %collective-permute-start.1 = (f32[256,128]{1,0:T(8,128)S(1)}, f32[256,128]{1,0:T(8,128)S(1)}, u32[]{:S(2)}, u32[]{:S(2)}) collective-permute-start(f32[256,128]{1,0:T(8,128)S(1)} %get-tuple-element.52), channel_id=1, source_target_pairs={{0,8},{1,17},{8,0},{9,25},{16,24},{17,1},{24,16},{25,9},{2,10},{3,... | collective-permute-start | bytes 393224 | tf_op jit(solution)/shard_map/ppermute | solution.py:713
  6.4 0.1 collective-permute-start.2
  6.5 3.3 %collective-permute-done = f32[256,128]{1,0:T(8,128)S(1)} collective-permute-done((f32[256,128]{1,0:T(8,128)S(1)}, f32[256,128]{1,0:T(8,128)S(1)}, u32[]{:S(2)}, u32[]{:S(2)}) %collective-permute-start) | collective-permute-done | bytes 131104 | tf_op jit(solution)/shard_map/ppermute | solution.py:713
  9.7 2.6 %collective-permute-done.1 = f32[256,128]{1,0:T(8,128)S(1)} collective-permute-done((f32[256,128]{1,0:T(8,128)S(1)}, f32[256,128]{1,0:T(8,128)S(1)}, u32[]{:S(2)}, u32[]{:S(2)}) %collective-permute-start.1) | collective-permute-done | bytes 131104 | tf_op jit(solution)/shard_map/ppermute | solution.py:713
  12.4 0.0 collective-permute-done.2
  12.4 0.1 shard_map.51
  12.5 1.6 %collective-permute-start.3 = (f32[4,13,8,128]{3,2,1,0:T(8,128)S(1)}, f32[4,13,8,128]{3,2,1,0:T(8,128)S(1)}, u32[]{:S(2)}, u32[]{:S(2)}) collective-permute-start(f32[4,13,8,128]{3,2,1,0:T(8,128)S(1)} %get-tuple-element.54), channel_id=1, source_target_pairs={{0,8},{1,9},{8,0},{9,1},{24,16},{25,17},{16,24},{17,25},{18,2},{19... | collective-permute-start | bytes 638984 | tf_op jit(solution)/shard_map/ppermute | solution.py:731
  14.1 0.0 collective-permute-start.4
  14.1 0.5 %collective-permute-start.6 = (f32[4,16,2,8,128]{4,3,2,1,0:T(8,128)S(1)}, f32[4,16,2,8,128]{4,3,2,1,0:T(8,128)S(1)}, u32[]{:S(2)}, u32[]{:S(2)}) collective-permute-start(f32[4,16,2,8,128]{4,3,2,1,0:T(8,128)S(1)} %get-tuple-element.56.c), channel_id=1, source_target_pairs={{0,1},{1,0},{2,3},{3,2},{4,5},{5,4},{6,7},{7,6},{8,9},{9,8},{10,11... | collective-permute-start | bytes 1572872 | tf_op jit(solution)/shard_map/ppermute | solution.py:698
  14.6 4.3 %collective-permute-done.3 = f32[4,13,8,128]{3,2,1,0:T(8,128)S(1)} collective-permute-done((f32[4,13,8,128]{3,2,1,0:T(8,128)S(1)}, f32[4,13,8,128]{3,2,1,0:T(8,128)S(1)}, u32[]{:S(2)}, u32[]{:S(2)}) %collective-permute-start.3) | collective-permute-done | bytes 213024 | tf_op jit(solution)/shard_map/ppermute | solution.py:731
  18.9 0.0 collective-permute-done.4
  18.9 0.1 collective-permute-start.5
  19.0 0.0 collective-permute-done.6.zc
  19.0 1.9 %shard_map.52 = (f32[30,2,32,128]{3,2,1,0:T(8,128)S(1)}, f32[30,2,32,128]{3,2,1,0:T(8,128)S(1)}, f32[30,2,32,128]{3,2,1,0:T(8,128)S(1)}, f32[30,2,32,128]{3,2,1,...) custom-call(f32[4,16,2,8,128]{4,3,2,1,0:T(8,128)S(1)} %get-tuple-ele, ...), custom_call_target="tpu_custom_call" | custom-call | bytes 9000000 | tf_op jit(solution)/shard_map/pallas_call | solution.py:791
  20.9 0.0 collective-permute-done.5.zsides
  21.0 3.4 %shard_map.53 = (f32[30,2,32,128]{3,2,1,0:T(8,128)S(1)}, f32[30,2,32,128]{3,2,1,0:T(8,128)S(1)}, f32[30,2,32,128]{3,2,1,0:T(8,128)S(1)}, f32[30,2,32,128]{3,2,1,...) custom-call(f32[8,13,8,128]{3,2,1,0:T(8,128)S(1)} %constant_dynamic-, ...), custom_call_target="tpu_custom_call", output_to_operand_aliasing={{0}: (2, {}), {1}: (3, {}), {2}: (4, {}), {3}: (5, {}), {4}... | custom-call | tf_op jit(solution)/shard_map/pallas_call | solution.py:795
  24.3 2.3 %collective-permute-start.7 = (f32[144,128]{1,0:T(8,128)S(1)}, f32[144,128]{1,0:T(8,128)S(1)}, u32[]{:S(2)}, u32[]{:S(2)}) collective-permute-start(f32[144,128]{1,0:T(8,128)S(1)} %get-tuple-element.73), channel_id=1, source_target_pairs={{0,8},{8,0},{24,16},{16,24},{18,2},{2,18},{10,26},{26,10},{28,20},... | collective-permute-start | bytes 221192 | tf_op jit(solution)/shard_map/ppermute | solution.py:747
  26.7 1.5 %collective-permute-start.9 = (f32[80,128]{1,0:T(8,128)S(1)}, f32[80,128]{1,0:T(8,128)S(1)}, u32[]{:S(2)}, u32[]{:S(2)}) collective-permute-start(f32[80,128]{1,0:T(8,128)S(1)} %get-tuple-element.74.pack), channel_id=1, source_target_pairs={{0,24},{8,16},{24,0},{16,8},{18,10},{2,26},{10,18},{26,2},{28,4},{... | collective-permute-start | bytes 122888 | tf_op jit(solution)/shard_map/ppermute | solution.py:747
  28.2 0.2 collective-permute-start.8
  28.4 0.6 %collective-permute-done.7 = f32[144,128]{1,0:T(8,128)S(1)} collective-permute-done((f32[144,128]{1,0:T(8,128)S(1)}, f32[144,128]{1,0:T(8,128)S(1)}, u32[]{:S(2)}, u32[]{:S(2)}) %collective-permute-start.7) | collective-permute-done | bytes 73760 | tf_op jit(solution)/shard_map/ppermute | solution.py:747
  29.0 3.2 %collective-permute-done.8 = f32[80,128]{1,0:T(8,128)S(1)} collective-permute-done((f32[80,128]{1,0:T(8,128)S(1)}, f32[80,128]{1,0:T(8,128)S(1)}, u32[]{:S(2)}, u32[]{:S(2)}) %collective-permute-start.8) | collective-permute-done | bytes 40992 | tf_op jit(solution)/shard_map/ppermute | solution.py:747
  32.2 0.0 collective-permute-done.9
  32.2 1.1 %collective-permute-start.10 = (f32[304,128]{1,0:T(8,128)S(1)}, f32[304,128]{1,0:T(8,128)S(1)}, u32[]{:S(2)}, u32[]{:S(2)}) collective-permute-start(f32[304,128]{1,0:T(8,128)S(1)} %constant_dynamic-update-slice_fusion.2.mine), channel_id=1, source_target_pairs={{0,1},{1,0},{2,3},{3,2},{4,5},{5,4},{6,7},{7,6},{8,9},{9,8},{10,11... | collective-permute-start | bytes 466952 | tf_op jit(solution)/shard_map/ppermute | solution.py:698
  33.4 0.3 shard_map.54
  33.7 0.7 %collective-permute-done.10.theirs = f32[304,128]{1,0:T(8,128)S(1)} collective-permute-done((f32[304,128]{1,0:T(8,128)S(1)}, f32[304,128]{1,0:T(8,128)S(1)}, u32[]{:S(2)}, u32[]{:S(2)}) %collective-permute-start.10) | collective-permute-done | bytes 155680 | tf_op jit(solution)/shard_map/ppermute | solution.py:698
  34.4 3.4 %shard_map.55 = (f32[4,16,2,8,128]{4,3,2,1,0:T(8,128)S(1)}, f32[29,2,8,128]{3,2,1,0:T(8,128)S(1)}, f32[29,2,8,128]{3,2,1,0:T(8,128)S(1)}, f32[29,2,8,128]{3,2,1,...) custom-call(f32[304,128]{1,0:T(8,128)S(1)} %collective-permute-done., ...), custom_call_target="tpu_custom_call", output_to_operand_aliasing={{1}: (1, {}), {2}: (2, {}), {3}: (3, {}), {4}: (4, {}), {5}... | custom-call | tf_op jit(solution)/shard_map/pallas_call | solution.py:811
  37.9 0.9 %collective-permute-start.12 = (f32[256,128]{1,0:T(8,128)S(1)}, f32[256,128]{1,0:T(8,128)S(1)}, u32[]{:S(2)}, u32[]{:S(2)}) collective-permute-start(f32[256,128]{1,0:T(8,128)S(1)} %bitcast.15), channel_id=1, source_target_pairs={{0,16},{1,9},{8,24},{9,1},{16,0},{17,25},{24,8},{25,17},{2,18},{3,... | collective-permute-start | bytes 393224 | tf_op jit(solution)/shard_map/ppermute | solution.py:713
  38.8 3.3 %collective-permute-start.13 = (f32[256,128]{1,0:T(8,128)S(1)}, f32[256,128]{1,0:T(8,128)S(1)}, u32[]{:S(2)}, u32[]{:S(2)}) collective-permute-start(f32[256,128]{1,0:T(8,128)S(1)} %bitcast.14), channel_id=1, source_target_pairs={{0,24},{1,25},{8,16},{9,17},{16,8},{17,9},{24,0},{25,1},{2,26},{3,... | collective-permute-start | bytes 393224 | tf_op jit(solution)/shard_map/ppermute | solution.py:713
  42.1 0.0 collective-permute-start.11
  42.1 0.8 %collective-permute-done.12.refs_2_ = f32[256,128]{1,0:T(8,128)S(1)} collective-permute-done((f32[256,128]{1,0:T(8,128)S(1)}, f32[256,128]{1,0:T(8,128)S(1)}, u32[]{:S(2)}, u32[]{:S(2)}) %collective-permute-start.12) | collective-permute-done | bytes 131104 | tf_op jit(solution)/shard_map/ppermute | solution.py:713
  42.9 3.4 %collective-permute-done.13.refs_3_ = f32[256,128]{1,0:T(8,128)S(1)} collective-permute-done((f32[256,128]{1,0:T(8,128)S(1)}, f32[256,128]{1,0:T(8,128)S(1)}, u32[]{:S(2)}, u32[]{:S(2)}) %collective-permute-start.13) | collective-permute-done | bytes 131104 | tf_op jit(solution)/shard_map/ppermute | solution.py:713
  46.3 1.0 %collective-permute-done.11.refs_1_ = f32[256,128]{1,0:T(8,128)S(1)} collective-permute-done((f32[256,128]{1,0:T(8,128)S(1)}, f32[256,128]{1,0:T(8,128)S(1)}, u32[]{:S(2)}, u32[]{:S(2)}) %collective-permute-start.11) | collective-permute-done | bytes 131104 | tf_op jit(solution)/shard_map/ppermute | solution.py:713
  47.3 0.9 %shard_map.56 = (f32[1,8,64,128]{3,2,1,0:T(8,128)}, f32[1,8,64,128]{3,2,1,0:T(8,128)}) custom-call(f32[256,128]{1,0:T(8,128)S(1)} %bitcast.8, f32[256,128]{1,0:T(8,128)S(1)} %collective-permute-done.11.refs_1_, f32[256,128]{1,0:T(8,128)S(1)} %collective-permute-done.12.refs_2_, f32[256,128]{1,0:T(8,128)S(1)} %collective-permute-done.13.refs_3_), custom_call_target="tpu_custom_call" | custom-call | tf_op jit(solution)/shard_map/pallas_call | solution.py:819
  (6 shorter events, 0.1 us)
Async XLA Ops:
  1.9 7.9 %collective-permute-start = (f32[256,128]{1,0:T(8,128)S(1)}, f32[256,128]{1,0:T(8,128)S(1)}, u32[]{:S(2)}, u32[]{:S(2)}) collective-permute-start(f32[256,128]{1,0:T(8,128)S(1)} %get-tuple-element.51), channel_id=1, source_target_pairs={{0,24},{1,25},{8,16},{9,17},{16,8},{17,9},{24,0},{25,1},{2,26},{3,... | collective-permute-start | bytes 393224 | tf_op jit(solution)/shard_map/ppermute | solution.py:713
  5.8 6.6 %collective-permute-start.1 = (f32[256,128]{1,0:T(8,128)S(1)}, f32[256,128]{1,0:T(8,128)S(1)}, u32[]{:S(2)}, u32[]{:S(2)}) collective-permute-start(f32[256,128]{1,0:T(8,128)S(1)} %get-tuple-element.52), channel_id=1, source_target_pairs={{0,8},{1,17},{8,0},{9,25},{16,24},{17,1},{24,16},{25,9},{2,10},{3,... | collective-permute-start | bytes 393224 | tf_op jit(solution)/shard_map/ppermute | solution.py:713
  6.4 6.0 %collective-permute-start.2 = (f32[256,128]{1,0:T(8,128)S(1)}, f32[256,128]{1,0:T(8,128)S(1)}, u32[]{:S(2)}, u32[]{:S(2)}) collective-permute-start(f32[256,128]{1,0:T(8,128)S(1)} %get-tuple-element.53), channel_id=1, source_target_pairs={{0,16},{1,9},{8,24},{9,1},{16,0},{17,25},{24,8},{25,17},{2,18},{3,... | collective-permute-start | bytes 393224 | tf_op jit(solution)/shard_map/ppermute | solution.py:713
  12.5 6.4 %collective-permute-start.3 = (f32[4,13,8,128]{3,2,1,0:T(8,128)S(1)}, f32[4,13,8,128]{3,2,1,0:T(8,128)S(1)}, u32[]{:S(2)}, u32[]{:S(2)}) collective-permute-start(f32[4,13,8,128]{3,2,1,0:T(8,128)S(1)} %get-tuple-element.54), channel_id=1, source_target_pairs={{0,8},{1,9},{8,0},{9,1},{24,16},{25,17},{16,24},{17,25},{18,2},{19... | collective-permute-start | bytes 638984 | tf_op jit(solution)/shard_map/ppermute | solution.py:731
  14.1 4.8 %collective-permute-start.4 = (f32[4,13,8,128]{3,2,1,0:T(8,128)S(1)}, f32[4,13,8,128]{3,2,1,0:T(8,128)S(1)}, u32[]{:S(2)}, u32[]{:S(2)}) collective-permute-start(f32[4,13,8,128]{3,2,1,0:T(8,128)S(1)} %get-tuple-element.55), channel_id=1, source_target_pairs={{0,1},{1,0},{8,24},{9,25},{24,8},{25,9},{16,18},{17,19},{18,16},{1... | collective-permute-start | bytes 638984 | tf_op jit(solution)/shard_map/ppermute | solution.py:731
  14.1 4.9 %collective-permute-start.6 = (f32[4,16,2,8,128]{4,3,2,1,0:T(8,128)S(1)}, f32[4,16,2,8,128]{4,3,2,1,0:T(8,128)S(1)}, u32[]{:S(2)}, u32[]{:S(2)}) collective-permute-start(f32[4,16,2,8,128]{4,3,2,1,0:T(8,128)S(1)} %get-tuple-element.56.c), channel_id=1, source_target_pairs={{0,1},{1,0},{2,3},{3,2},{4,5},{5,4},{6,7},{7,6},{8,9},{9,8},{10,11... | collective-permute-start | bytes 1572872 | tf_op jit(solution)/shard_map/ppermute | solution.py:698
  18.9 2.0 %collective-permute-start.5 = (f32[8,13,8,128]{3,2,1,0:T(8,128)S(1)}, f32[8,13,8,128]{3,2,1,0:T(8,128)S(1)}, u32[]{:S(2)}, u32[]{:S(2)}) collective-permute-start(f32[8,13,8,128]{3,2,1,0:T(8,128)S(1)} %constant_dynamic-update-slice_fusion.sides), channel_id=1, source_target_pairs={{0,1},{1,0},{2,3},{3,2},{4,5},{5,4},{6,7},{7,6},{8,9},{9,8},{10,11... | collective-permute-start | bytes 1277960 | tf_op jit(solution)/shard_map/ppermute | solution.py:698
  24.3 4.6 %collective-permute-start.7 = (f32[144,128]{1,0:T(8,128)S(1)}, f32[144,128]{1,0:T(8,128)S(1)}, u32[]{:S(2)}, u32[]{:S(2)}) collective-permute-start(f32[144,128]{1,0:T(8,128)S(1)} %get-tuple-element.73), channel_id=1, source_target_pairs={{0,8},{8,0},{24,16},{16,24},{18,2},{2,18},{10,26},{26,10},{28,20},... | collective-permute-start | bytes 221192 | tf_op jit(solution)/shard_map/ppermute | solution.py:747
  26.7 5.5 %collective-permute-start.9 = (f32[80,128]{1,0:T(8,128)S(1)}, f32[80,128]{1,0:T(8,128)S(1)}, u32[]{:S(2)}, u32[]{:S(2)}) collective-permute-start(f32[80,128]{1,0:T(8,128)S(1)} %get-tuple-element.74.pack), channel_id=1, source_target_pairs={{0,24},{8,16},{24,0},{16,8},{18,10},{2,26},{10,18},{26,2},{28,4},{... | collective-permute-start | bytes 122888 | tf_op jit(solution)/shard_map/ppermute | solution.py:747
  28.2 4.0 %collective-permute-start.8 = (f32[80,128]{1,0:T(8,128)S(1)}, f32[80,128]{1,0:T(8,128)S(1)}, u32[]{:S(2)}, u32[]{:S(2)}) collective-permute-start(f32[80,128]{1,0:T(8,128)S(1)} %get-tuple-element.74.pack), channel_id=1, source_target_pairs={{0,16},{8,18},{24,2},{16,0},{18,8},{2,24},{10,20},{26,4},{28,12},{... | collective-permute-start | bytes 122888 | tf_op jit(solution)/shard_map/ppermute | solution.py:747
  32.2 2.2 %collective-permute-start.10 = (f32[304,128]{1,0:T(8,128)S(1)}, f32[304,128]{1,0:T(8,128)S(1)}, u32[]{:S(2)}, u32[]{:S(2)}) collective-permute-start(f32[304,128]{1,0:T(8,128)S(1)} %constant_dynamic-update-slice_fusion.2.mine), channel_id=1, source_target_pairs={{0,1},{1,0},{2,3},{3,2},{4,5},{5,4},{6,7},{7,6},{8,9},{9,8},{10,11... | collective-permute-start | bytes 466952 | tf_op jit(solution)/shard_map/ppermute | solution.py:698
  37.9 5.0 %collective-permute-start.12 = (f32[256,128]{1,0:T(8,128)S(1)}, f32[256,128]{1,0:T(8,128)S(1)}, u32[]{:S(2)}, u32[]{:S(2)}) collective-permute-start(f32[256,128]{1,0:T(8,128)S(1)} %bitcast.15), channel_id=1, source_target_pairs={{0,16},{1,9},{8,24},{9,1},{16,0},{17,25},{24,8},{25,17},{2,18},{3,... | collective-permute-start | bytes 393224 | tf_op jit(solution)/shard_map/ppermute | solution.py:713
  38.8 7.5 %collective-permute-start.13 = (f32[256,128]{1,0:T(8,128)S(1)}, f32[256,128]{1,0:T(8,128)S(1)}, u32[]{:S(2)}, u32[]{:S(2)}) collective-permute-start(f32[256,128]{1,0:T(8,128)S(1)} %bitcast.14), channel_id=1, source_target_pairs={{0,24},{1,25},{8,16},{9,17},{16,8},{17,9},{24,0},{25,1},{2,26},{3,... | collective-permute-start | bytes 393224 | tf_op jit(solution)/shard_map/ppermute | solution.py:713
  42.1 5.2 %collective-permute-start.11 = (f32[256,128]{1,0:T(8,128)S(1)}, f32[256,128]{1,0:T(8,128)S(1)}, u32[]{:S(2)}, u32[]{:S(2)}) collective-permute-start(f32[256,128]{1,0:T(8,128)S(1)} %bitcast.13), channel_id=1, source_target_pairs={{0,8},{1,17},{8,0},{9,25},{16,24},{17,1},{24,16},{25,9},{2,10},{3,... | collective-permute-start | bytes 393224 | tf_op jit(solution)/shard_map/ppermute | solution.py:713

commit v13 on v11

--- a/solution.py
+++ b/solution.py
@@ -29,7 +29,7 @@
         self.paired = self.gz == 2
         self.ring = [0, 1, 3, 2] if self.gx == 4 else list(range(self.gx))
         self.place = [self.ring.index(i) for i in range(self.gx)]
-        self.back = [0, 2, 3, 1] if self.gx == 4 else list(range(self.gx))
+        self.back = [0, 3, 1, 2] if self.gx == 4 else list(range(self.gx))
 
     def device(self, block):
         j, q = divmod(block, self.gx)
@@ -45,7 +45,7 @@
     def distances(self, core):
         if self.gx != 4:
             return list(range(self.gx))
-        return [0, 3, 2, 1] if core else [0, 3, 1, 2]
+        return [0, 1, 3, 2] if core else [0, 2, 3, 1]
 
     def by_core(self, even, odd):
         return even if even == odd else jnp.where(lax.rem(lax.axis_index("gz"), 2) == 0, even, odd)

time: 48.3 us -> 48.5 us (level)
  waiting for transfers between devices: 19.3 us -> 20.6 us
  starting transfers between devices: 16.8 us -> 15.8 us
    ppermute x2, waiting for transfers between devices: 4.31 us -> 5.91 us  [swap_blocks(): return lax.ppermute(a, ('gx', 'gy', 'gz'), pairs)]
where the time goes in v13:
time: 48.5 us; the launch traced here: 48.4 us
  waiting for transfers between devices  20.6 us (42%)
  starting transfers between devices  15.8 us (33%)
  Pallas kernels  11.2 us (23%)
  between operations  0.74 us (2%)
    ppermute x6, waiting for transfers between devices, exchange(): got.append(lax.ppermute(parts[slot], ('gx', 'gz'), pairs))  11 us
    ppermute x6, starting transfers between devices, exchange(): got.append(lax.ppermute(parts[slot], ('gx', 'gz'), pairs))  8.4 us
    ppermute x2, waiting for transfers between devices, swap_blocks(): return lax.ppermute(a, ('gx', 'gy', 'gz'), pairs)  5.91 us
    ppermute x3, starting transfers between devices, swap_blocks_apart(): return lax.ppermute(a, ('gx', 'gy', 'gz'), pairs)  5.75 us
    pallas_call x1, Pallas kernels, on_device(): call(functools.partial(up_kernel, plan), [in_vmem(gx, by, 2, px, LANES)]...  3.43 us
    pallas_call x1, Pallas kernels, on_device(): call(functools.partial(down_kernel, plan), outs, scratch, input_output_al...  3.38 us
    ppermute x3, waiting for transfers between devices, swap_blocks_apart(): return lax.ppermute(a, ('gx', 'gy', 'gz'), pairs)  2.67 us
    pallas_call x1, Pallas kernels, on_device(): call(functools.partial(inner_kernel, plan), Finest.shapes(plan), work=900...  1.91 us
  transfers between devices with their start and end apart: 14, of which 8 were waited for; matrix products, arithmetic and copies ran while one was open for 0% of the time, Pallas kernels for 5%

profile of v13, /device:TPU:0, one launch (start us, length us, event | category | flops | bytes accessed | tf_op | source)
XLA Modules:
  0.0 48.4 jit_solution(11072666685970379850)
XLA Ops:
  0.6 1.2 %shard_map.50 = (f32[256,128]{1,0:T(8,128)S(1)}, f32[256,128]{1,0:T(8,128)S(1)}, f32[256,128]{1,0:T(8,128)S(1)}, f32[256,128]{1,0:T(8,128)S(1)}) custom-call(s32[8,64,128]{2,1,0:T(8,128)} %phase_in.1, f32[8,64,128]{2,1,0:T(8,128)} %density_in.1, f32[1,8,64,128]{3,2,1,0:T(8,128)} %rhs_in.1), custom_call_target="tpu_custom_call" | custom-call | tf_op jit(solution)/shard_map/pallas_call | solution.py:766
  1.9 3.0 %collective-permute-start = (f32[256,128]{1,0:T(8,128)S(1)}, f32[256,128]{1,0:T(8,128)S(1)}, u32[]{:S(2)}, u32[]{:S(2)}) collective-permute-start(f32[256,128]{1,0:T(8,128)S(1)} %get-tuple-element.51), channel_id=1, source_target_pairs={{0,16},{1,9},{8,24},{9,1},{16,0},{17,25},{24,8},{25,17},{2,18},{3,... | collective-permute-start | bytes 393224 | tf_op jit(solution)/shard_map/ppermute | solution.py:713
  4.9 1.4 %collective-permute-start.1 = (f32[256,128]{1,0:T(8,128)S(1)}, f32[256,128]{1,0:T(8,128)S(1)}, u32[]{:S(2)}, u32[]{:S(2)}) collective-permute-start(f32[256,128]{1,0:T(8,128)S(1)} %get-tuple-element.52), channel_id=1, source_target_pairs={{0,24},{1,25},{8,16},{9,17},{16,8},{17,9},{24,0},{25,1},{2,26},{3,... | collective-permute-start | bytes 393224 | tf_op jit(solution)/shard_map/ppermute | solution.py:713
  6.3 0.1 collective-permute-start.2
  6.5 5.1 %collective-permute-done = f32[256,128]{1,0:T(8,128)S(1)} collective-permute-done((f32[256,128]{1,0:T(8,128)S(1)}, f32[256,128]{1,0:T(8,128)S(1)}, u32[]{:S(2)}, u32[]{:S(2)}) %collective-permute-start) | collective-permute-done | bytes 131104 | tf_op jit(solution)/shard_map/ppermute | solution.py:713
  11.5 0.0 collective-permute-done.1
  11.5 0.7 %collective-permute-done.2 = f32[256,128]{1,0:T(8,128)S(1)} collective-permute-done((f32[256,128]{1,0:T(8,128)S(1)}, f32[256,128]{1,0:T(8,128)S(1)}, u32[]{:S(2)}, u32[]{:S(2)}) %collective-permute-start.2) | collective-permute-done | bytes 131104 | tf_op jit(solution)/shard_map/ppermute | solution.py:713
  12.2 0.1 shard_map.51
  12.3 0.8 %collective-permute-start.3 = (f32[4,13,8,128]{3,2,1,0:T(8,128)S(1)}, f32[4,13,8,128]{3,2,1,0:T(8,128)S(1)}, u32[]{:S(2)}, u32[]{:S(2)}) collective-permute-start(f32[4,13,8,128]{3,2,1,0:T(8,128)S(1)} %get-tuple-element.54), channel_id=1, source_target_pairs={{0,8},{1,9},{8,0},{9,1},{24,16},{25,17},{16,24},{17,25},{18,2},{19... | collective-permute-start | bytes 638984 | tf_op jit(solution)/shard_map/ppermute | solution.py:731
  13.1 0.6 %collective-permute-start.4 = (f32[4,13,8,128]{3,2,1,0:T(8,128)S(1)}, f32[4,13,8,128]{3,2,1,0:T(8,128)S(1)}, u32[]{:S(2)}, u32[]{:S(2)}) collective-permute-start(f32[4,13,8,128]{3,2,1,0:T(8,128)S(1)} %get-tuple-element.55), channel_id=1, source_target_pairs={{0,1},{1,0},{8,24},{9,25},{24,8},{25,9},{16,18},{17,19},{18,16},{1... | collective-permute-start | bytes 638984 | tf_op jit(solution)/shard_map/ppermute | solution.py:731
  13.7 0.0 collective-permute-start.6
  13.7 5.9 %collective-permute-done.3 = f32[4,13,8,128]{3,2,1,0:T(8,128)S(1)} collective-permute-done((f32[4,13,8,128]{3,2,1,0:T(8,128)S(1)}, f32[4,13,8,128]{3,2,1,0:T(8,128)S(1)}, u32[]{:S(2)}, u32[]{:S(2)}) %collective-permute-start.3) | collective-permute-done | bytes 213024 | tf_op jit(solution)/shard_map/ppermute | solution.py:731
  19.7 0.0 collective-permute-done.4
  19.7 0.1 collective-permute-start.5
  19.8 0.0 collective-permute-done.6.zc
  19.8 1.9 %shard_map.52 = (f32[30,2,32,128]{3,2,1,0:T(8,128)S(1)}, f32[30,2,32,128]{3,2,1,0:T(8,128)S(1)}, f32[30,2,32,128]{3,2,1,0:T(8,128)S(1)}, f32[30,2,32,128]{3,2,1,...) custom-call(f32[4,16,2,8,128]{4,3,2,1,0:T(8,128)S(1)} %get-tuple-ele, ...), custom_call_target="tpu_custom_call" | custom-call | bytes 9000000 | tf_op jit(solution)/shard_map/pallas_call | solution.py:791
  21.7 0.0 collective-permute-done.5.zsides
  21.7 3.4 %shard_map.53 = (f32[30,2,32,128]{3,2,1,0:T(8,128)S(1)}, f32[30,2,32,128]{3,2,1,0:T(8,128)S(1)}, f32[30,2,32,128]{3,2,1,0:T(8,128)S(1)}, f32[30,2,32,128]{3,2,1,...) custom-call(f32[8,13,8,128]{3,2,1,0:T(8,128)S(1)} %constant_dynamic-, ...), custom_call_target="tpu_custom_call", output_to_operand_aliasing={{0}: (2, {}), {1}: (3, {}), {2}: (4, {}), {3}: (5, {}), {4}... | custom-call | tf_op jit(solution)/shard_map/pallas_call | solution.py:795
  25.1 1.8 %collective-permute-start.7 = (f32[144,128]{1,0:T(8,128)S(1)}, f32[144,128]{1,0:T(8,128)S(1)}, u32[]{:S(2)}, u32[]{:S(2)}) collective-permute-start(f32[144,128]{1,0:T(8,128)S(1)} %get-tuple-element.73), channel_id=1, source_target_pairs={{0,8},{8,0},{24,16},{16,24},{18,2},{2,18},{10,26},{26,10},{28,20},... | collective-permute-start | bytes 221192 | tf_op jit(solution)/shard_map/ppermute | solution.py:747
  26.9 1.7 %collective-permute-start.9 = (f32[80,128]{1,0:T(8,128)S(1)}, f32[80,128]{1,0:T(8,128)S(1)}, u32[]{:S(2)}, u32[]{:S(2)}) collective-permute-start(f32[80,128]{1,0:T(8,128)S(1)} %get-tuple-element.74.pack), channel_id=1, source_target_pairs={{0,16},{8,18},{24,2},{16,0},{18,8},{2,24},{10,20},{26,4},{28,12},{... | collective-permute-start | bytes 122888 | tf_op jit(solution)/shard_map/ppermute | solution.py:747
  28.6 2.2 %collective-permute-start.8 = (f32[80,128]{1,0:T(8,128)S(1)}, f32[80,128]{1,0:T(8,128)S(1)}, u32[]{:S(2)}, u32[]{:S(2)}) collective-permute-start(f32[80,128]{1,0:T(8,128)S(1)} %get-tuple-element.74.pack), channel_id=1, source_target_pairs={{0,24},{8,16},{24,0},{16,8},{18,10},{2,26},{10,18},{26,2},{28,4},{... | collective-permute-start | bytes 122888 | tf_op jit(solution)/shard_map/ppermute | solution.py:747
  30.9 0.0 collective-permute-done.7
  30.9 2.7 %collective-permute-done.8 = f32[80,128]{1,0:T(8,128)S(1)} collective-permute-done((f32[80,128]{1,0:T(8,128)S(1)}, f32[80,128]{1,0:T(8,128)S(1)}, u32[]{:S(2)}, u32[]{:S(2)}) %collective-permute-start.8) | collective-permute-done | bytes 40992 | tf_op jit(solution)/shard_map/ppermute | solution.py:747
  33.5 0.0 collective-permute-done.9
  33.6 0.1 collective-permute-start.10
  33.7 0.3 shard_map.54
  34.0 1.0 %collective-permute-done.10.theirs = f32[304,128]{1,0:T(8,128)S(1)} collective-permute-done((f32[304,128]{1,0:T(8,128)S(1)}, f32[304,128]{1,0:T(8,128)S(1)}, u32[]{:S(2)}, u32[]{:S(2)}) %collective-permute-start.10) | collective-permute-done | bytes 155680 | tf_op jit(solution)/shard_map/ppermute | solution.py:698
  35.0 3.4 %shard_map.55 = (f32[4,16,2,8,128]{4,3,2,1,0:T(8,128)S(1)}, f32[29,2,8,128]{3,2,1,0:T(8,128)S(1)}, f32[29,2,8,128]{3,2,1,0:T(8,128)S(1)}, f32[29,2,8,128]{3,2,1,...) custom-call(f32[304,128]{1,0:T(8,128)S(1)} %collective-permute-done., ...), custom_call_target="tpu_custom_call", output_to_operand_aliasing={{1}: (1, {}), {2}: (2, {}), {3}: (3, {}), {4}: (4, {}), {5}... | custom-call | tf_op jit(solution)/shard_map/pallas_call | solution.py:811
  38.5 1.0 %collective-permute-start.12 = (f32[256,128]{1,0:T(8,128)S(1)}, f32[256,128]{1,0:T(8,128)S(1)}, u32[]{:S(2)}, u32[]{:S(2)}) collective-permute-start(f32[256,128]{1,0:T(8,128)S(1)} %bitcast.15), channel_id=1, source_target_pairs={{0,16},{1,9},{8,24},{9,1},{16,0},{17,25},{24,8},{25,17},{2,18},{3,... | collective-permute-start | bytes 393224 | tf_op jit(solution)/shard_map/ppermute | solution.py:713
  39.5 2.9 %collective-permute-start.13 = (f32[256,128]{1,0:T(8,128)S(1)}, f32[256,128]{1,0:T(8,128)S(1)}, u32[]{:S(2)}, u32[]{:S(2)}) collective-permute-start(f32[256,128]{1,0:T(8,128)S(1)} %bitcast.14), channel_id=1, source_target_pairs={{0,24},{1,25},{8,16},{9,17},{16,8},{17,9},{24,0},{25,1},{2,26},{3,... | collective-permute-start | bytes 393224 | tf_op jit(solution)/shard_map/ppermute | solution.py:713
  42.3 0.0 collective-permute-start.11
  42.3 1.4 %collective-permute-done.12.refs_2_ = f32[256,128]{1,0:T(8,128)S(1)} collective-permute-done((f32[256,128]{1,0:T(8,128)S(1)}, f32[256,128]{1,0:T(8,128)S(1)}, u32[]{:S(2)}, u32[]{:S(2)}) %collective-permute-start.12) | collective-permute-done | bytes 131104 | tf_op jit(solution)/shard_map/ppermute | solution.py:713
  43.7 2.8 %collective-permute-done.13.refs_3_ = f32[256,128]{1,0:T(8,128)S(1)} collective-permute-done((f32[256,128]{1,0:T(8,128)S(1)}, f32[256,128]{1,0:T(8,128)S(1)}, u32[]{:S(2)}, u32[]{:S(2)}) %collective-permute-start.13) | collective-permute-done | bytes 131104 | tf_op jit(solution)/shard_map/ppermute | solution.py:713
  46.5 1.0 %collective-permute-done.11.refs_1_ = f32[256,128]{1,0:T(8,128)S(1)} collective-permute-done((f32[256,128]{1,0:T(8,128)S(1)}, f32[256,128]{1,0:T(8,128)S(1)}, u32[]{:S(2)}, u32[]{:S(2)}) %collective-permute-start.11) | collective-permute-done | bytes 131104 | tf_op jit(solution)/shard_map/ppermute | solution.py:713
  47.5 0.9 %shard_map.56 = (f32[1,8,64,128]{3,2,1,0:T(8,128)}, f32[1,8,64,128]{3,2,1,0:T(8,128)}) custom-call(f32[256,128]{1,0:T(8,128)S(1)} %bitcast.8, f32[256,128]{1,0:T(8,128)S(1)} %collective-permute-done.11.refs_1_, f32[256,128]{1,0:T(8,128)S(1)} %collective-permute-done.12.refs_2_, f32[256,128]{1,0:T(8,128)S(1)} %collective-permute-done.13.refs_3_), custom_call_target="tpu_custom_call" | custom-call | tf_op jit(solution)/shard_map/pallas_call | solution.py:819
  (6 shorter events, 0.1 us)
Async XLA Ops:
  1.9 9.6 %collective-permute-start = (f32[256,128]{1,0:T(8,128)S(1)}, f32[256,128]{1,0:T(8,128)S(1)}, u32[]{:S(2)}, u32[]{:S(2)}) collective-permute-start(f32[256,128]{1,0:T(8,128)S(1)} %get-tuple-element.51), channel_id=1, source_target_pairs={{0,16},{1,9},{8,24},{9,1},{16,0},{17,25},{24,8},{25,17},{2,18},{3,... | collective-permute-start | bytes 393224 | tf_op jit(solution)/shard_map/ppermute | solution.py:713
  4.9 6.6 %collective-permute-start.1 = (f32[256,128]{1,0:T(8,128)S(1)}, f32[256,128]{1,0:T(8,128)S(1)}, u32[]{:S(2)}, u32[]{:S(2)}) collective-permute-start(f32[256,128]{1,0:T(8,128)S(1)} %get-tuple-element.52), channel_id=1, source_target_pairs={{0,24},{1,25},{8,16},{9,17},{16,8},{17,9},{24,0},{25,1},{2,26},{3,... | collective-permute-start | bytes 393224 | tf_op jit(solution)/shard_map/ppermute | solution.py:713
  6.3 5.9 %collective-permute-start.2 = (f32[256,128]{1,0:T(8,128)S(1)}, f32[256,128]{1,0:T(8,128)S(1)}, u32[]{:S(2)}, u32[]{:S(2)}) collective-permute-start(f32[256,128]{1,0:T(8,128)S(1)} %get-tuple-element.53), channel_id=1, source_target_pairs={{0,8},{1,17},{8,0},{9,25},{16,24},{17,1},{24,16},{25,9},{2,10},{3,... | collective-permute-start | bytes 393224 | tf_op jit(solution)/shard_map/ppermute | solution.py:713
  12.3 7.3 %collective-permute-start.3 = (f32[4,13,8,128]{3,2,1,0:T(8,128)S(1)}, f32[4,13,8,128]{3,2,1,0:T(8,128)S(1)}, u32[]{:S(2)}, u32[]{:S(2)}) collective-permute-start(f32[4,13,8,128]{3,2,1,0:T(8,128)S(1)} %get-tuple-element.54), channel_id=1, source_target_pairs={{0,8},{1,9},{8,0},{9,1},{24,16},{25,17},{16,24},{17,25},{18,2},{19... | collective-permute-start | bytes 638984 | tf_op jit(solution)/shard_map/ppermute | solution.py:731
  13.1 6.6 %collective-permute-start.4 = (f32[4,13,8,128]{3,2,1,0:T(8,128)S(1)}, f32[4,13,8,128]{3,2,1,0:T(8,128)S(1)}, u32[]{:S(2)}, u32[]{:S(2)}) collective-permute-start(f32[4,13,8,128]{3,2,1,0:T(8,128)S(1)} %get-tuple-element.55), channel_id=1, source_target_pairs={{0,1},{1,0},{8,24},{9,25},{24,8},{25,9},{16,18},{17,19},{18,16},{1... | collective-permute-start | bytes 638984 | tf_op jit(solution)/shard_map/ppermute | solution.py:731
  13.7 6.0 %collective-permute-start.6 = (f32[4,16,2,8,128]{4,3,2,1,0:T(8,128)S(1)}, f32[4,16,2,8,128]{4,3,2,1,0:T(8,128)S(1)}, u32[]{:S(2)}, u32[]{:S(2)}) collective-permute-start(f32[4,16,2,8,128]{4,3,2,1,0:T(8,128)S(1)} %get-tuple-element.56.c), channel_id=1, source_target_pairs={{0,1},{1,0},{2,3},{3,2},{4,5},{5,4},{6,7},{7,6},{8,9},{9,8},{10,11... | collective-permute-start | bytes 1572872 | tf_op jit(solution)/shard_map/ppermute | solution.py:698
  19.7 2.0 %collective-permute-start.5 = (f32[8,13,8,128]{3,2,1,0:T(8,128)S(1)}, f32[8,13,8,128]{3,2,1,0:T(8,128)S(1)}, u32[]{:S(2)}, u32[]{:S(2)}) collective-permute-start(f32[8,13,8,128]{3,2,1,0:T(8,128)S(1)} %constant_dynamic-update-slice_fusion.sides), channel_id=1, source_target_pairs={{0,1},{1,0},{2,3},{3,2},{4,5},{5,4},{6,7},{7,6},{8,9},{9,8},{10,11... | collective-permute-start | bytes 1277960 | tf_op jit(solution)/shard_map/ppermute | solution.py:698
  25.1 5.8 %collective-permute-start.7 = (f32[144,128]{1,0:T(8,128)S(1)}, f32[144,128]{1,0:T(8,128)S(1)}, u32[]{:S(2)}, u32[]{:S(2)}) collective-permute-start(f32[144,128]{1,0:T(8,128)S(1)} %get-tuple-element.73), channel_id=1, source_target_pairs={{0,8},{8,0},{24,16},{16,24},{18,2},{2,18},{10,26},{26,10},{28,20},... | collective-permute-start | bytes 221192 | tf_op jit(solution)/shard_map/ppermute | solution.py:747
  26.9 6.7 %collective-permute-start.9 = (f32[80,128]{1,0:T(8,128)S(1)}, f32[80,128]{1,0:T(8,128)S(1)}, u32[]{:S(2)}, u32[]{:S(2)}) collective-permute-start(f32[80,128]{1,0:T(8,128)S(1)} %get-tuple-element.74.pack), channel_id=1, source_target_pairs={{0,16},{8,18},{24,2},{16,0},{18,8},{2,24},{10,20},{26,4},{28,12},{... | collective-permute-start | bytes 122888 | tf_op jit(solution)/shard_map/ppermute | solution.py:747
  28.6 4.9 %collective-permute-start.8 = (f32[80,128]{1,0:T(8,128)S(1)}, f32[80,128]{1,0:T(8,128)S(1)}, u32[]{:S(2)}, u32[]{:S(2)}) collective-permute-start(f32[80,128]{1,0:T(8,128)S(1)} %get-tuple-element.74.pack), channel_id=1, source_target_pairs={{0,24},{8,16},{24,0},{16,8},{18,10},{2,26},{10,18},{26,2},{28,4},{... | collective-permute-start | bytes 122888 | tf_op jit(solution)/shard_map/ppermute | solution.py:747
  33.6 1.4 %collective-permute-start.10 = (f32[304,128]{1,0:T(8,128)S(1)}, f32[304,128]{1,0:T(8,128)S(1)}, u32[]{:S(2)}, u32[]{:S(2)}) collective-permute-start(f32[304,128]{1,0:T(8,128)S(1)} %constant_dynamic-update-slice_fusion.2.mine), channel_id=1, source_target_pairs={{0,1},{1,0},{2,3},{3,2},{4,5},{5,4},{6,7},{7,6},{8,9},{9,8},{10,11... | collective-permute-start | bytes 466952 | tf_op jit(solution)/shard_map/ppermute | solution.py:698
  38.5 5.2 %collective-permute-start.12 = (f32[256,128]{1,0:T(8,128)S(1)}, f32[256,128]{1,0:T(8,128)S(1)}, u32[]{:S(2)}, u32[]{:S(2)}) collective-permute-start(f32[256,128]{1,0:T(8,128)S(1)} %bitcast.15), channel_id=1, source_target_pairs={{0,16},{1,9},{8,24},{9,1},{16,0},{17,25},{24,8},{25,17},{2,18},{3,... | collective-permute-start | bytes 393224 | tf_op jit(solution)/shard_map/ppermute | solution.py:713
  39.5 7.1 %collective-permute-start.13 = (f32[256,128]{1,0:T(8,128)S(1)}, f32[256,128]{1,0:T(8,128)S(1)}, u32[]{:S(2)}, u32[]{:S(2)}) collective-permute-start(f32[256,128]{1,0:T(8,128)S(1)} %bitcast.14), channel_id=1, source_target_pairs={{0,24},{1,25},{8,16},{9,17},{16,8},{17,9},{24,0},{25,1},{2,26},{3,... | collective-permute-start | bytes 393224 | tf_op jit(solution)/shard_map/ppermute | solution.py:713
  42.3 5.2 %collective-permute-start.11 = (f32[256,128]{1,0:T(8,128)S(1)}, f32[256,128]{1,0:T(8,128)S(1)}, u32[]{:S(2)}, u32[]{:S(2)}) collective-permute-start(f32[256,128]{1,0:T(8,128)S(1)} %bitcast.13), channel_id=1, source_target_pairs={{0,8},{1,17},{8,0},{9,25},{16,24},{17,1},{24,16},{25,9},{2,10},{3,... | collective-permute-start | bytes 393224 | tf_op jit(solution)/shard_map/ppermute | solution.py:713

commit v14 on v11

--- a/solution.py
+++ b/solution.py
@@ -45,7 +45,7 @@
     def distances(self, core):
         if self.gx != 4:
             return list(range(self.gx))
-        return [0, 3, 2, 1] if core else [0, 3, 1, 2]
+        return [0, 3, 1, 2]
 
     def by_core(self, even, odd):
         return even if even == odd else jnp.where(lax.rem(lax.axis_index("gz"), 2) == 0, even, odd)

time: 48.3 us -> 48.9 us (1.012)
  waiting for transfers between devices: 19.3 us -> 19.8 us
    ppermute x6, waiting for transfers between devices: 11.1 us -> 11.7 us  [exchange(): got.append(lax.ppermute(parts[slot], ('gx', 'gz'), pairs))]
where the time goes in v14:
time: 48.9 us; the launch traced here: 48.8 us
  waiting for transfers between devices  19.8 us (40%)
  starting transfers between devices  16.9 us (35%)
  Pallas kernels  11.2 us (23%)
  between operations  0.75 us (2%)
    ppermute x6, waiting for transfers between devices, exchange(): got.append(lax.ppermute(parts[slot], ('gx', 'gz'), pairs))  11.7 us
    ppermute x6, starting transfers between devices, exchange(): got.append(lax.ppermute(parts[slot], ('gx', 'gz'), pairs))  8.44 us
    ppermute x3, starting transfers between devices, swap_blocks_apart(): return lax.ppermute(a, ('gx', 'gy', 'gz'), pairs)  6.27 us
    ppermute x2, waiting for transfers between devices, swap_blocks(): return lax.ppermute(a, ('gx', 'gy', 'gz'), pairs)  4.24 us
    pallas_call x1, Pallas kernels, on_device(): call(functools.partial(up_kernel, plan), [in_vmem(gx, by, 2, px, LANES)]...  3.44 us
    pallas_call x1, Pallas kernels, on_device(): call(functools.partial(down_kernel, plan), outs, scratch, input_output_al...  3.38 us
    ppermute x3, waiting for transfers between devices, swap_blocks_apart(): return lax.ppermute(a, ('gx', 'gy', 'gz'), pairs)  2.79 us
    pallas_call x1, Pallas kernels, on_device(): call(functools.partial(inner_kernel, plan), Finest.shapes(plan), work=900...  1.91 us
  transfers between devices with their start and end apart: 14, of which 8 were waited for; matrix products, arithmetic and copies ran while one was open for 0% of the time, Pallas kernels for 5%

profile of v14, /device:TPU:0, one launch (start us, length us, event | category | flops | bytes accessed | tf_op | source)
XLA Modules:
  0.0 48.8 jit_solution(11965864062181805587)
XLA Ops:
  0.6 1.2 %shard_map.50 = (f32[256,128]{1,0:T(8,128)S(1)}, f32[256,128]{1,0:T(8,128)S(1)}, f32[256,128]{1,0:T(8,128)S(1)}, f32[256,128]{1,0:T(8,128)S(1)}) custom-call(s32[8,64,128]{2,1,0:T(8,128)} %phase_in.1, f32[8,64,128]{2,1,0:T(8,128)} %density_in.1, f32[1,8,64,128]{3,2,1,0:T(8,128)} %rhs_in.1), custom_call_target="tpu_custom_call" | custom-call | tf_op jit(solution)/shard_map/pallas_call | solution.py:766
  1.9 4.0 %collective-permute-start = (f32[256,128]{1,0:T(8,128)S(1)}, f32[256,128]{1,0:T(8,128)S(1)}, u32[]{:S(2)}, u32[]{:S(2)}) collective-permute-start(f32[256,128]{1,0:T(8,128)S(1)} %get-tuple-element.51), channel_id=1, source_target_pairs={{0,24},{1,25},{8,16},{9,17},{16,8},{17,9},{24,0},{25,1},{2,26},{3,... | collective-permute-start | bytes 393224 | tf_op jit(solution)/shard_map/ppermute | solution.py:713
  5.8 0.5 %collective-permute-start.1 = (f32[256,128]{1,0:T(8,128)S(1)}, f32[256,128]{1,0:T(8,128)S(1)}, u32[]{:S(2)}, u32[]{:S(2)}) collective-permute-start(f32[256,128]{1,0:T(8,128)S(1)} %get-tuple-element.52), channel_id=1, source_target_pairs={{0,8},{1,9},{8,0},{9,1},{16,24},{17,25},{24,16},{25,17},{2,10},{3,... | collective-permute-start | bytes 393224 | tf_op jit(solution)/shard_map/ppermute | solution.py:713
  6.4 0.1 collective-permute-start.2
  6.5 3.7 %collective-permute-done = f32[256,128]{1,0:T(8,128)S(1)} collective-permute-done((f32[256,128]{1,0:T(8,128)S(1)}, f32[256,128]{1,0:T(8,128)S(1)}, u32[]{:S(2)}, u32[]{:S(2)}) %collective-permute-start) | collective-permute-done | bytes 131104 | tf_op jit(solution)/shard_map/ppermute | solution.py:713
  10.2 2.2 %collective-permute-done.1 = f32[256,128]{1,0:T(8,128)S(1)} collective-permute-done((f32[256,128]{1,0:T(8,128)S(1)}, f32[256,128]{1,0:T(8,128)S(1)}, u32[]{:S(2)}, u32[]{:S(2)}) %collective-permute-start.1) | collective-permute-done | bytes 131104 | tf_op jit(solution)/shard_map/ppermute | solution.py:713
  12.4 0.0 collective-permute-done.2
  12.4 0.1 shard_map.51
  12.5 1.6 %collective-permute-start.3 = (f32[4,13,8,128]{3,2,1,0:T(8,128)S(1)}, f32[4,13,8,128]{3,2,1,0:T(8,128)S(1)}, u32[]{:S(2)}, u32[]{:S(2)}) collective-permute-start(f32[4,13,8,128]{3,2,1,0:T(8,128)S(1)} %get-tuple-element.54), channel_id=1, source_target_pairs={{0,8},{1,9},{8,0},{9,1},{24,16},{25,17},{16,24},{17,25},{18,2},{19... | collective-permute-start | bytes 638984 | tf_op jit(solution)/shard_map/ppermute | solution.py:731
  14.0 0.0 collective-permute-start.4
  14.0 0.5 %collective-permute-start.6 = (f32[4,16,2,8,128]{4,3,2,1,0:T(8,128)S(1)}, f32[4,16,2,8,128]{4,3,2,1,0:T(8,128)S(1)}, u32[]{:S(2)}, u32[]{:S(2)}) collective-permute-start(f32[4,16,2,8,128]{4,3,2,1,0:T(8,128)S(1)} %get-tuple-element.56.c), channel_id=1, source_target_pairs={{0,1},{1,0},{2,3},{3,2},{4,5},{5,4},{6,7},{7,6},{8,9},{9,8},{10,11... | collective-permute-start | bytes 1572872 | tf_op jit(solution)/shard_map/ppermute | solution.py:698
  14.5 4.2 %collective-permute-done.3 = f32[4,13,8,128]{3,2,1,0:T(8,128)S(1)} collective-permute-done((f32[4,13,8,128]{3,2,1,0:T(8,128)S(1)}, f32[4,13,8,128]{3,2,1,0:T(8,128)S(1)}, u32[]{:S(2)}, u32[]{:S(2)}) %collective-permute-start.3) | collective-permute-done | bytes 213024 | tf_op jit(solution)/shard_map/ppermute | solution.py:731
  18.8 0.0 collective-permute-done.4
  18.8 0.1 collective-permute-start.5
  18.9 0.0 collective-permute-done.6.zc
  18.9 1.9 %shard_map.52 = (f32[30,2,32,128]{3,2,1,0:T(8,128)S(1)}, f32[30,2,32,128]{3,2,1,0:T(8,128)S(1)}, f32[30,2,32,128]{3,2,1,0:T(8,128)S(1)}, f32[30,2,32,128]{3,2,1,...) custom-call(f32[4,16,2,8,128]{4,3,2,1,0:T(8,128)S(1)} %get-tuple-ele, ...), custom_call_target="tpu_custom_call" | custom-call | bytes 9000000 | tf_op jit(solution)/shard_map/pallas_call | solution.py:791
  20.8 0.0 collective-permute-done.5.zsides
  20.8 3.4 %shard_map.53 = (f32[30,2,32,128]{3,2,1,0:T(8,128)S(1)}, f32[30,2,32,128]{3,2,1,0:T(8,128)S(1)}, f32[30,2,32,128]{3,2,1,0:T(8,128)S(1)}, f32[30,2,32,128]{3,2,1,...) custom-call(f32[8,13,8,128]{3,2,1,0:T(8,128)S(1)} %constant_dynamic-, ...), custom_call_target="tpu_custom_call", output_to_operand_aliasing={{0}: (2, {}), {1}: (3, {}), {2}: (4, {}), {3}: (5, {}), {4}... | custom-call | tf_op jit(solution)/shard_map/pallas_call | solution.py:795
  24.2 2.4 %collective-permute-start.7 = (f32[144,128]{1,0:T(8,128)S(1)}, f32[144,128]{1,0:T(8,128)S(1)}, u32[]{:S(2)}, u32[]{:S(2)}) collective-permute-start(f32[144,128]{1,0:T(8,128)S(1)} %get-tuple-element.73), channel_id=1, source_target_pairs={{0,8},{8,0},{24,16},{16,24},{18,2},{2,18},{10,26},{26,10},{28,20},... | collective-permute-start | bytes 221192 | tf_op jit(solution)/shard_map/ppermute | solution.py:747
  26.6 1.7 %collective-permute-start.9 = (f32[80,128]{1,0:T(8,128)S(1)}, f32[80,128]{1,0:T(8,128)S(1)}, u32[]{:S(2)}, u32[]{:S(2)}) collective-permute-start(f32[80,128]{1,0:T(8,128)S(1)} %get-tuple-element.74.pack), channel_id=1, source_target_pairs={{0,16},{8,18},{24,2},{16,0},{18,8},{2,24},{10,20},{26,4},{28,12},{... | collective-permute-start | bytes 122888 | tf_op jit(solution)/shard_map/ppermute | solution.py:747
  28.4 2.1 %collective-permute-start.8 = (f32[80,128]{1,0:T(8,128)S(1)}, f32[80,128]{1,0:T(8,128)S(1)}, u32[]{:S(2)}, u32[]{:S(2)}) collective-permute-start(f32[80,128]{1,0:T(8,128)S(1)} %get-tuple-element.74.pack), channel_id=1, source_target_pairs={{0,24},{8,16},{24,0},{16,8},{18,10},{2,26},{10,18},{26,2},{28,4},{... | collective-permute-start | bytes 122888 | tf_op jit(solution)/shard_map/ppermute | solution.py:747
  30.5 0.0 collective-permute-done.7
  30.5 2.8 %collective-permute-done.8 = f32[80,128]{1,0:T(8,128)S(1)} collective-permute-done((f32[80,128]{1,0:T(8,128)S(1)}, f32[80,128]{1,0:T(8,128)S(1)}, u32[]{:S(2)}, u32[]{:S(2)}) %collective-permute-start.8) | collective-permute-done | bytes 40992 | tf_op jit(solution)/shard_map/ppermute | solution.py:747
  33.3 0.0 collective-permute-done.9
  33.3 0.1 collective-permute-start.10
  33.4 0.3 shard_map.54
  33.7 1.0 %collective-permute-done.10.theirs = f32[304,128]{1,0:T(8,128)S(1)} collective-permute-done((f32[304,128]{1,0:T(8,128)S(1)}, f32[304,128]{1,0:T(8,128)S(1)}, u32[]{:S(2)}, u32[]{:S(2)}) %collective-permute-start.10) | collective-permute-done | bytes 155680 | tf_op jit(solution)/shard_map/ppermute | solution.py:698
  34.8 3.4 %shard_map.55 = (f32[4,16,2,8,128]{4,3,2,1,0:T(8,128)S(1)}, f32[29,2,8,128]{3,2,1,0:T(8,128)S(1)}, f32[29,2,8,128]{3,2,1,0:T(8,128)S(1)}, f32[29,2,8,128]{3,2,1,...) custom-call(f32[304,128]{1,0:T(8,128)S(1)} %collective-permute-done., ...), custom_call_target="tpu_custom_call", output_to_operand_aliasing={{1}: (1, {}), {2}: (2, {}), {3}: (3, {}), {4}: (4, {}), {5}... | custom-call | tf_op jit(solution)/shard_map/pallas_call | solution.py:811
  38.3 1.2 %collective-permute-start.12 = (f32[256,128]{1,0:T(8,128)S(1)}, f32[256,128]{1,0:T(8,128)S(1)}, u32[]{:S(2)}, u32[]{:S(2)}) collective-permute-start(f32[256,128]{1,0:T(8,128)S(1)} %bitcast.15), channel_id=1, source_target_pairs={{0,16},{1,17},{8,24},{9,25},{16,0},{17,1},{24,8},{25,9},{2,18},{3,... | collective-permute-start | bytes 393224 | tf_op jit(solution)/shard_map/ppermute | solution.py:713
  39.5 2.6 %collective-permute-start.13 = (f32[256,128]{1,0:T(8,128)S(1)}, f32[256,128]{1,0:T(8,128)S(1)}, u32[]{:S(2)}, u32[]{:S(2)}) collective-permute-start(f32[256,128]{1,0:T(8,128)S(1)} %bitcast.14), channel_id=1, source_target_pairs={{0,24},{1,25},{8,16},{9,17},{16,8},{17,9},{24,0},{25,1},{2,26},{3,... | collective-permute-start | bytes 393224 | tf_op jit(solution)/shard_map/ppermute | solution.py:713
  42.1 0.0 collective-permute-start.11
  42.1 4.5 %collective-permute-done.12.refs_2_ = f32[256,128]{1,0:T(8,128)S(1)} collective-permute-done((f32[256,128]{1,0:T(8,128)S(1)}, f32[256,128]{1,0:T(8,128)S(1)}, u32[]{:S(2)}, u32[]{:S(2)}) %collective-permute-start.12) | collective-permute-done | bytes 131104 | tf_op jit(solution)/shard_map/ppermute | solution.py:713
  46.6 0.2 collective-permute-done.13.refs_3_
  46.8 1.1 %collective-permute-done.11.refs_1_ = f32[256,128]{1,0:T(8,128)S(1)} collective-permute-done((f32[256,128]{1,0:T(8,128)S(1)}, f32[256,128]{1,0:T(8,128)S(1)}, u32[]{:S(2)}, u32[]{:S(2)}) %collective-permute-start.11) | collective-permute-done | bytes 131104 | tf_op jit(solution)/shard_map/ppermute | solution.py:713
  47.9 0.9 %shard_map.56 = (f32[1,8,64,128]{3,2,1,0:T(8,128)}, f32[1,8,64,128]{3,2,1,0:T(8,128)}) custom-call(f32[256,128]{1,0:T(8,128)S(1)} %bitcast.8, f32[256,128]{1,0:T(8,128)S(1)} %collective-permute-done.11.refs_1_, f32[256,128]{1,0:T(8,128)S(1)} %collective-permute-done.12.refs_2_, f32[256,128]{1,0:T(8,128)S(1)} %collective-permute-done.13.refs_3_), custom_call_target="tpu_custom_call" | custom-call | tf_op jit(solution)/shard_map/pallas_call | solution.py:819
  (6 shorter events, 0.1 us)
Async XLA Ops:
  1.9 8.3 %collective-permute-start = (f32[256,128]{1,0:T(8,128)S(1)}, f32[256,128]{1,0:T(8,128)S(1)}, u32[]{:S(2)}, u32[]{:S(2)}) collective-permute-start(f32[256,128]{1,0:T(8,128)S(1)} %get-tuple-element.51), channel_id=1, source_target_pairs={{0,24},{1,25},{8,16},{9,17},{16,8},{17,9},{24,0},{25,1},{2,26},{3,... | collective-permute-start | bytes 393224 | tf_op jit(solution)/shard_map/ppermute | solution.py:713
  5.8 6.6 %collective-permute-start.1 = (f32[256,128]{1,0:T(8,128)S(1)}, f32[256,128]{1,0:T(8,128)S(1)}, u32[]{:S(2)}, u32[]{:S(2)}) collective-permute-start(f32[256,128]{1,0:T(8,128)S(1)} %get-tuple-element.52), channel_id=1, source_target_pairs={{0,8},{1,9},{8,0},{9,1},{16,24},{17,25},{24,16},{25,17},{2,10},{3,... | collective-permute-start | bytes 393224 | tf_op jit(solution)/shard_map/ppermute | solution.py:713
  6.4 6.0 %collective-permute-start.2 = (f32[256,128]{1,0:T(8,128)S(1)}, f32[256,128]{1,0:T(8,128)S(1)}, u32[]{:S(2)}, u32[]{:S(2)}) collective-permute-start(f32[256,128]{1,0:T(8,128)S(1)} %get-tuple-element.53), channel_id=1, source_target_pairs={{0,16},{1,17},{8,24},{9,25},{16,0},{17,1},{24,8},{25,9},{2,18},{3,... | collective-permute-start | bytes 393224 | tf_op jit(solution)/shard_map/ppermute | solution.py:713
  12.5 6.3 %collective-permute-start.3 = (f32[4,13,8,128]{3,2,1,0:T(8,128)S(1)}, f32[4,13,8,128]{3,2,1,0:T(8,128)S(1)}, u32[]{:S(2)}, u32[]{:S(2)}) collective-permute-start(f32[4,13,8,128]{3,2,1,0:T(8,128)S(1)} %get-tuple-element.54), channel_id=1, source_target_pairs={{0,8},{1,9},{8,0},{9,1},{24,16},{25,17},{16,24},{17,25},{18,2},{19... | collective-permute-start | bytes 638984 | tf_op jit(solution)/shard_map/ppermute | solution.py:731
  14.0 4.8 %collective-permute-start.4 = (f32[4,13,8,128]{3,2,1,0:T(8,128)S(1)}, f32[4,13,8,128]{3,2,1,0:T(8,128)S(1)}, u32[]{:S(2)}, u32[]{:S(2)}) collective-permute-start(f32[4,13,8,128]{3,2,1,0:T(8,128)S(1)} %get-tuple-element.55), channel_id=1, source_target_pairs={{0,1},{1,0},{8,24},{9,25},{24,8},{25,9},{16,18},{17,19},{18,16},{1... | collective-permute-start | bytes 638984 | tf_op jit(solution)/shard_map/ppermute | solution.py:731
  14.0 4.9 %collective-permute-start.6 = (f32[4,16,2,8,128]{4,3,2,1,0:T(8,128)S(1)}, f32[4,16,2,8,128]{4,3,2,1,0:T(8,128)S(1)}, u32[]{:S(2)}, u32[]{:S(2)}) collective-permute-start(f32[4,16,2,8,128]{4,3,2,1,0:T(8,128)S(1)} %get-tuple-element.56.c), channel_id=1, source_target_pairs={{0,1},{1,0},{2,3},{3,2},{4,5},{5,4},{6,7},{7,6},{8,9},{9,8},{10,11... | collective-permute-start | bytes 1572872 | tf_op jit(solution)/shard_map/ppermute | solution.py:698
  18.8 2.0 %collective-permute-start.5 = (f32[8,13,8,128]{3,2,1,0:T(8,128)S(1)}, f32[8,13,8,128]{3,2,1,0:T(8,128)S(1)}, u32[]{:S(2)}, u32[]{:S(2)}) collective-permute-start(f32[8,13,8,128]{3,2,1,0:T(8,128)S(1)} %constant_dynamic-update-slice_fusion.sides), channel_id=1, source_target_pairs={{0,1},{1,0},{2,3},{3,2},{4,5},{5,4},{6,7},{7,6},{8,9},{9,8},{10,11... | collective-permute-start | bytes 1277960 | tf_op jit(solution)/shard_map/ppermute | solution.py:698
  24.2 6.3 %collective-permute-start.7 = (f32[144,128]{1,0:T(8,128)S(1)}, f32[144,128]{1,0:T(8,128)S(1)}, u32[]{:S(2)}, u32[]{:S(2)}) collective-permute-start(f32[144,128]{1,0:T(8,128)S(1)} %get-tuple-element.73), channel_id=1, source_target_pairs={{0,8},{8,0},{24,16},{16,24},{18,2},{2,18},{10,26},{26,10},{28,20},... | collective-permute-start | bytes 221192 | tf_op jit(solution)/shard_map/ppermute | solution.py:747
  26.6 6.7 %collective-permute-start.9 = (f32[80,128]{1,0:T(8,128)S(1)}, f32[80,128]{1,0:T(8,128)S(1)}, u32[]{:S(2)}, u32[]{:S(2)}) collective-permute-start(f32[80,128]{1,0:T(8,128)S(1)} %get-tuple-element.74.pack), channel_id=1, source_target_pairs={{0,16},{8,18},{24,2},{16,0},{18,8},{2,24},{10,20},{26,4},{28,12},{... | collective-permute-start | bytes 122888 | tf_op jit(solution)/shard_map/ppermute | solution.py:747
  28.4 4.9 %collective-permute-start.8 = (f32[80,128]{1,0:T(8,128)S(1)}, f32[80,128]{1,0:T(8,128)S(1)}, u32[]{:S(2)}, u32[]{:S(2)}) collective-permute-start(f32[80,128]{1,0:T(8,128)S(1)} %get-tuple-element.74.pack), channel_id=1, source_target_pairs={{0,24},{8,16},{24,0},{16,8},{18,10},{2,26},{10,18},{26,2},{28,4},{... | collective-permute-start | bytes 122888 | tf_op jit(solution)/shard_map/ppermute | solution.py:747
  33.3 1.4 %collective-permute-start.10 = (f32[304,128]{1,0:T(8,128)S(1)}, f32[304,128]{1,0:T(8,128)S(1)}, u32[]{:S(2)}, u32[]{:S(2)}) collective-permute-start(f32[304,128]{1,0:T(8,128)S(1)} %constant_dynamic-update-slice_fusion.2.mine), channel_id=1, source_target_pairs={{0,1},{1,0},{2,3},{3,2},{4,5},{5,4},{6,7},{7,6},{8,9},{9,8},{10,11... | collective-permute-start | bytes 466952 | tf_op jit(solution)/shard_map/ppermute | solution.py:698
  38.3 8.3 %collective-permute-start.12 = (f32[256,128]{1,0:T(8,128)S(1)}, f32[256,128]{1,0:T(8,128)S(1)}, u32[]{:S(2)}, u32[]{:S(2)}) collective-permute-start(f32[256,128]{1,0:T(8,128)S(1)} %bitcast.15), channel_id=1, source_target_pairs={{0,16},{1,17},{8,24},{9,25},{16,0},{17,1},{24,8},{25,9},{2,18},{3,... | collective-permute-start | bytes 393224 | tf_op jit(solution)/shard_map/ppermute | solution.py:713
  39.5 7.3 %collective-permute-start.13 = (f32[256,128]{1,0:T(8,128)S(1)}, f32[256,128]{1,0:T(8,128)S(1)}, u32[]{:S(2)}, u32[]{:S(2)}) collective-permute-start(f32[256,128]{1,0:T(8,128)S(1)} %bitcast.14), channel_id=1, source_target_pairs={{0,24},{1,25},{8,16},{9,17},{16,8},{17,9},{24,0},{25,1},{2,26},{3,... | collective-permute-start | bytes 393224 | tf_op jit(solution)/shard_map/ppermute | solution.py:713
  42.1 5.8 %collective-permute-start.11 = (f32[256,128]{1,0:T(8,128)S(1)}, f32[256,128]{1,0:T(8,128)S(1)}, u32[]{:S(2)}, u32[]{:S(2)}) collective-permute-start(f32[256,128]{1,0:T(8,128)S(1)} %bitcast.13), channel_id=1, source_target_pairs={{0,8},{1,9},{8,0},{9,1},{16,24},{17,25},{24,16},{25,17},{2,10},{3,... | collective-permute-start | bytes 393224 | tf_op jit(solution)/shard_map/ppermute | solution.py:713
